TPU v7x, 32 devices: a whole 2x2x4 slice. The times are simulated.
32 devices in a mesh: sub: 8 (over z, y), grp: 4 (over x, core).
Axes of the slice: x: 2, y: 2, z: 4, core: 2. Of those that a mesh axis runs over, the one named last changes fastest.
Arguments:
- coarse: float32 [768, 128], P(('sub', 'grp')), may hold values from -6 to 6
- corner_idx: int32 [32, 24], P(('sub', 'grp')), may hold values from 0 to 767, as said below
- coupling: bfloat16 [49152, 24], P(('sub', 'grp')), may hold values from -1.25 to 1.25
- force: bfloat16 [16384, 3, 128], P(('sub', 'grp')), may hold values from -6 to 6
- panel_inv: bfloat16 [128, 384, 384], P(('sub', 'grp')), as said below
- panel_nodes: int32 [32, 4], P(('sub', 'grp')), may hold values from 64 to 128, as said below
- strain_disp: bfloat16 [6, 24, 4096], P(None, None, ('sub', 'grp')), may hold values from -1.25 to 1.25
- modulus: float32 [4096], P(('sub', 'grp')), may hold values from 0.5 to 4
- connect: int32 [8, 4096], P(None, ('sub', 'grp')), may hold values from 0 to 511, as said below
- interface: int32 [32, 224], P(('sub', 'grp')), may hold values from 0 to 511, as said below
- nodal_volume: float32 [16384], P(('sub', 'grp')), may hold values from 4 to 16
Outputs:
- displacement: bfloat16 [16384, 3, 128], P(('sub', 'grp'))
- nodal_stress: bfloat16 [16384, 6, 128], P(('sub', 'grp'))
Inputs may be any that keep to these rules, and one draw needn't show every extreme that they name: `corner_idx`: the rows of subdomain (s, g) lie in the coarse blocks of subdomains (s', g') with |s' - s| <= 1 that exist, including blocks of all grp indices; they come in triples of consecutive rows. `panel_nodes`: every subdomain has one panel with exactly 128 live nodes and one with 64. `connect`: every entry is a live node of its subdomain (slot j < panel_nodes of its panel). `interface`: each row holds 224 distinct live nodes as eight lists: sub-lo (64), sub-hi (64), grp-lo (32), grp-hi (32), then edges ll, lh, hl, hh (8 each; first letter the sub side, second the grp side). Entry k of a list of (s, g) is the same physical node as entry k of the facing list of each neighbour: sub-hi with sub-lo of (s + 1, g), grp-hi with grp-lo of (s, g + 1); edge (x, y) with the edge of the neighbour across it that has the opposite letter on each side crossed. `panel_inv`: given inverses of the padded panels.
All inputs are finite; a program needn't handle non-finite values.
Results may differ from a plain program's by a relative error of at most 0.0058.
Values sent between devices are 32-bit elements; how exact they have to be, the bound alone decides.
No kernel may reach another device: no remote copies, remote signals or barrier semaphores. Data moves between devices by JAX's collectives and lax.ppermute only.
A program may use at most 64 MiB of HBM per device.

v0:
```python
import jax
import jax.numpy as jnp
from jax import lax
from jax.sharding import PartitionSpec as P

NIS = 64
NIG = 32
NED = 8


POISSON = 0.3


def padded(block, sides, width):
    for axis, dim in sides:
        count = lax.axis_size(axis)
        forward = [(i, i + 1) for i in range(count - 1)]
        backward = [(target, source) for source, target in forward]
        low = lax.ppermute(
            lax.slice_in_dim(block, block.shape[dim] - width, None, axis=dim), axis, forward
        )
        high = lax.ppermute(lax.slice_in_dim(block, 0, width, axis=dim), axis, backward)
        block = jnp.concatenate([low, block, high], axis=dim)
    return block


def iso_matrix():
    lame_first = POISSON / ((1.0 + POISSON) * (1.0 - 2.0 * POISSON))
    shear_mod = 0.5 / (1.0 + POISSON)
    upper_block = jnp.full((3, 3), lame_first, jnp.float32) + jnp.eye(3, dtype=jnp.float32) * (
        2.0 * shear_mod
    )
    shear_block = jnp.eye(3, dtype=jnp.float32) * shear_mod
    zero_block = jnp.zeros((3, 3), jnp.float32)
    return jnp.concatenate(
        [
            jnp.concatenate([upper_block, zero_block], 1),
            jnp.concatenate([zero_block, shear_block], 1),
        ],
        0,
    )


def shards(
    coarse,
    corner_idx,
    coupling,
    force,
    panel_inv,
    panel_nodes,
    strain_disp,
    modulus,
    connect,
    interface,
    nodal_volume,
):
    group_rows = lax.all_gather(coarse, "grp", axis=0, tiled=True)
    block_rows = group_rows.shape[0]
    nearby = padded(group_rows, (("sub", 0),), block_rows)
    offset = (lax.axis_index("sub") - 1) * block_rows
    local_rows = corner_idx[0] - offset
    selector = (local_rows[:, None] == jnp.arange(3 * block_rows, dtype=jnp.int32)[None, :]).astype(
        jnp.float32
    )
    corner_vals = jnp.dot(selector, nearby, precision=lax.Precision.HIGHEST)
    node_count = force.shape[0]
    load_cases = force.shape[2]
    panels = panel_inv.shape[0]
    panel_rows = panel_inv.shape[1]
    correction = jnp.dot(coupling.astype(jnp.float32), corner_vals, precision=lax.Precision.HIGHEST)
    live_mask = jnp.arange(panel_rows)[None, :] < 3 * panel_nodes[0][:, None]
    reduced = (force.reshape(3 * node_count, load_cases).astype(jnp.float32) - correction).reshape(
        panels, panel_rows, load_cases
    )
    reduced = jnp.where(live_mask[:, :, None], reduced, 0.0).astype(jnp.bfloat16)
    solved = jnp.einsum("prc,pcl->prl", panel_inv, reduced, preferred_element_type=jnp.float32)
    displaced = (
        jnp.where(live_mask[:, :, None], solved, 0.0)
        .astype(jnp.bfloat16)
        .reshape(node_count, 3 * load_cases)
    )
    elem_count = connect.shape[1]
    element = displaced[connect.T].reshape(elem_count, 24, load_cases)
    strain = jnp.einsum("ije,ejl->eil", strain_disp, element, preferred_element_type=jnp.float32)
    stress = (
        jnp.einsum("ik,ekl->eil", iso_matrix(), strain, precision=lax.Precision.HIGHEST)
        * modulus[:, None, None]
    )
    node_range = jnp.arange(node_count, dtype=jnp.int32)
    incidence = jnp.sum(
        (connect[:, None, :] == node_range[None, :, None]).astype(jnp.float32), axis=0
    )
    partial_value = jnp.dot(
        incidence, stress.reshape(elem_count, 6 * load_cases), precision=lax.Precision.HIGHEST
    ).reshape(node_count, 6, load_cases)
    node_ids = interface[0]
    picker = (node_ids[:, None] == node_range[None, :]).astype(jnp.float32)
    iface_rows = jnp.dot(
        picker, partial_value.reshape(node_count, 6 * load_cases), precision=lax.Precision.HIGHEST
    ).reshape(-1, 6, load_cases)
    start_edge = 2 * NIS + 2 * NIG
    faces_sub = iface_rows[: 2 * NIS].reshape(2, NIS, 6, load_cases)
    near_sub = padded(faces_sub, (("sub", 0),), 1)
    faces_sub = faces_sub + jnp.stack([near_sub[0], near_sub[3]])
    faces_grp = iface_rows[2 * NIS : start_edge].reshape(2, NIG, 6, load_cases)
    near_grp = padded(faces_grp, (("grp", 0),), 1)
    faces_grp = faces_grp + jnp.stack([near_grp[0], near_grp[3]])
    edge_block = iface_rows[start_edge:].reshape(2, 2, NED, 6, load_cases)
    beside_all = padded(edge_block, (("sub", 0), ("grp", 1)), 1)
    along_sub = jnp.stack([beside_all[0, 1:3], beside_all[3, 1:3]])
    along_grp = jnp.stack([beside_all[1:3, 0], beside_all[1:3, 3]], axis=1)
    diagonal = jnp.stack(
        [
            jnp.stack([beside_all[0, 0], beside_all[0, 3]]),
            jnp.stack([beside_all[3, 0], beside_all[3, 3]]),
        ]
    )
    edge_block = edge_block + along_sub + along_grp + diagonal
    summed_rows = jnp.concatenate(
        [
            faces_sub.reshape(-1, 6, load_cases),
            faces_grp.reshape(-1, 6, load_cases),
            edge_block.reshape(-1, 6, load_cases),
        ]
    )
    placed = jnp.dot(
        picker.T, summed_rows.reshape(-1, 6 * load_cases), precision=lax.Precision.HIGHEST
    ).reshape(node_count, 6, load_cases)
    on_face = jnp.sum(picker, axis=0) > 0.5
    summed = jnp.where(on_face[:, None, None], placed, partial_value)
    stress_out = (summed / nodal_volume[:, None, None]).astype(jnp.bfloat16)
    return (displaced.reshape(node_count, 3, load_cases), stress_out)


def solution(mesh):
    placed = (
        P(("sub", "grp"), None),
        P(("sub", "grp"), None),
        P(("sub", "grp"), None),
        P(("sub", "grp"), None, None),
        P(("sub", "grp"), None, None),
        P(("sub", "grp"), None),
        P(None, None, ("sub", "grp")),
        P(("sub", "grp")),
        P(None, ("sub", "grp")),
        P(("sub", "grp"), None),
        P(("sub", "grp")),
    )
    return jax.shard_map(
        shards,
        mesh=mesh,
        in_specs=placed,
        out_specs=(P(("sub", "grp"), None, None), P(("sub", "grp"), None, None)),
        check_vma=False,
    )
```

profile of v0, /device:TPU:10, one launch (start us, length us, event | category | flops | bytes accessed | tf_op | source)
XLA Modules:
  0.0 88.5 jit_solution(17429990751475213380)
XLA Ops:
  0.6 5.6 %all_gather.3 = f32[96,128]{1,0:T(8,128)S(1)} all-gather(f32[24,128]{1,0:T(8,128)} %param.11), channel_id=1, replica_groups=mesh['sub'=8,'grp'=4] {'grp'}, dimensions={0}, use_global_device_ids=true | all-gather | bytes 61440 | tf_op jit(solution)/shard_map/all_gather | solution.py:57
  6.2 3.3 %collective-permute-start.1 = (f32[96,128]{1,0:T(8,128)S(1)}, f32[96,128]{1,0:T(8,128)S(1)}, u32[]{:S(2)}, u32[]{:S(2)}) collective-permute-start(f32[96,128]{1,0:T(8,128)S(1)} %all_gather.3), channel_id=1, source_target_pairs={{4,0},{8,4},{12,8},{16,12},{20,16},{24,20},{28,24},{5,1},{9,5},{13... | collective-permute-start | bytes 147464 | tf_op jit(solution)/shard_map/ppermute | solution.py:22
  9.5 2.5 %collective-permute-start = (f32[96,128]{1,0:T(8,128)S(1)}, f32[96,128]{1,0:T(8,128)S(1)}, u32[]{:S(2)}, u32[]{:S(2)}) collective-permute-start(f32[96,128]{1,0:T(8,128)S(1)} %all_gather.3), channel_id=1, source_target_pairs={{0,4},{4,8},{8,12},{12,16},{16,20},{20,24},{24,28},{1,5},{5,9},{9,... | collective-permute-start | bytes 147464 | tf_op jit(solution)/shard_map/ppermute | solution.py:19
  12.1 0.7 compare_select_fusion
  12.8 1.6 %convert_reduce_fusion = f32[512,128]{1,0:T(8,128)} fusion(s32[8,128]{1,0:T(8,128)} %param.19), kind=kLoop, calls=%fused_computation.3 | loop fusion | flops 1507328 | bytes 266240 | tf_op jit(solution)/shard_map/reduce_sum | solution.py:90
  14.4 0.7 multiply_bitcast_fusion
  15.3 0.7 subtract_bitcast_fusion
  16.0 1.6 %copy.35 = bf16[6,24,128]{1,0,2:T(8,128)(2,1)} copy(bf16[6,24,128]{2,1,0:T(8,128)(2,1)} %param.17) | data formatting | bytes 73728 | tf_op args[6]
  17.6 1.3 %copy.29 = f32[512,3,128]{2,1,0:T(4,128)S(1)} copy(bf16[512,3,128]{2,0,1:T(8,128)(2,1)} %param.14) | data formatting | bytes 1179648 | tf_op jit(solution)/shard_map/convert_element_type | solution.py:72
  19.0 1.2 %reshape.111 = f32[1536,128]{1,0:T(8,128)} reshape(f32[512,3,128]{2,1,0:T(4,128)S(1)} %copy.29) | data formatting | bytes 1572864 | tf_op jit(solution)/shard_map/convert_element_type | solution.py:72
  20.2 1.4 %copy.30 = f32[1536,128]{0,1:T(8,128)S(1)} copy(f32[1536,128]{1,0:T(8,128)} %reshape.111) | data formatting | bytes 1572864 | tf_op jit(solution)/shard_map/convert_element_type | solution.py:72
  21.6 0.2 fusion.14
  21.9 0.5 fusion
  22.4 0.5 fusion.3
  22.9 0.2 copy.32
  23.4 3.9 %gather_fusion = bf16[1024,384]{1,0:T(8,128)(2,1)S(1)} fusion(bf16[512,384]{1,0:T(8,128)(2,1)S(1)} %reshape.106, s32[1024]{0:T(1024)S(1)} %broadcast_clamp_fusion), kind=kCustom, calls=%fused_computation | custom fusion | bytes 1576960 | tf_op jit(solution)/shard_map/gather | solution.py:83
  27.3 0.4 reshape.107
  27.7 1.3 %convolution_bitcast_fusion.1 = f32[128,6,128]{2,1,0:T(8,128)S(1)} fusion(bf16[128,24,128]{2,1,0:T(8,128)(2,1)S(1)} %reshape.107, bf16[6,24,128]{1,0,2:T(8,128)(2,1)} %copy.35), kind=kOutput, calls=%fused_computation.10 | convolution fusion | flops 4718592 | bytes 1216512 | tf_op jit(solution)/shard_map/ije,ejl->eil/dot_general | solution.py:84
  29.0 0.7 fusion.2
  29.8 2.3 %fusion.37 = f32[512,768]{1,0:T(8,128)S(1)} fusion(f32[512,128]{1,0:T(8,128)} %convert_reduce_fusion, f32[128,768]{0,1:T(8,128)S(1)} %bitcast.76), kind=kOutput, calls=%fused_computation.75 | convolution fusion | flops 603979776 | bytes 2228224 | tf_op jit(solution)/shard_map/dot_general | solution.py:93
  32.2 1.0 %fusion.6 = f32[224,768]{1,0:T(8,128)S(1)} fusion(f32[512,768]{1,0:T(8,128)S(1)} %fusion.37, s32[224]{0:T(256)S(1)} %bitcast.84), kind=kOutput, calls=%fused_computation.19 | convolution fusion | flops 1057079296 | bytes 2261888 | tf_op jit(solution)/shard_map/dot_general | solution.py:98
  33.2 4.3 %collective-permute-start.6 = (f32[1,2,8,6,128]{4,2,3,1,0:T(8,128)S(1)}, f32[1,2,8,6,128]{4,2,3,1,0:T(8,128)S(1)}, u32[]{:S(2)}, u32[]{:S(2)}) collective-permute-start(f32[1,2,8,6,128]{4,2,3,1,0:T(8,128)S(1)} %get-tuple-element.12), channel_id=1, source_target_pairs={{0,4},{4,8},{8,12},{12,16},{16,20},{20,24},{24,28},{1,5},{5,9},{9,... | collective-permute-start | bytes 147464 | tf_op jit(solution)/shard_map/ppermute | solution.py:19
  37.5 2.4 %collective-permute-start.7 = (f32[1,2,8,6,128]{4,2,3,1,0:T(8,128)S(1)}, f32[1,2,8,6,128]{4,2,3,1,0:T(8,128)S(1)}, u32[]{:S(2)}, u32[]{:S(2)}) collective-permute-start(f32[1,2,8,6,128]{4,2,3,1,0:T(8,128)S(1)} %get-tuple-element.13), channel_id=1, source_target_pairs={{4,0},{8,4},{12,8},{16,12},{20,16},{24,20},{28,24},{5,1},{9,5},{13... | collective-permute-start | bytes 147464 | tf_op jit(solution)/shard_map/ppermute | solution.py:22
  40.1 3.4 %collective-permute-done.7 = f32[1,2,8,6,128]{4,2,3,1,0:T(8,128)S(1)} collective-permute-done((f32[1,2,8,6,128]{4,2,3,1,0:T(8,128)S(1)}, f32[1,2,8,6,128]{4,2,3,1,0:T(8,128)S(1)}, u32[]{:S(2)}, u32[]{:S(2)}) %collective-permute-start.7) | collective-permute-done | bytes 49184 | tf_op jit(solution)/shard_map/ppermute | solution.py:22
  43.5 1.9 %collective-permute-start.8 = (f32[4,1,8,6,128]{4,2,3,1,0:T(8,128)S(1)}, f32[4,1,8,6,128]{4,2,3,1,0:T(8,128)S(1)}, u32[]{:S(2)}, u32[]{:S(2)}) collective-permute-start(f32[4,1,8,6,128]{4,2,3,1,0:T(8,128)S(1)} %get-tuple-element.14), channel_id=1, source_target_pairs={{0,1},{1,2},{2,3},{4,5},{5,6},{6,7},{8,9},{9,10},{10,11},{12,13},{... | collective-permute-start | bytes 294920 | tf_op jit(solution)/shard_map/ppermute | solution.py:19
  45.5 3.6 %collective-permute-start.9 = (f32[4,1,8,6,128]{4,2,3,1,0:T(8,128)S(1)}, f32[4,1,8,6,128]{4,2,3,1,0:T(8,128)S(1)}, u32[]{:S(2)}, u32[]{:S(2)}) collective-permute-start(f32[4,1,8,6,128]{4,2,3,1,0:T(8,128)S(1)} %get-tuple-element.15), channel_id=1, source_target_pairs={{1,0},{2,1},{3,2},{5,4},{6,5},{7,6},{9,8},{10,9},{11,10},{13,12},{... | collective-permute-start | bytes 294920 | tf_op jit(solution)/shard_map/ppermute | solution.py:22
  49.1 0.3 collective-permute-done.8
  49.5 1.8 %collective-permute-done.9 = f32[4,1,8,6,128]{4,2,3,1,0:T(8,128)S(1)} collective-permute-done((f32[4,1,8,6,128]{4,2,3,1,0:T(8,128)S(1)}, f32[4,1,8,6,128]{4,2,3,1,0:T(8,128)S(1)}, u32[]{:S(2)}, u32[]{:S(2)}) %collective-permute-start.9) | collective-permute-done | bytes 98336 | tf_op jit(solution)/shard_map/ppermute | solution.py:22
  51.4 0.7 fusion.35
  52.1 1.6 %slice.85 = f32[1,32,6,128]{3,2,1,0:T(8,128)} reshape(f32[32,768]{1,0:T(8,128)} %get-tuple-element.9) | data formatting | bytes 196608 | tf_op jit(solution)/shard_map/slice | solution.py:20
  53.7 0.7 slice.87
  54.3 3.7 %collective-permute-start.5 = (f32[1,32,6,128]{3,2,1,0:T(8,128)}, f32[1,32,6,128]{3,2,1,0:T(8,128)S(1)}, u32[]{:S(2)}, u32[]{:S(2)}) collective-permute-start(f32[1,32,6,128]{3,2,1,0:T(8,128)} %slice.87), channel_id=1, source_target_pairs={{1,0},{2,1},{3,2},{5,4},{6,5},{7,6},{9,8},{10,9},{11,10},{13,12},{... | collective-permute-start | bytes 294920 | tf_op jit(solution)/shard_map/ppermute | solution.py:22
  58.1 1.9 %collective-permute-start.4 = (f32[1,32,6,128]{3,2,1,0:T(8,128)}, f32[1,32,6,128]{3,2,1,0:T(8,128)S(1)}, u32[]{:S(2)}, u32[]{:S(2)}) collective-permute-start(f32[1,32,6,128]{3,2,1,0:T(8,128)} %slice.85), channel_id=1, source_target_pairs={{0,1},{1,2},{2,3},{4,5},{5,6},{6,7},{8,9},{9,10},{10,11},{12,13},{... | collective-permute-start | bytes 294920 | tf_op jit(solution)/shard_map/ppermute | solution.py:19
  60.1 0.8 collective-permute-done.5
  60.9 3.7 %collective-permute-done.4 = f32[1,32,6,128]{3,2,1,0:T(8,128)S(1)} collective-permute-done((f32[1,32,6,128]{3,2,1,0:T(8,128)}, f32[1,32,6,128]{3,2,1,0:T(8,128)S(1)}, u32[]{:S(2)}, u32[]{:S(2)}) %collective-permute-start.4) | collective-permute-done | bytes 98336 | tf_op jit(solution)/shard_map/ppermute | solution.py:19
  64.6 0.9 fusion.34
  65.4 1.7 %slice.80 = f32[1,64,6,128]{3,2,1,0:T(8,128)} reshape(f32[64,768]{1,0:T(8,128)} %get-tuple-element.6) | data formatting | bytes 393216 | tf_op jit(solution)/shard_map/slice | solution.py:20
  67.1 1.7 %slice.82 = f32[1,64,6,128]{3,2,1,0:T(8,128)} reshape(f32[64,768]{1,0:T(8,128)} %get-tuple-element.8) | data formatting | bytes 393216 | tf_op jit(solution)/shard_map/slice | solution.py:22
  68.8 3.3 %collective-permute-start.3 = (f32[1,64,6,128]{3,2,1,0:T(8,128)}, f32[1,64,6,128]{3,2,1,0:T(8,128)}, u32[]{:S(2)}, u32[]{:S(2)}) collective-permute-start(f32[1,64,6,128]{3,2,1,0:T(8,128)} %slice.82), channel_id=1, source_target_pairs={{4,0},{8,4},{12,8},{16,12},{20,16},{24,20},{28,24},{5,1},{9,5},{13... | collective-permute-start | bytes 589832 | tf_op jit(solution)/shard_map/ppermute | solution.py:22
  72.1 2.5 %collective-permute-start.2 = (f32[1,64,6,128]{3,2,1,0:T(8,128)}, f32[1,64,6,128]{3,2,1,0:T(8,128)}, u32[]{:S(2)}, u32[]{:S(2)}) collective-permute-start(f32[1,64,6,128]{3,2,1,0:T(8,128)} %slice.80), channel_id=1, source_target_pairs={{0,4},{4,8},{8,12},{12,16},{16,20},{20,24},{24,28},{1,5},{5,9},{9,... | collective-permute-start | bytes 589832 | tf_op jit(solution)/shard_map/ppermute | solution.py:19
  74.6 2.1 %reshape_reshape.3 = bf16[512,3,128]{2,1,0:T(4,128)(2,1)} reshape(bf16[4,384,128]{2,1,0:T(8,128)(2,1)} %copy-done.1) | data formatting | bytes 786432 | tf_op jit(solution)/shard_map/reshape;reshape | solution.py:132
  76.7 1.6 %copy.39 = f32[512,768]{0,1:T(8,128)} copy(f32[512,768]{1,0:T(8,128)S(1)} %fusion.37) | data formatting | bytes 3145728 | tf_op jit(solution)/shard_map/dot_general | solution.py:93
  78.4 1.8 %copy.41 = bf16[512,3,128]{2,0,1:T(8,128)(2,1)} copy(bf16[512,3,128]{2,1,0:T(4,128)(2,1)} %reshape_reshape.3) | data formatting | bytes 786432
  80.2 1.9 %copy.40 = f32[512,6,128]{2,0,1:T(8,128)S(1)} copy(f32[512,6,128]{0,2,1:T(8,128)} %bitcast.74) | data formatting | bytes 3145728 | tf_op jit(solution)/shard_map/reshape | solution.py:95
  82.1 0.8 collective-permute-done.3
  82.9 1.1 %pad_maximum_fusion = f32[2,64,6,128]{3,2,1,0:T(8,128)S(1)} fusion(f32[1,64,6,128]{3,2,1,0:T(8,128)} %collective-permute-done.3, f32[1,64,6,128]{3,2,1,0:T(8,128)} %collective-permute-done.2), kind=kLoop, calls=%fused_computation.15 | loop fusion | flops 98304 | bytes 786432 | tf_op jit(solution)/shard_map/stack | solution.py:104
  84.2 1.2 %copy.37 = f32[768,224]{1,0:T(8,128)} copy(f32[768,224]{0,1:T(8,128)S(1)} %maximum_bitcast_fusion) | data formatting | bytes 1376256 | tf_op jit(solution)/shard_map/dot_general | solution.py:126
  85.4 3.2 %divide_convert_fusion = bf16[512,6,128]{2,0,1:T(8,128)(2,1)} fusion(f32[512,6,128]{2,0,1:T(8,128)S(1)} %copy.40, f32[6,128,224]{2,1,0:T(8,128)} %bitcast.78, f32[512]{0:T(512)S(1)} %copy-done.7, pred[512]{0:T(512)(128)(4,1)S(1)} %broadcast_compare_fusion, s32[224]{0:T(256)S(1)} %bitcast.86), kind=kOutput, calls=%fused_computation.5 | convolution fusion | flops 1058373632 | bytes 3050880 | tf_op jit(solution)/shard_map/dot_general | solution.py:126
  (45 shorter events, 1.2 us)
Async XLA Ops:
  0.6 21.8 %copy-start = (bf16[4,384,384]{2,1,0:T(8,128)(2,1)S(1)}, bf16[4,384,384]{2,1,0:T(8,128)(2,1)}, u32[]{:S(2)}) copy-start(bf16[4,384,384]{2,1,0:T(8,128)(2,1)} %param.15) | copy-start | bytes 3538948
  6.2 15.4 %collective-permute-start.1 = (f32[96,128]{1,0:T(8,128)S(1)}, f32[96,128]{1,0:T(8,128)S(1)}, u32[]{:S(2)}, u32[]{:S(2)}) collective-permute-start(f32[96,128]{1,0:T(8,128)S(1)} %all_gather.3), channel_id=1, source_target_pairs={{4,0},{8,4},{12,8},{16,12},{20,16},{24,20},{28,24},{5,1},{9,5},{13... | collective-permute-start | bytes 147464 | tf_op jit(solution)/shard_map/ppermute | solution.py:22
  9.5 12.1 %collective-permute-start = (f32[96,128]{1,0:T(8,128)S(1)}, f32[96,128]{1,0:T(8,128)S(1)}, u32[]{:S(2)}, u32[]{:S(2)}) collective-permute-start(f32[96,128]{1,0:T(8,128)S(1)} %all_gather.3), channel_id=1, source_target_pairs={{0,4},{4,8},{8,12},{12,16},{16,20},{20,24},{24,28},{1,5},{5,9},{9,... | collective-permute-start | bytes 147464 | tf_op jit(solution)/shard_map/ppermute | solution.py:19
  19.0 2.9 %copy-start.4 = (bf16[1536,24]{0,1:T(8,128)(2,1)S(1)}, bf16[1536,24]{0,1:T(8,128)(2,1)}, u32[]{:S(2)}) copy-start(bf16[1536,24]{0,1:T(8,128)(2,1)} %param.13) | copy-start | bytes 221188
  23.1 4.1 %copy-start.1 = (bf16[4,384,128]{2,1,0:T(8,128)(2,1)}, bf16[4,384,128]{2,1,0:T(8,128)(2,1)S(1)}, u32[]{:S(2)}) copy-start(bf16[4,384,128]{2,1,0:T(8,128)(2,1)S(1)} %copy.32) | copy-start | bytes 1179652
  27.3 1.7 %copy-start.6 = (f32[128]{0:T(128)S(1)}, f32[128]{0:T(128)}, u32[]{:S(2)}) copy-start(f32[128]{0:T(128)} %param.18) | copy-start | bytes 1540
  29.6 2.6 %copy-start.5 = (s32[1,224]{1,0:T(1,128)S(1)}, s32[1,224]{1,0:T(1,128)}, u32[]{:S(2)}) copy-start(s32[1,224]{1,0:T(1,128)} %param.20) | copy-start | bytes 2692
  33.2 6.9 %collective-permute-start.6 = (f32[1,2,8,6,128]{4,2,3,1,0:T(8,128)S(1)}, f32[1,2,8,6,128]{4,2,3,1,0:T(8,128)S(1)}, u32[]{:S(2)}, u32[]{:S(2)}) collective-permute-start(f32[1,2,8,6,128]{4,2,3,1,0:T(8,128)S(1)} %get-tuple-element.12), channel_id=1, source_target_pairs={{0,4},{4,8},{8,12},{12,16},{16,20},{20,24},{24,28},{1,5},{5,9},{9,... | collective-permute-start | bytes 147464 | tf_op jit(solution)/shard_map/ppermute | solution.py:19
  37.5 6.0 %collective-permute-start.7 = (f32[1,2,8,6,128]{4,2,3,1,0:T(8,128)S(1)}, f32[1,2,8,6,128]{4,2,3,1,0:T(8,128)S(1)}, u32[]{:S(2)}, u32[]{:S(2)}) collective-permute-start(f32[1,2,8,6,128]{4,2,3,1,0:T(8,128)S(1)} %get-tuple-element.13), channel_id=1, source_target_pairs={{4,0},{8,4},{12,8},{16,12},{20,16},{24,20},{28,24},{5,1},{9,5},{13... | collective-permute-start | bytes 147464 | tf_op jit(solution)/shard_map/ppermute | solution.py:22
  43.5 5.9 %collective-permute-start.8 = (f32[4,1,8,6,128]{4,2,3,1,0:T(8,128)S(1)}, f32[4,1,8,6,128]{4,2,3,1,0:T(8,128)S(1)}, u32[]{:S(2)}, u32[]{:S(2)}) collective-permute-start(f32[4,1,8,6,128]{4,2,3,1,0:T(8,128)S(1)} %get-tuple-element.14), channel_id=1, source_target_pairs={{0,1},{1,2},{2,3},{4,5},{5,6},{6,7},{8,9},{9,10},{10,11},{12,13},{... | collective-permute-start | bytes 294920 | tf_op jit(solution)/shard_map/ppermute | solution.py:19
  45.5 5.8 %collective-permute-start.9 = (f32[4,1,8,6,128]{4,2,3,1,0:T(8,128)S(1)}, f32[4,1,8,6,128]{4,2,3,1,0:T(8,128)S(1)}, u32[]{:S(2)}, u32[]{:S(2)}) collective-permute-start(f32[4,1,8,6,128]{4,2,3,1,0:T(8,128)S(1)} %get-tuple-element.15), channel_id=1, source_target_pairs={{1,0},{2,1},{3,2},{5,4},{6,5},{7,6},{9,8},{10,9},{11,10},{13,12},{... | collective-permute-start | bytes 294920 | tf_op jit(solution)/shard_map/ppermute | solution.py:22
  54.3 6.5 %collective-permute-start.5 = (f32[1,32,6,128]{3,2,1,0:T(8,128)}, f32[1,32,6,128]{3,2,1,0:T(8,128)S(1)}, u32[]{:S(2)}, u32[]{:S(2)}) collective-permute-start(f32[1,32,6,128]{3,2,1,0:T(8,128)} %slice.87), channel_id=1, source_target_pairs={{1,0},{2,1},{3,2},{5,4},{6,5},{7,6},{9,8},{10,9},{11,10},{13,12},{... | collective-permute-start | bytes 294920 | tf_op jit(solution)/shard_map/ppermute | solution.py:22
  58.1 6.5 %collective-permute-start.4 = (f32[1,32,6,128]{3,2,1,0:T(8,128)}, f32[1,32,6,128]{3,2,1,0:T(8,128)S(1)}, u32[]{:S(2)}, u32[]{:S(2)}) collective-permute-start(f32[1,32,6,128]{3,2,1,0:T(8,128)} %slice.85), channel_id=1, source_target_pairs={{0,1},{1,2},{2,3},{4,5},{5,6},{6,7},{8,9},{9,10},{10,11},{12,13},{... | collective-permute-start | bytes 294920 | tf_op jit(solution)/shard_map/ppermute | solution.py:19
  68.8 14.1 %collective-permute-start.3 = (f32[1,64,6,128]{3,2,1,0:T(8,128)}, f32[1,64,6,128]{3,2,1,0:T(8,128)}, u32[]{:S(2)}, u32[]{:S(2)}) collective-permute-start(f32[1,64,6,128]{3,2,1,0:T(8,128)} %slice.82), channel_id=1, source_target_pairs={{4,0},{8,4},{12,8},{16,12},{20,16},{24,20},{28,24},{5,1},{9,5},{13... | collective-permute-start | bytes 589832 | tf_op jit(solution)/shard_map/ppermute | solution.py:22
  72.1 10.8 %collective-permute-start.2 = (f32[1,64,6,128]{3,2,1,0:T(8,128)}, f32[1,64,6,128]{3,2,1,0:T(8,128)}, u32[]{:S(2)}, u32[]{:S(2)}) collective-permute-start(f32[1,64,6,128]{3,2,1,0:T(8,128)} %slice.80), channel_id=1, source_target_pairs={{0,4},{4,8},{8,12},{12,16},{16,20},{20,24},{24,28},{1,5},{5,9},{9,... | collective-permute-start | bytes 589832 | tf_op jit(solution)/shard_map/ppermute | solution.py:19
  82.1 2.0 %copy-start.2 = (f32[64,768]{1,0:T(8,128)S(1)}, f32[64,768]{1,0:T(8,128)}, u32[]{:S(2)}) copy-start(f32[64,768]{1,0:T(8,128)} %get-tuple-element.7) | copy-start | bytes 589828
  82.1 2.0 %copy-start.3 = (f32[32,768]{1,0:T(8,128)S(1)}, f32[32,768]{1,0:T(8,128)}, u32[]{:S(2)}) copy-start(f32[32,768]{1,0:T(8,128)} %get-tuple-element.10) | copy-start | bytes 294916
  84.1 1.2 %copy-start.7 = (f32[512]{0:T(512)S(1)}, f32[512]{0:T(512)}, u32[]{:S(2)}) copy-start(f32[512]{0:T(512)} %param.21) | copy-start | bytes 6148
where the time goes:
time: 90 us; the launch traced here: 88.5 us
  starting transfers between devices  29.6 us (33%)
  local copies, waits for them, and re-layouts  24.9 us (28%)
  waiting for transfers between devices  11 us (12%)
  matrix products  9.65 us (11%)
  other arithmetic  6.72 us (7%)
  blocking collectives  5.57 us (6%)
  between operations  1.08 us (1%)
    ppermute x5, starting transfers between devices, padded(): lax.ppermute(lax.slice_in_dim(block, 0, width, axis=dim), axis, backward)  16.4 us
    ppermute x5, starting transfers between devices, padded(): lax.ppermute(lax.slice_in_dim(block, block.shape[dim] - width, None, axis...  13.2 us
    ppermute x5, waiting for transfers between devices, padded(): lax.ppermute(lax.slice_in_dim(block, 0, width, axis=dim), axis, backward)  6.83 us
    all_gather x1, blocking collectives, shards(): group_rows = lax.all_gather(coarse, 'grp', axis=0, tiled=True)  5.57 us
    ppermute x5, waiting for transfers between devices, padded(): lax.ppermute(lax.slice_in_dim(block, block.shape[dim] - width, None, axis...  4.14 us
    convert_element_type x3, local copies, waits for them, and re-layouts, shards(): force.reshape(3 * node_count, load_cases).astype(jnp.float32) - correction  3.97 us
    gather x1, local copies, waits for them, and re-layouts, shards(): element = displaced[connect.T].reshape(elem_count, 24, load_cases)  3.92 us
    unnamed x18, local copies, waits for them, and re-layouts  3.52 us
  transfers between devices with their start and end apart: 10, of which 7 were waited for; matrix products, arithmetic and copies ran while one was open for 19% of the time, Pallas kernels for 0%

commit v1 on v0

v1 whole, which is shorter than its diff:
```python
import functools

import jax
import jax.numpy as jnp
from jax import lax
from jax.experimental import pallas as pl
from jax.experimental.pallas import tpu as pltpu
from jax.sharding import PartitionSpec as P

NIS = 64
NIG = 32
NED = 8
EDGES = 2 * NIS + 2 * NIG
NIF = EDGES + 4 * NED
CORNERS = 8
COMPS = 6
LANES = 128

POISSON = 0.3
LAME = POISSON / ((1.0 + POISSON) * (1.0 - 2.0 * POISSON))
SHEAR = 0.5 / (1.0 + POISSON)

F32 = jnp.float32
BF16 = jnp.bfloat16
VMEM_LIMIT = 24 * 1024 * 1024


def split_two(x):
    high = x.astype(BF16)
    return high, (x - high.astype(F32)).astype(BF16)


def dot_nt(a, b):
    return lax.dot_general(a, b, (((1,), (1,)), ((), ())), preferred_element_type=F32)


def dot_tn(a, b):
    return lax.dot_general(a, b, (((0,), (0,)), ((), ())), preferred_element_type=F32)


def column(row):
    return jnp.broadcast_to(row, (LANES, LANES)).T


def scaled_strain_map(strain_ref, modulus_ref, out_ref):
    modulus = modulus_ref[...]
    rows = [strain_ref[i].astype(F32) for i in range(COMPS)]
    trace = (rows[0] + rows[1] + rows[2]) * LAME
    for i in range(COMPS):
        value = trace + rows[i] * (2.0 * SHEAR) if i < 3 else rows[i] * SHEAR
        out_ref[24 * i : 24 * (i + 1), :] = value * modulus


def main_kernel(
    corner_idx,
    panel_nodes,
    nearby,
    coupling,
    force,
    inverse,
    strain_map,
    modulus,
    connect,
    interface,
    disp,
    stress,
    sub_lo,
    sub_hi,
    grp_lo,
    grp_hi,
    corners,
    loads,
    solved,
    disp_t,
    onehot,
    elem_t,
    scaled,
    ids,
):
    panels, panel_rows, _ = inverse.shape
    nodes = force.shape[1]
    panel_size = panel_rows // 3

    scaled_strain_map(strain_map, modulus, scaled)
    node_of = lax.broadcasted_iota(jnp.int32, (nodes, LANES), 0)
    for a in range(CORNERS):
        hit = connect[a : a + 1, :] == node_of
        onehot[:, a * LANES : (a + 1) * LANES] = jnp.where(hit, 1.0, 0.0).astype(BF16)
    ids[...] = jnp.full(ids.shape, -1.0, F32)
    ids[0:1, 0:NIF] = interface[...].astype(F32)
    connect_f = connect[...].astype(F32)
    face = []
    for half in range(2):
        id_col = column(ids[0:1, half * LANES : (half + 1) * LANES])
        count = jnp.zeros((LANES, LANES), F32)
        for a in range(CORNERS):
            count = count + jnp.where(connect_f[a : a + 1, :] == id_col, 1.0, 0.0)
        face.append(count)
    face = jnp.concatenate(face, axis=0)[:NIF].astype(BF16)
    face = jnp.concatenate([face, face], axis=1)

    for c in range(3):
        loads[pl.ds(c, nodes, stride=3), :] = force[c].astype(F32)

    for k in range(corner_idx.shape[1]):
        corners[k : k + 1, :] = nearby[pl.ds(corner_idx[0, k], 1), :]
    values = corners[...]
    high = values.astype(BF16).astype(F32)
    middle = (values - high).astype(BF16).astype(F32)
    low = values - high - middle
    values = jnp.concatenate([high, middle, low], axis=0).astype(BF16)
    coupled = coupling[...].astype(F32)
    coupled = jnp.concatenate([coupled, coupled, coupled], axis=0).astype(BF16)

    row_of = lax.broadcasted_iota(jnp.int32, (panel_rows, LANES), 0)
    for p in range(panels):
        start = p * panel_rows
        live = row_of < 3 * panel_nodes[0, p]
        correction = dot_tn(coupled[:, start : start + panel_rows], values)
        reduced = loads[start : start + panel_rows, :] - correction
        reduced = jnp.where(live, reduced, 0.0).astype(BF16)
        result = jnp.dot(inverse[p], reduced, preferred_element_type=F32)
        solved[start : start + panel_rows, :] = jnp.where(live, result, 0.0)
        for c in range(3):
            part = solved[pl.ds(start + c, panel_size, stride=3), :].astype(BF16)
            disp[c, p * panel_size : (p + 1) * panel_size, :] = part
            disp_t[c * LANES : (c + 1) * LANES, p * panel_size : (p + 1) * panel_size] = (
                part.astype(F32).T.astype(BF16)
            )

    for c in range(3):
        elem_t[c] = jnp.dot(
            disp_t[c * LANES : (c + 1) * LANES, :], onehot[...], preferred_element_type=F32
        )
    step = 32
    for start in range(0, LANES, step):
        sums = [None] * COMPS
        for a in range(CORNERS):
            for c in range(3):
                x = elem_t[c, start : start + step, a * LANES : (a + 1) * LANES]
                for i in range(COMPS):
                    r = 24 * i + 3 * a + c
                    term = scaled[r : r + 1, :] * x
                    sums[i] = term if sums[i] is None else sums[i] + term
        for i in range(COMPS):
            high, low = split_two(sums[i])
            stress[i * LANES + start : i * LANES + start + step, 0:LANES] = high
            stress[i * LANES + start : i * LANES + start + step, LANES : 2 * LANES] = low

    rows = dot_nt(face, stress[...])
    for i in range(COMPS):
        part = rows[:, i * LANES : (i + 1) * LANES]
        sub_lo[i] = part[:NIS]
        sub_hi[i] = part[NIS : 2 * NIS]
        edge = [part[EDGES + NED * k : EDGES + NED * (k + 1)] for k in range(4)]
        grp_lo[i] = jnp.concatenate([part[2 * NIS : 2 * NIS + NIG], edge[0], edge[2]], axis=0)
        grp_hi[i] = jnp.concatenate([part[2 * NIS + NIG : EDGES], edge[1], edge[3]], axis=0)


def partial_kernel(connect, volume, stress, partial, inverse_volume):
    nodes = partial.shape[1]
    node_of = lax.broadcasted_iota(jnp.int32, (nodes, LANES), 0)
    count = jnp.zeros((nodes, LANES), F32)
    for a in range(CORNERS):
        count = count + jnp.where(connect[a : a + 1, :] == node_of, 1.0, 0.0)
    count = count.astype(BF16)
    count = jnp.concatenate([count, count], axis=1)
    for i in range(COMPS):
        partial[i] = dot_nt(count, stress[i * LANES : (i + 1) * LANES, :])
    for k in range(nodes // LANES):
        inverse_volume[k * LANES : (k + 1) * LANES, :] = column(1.0 / volume[k : k + 1, :])


def edge_kernel(grp_lo, grp_hi, from_lo, from_hi, edge_lo, edge_hi):
    split = NIG + NED
    edge_lo[:, 0:NED, :] = grp_lo[:, NIG:split, :] + from_lo[:, NIG:split, :]
    edge_lo[:, NED:, :] = grp_hi[:, NIG:split, :] + from_hi[:, NIG:split, :]
    edge_hi[:, 0:NED, :] = grp_lo[:, split:, :] + from_lo[:, split:, :]
    edge_hi[:, NED:, :] = grp_hi[:, split:, :] + from_hi[:, split:, :]


def finish_kernel(
    interface, partial, inverse_volume, sub_lo, sub_hi, grp_lo, grp_hi, edge_lo, edge_hi, out, ids, received
):
    nodes = partial.shape[1]
    split = NIG + NED
    ids[...] = jnp.full(ids.shape, -1, jnp.int32)
    ids[0:1, 0:NIF] = interface[...]
    node_of = lax.broadcasted_iota(jnp.int32, (nodes, 2 * LANES), 0)
    placing = jnp.where(ids[0:1, :] == node_of, 1.0, 0.0).astype(BF16)
    for i in range(COMPS):
        lo, hi, low_edge, high_edge = grp_lo[i], grp_hi[i], edge_lo[i], edge_hi[i]
        rows = jnp.concatenate(
            [
                sub_lo[i],
                sub_hi[i],
                lo[:NIG],
                hi[:NIG],
                lo[NIG:split] + low_edge[:NED],
                hi[NIG:split] + low_edge[NED:],
                lo[split:] + high_edge[:NED],
                hi[split:] + high_edge[NED:],
                jnp.zeros((2 * LANES - NIF, LANES), F32),
            ],
            axis=0,
        )
        high, low = split_two(rows)
        received[0, :, i * LANES : (i + 1) * LANES] = high
        received[1, :, i * LANES : (i + 1) * LANES] = low
    scale = inverse_volume[...]
    for i in range(0, COMPS, 2):
        cols = slice(i * LANES, (i + 2) * LANES)
        added = jnp.dot(placing, received[0, :, cols], preferred_element_type=F32)
        added = added + jnp.dot(placing, received[1, :, cols], preferred_element_type=F32)
        out[i] = ((partial[i] + added[:, :LANES]) * scale).astype(BF16)
        out[i + 1] = ((partial[i + 1] + added[:, LANES:]) * scale).astype(BF16)


def vmem(count):
    return [pl.BlockSpec(memory_space=pltpu.VMEM)] * count


def smem(count):
    return [pl.BlockSpec(memory_space=pltpu.SMEM)] * count


def array(shape, dtype=F32):
    return jax.ShapeDtypeStruct(shape, dtype)


def call(kernel, name, out_shape, in_specs, scratch=(), cost=None):
    return pl.pallas_call(
        kernel,
        name=name,
        out_shape=out_shape,
        in_specs=in_specs,
        out_specs=vmem(len(out_shape)),
        scratch_shapes=list(scratch),
        compiler_params=pltpu.CompilerParams(vmem_limit_bytes=VMEM_LIMIT),
        cost_estimate=cost,
    )


def shift(block, axis, up):
    count = lax.axis_size(axis)
    pairs = [(i, i + 1) if up else (i + 1, i) for i in range(count - 1)]
    return lax.ppermute(block, axis, pairs)


def shards(
    coarse,
    corner_idx,
    coupling,
    force,
    panel_inv,
    panel_nodes,
    strain_disp,
    modulus,
    connect,
    interface,
    nodal_volume,
):
    nodes, _, loads = force.shape
    nearby = lax.all_gather(coarse, ("sub", "grp"), axis=0, tiled=True)
    force_t = jnp.transpose(force, (1, 0, 2))
    coupling_t = coupling.T
    disp, stress, sub_lo, sub_hi, grp_lo, grp_hi = call(
        main_kernel,
        "solve_and_stress",
        (
            array((3, nodes, loads), BF16),
            array((COMPS * loads, 2 * LANES), BF16),
            array((COMPS, NIS, loads)),
            array((COMPS, NIS, loads)),
            array((COMPS, NIG + 2 * NED, loads)),
            array((COMPS, NIG + 2 * NED, loads)),
        ),
        smem(2) + vmem(8),
        (
            pltpu.VMEM((corner_idx.shape[1], loads), F32),
            pltpu.VMEM((3 * nodes, loads), F32),
            pltpu.VMEM((3 * nodes, loads), F32),
            pltpu.VMEM((3 * loads, nodes), BF16),
            pltpu.VMEM((nodes, CORNERS * LANES), BF16),
            pltpu.VMEM((3, loads, CORNERS * LANES), F32),
            pltpu.VMEM((COMPS * 24, LANES), F32),
            pltpu.VMEM((8, 2 * LANES), F32),
        ),
        pl.CostEstimate(flops=1500000000, bytes_accessed=4000000, transcendentals=0),
    )(
        corner_idx,
        panel_nodes,
        nearby,
        coupling_t,
        force_t,
        panel_inv,
        strain_disp,
        modulus.reshape(1, -1),
        connect,
        interface,
    )
    from_sub_lo = shift(sub_hi, "sub", True)
    from_sub_hi = shift(sub_lo, "sub", False)
    from_grp_lo = shift(grp_hi, "grp", True)
    from_grp_hi = shift(grp_lo, "grp", False)
    partial, inverse_volume = call(
        partial_kernel,
        "assemble_nodes",
        (array((COMPS, nodes, loads)), array((nodes, LANES))),
        vmem(3),
        cost=pl.CostEstimate(flops=400000000, bytes_accessed=2000000, transcendentals=0),
    )(connect, nodal_volume.reshape(-1, LANES), stress)
    edge_lo, edge_hi = call(
        edge_kernel,
        "sum_edges",
        (array((COMPS, 2 * NED, loads)), array((COMPS, 2 * NED, loads))),
        vmem(4),
    )(grp_lo, grp_hi, from_grp_lo, from_grp_hi)
    from_edge_lo = shift(edge_hi, "sub", True)
    from_edge_hi = shift(edge_lo, "sub", False)
    (nodal,) = call(
        finish_kernel,
        "add_received",
        (array((COMPS, nodes, loads), BF16),),
        vmem(9),
        (
            pltpu.VMEM((8, 2 * LANES), jnp.int32),
            pltpu.VMEM((2, 2 * LANES, COMPS * LANES), BF16),
        ),
    )(
        interface,
        partial,
        inverse_volume,
        from_sub_lo,
        from_sub_hi,
        from_grp_lo,
        from_grp_hi,
        from_edge_lo,
        from_edge_hi,
    )
    return jnp.transpose(disp, (1, 0, 2)), jnp.transpose(nodal, (1, 0, 2))


def solution(mesh):
    owner = ("sub", "grp")
    placed = (
        P(owner, None),
        P(owner, None),
        P(owner, None),
        P(owner, None, None),
        P(owner, None, None),
        P(owner, None),
        P(None, None, owner),
        P(owner),
        P(None, owner),
        P(owner, None),
        P(owner),
    )
    return jax.shard_map(
        shards,
        mesh=mesh,
        in_specs=placed,
        out_specs=(P(owner, None, None), P(owner, None, None)),
        check_vma=False,
    )
```

time: 90 us -> 75.1 us (0.83)
  the two profiles are of different devices: /device:TPU:10 before, /device:TPU:0 now
where the time goes in v1:
time: 75.1 us; the launch traced here: 74.6 us
  blocking collectives  44.5 us (59%)
  starting transfers between devices  12 us (16%)
  local copies, waits for them, and re-layouts  7.25 us (10%)
  Pallas kernels  5.95 us (8%)
  waiting for transfers between devices  4.18 us (6%)
    all_gather x1, blocking collectives, shards(): nearby = lax.all_gather(coarse, ('sub', 'grp'), axis=0, tiled=True)  44.5 us
    ppermute x6, starting transfers between devices, shift(): return lax.ppermute(block, axis, pairs)  12 us
    unnamed x20, local copies, waits for them, and re-layouts  7.25 us
    ppermute x6, waiting for transfers between devices, shift(): return lax.ppermute(block, axis, pairs)  4.18 us
    pallas_call x1, Pallas kernels, shards(): call(main_kernel, 'solve_and_stress', (array((3, nodes, loads), BF16), ar...  3.76 us
    pallas_call x1, Pallas kernels, shards(): call(finish_kernel, 'add_received', (array((COMPS, nodes, loads), BF16),)...  1.55 us
  transfers between devices with their start and end apart: 6, of which 2 were waited for; matrix products, arithmetic and copies ran while one was open for 0% of the time, Pallas kernels for 1%

profile of v1, /device:TPU:0, one launch (start us, length us, event | category | flops | bytes accessed | tf_op | source)
XLA Modules:
  0.0 74.6 jit_solution(12412433097598806648)
XLA Ops:
  0.6 44.5 %all_gather.3.nearby = f32[768,128]{1,0:T(8,128)S(1)} all-gather(f32[24,128]{1,0:T(8,128)} %param.11), channel_id=1, replica_groups=mesh['sub'=8,'grp'=4] {'sub','grp'}, dimensions={0}, use_global_device_ids=true | all-gather | bytes 405504 | tf_op jit(solution)/shard_map/all_gather | solution.py:264
  45.2 0.0 copy-start
  45.2 0.7 copy-done
  45.8 0.0 copy-start.1
  45.9 1.3 %copy-done.1 = bf16[4,384,384]{2,1,0:T(8,128)(2,1)S(1)} copy-done((bf16[4,384,384]{2,1,0:T(8,128)(2,1)S(1)}, bf16[4,384,384]{2,1,0:T(8,128)(2,1)}, u32[]{:S(2)}) %copy-start.1) | copy-done | bytes 1179672
  47.1 0.0 copy-start.2
  47.1 1.0 %copy-done.2 = bf16[512,3,128]{2,0,1:T(8,128)(2,1)S(1)} copy-done((bf16[512,3,128]{2,0,1:T(8,128)(2,1)S(1)}, bf16[512,3,128]{2,0,1:T(8,128)(2,1)}, u32[]{:S(2)}) %copy-start.2) | copy-done | bytes 393240
  48.1 0.0 copy-start.3
  48.1 0.9 %copy-done.3 = bf16[1536,24]{0,1:T(8,128)(2,1)S(1)} copy-done((bf16[1536,24]{0,1:T(8,128)(2,1)S(1)}, bf16[1536,24]{0,1:T(8,128)(2,1)}, u32[]{:S(2)}) %copy-start.3) | copy-done | bytes 73752
  49.0 0.0 copy-start.4
  49.0 0.8 %copy-done.4 = bf16[6,24,128]{2,1,0:T(8,128)(2,1)S(1)} copy-done((bf16[6,24,128]{2,1,0:T(8,128)(2,1)S(1)}, bf16[6,24,128]{2,1,0:T(8,128)(2,1)}, u32[]{:S(2)}) %copy-start.4) | copy-done | bytes 36888
  49.8 0.0 copy-start.5
  49.8 0.7 copy-done.5
  50.5 0.0 copy-start.7
  50.5 0.7 copy-done.7
  51.1 0.0 copy-start.8
  51.1 0.7 copy-done.8
  51.8 0.0 copy-start.9
  51.8 0.7 copy-done.9
  52.4 0.0 copy-start.6
  52.4 3.8 %solve_and_stress.1 = (bf16[3,512,128]{2,1,0:T(8,128)(2,1)}, bf16[768,256]{1,0:T(8,128)(2,1)S(1)}, f32[6,64,128]{2,1,0:T(8,128)S(1)}, f32[6,64,128]{2,1,0:T(8,12...) custom-call(s32[1,24]{1,0:T(1,128)S(1)} %copy-done.7, s32[1,4]{1,0:T(1,128)S(1)} %copy-done.8, ...), custom_call_target="tpu_custom_call" | custom-call | flops 1500000000 | bytes 4000000 | tf_op jit(solution)/shard_map/solve_and_stress/pallas_call | solution.py:267
  56.2 2.2 %collective-permute-start.2 = (f32[6,48,128]{2,1,0:T(8,128)S(1)}, f32[6,48,128]{2,1,0:T(8,128)S(1)}, u32[]{:S(2)}, u32[]{:S(2)}) collective-permute-start(f32[6,48,128]{2,1,0:T(8,128)S(1)} %get-tuple-element.18.grp_hi), channel_id=1, source_target_pairs={{0,1},{1,2},{2,3},{4,5},{5,6},{6,7},{8,9},{9,10},{10,11},{12,13},{... | collective-permute-start | bytes 442376 | tf_op jit(solution)/shard_map/ppermute | solution.py:247
  58.4 1.3 %collective-permute-start.3 = (f32[6,48,128]{2,1,0:T(8,128)S(1)}, f32[6,48,128]{2,1,0:T(8,128)S(1)}, u32[]{:S(2)}, u32[]{:S(2)}) collective-permute-start(f32[6,48,128]{2,1,0:T(8,128)S(1)} %get-tuple-element.19.grp_lo), channel_id=1, source_target_pairs={{1,0},{2,1},{3,2},{5,4},{6,5},{7,6},{9,8},{10,9},{11,10},{13,12},{... | collective-permute-start | bytes 442376 | tf_op jit(solution)/shard_map/ppermute | solution.py:247
  59.7 1.3 %collective-permute-start = (f32[6,64,128]{2,1,0:T(8,128)S(1)}, f32[6,64,128]{2,1,0:T(8,128)S(1)}, u32[]{:S(2)}, u32[]{:S(2)}) collective-permute-start(f32[6,64,128]{2,1,0:T(8,128)S(1)} %get-tuple-element.16), channel_id=1, source_target_pairs={{0,4},{4,8},{8,12},{12,16},{16,20},{20,24},{24,28},{1,5},{5,9},{9,... | collective-permute-start | bytes 589832 | tf_op jit(solution)/shard_map/ppermute | solution.py:247
  61.1 1.3 %collective-permute-start.1 = (f32[6,64,128]{2,1,0:T(8,128)S(1)}, f32[6,64,128]{2,1,0:T(8,128)S(1)}, u32[]{:S(2)}, u32[]{:S(2)}) collective-permute-start(f32[6,64,128]{2,1,0:T(8,128)S(1)} %get-tuple-element.17), channel_id=1, source_target_pairs={{4,0},{8,4},{12,8},{16,12},{20,16},{24,20},{28,24},{5,1},{9,5},{13... | collective-permute-start | bytes 589832 | tf_op jit(solution)/shard_map/ppermute | solution.py:247
  62.4 0.0 collective-permute-done.2.from_lo.grp_lo
  62.4 0.0 collective-permute-done.3.from_hi.grp_hi
  62.4 4.5 %collective-permute-start.4 = (f32[6,16,128]{2,1,0:T(8,128)S(1)}, f32[6,16,128]{2,1,0:T(8,128)S(1)}, u32[]{:S(2)}, u32[]{:S(2)}) collective-permute-start(f32[6,16,128]{2,1,0:T(8,128)S(1)} %get-tuple-element.20), channel_id=1, source_target_pairs={{0,4},{4,8},{8,12},{12,16},{16,20},{20,24},{24,28},{1,5},{5,9},{9,... | collective-permute-start | bytes 147464 | tf_op jit(solution)/shard_map/ppermute | solution.py:247
  67.0 1.3 %collective-permute-start.5 = (f32[6,16,128]{2,1,0:T(8,128)S(1)}, f32[6,16,128]{2,1,0:T(8,128)S(1)}, u32[]{:S(2)}, u32[]{:S(2)}) collective-permute-start(f32[6,16,128]{2,1,0:T(8,128)S(1)} %get-tuple-element.21), channel_id=1, source_target_pairs={{4,0},{8,4},{12,8},{16,12},{20,16},{24,20},{28,24},{5,1},{9,5},{13... | collective-permute-start | bytes 147464 | tf_op jit(solution)/shard_map/ppermute | solution.py:247
  68.3 0.0 copy-done.6
  68.3 0.6 assemble_nodes.1
  68.9 3.3 %collective-permute-done.4.edge_lo = f32[6,16,128]{2,1,0:T(8,128)S(1)} collective-permute-done((f32[6,16,128]{2,1,0:T(8,128)S(1)}, f32[6,16,128]{2,1,0:T(8,128)S(1)}, u32[]{:S(2)}, u32[]{:S(2)}) %collective-permute-start.4) | collective-permute-done | bytes 49184 | tf_op jit(solution)/shard_map/ppermute | solution.py:247
  72.1 0.9 %collective-permute-done.5.edge_hi = f32[6,16,128]{2,1,0:T(8,128)S(1)} collective-permute-done((f32[6,16,128]{2,1,0:T(8,128)S(1)}, f32[6,16,128]{2,1,0:T(8,128)S(1)}, u32[]{:S(2)}, u32[]{:S(2)}) %collective-permute-start.5) | collective-permute-done | bytes 49184 | tf_op jit(solution)/shard_map/ppermute | solution.py:247
  73.1 0.0 collective-permute-done.sub_lo
  73.1 0.0 collective-permute-done.1.sub_hi
  73.1 1.6 %add_received.1 = bf16[6,512,128]{2,1,0:T(8,128)(2,1)} custom-call(s32[1,224]{1,0:T(1,128)S(1)} %copy-done, f32[6,512,128]{2,1,0:T(8,128)S(1)} %get-tuple-element.14.partial, f32[512,128]{1,0:T(8,128)S(1)} %get-tuple-element.15.inverse_volume, f32[6,64,128]{2,1,0:T(8,128)S(1)} %collective-permute-done.sub_lo, ...), custom_call_target="tpu_custom_call" | custom-call | tf_op jit(solution)/shard_map/add_received/pallas_call | solution.py:321
  (1 shorter events, 0.0 us)
Async XLA Ops:
  45.2 0.7 copy-start
  45.8 1.3 %copy-start.1 = (bf16[4,384,384]{2,1,0:T(8,128)(2,1)S(1)}, bf16[4,384,384]{2,1,0:T(8,128)(2,1)}, u32[]{:S(2)}) copy-start(bf16[4,384,384]{2,1,0:T(8,128)(2,1)} %inverse.1) | copy-start | bytes 3538948
  47.1 1.0 %copy-start.2 = (bf16[512,3,128]{2,0,1:T(8,128)(2,1)S(1)}, bf16[512,3,128]{2,0,1:T(8,128)(2,1)}, u32[]{:S(2)}) copy-start(bf16[512,3,128]{2,0,1:T(8,128)(2,1)} %param.14) | copy-start | bytes 1179652
  48.1 0.9 %copy-start.3 = (bf16[1536,24]{0,1:T(8,128)(2,1)S(1)}, bf16[1536,24]{0,1:T(8,128)(2,1)}, u32[]{:S(2)}) copy-start(bf16[1536,24]{0,1:T(8,128)(2,1)} %param.13) | copy-start | bytes 221188
  49.0 0.8 %copy-start.4 = (bf16[6,24,128]{2,1,0:T(8,128)(2,1)S(1)}, bf16[6,24,128]{2,1,0:T(8,128)(2,1)}, u32[]{:S(2)}) copy-start(bf16[6,24,128]{2,1,0:T(8,128)(2,1)} %strain_map.1) | copy-start | bytes 110596
  49.8 0.7 copy-start.5
  50.5 0.7 copy-start.7
  51.1 0.7 copy-start.8
  51.8 0.7 copy-start.9
  52.4 15.8 %copy-start.6 = (f32[512]{0:T(512)S(1)}, f32[512]{0:T(512)}, u32[]{:S(2)}) copy-start(f32[512]{0:T(512)} %param.21) | copy-start | bytes 6148
  56.2 6.2 %collective-permute-start.2 = (f32[6,48,128]{2,1,0:T(8,128)S(1)}, f32[6,48,128]{2,1,0:T(8,128)S(1)}, u32[]{:S(2)}, u32[]{:S(2)}) collective-permute-start(f32[6,48,128]{2,1,0:T(8,128)S(1)} %get-tuple-element.18.grp_hi), channel_id=1, source_target_pairs={{0,1},{1,2},{2,3},{4,5},{5,6},{6,7},{8,9},{9,10},{10,11},{12,13},{... | collective-permute-start | bytes 442376 | tf_op jit(solution)/shard_map/ppermute | solution.py:247
  58.4 3.9 %collective-permute-start.3 = (f32[6,48,128]{2,1,0:T(8,128)S(1)}, f32[6,48,128]{2,1,0:T(8,128)S(1)}, u32[]{:S(2)}, u32[]{:S(2)}) collective-permute-start(f32[6,48,128]{2,1,0:T(8,128)S(1)} %get-tuple-element.19.grp_lo), channel_id=1, source_target_pairs={{1,0},{2,1},{3,2},{5,4},{6,5},{7,6},{9,8},{10,9},{11,10},{13,12},{... | collective-permute-start | bytes 442376 | tf_op jit(solution)/shard_map/ppermute | solution.py:247
  59.7 13.3 %collective-permute-start = (f32[6,64,128]{2,1,0:T(8,128)S(1)}, f32[6,64,128]{2,1,0:T(8,128)S(1)}, u32[]{:S(2)}, u32[]{:S(2)}) collective-permute-start(f32[6,64,128]{2,1,0:T(8,128)S(1)} %get-tuple-element.16), channel_id=1, source_target_pairs={{0,4},{4,8},{8,12},{12,16},{16,20},{20,24},{24,28},{1,5},{5,9},{9,... | collective-permute-start | bytes 589832 | tf_op jit(solution)/shard_map/ppermute | solution.py:247
  61.1 12.0 %collective-permute-start.1 = (f32[6,64,128]{2,1,0:T(8,128)S(1)}, f32[6,64,128]{2,1,0:T(8,128)S(1)}, u32[]{:S(2)}, u32[]{:S(2)}) collective-permute-start(f32[6,64,128]{2,1,0:T(8,128)S(1)} %get-tuple-element.17), channel_id=1, source_target_pairs={{4,0},{8,4},{12,8},{16,12},{20,16},{24,20},{28,24},{5,1},{9,5},{13... | collective-permute-start | bytes 589832 | tf_op jit(solution)/shard_map/ppermute | solution.py:247
  62.4 9.7 %collective-permute-start.4 = (f32[6,16,128]{2,1,0:T(8,128)S(1)}, f32[6,16,128]{2,1,0:T(8,128)S(1)}, u32[]{:S(2)}, u32[]{:S(2)}) collective-permute-start(f32[6,16,128]{2,1,0:T(8,128)S(1)} %get-tuple-element.20), channel_id=1, source_target_pairs={{0,4},{4,8},{8,12},{12,16},{16,20},{20,24},{24,28},{1,5},{5,9},{9,... | collective-permute-start | bytes 147464 | tf_op jit(solution)/shard_map/ppermute | solution.py:247
  67.0 6.1 %collective-permute-start.5 = (f32[6,16,128]{2,1,0:T(8,128)S(1)}, f32[6,16,128]{2,1,0:T(8,128)S(1)}, u32[]{:S(2)}, u32[]{:S(2)}) collective-permute-start(f32[6,16,128]{2,1,0:T(8,128)S(1)} %get-tuple-element.21), channel_id=1, source_target_pairs={{4,0},{8,4},{12,8},{16,12},{20,16},{24,20},{28,24},{5,1},{9,5},{13... | collective-permute-start | bytes 147464 | tf_op jit(solution)/shard_map/ppermute | solution.py:247

commit v2 on v1

v2 whole, which is shorter than its diff:
```python
import jax
import jax.numpy as jnp
from jax import lax
from jax.experimental import pallas as pl
from jax.experimental.pallas import tpu as pltpu
from jax.sharding import PartitionSpec as P

NIS = 64
NIG = 32
NED = 8
EDGES = 2 * NIS + 2 * NIG
NIF = EDGES + 4 * NED
CORNERS = 8
COMPS = 6
LANES = 128
TERM = 32

POISSON = 0.3
LAME = POISSON / ((1.0 + POISSON) * (1.0 - 2.0 * POISSON))
SHEAR = 0.5 / (1.0 + POISSON)

F32 = jnp.float32
BF16 = jnp.bfloat16
VMEM_LIMIT = 24 * 1024 * 1024


def split_two(x):
    high = x.astype(BF16)
    return high, (x - high.astype(F32)).astype(BF16)


def dot(a, b):
    return jnp.dot(a, b, preferred_element_type=F32)


def dot_nt(a, b):
    return lax.dot_general(a, b, (((1,), (1,)), ((), ())), preferred_element_type=F32)


def column(row):
    return jnp.broadcast_to(row, (LANES, LANES)).T


def prepare_kernel(
    blocks,
    corner_idx,
    panel_nodes,
    coupling,
    force,
    panel_inv,
    strain_disp,
    modulus,
    connect,
    interface,
    volume,
    coarse,
    inverse,
    coupled,
    loads,
    live,
    select,
    onehot,
    face,
    scaled,
    count,
    placing,
    inverse_volume,
    own,
    corner_v,
    panel_v,
    coupling_v,
    force_v,
    strain_v,
    modulus_v,
    connect_v,
    interface_v,
    volume_v,
    ids,
    sems,
):
    pairs = [
        (connect, connect_v),
        (interface, interface_v),
        (corner_idx, corner_v),
        (panel_nodes, panel_v),
        (volume, volume_v),
        (modulus, modulus_v),
        (strain_disp, strain_v),
        (coupling, coupling_v),
        (force, force_v),
        (panel_inv, inverse),
        (coarse, own),
    ]
    copies = [pltpu.make_async_copy(src, dst, sems.at[k]) for k, (src, dst) in enumerate(pairs)]
    for copy in copies:
        copy.start()
    panels, panel_rows, _ = inverse.shape
    nodes = force_v.shape[1]
    q = corner_idx.shape[1]

    copies[0].wait()
    node_of = lax.broadcasted_iota(jnp.int32, (nodes, LANES), 0)
    total = jnp.zeros((nodes, LANES), F32)
    for a in range(CORNERS):
        hit = jnp.where(connect_v[a : a + 1, :] == node_of, 1.0, 0.0)
        onehot[:, a * LANES : (a + 1) * LANES] = hit.astype(BF16)
        total = total + hit
    total = total.astype(BF16)
    count[:, :LANES] = total
    count[:, LANES:] = total

    copies[1].wait()
    ids[...] = jnp.full(ids.shape, -1.0, F32)
    ids[0:1, 0:NIF] = interface_v[...].astype(F32)
    node_of = lax.broadcasted_iota(jnp.int32, (nodes, 2 * LANES), 0)
    placing[...] = jnp.where(ids[0:1, :].astype(jnp.int32) == node_of, 1.0, 0.0).astype(BF16)
    connect_f = connect_v[...].astype(F32)
    for half in range(2):
        id_col = column(ids[0:1, half * LANES : (half + 1) * LANES])
        rows = jnp.zeros((LANES, LANES), F32)
        for a in range(CORNERS):
            rows = rows + jnp.where(connect_f[a : a + 1, :] == id_col, 1.0, 0.0)
        rows = rows.astype(BF16)[: min(LANES, NIF - half * LANES)]
        face[half * LANES : half * LANES + rows.shape[0], :LANES] = rows
        face[half * LANES : half * LANES + rows.shape[0], LANES:] = rows

    copies[2].wait()
    ids[0:1, 0:q] = corner_v[...].astype(F32)
    wanted = column(ids[0:1, :LANES])[:TERM]
    lane = lax.broadcasted_iota(jnp.int32, (TERM, LANES), 1)
    entry = lax.broadcasted_iota(jnp.int32, (TERM, LANES), 0)
    for b in range(3):
        row = (lax.axis_index("sub") - 1 + b) * blocks + lane
        hit = (wanted == row.astype(F32)) & (lane < blocks) & (entry < q)
        select[:, b * LANES : (b + 1) * LANES] = jnp.where(hit, 1.0, 0.0).astype(BF16)

    copies[3].wait()
    row_of = lax.broadcasted_iota(jnp.int32, (panel_rows, LANES), 0)
    for p in range(panels):
        alive = row_of < 3 * panel_v[0:1, p : p + 1]
        live[p * panel_rows : (p + 1) * panel_rows, :] = jnp.where(alive, 1.0, 0.0)

    copies[4].wait()
    for k in range(nodes // LANES):
        inverse_volume[k * LANES : (k + 1) * LANES, :] = column(1.0 / volume_v[k : k + 1, :])

    copies[5].wait()
    copies[6].wait()
    factor = modulus_v[...]
    rows = [strain_v[i].astype(F32) for i in range(COMPS)]
    trace = (rows[0] + rows[1] + rows[2]) * LAME
    for i in range(COMPS):
        value = trace + rows[i] * (2.0 * SHEAR) if i < 3 else rows[i] * SHEAR
        scaled[24 * i : 24 * (i + 1), :] = value * factor

    copies[7].wait()
    for k in range(coupling_v.shape[1] // LANES):
        part = coupling_v[:, k * LANES : (k + 1) * LANES].astype(F32)
        gap = jnp.zeros((TERM - q, LANES), F32)
        stack = jnp.concatenate([part, gap] * 3 + [jnp.zeros((LANES - 3 * TERM, LANES), F32)], axis=0)
        rows = slice(k * LANES, (k + 1) * LANES)
        coupled[rows, :] = (stack.T * live[rows, :]).astype(BF16)

    copies[8].wait()
    for c in range(3):
        loads[pl.ds(c, nodes, stride=3), :] = force_v[c].astype(F32)
    loads[...] = loads[...] * live[...]
    copies[9].wait()
    copies[10].wait()


def merge_kernel(bit, own, other, out):
    rows = own.shape[0]
    place = (lax.axis_index("grp") >> bit) & 1
    out[pl.ds(pl.multiple_of(place * rows, 8), rows), :] = own[...]
    out[pl.ds(pl.multiple_of((1 - place) * rows, 8), rows), :] = other[...]


def solve_kernel(
    below,
    here,
    above,
    inverse,
    coupled,
    loads,
    live,
    select,
    onehot,
    face,
    scaled,
    disp,
    stress,
    sub_hi,
    terms,
    solved,
    disp_t,
    elem_t,
):
    panels, panel_rows, _ = inverse.shape
    panel_size = panel_rows // 3
    rows = here.shape[0]

    terms[...] = jnp.zeros(terms.shape, BF16)
    for b, block in enumerate((below, here, above)):
        x = block[...]
        high = x.astype(BF16)
        rest = x - high.astype(F32)
        middle = rest.astype(BF16)
        low = (rest - middle.astype(F32)).astype(BF16)
        for t, value in enumerate((high, middle, low)):
            terms[t, b * LANES : b * LANES + rows, :] = value
    picked = [dot(select[...], terms[t]) for t in range(3)]
    picked.append(jnp.zeros((LANES - 3 * TERM, LANES), F32))
    values = jnp.concatenate(picked, axis=0).astype(BF16)

    for p in range(panels):
        start = p * panel_rows
        span = slice(start, start + panel_rows)
        reduced = (loads[span, :] - dot(coupled[span, :], values)).astype(BF16)
        solved[span, :] = dot(inverse[p], reduced) * live[span, :]
        for c in range(3):
            part = solved[pl.ds(start + c, panel_size, stride=3), :].astype(BF16)
            disp[c, p * panel_size : (p + 1) * panel_size, :] = part
            disp_t[c * LANES : (c + 1) * LANES, p * panel_size : (p + 1) * panel_size] = (
                part.astype(F32).T.astype(BF16)
            )

    for c in range(3):
        elem_t[c] = dot(disp_t[c * LANES : (c + 1) * LANES, :], onehot[...])
    step = 32
    for start in range(0, LANES, step):
        sums = [None] * COMPS
        for a in range(CORNERS):
            for c in range(3):
                x = elem_t[c, start : start + step, a * LANES : (a + 1) * LANES]
                for i in range(COMPS):
                    r = 24 * i + 3 * a + c
                    term = scaled[r : r + 1, :] * x
                    sums[i] = term if sums[i] is None else sums[i] + term
        for i in range(COMPS):
            high, low = split_two(sums[i])
            stress[i * LANES + start : i * LANES + start + step, 0:LANES] = high
            stress[i * LANES + start : i * LANES + start + step, LANES : 2 * LANES] = low

    rows = dot_nt(face[NIS : 2 * NIS, :], stress[...])
    for i in range(COMPS):
        sub_hi[i] = rows[:, i * LANES : (i + 1) * LANES]


def face_kernel(face, stress, sub_lo, grp_lo, grp_hi):
    low = dot_nt(face[:NIS, :], stress[...])
    rows = dot_nt(face[2 * NIS :, :], stress[...])
    base = EDGES - 2 * NIS
    for i in range(COMPS):
        part = rows[:, i * LANES : (i + 1) * LANES]
        edge = [part[base + NED * k : base + NED * (k + 1)] for k in range(4)]
        first = low[:, i * LANES : (i + 1) * LANES]
        sub_lo[i] = jnp.concatenate([first, edge[0], edge[1]], axis=0)
        grp_lo[i] = jnp.concatenate([part[:NIG], edge[0], edge[2]], axis=0)
        grp_hi[i] = jnp.concatenate([part[NIG:base], edge[1], edge[3]], axis=0)


def edge_kernel(sub_lo, grp_lo, grp_hi, from_lo, from_hi, _, sub_out, edge_hi):
    split = NIG + NED
    sub_out[:, :NIS, :] = sub_lo[:, :NIS, :]
    sub_out[:, NIS : NIS + NED, :] = grp_lo[:, NIG:split, :] + from_lo[:, NIG:split, :]
    sub_out[:, NIS + NED :, :] = grp_hi[:, NIG:split, :] + from_hi[:, NIG:split, :]
    edge_hi[:, 0:NED, :] = grp_lo[:, split:, :] + from_lo[:, split:, :]
    edge_hi[:, NED:, :] = grp_hi[:, split:, :] + from_hi[:, split:, :]


def partial_kernel(count, stress, disp, partial, disp_out):
    disp_out[...] = disp[...]
    for i in range(COMPS):
        partial[i] = dot_nt(count[...], stress[i * LANES : (i + 1) * LANES, :])


def finish_kernel(
    placing, partial, inverse_volume, sub_lo, sub_hi, grp_lo, grp_hi, edge_lo, out, received
):
    split = NIG + NED
    for i in range(COMPS):
        lo, hi, low_edge, high = grp_lo[i], grp_hi[i], edge_lo[i], sub_hi[i]
        rows = jnp.concatenate(
            [
                sub_lo[i],
                high[:NIS],
                lo[:NIG],
                hi[:NIG],
                lo[NIG:split] + low_edge[:NED],
                hi[NIG:split] + low_edge[NED:],
                lo[split:] + high[NIS : NIS + NED],
                hi[split:] + high[NIS + NED :],
                jnp.zeros((2 * LANES - NIF, LANES), F32),
            ],
            axis=0,
        )
        first, second = split_two(rows)
        received[0, :, i * LANES : (i + 1) * LANES] = first
        received[1, :, i * LANES : (i + 1) * LANES] = second
    scale = inverse_volume[...]
    for i in range(0, COMPS, 2):
        cols = slice(i * LANES, (i + 2) * LANES)
        added = dot(placing[...], received[0, :, cols]) + dot(placing[...], received[1, :, cols])
        out[i] = ((partial[i] + added[:, :LANES]) * scale).astype(BF16)
        out[i + 1] = ((partial[i + 1] + added[:, LANES:]) * scale).astype(BF16)


def vmem(count):
    return [pl.BlockSpec(memory_space=pltpu.VMEM)] * count


def array(shape, dtype=F32):
    return jax.ShapeDtypeStruct(shape, dtype)


def call(kernel, name, out_shape, in_specs, scratch=(), flops=0, moved=0):
    return pl.pallas_call(
        kernel,
        name=name,
        out_shape=out_shape,
        in_specs=in_specs,
        out_specs=vmem(len(out_shape)),
        scratch_shapes=list(scratch),
        compiler_params=pltpu.CompilerParams(vmem_limit_bytes=VMEM_LIMIT),
        cost_estimate=pl.CostEstimate(flops=flops, bytes_accessed=moved, transcendentals=0),
    )


def shift(block, axis, up):
    count = lax.axis_size(axis)
    pairs = [(i, i + 1) if up else (i + 1, i) for i in range(count - 1)]
    return lax.ppermute(block, axis, pairs)


def in_hbm(*arrays):
    return [pltpu.with_memory_space_constraint(x, pltpu.HBM) for x in arrays]


def gather_group(block, own):
    count = lax.axis_size("grp")
    bit = 0
    while 1 << bit < count:
        other = lax.ppermute(block, "grp", [(i, i ^ (1 << bit)) for i in range(count)])
        rows, lanes = block.shape

        def merge(own, received, out, bit=bit):
            merge_kernel(bit, own, received, out)

        (block,) = call(merge, "merge_blocks", (array((2 * rows, lanes)),), vmem(2))(own, other)
        own = block
        bit += 1
    return block


def shards(
    coarse,
    corner_idx,
    coupling,
    force,
    panel_inv,
    panel_nodes,
    strain_disp,
    modulus,
    connect,
    interface,
    nodal_volume,
):
    nodes, _, cases = force.shape
    dofs = 3 * nodes
    q = corner_idx.shape[1]
    blocks = coarse.shape[0] * lax.axis_size("grp")

    def prepare(*refs):
        prepare_kernel(blocks, *refs)

    prepared = call(
        prepare,
        "prepare",
        (
            array(panel_inv.shape, BF16),
            array((dofs, LANES), BF16),
            array((dofs, cases)),
            array((dofs, LANES)),
            array((TERM, 3 * LANES), BF16),
            array((nodes, CORNERS * LANES), BF16),
            array((NIF, 2 * LANES), BF16),
            array((COMPS * 24, LANES)),
            array((nodes, 2 * LANES), BF16),
            array((nodes, 2 * LANES), BF16),
            array((nodes, LANES)),
            array(coarse.shape),
        ),
        [pl.BlockSpec(memory_space=pltpu.HBM)] * 11,
        (
            pltpu.VMEM((1, q), jnp.int32),
            pltpu.VMEM(panel_nodes.shape, jnp.int32),
            pltpu.VMEM((q, dofs), BF16),
            pltpu.VMEM((3, nodes, cases), BF16),
            pltpu.VMEM(strain_disp.shape, BF16),
            pltpu.VMEM((1, LANES), F32),
            pltpu.VMEM(connect.shape, jnp.int32),
            pltpu.VMEM(interface.shape, jnp.int32),
            pltpu.VMEM((nodes // LANES, LANES), F32),
            pltpu.VMEM((8, 2 * LANES), F32),
            pltpu.SemaphoreType.DMA((11,)),
        ),
        flops=200000000,
        moved=8000000,
    )(
        *in_hbm(
            corner_idx,
            panel_nodes,
            coupling.T,
            jnp.transpose(force, (1, 0, 2)),
            panel_inv,
            strain_disp,
            modulus.reshape(1, -1),
            connect,
            interface,
            nodal_volume.reshape(-1, LANES),
            coarse,
        )
    )
    *operands, count, placing, inverse_volume, own = prepared

    here = gather_group(coarse, own)
    below = shift(here, "sub", True)
    above = shift(here, "sub", False)
    disp, stress, sub_hi = call(
        solve_kernel,
        "solve_and_stress",
        (
            array((3, nodes, cases), BF16),
            array((COMPS * cases, 2 * LANES), BF16),
            array((COMPS, NIS, cases)),
        ),
        vmem(11),
        (
            pltpu.VMEM((3, 3 * LANES, cases), BF16),
            pltpu.VMEM((dofs, cases), F32),
            pltpu.VMEM((3 * cases, nodes), BF16),
            pltpu.VMEM((3, cases, CORNERS * LANES), F32),
        ),
        flops=1500000000,
        moved=4000000,
    )(below, here, above, *operands)
    from_sub_lo = shift(sub_hi, "sub", True)
    sub_lo, grp_lo, grp_hi = call(
        face_kernel,
        "interface_rows",
        (
            array((COMPS, NIS + 2 * NED, cases)),
            array((COMPS, NIG + 2 * NED, cases)),
            array((COMPS, NIG + 2 * NED, cases)),
        ),
        vmem(2),
        flops=100000000,
        moved=1000000,
    )(operands[6], stress)
    from_grp_lo = shift(grp_hi, "grp", True)
    from_grp_hi = shift(grp_lo, "grp", False)
    sub_lo, edge_hi = call(
        edge_kernel,
        "sum_edges",
        (array(sub_lo.shape), array((COMPS, 2 * NED, cases))),
        vmem(5) + [pl.BlockSpec(memory_space=pl.ANY)],
    )(sub_lo, grp_lo, grp_hi, from_grp_lo, from_grp_hi, from_sub_lo)
    from_edge_lo = shift(edge_hi, "sub", True)
    from_sub_hi = shift(sub_lo, "sub", False)
    partial, disp = call(
        partial_kernel,
        "assemble_nodes",
        (array((COMPS, nodes, cases)), array(disp.shape, BF16)),
        vmem(3),
        flops=400000000,
        moved=2000000,
    )(count, stress, disp)
    (nodal,) = call(
        finish_kernel,
        "add_received",
        (array((COMPS, nodes, cases), BF16),),
        vmem(8),
        (pltpu.VMEM((2, 2 * LANES, COMPS * cases), BF16),),
        flops=800000000,
        moved=3000000,
    )(
        placing,
        partial,
        inverse_volume,
        from_sub_lo,
        from_sub_hi,
        from_grp_lo,
        from_grp_hi,
        from_edge_lo,
    )
    return jnp.transpose(disp, (1, 0, 2)), jnp.transpose(nodal, (1, 0, 2))


def solution(mesh):
    owner = ("sub", "grp")
    placed = (
        P(owner, None),
        P(owner, None),
        P(owner, None),
        P(owner, None, None),
        P(owner, None, None),
        P(owner, None),
        P(None, None, owner),
        P(owner),
        P(None, owner),
        P(owner, None),
        P(owner),
    )
    return jax.shard_map(
        shards,
        mesh=mesh,
        in_specs=placed,
        out_specs=(P(owner, None, None), P(owner, None, None)),
        check_vma=False,
    )
```

time: 75.1 us -> 44.1 us (0.59)
  the two profiles are of different devices: /device:TPU:0 before, /device:TPU:10 now
where the time goes in v2:
time: 44.1 us; the launch traced here: 43.8 us
  starting transfers between devices  19.6 us (44%)
  waiting for transfers between devices  15.3 us (35%)
  Pallas kernels  8.17 us (19%)
  between operations  0.74 us (2%)
    ppermute x7, starting transfers between devices, shift(): return lax.ppermute(block, axis, pairs)  18.9 us
    ppermute x7, waiting for transfers between devices, shift(): return lax.ppermute(block, axis, pairs)  12 us
    ppermute x2, waiting for transfers between devices, gather_group(): lax.ppermute(block, 'grp', [(i, i ^ 1 << bit) for i in range(count)])  3.29 us
    pallas_call x1, Pallas kernels, shards(): call(solve_kernel, 'solve_and_stress', (array((3, nodes, cases), BF16), a...  2.83 us
    pallas_call x1, Pallas kernels, shards(): call(prepare, 'prepare', (array(panel_inv.shape, BF16), array((dofs, LANE...  2.15 us
    pallas_call x1, Pallas kernels, shards(): call(finish_kernel, 'add_received', (array((COMPS, nodes, cases), BF16),)...  1.51 us
    pallas_call x1, Pallas kernels, shards(): call(partial_kernel, 'assemble_nodes', (array((COMPS, nodes, cases)), arr...  1.25 us
  transfers between devices with their start and end apart: 9, of which 6 were waited for; matrix products, arithmetic and copies ran while one was open for 0% of the time, Pallas kernels for 9%

profile of v2, /device:TPU:10, one launch (start us, length us, event | category | flops | bytes accessed | tf_op | source)
XLA Modules:
  0.0 43.8 jit_solution(7993259816943227389)
XLA Ops:
  0.6 0.1 collective-permute-start
  0.7 2.2 %prepare.1 = (bf16[4,384,384]{2,1,0:T(8,128)(2,1)S(1)}, bf16[1536,128]{1,0:T(8,128)(2,1)S(1)}, f32[1536,128]{1,0:T(8,128)S(1)}, f32[1536,128]{1,0:T(8,128)S(1)},...) custom-call(s32[1,24]{1,0:T(1,128)} %refs_0_.1, ...), custom_call_target="tpu_custom_call" | custom-call | flops 200000000 | bytes 8000000 | tf_op jit(solution)/shard_map/prepare/pallas_call | solution.py:377
  2.9 0.0 collective-permute-done.received
  2.9 0.6 %collective-permute-start.1 = (f32[48,128]{1,0:T(8,128)S(1)}, f32[48,128]{1,0:T(8,128)S(1)}, u32[]{:S(2)}, u32[]{:S(2)}) collective-permute-start(f32[48,128]{1,0:T(8,128)S(1)} %merge_blocks.2.own), channel_id=1, source_target_pairs={{0,2},{1,3},{2,0},{3,1},{4,6},{5,7},{6,4},{7,5},{8,10},{9,11},{10,... | collective-permute-start | bytes 73736 | tf_op jit(solution)/shard_map/ppermute | solution.py:344
  3.5 3.3 %collective-permute-done.1.received = f32[48,128]{1,0:T(8,128)S(1)} collective-permute-done((f32[48,128]{1,0:T(8,128)S(1)}, f32[48,128]{1,0:T(8,128)S(1)}, u32[]{:S(2)}, u32[]{:S(2)}) %collective-permute-start.1) | collective-permute-done | bytes 24608 | tf_op jit(solution)/shard_map/ppermute | solution.py:344
  6.8 3.3 %collective-permute-start.3 = (f32[96,128]{1,0:T(8,128)S(1)}, f32[96,128]{1,0:T(8,128)S(1)}, u32[]{:S(2)}, u32[]{:S(2)}) collective-permute-start(f32[96,128]{1,0:T(8,128)S(1)} %merge_blocks.3.here), channel_id=1, source_target_pairs={{4,0},{8,4},{12,8},{16,12},{20,16},{24,20},{28,24},{5,1},{9,5},{13... | collective-permute-start | bytes 147464 | tf_op jit(solution)/shard_map/ppermute | solution.py:333
  10.1 2.5 %collective-permute-start.2 = (f32[96,128]{1,0:T(8,128)S(1)}, f32[96,128]{1,0:T(8,128)S(1)}, u32[]{:S(2)}, u32[]{:S(2)}) collective-permute-start(f32[96,128]{1,0:T(8,128)S(1)} %merge_blocks.3.here), channel_id=1, source_target_pairs={{0,4},{4,8},{8,12},{12,16},{16,20},{20,24},{24,28},{1,5},{5,9},{9,... | collective-permute-start | bytes 147464 | tf_op jit(solution)/shard_map/ppermute | solution.py:333
  12.7 0.1 collective-permute-done.3.above
  12.8 4.2 %collective-permute-done.2.below = f32[96,128]{1,0:T(8,128)S(1)} collective-permute-done((f32[96,128]{1,0:T(8,128)S(1)}, f32[96,128]{1,0:T(8,128)S(1)}, u32[]{:S(2)}, u32[]{:S(2)}) %collective-permute-start.2) | collective-permute-done | bytes 49184 | tf_op jit(solution)/shard_map/ppermute | solution.py:333
  17.0 2.8 %solve_and_stress.1 = (bf16[3,512,128]{2,1,0:T(8,128)(2,1)S(1)}, bf16[768,256]{1,0:T(8,128)(2,1)S(1)}, f32[6,64,128]{2,1,0:T(8,128)S(1)}) custom-call(f32[96,128]{1,0:T(8,128)S(1)} %collective-permute-done.2.below, f32[96,128]{1,0:T(8,128)S(1)} %merge_blocks.3.here, f32[96,128]{1,0:T(8,128)S(1)} %collective-permute-done.3.above, ...), custom_call_target="tpu_custom_call" | custom-call | flops 1500000000 | bytes 4000000 | tf_op jit(solution)/shard_map/solve_and_stress/pallas_call | solution.py:430
  19.8 1.9 %collective-permute-start.4 = (f32[6,64,128]{2,1,0:T(8,128)S(1)}, f32[6,64,128]{2,1,0:T(8,128)S(1)}, u32[]{:S(2)}, u32[]{:S(2)}) collective-permute-start(f32[6,64,128]{2,1,0:T(8,128)S(1)} %get-tuple-element.40), channel_id=1, source_target_pairs={{0,4},{4,8},{8,12},{12,16},{16,20},{20,24},{24,28},{1,5},{5,9},{9,... | collective-permute-start | bytes 589832 | tf_op jit(solution)/shard_map/ppermute | solution.py:333
  21.8 0.4 interface_rows.1
  22.1 1.9 %collective-permute-start.6 = (f32[6,48,128]{2,1,0:T(8,128)S(1)}, f32[6,48,128]{2,1,0:T(8,128)S(1)}, u32[]{:S(2)}, u32[]{:S(2)}) collective-permute-start(f32[6,48,128]{2,1,0:T(8,128)S(1)} %get-tuple-element.42.grp_lo), channel_id=1, source_target_pairs={{1,0},{2,1},{3,2},{5,4},{6,5},{7,6},{9,8},{10,9},{11,10},{13,12},{... | collective-permute-start | bytes 442376 | tf_op jit(solution)/shard_map/ppermute | solution.py:333
  24.1 2.4 %collective-permute-start.5 = (f32[6,48,128]{2,1,0:T(8,128)S(1)}, f32[6,48,128]{2,1,0:T(8,128)S(1)}, u32[]{:S(2)}, u32[]{:S(2)}) collective-permute-start(f32[6,48,128]{2,1,0:T(8,128)S(1)} %get-tuple-element.43.grp_hi), channel_id=1, source_target_pairs={{0,1},{1,2},{2,3},{4,5},{5,6},{6,7},{8,9},{9,10},{10,11},{12,13},{... | collective-permute-start | bytes 442376 | tf_op jit(solution)/shard_map/ppermute | solution.py:333
  26.5 0.2 collective-permute-done.6.from_hi.grp_hi
  26.7 3.8 %collective-permute-done.5.from_lo.grp_lo = f32[6,48,128]{2,1,0:T(8,128)S(1)} collective-permute-done((f32[6,48,128]{2,1,0:T(8,128)S(1)}, f32[6,48,128]{2,1,0:T(8,128)S(1)}, u32[]{:S(2)}, u32[]{:S(2)}) %collective-permute-start.5) | collective-permute-done | bytes 147488 | tf_op jit(solution)/shard_map/ppermute | solution.py:333
  30.5 0.0 collective-permute-done.4._.sub_lo
  30.6 4.8 %collective-permute-start.7 = (f32[6,80,128]{2,1,0:T(8,128)S(1)}, f32[6,80,128]{2,1,0:T(8,128)S(1)}, u32[]{:S(2)}, u32[]{:S(2)}) collective-permute-start(f32[6,80,128]{2,1,0:T(8,128)S(1)} %get-tuple-element.44), channel_id=1, source_target_pairs={{4,0},{8,4},{12,8},{16,12},{20,16},{24,20},{28,24},{5,1},{9,5},{13... | collective-permute-start | bytes 737288 | tf_op jit(solution)/shard_map/ppermute | solution.py:333
  35.4 2.0 %collective-permute-start.8 = (f32[6,16,128]{2,1,0:T(8,128)S(1)}, f32[6,16,128]{2,1,0:T(8,128)S(1)}, u32[]{:S(2)}, u32[]{:S(2)}) collective-permute-start(f32[6,16,128]{2,1,0:T(8,128)S(1)} %get-tuple-element.45), channel_id=1, source_target_pairs={{0,4},{4,8},{8,12},{12,16},{16,20},{20,24},{24,28},{1,5},{5,9},{9,... | collective-permute-start | bytes 147464 | tf_op jit(solution)/shard_map/ppermute | solution.py:333
  37.4 1.3 %assemble_nodes.1 = (f32[6,512,128]{2,1,0:T(8,128)S(1)}, bf16[3,512,128]{2,1,0:T(8,128)(2,1)}) custom-call(bf16[512,256]{1,0:T(8,128)(2,1)S(1)} %get-tuple-element.24.count, bf16[768,256]{1,0:T(8,128)(2,1)S(1)} %get-tuple-element.34.stress, bf16[3,512,128]{2,1,0:T(8,128)(2,1)S(1)} %get-tuple-element.35.disp), custom_call_target="tpu_custom_call" | custom-call | flops 400000000 | bytes 2000000 | tf_op jit(solution)/shard_map/assemble_nodes/pallas_call | solution.py:471
  38.7 3.6 %collective-permute-done.8.edge_lo = f32[6,16,128]{2,1,0:T(8,128)S(1)} collective-permute-done((f32[6,16,128]{2,1,0:T(8,128)S(1)}, f32[6,16,128]{2,1,0:T(8,128)S(1)}, u32[]{:S(2)}, u32[]{:S(2)}) %collective-permute-start.8) | collective-permute-done | bytes 49184 | tf_op jit(solution)/shard_map/ppermute | solution.py:333
  42.3 0.0 collective-permute-done.7.sub_hi
  42.3 1.5 %add_received.1 = bf16[6,512,128]{2,1,0:T(8,128)(2,1)} custom-call(bf16[512,256]{1,0:T(8,128)(2,1)S(1)} %get-tuple-element.37.placing, f32[6,512,128]{2,1,0:T(8,128)S(1)} %get-tuple-element.38.partial, f32[512,128]{1,0:T(8,128)S(1)} %get-tuple-element.39.inverse_volume, f32[6,64,128]{2,1,0:T(8,128)S(1)} %collective-permute-done.4._.sub_lo, ...), custom_call_target="tpu_custom_call" | custom-call | flops 800000000 | bytes 3000000 | tf_op jit(solution)/shard_map/add_received/pallas_call | solution.py:479
  (3 shorter events, 0.0 us)
Async XLA Ops:
  0.6 2.2 %collective-permute-start = (f32[24,128]{1,0:T(8,128)}, f32[24,128]{1,0:T(8,128)S(1)}, u32[]{:S(2)}, u32[]{:S(2)}) collective-permute-start(f32[24,128]{1,0:T(8,128)} %refs_10_.1), channel_id=1, source_target_pairs={{0,1},{1,0},{2,3},{3,2},{4,5},{5,4},{6,7},{7,6},{8,9},{9,8},{10,11... | collective-permute-start | bytes 36872 | tf_op jit(solution)/shard_map/ppermute | solution.py:344
  2.9 3.9 %collective-permute-start.1 = (f32[48,128]{1,0:T(8,128)S(1)}, f32[48,128]{1,0:T(8,128)S(1)}, u32[]{:S(2)}, u32[]{:S(2)}) collective-permute-start(f32[48,128]{1,0:T(8,128)S(1)} %merge_blocks.2.own), channel_id=1, source_target_pairs={{0,2},{1,3},{2,0},{3,1},{4,6},{5,7},{6,4},{7,5},{8,10},{9,11},{10,... | collective-permute-start | bytes 73736 | tf_op jit(solution)/shard_map/ppermute | solution.py:344
  6.8 6.0 %collective-permute-start.3 = (f32[96,128]{1,0:T(8,128)S(1)}, f32[96,128]{1,0:T(8,128)S(1)}, u32[]{:S(2)}, u32[]{:S(2)}) collective-permute-start(f32[96,128]{1,0:T(8,128)S(1)} %merge_blocks.3.here), channel_id=1, source_target_pairs={{4,0},{8,4},{12,8},{16,12},{20,16},{24,20},{28,24},{5,1},{9,5},{13... | collective-permute-start | bytes 147464 | tf_op jit(solution)/shard_map/ppermute | solution.py:333
  10.1 6.9 %collective-permute-start.2 = (f32[96,128]{1,0:T(8,128)S(1)}, f32[96,128]{1,0:T(8,128)S(1)}, u32[]{:S(2)}, u32[]{:S(2)}) collective-permute-start(f32[96,128]{1,0:T(8,128)S(1)} %merge_blocks.3.here), channel_id=1, source_target_pairs={{0,4},{4,8},{8,12},{12,16},{16,20},{20,24},{24,28},{1,5},{5,9},{9,... | collective-permute-start | bytes 147464 | tf_op jit(solution)/shard_map/ppermute | solution.py:333
  19.8 10.7 %collective-permute-start.4 = (f32[6,64,128]{2,1,0:T(8,128)S(1)}, f32[6,64,128]{2,1,0:T(8,128)S(1)}, u32[]{:S(2)}, u32[]{:S(2)}) collective-permute-start(f32[6,64,128]{2,1,0:T(8,128)S(1)} %get-tuple-element.40), channel_id=1, source_target_pairs={{0,4},{4,8},{8,12},{12,16},{16,20},{20,24},{24,28},{1,5},{5,9},{9,... | collective-permute-start | bytes 589832 | tf_op jit(solution)/shard_map/ppermute | solution.py:333
  22.1 4.6 %collective-permute-start.6 = (f32[6,48,128]{2,1,0:T(8,128)S(1)}, f32[6,48,128]{2,1,0:T(8,128)S(1)}, u32[]{:S(2)}, u32[]{:S(2)}) collective-permute-start(f32[6,48,128]{2,1,0:T(8,128)S(1)} %get-tuple-element.42.grp_lo), channel_id=1, source_target_pairs={{1,0},{2,1},{3,2},{5,4},{6,5},{7,6},{9,8},{10,9},{11,10},{13,12},{... | collective-permute-start | bytes 442376 | tf_op jit(solution)/shard_map/ppermute | solution.py:333
  24.1 6.5 %collective-permute-start.5 = (f32[6,48,128]{2,1,0:T(8,128)S(1)}, f32[6,48,128]{2,1,0:T(8,128)S(1)}, u32[]{:S(2)}, u32[]{:S(2)}) collective-permute-start(f32[6,48,128]{2,1,0:T(8,128)S(1)} %get-tuple-element.43.grp_hi), channel_id=1, source_target_pairs={{0,1},{1,2},{2,3},{4,5},{5,6},{6,7},{8,9},{9,10},{10,11},{12,13},{... | collective-permute-start | bytes 442376 | tf_op jit(solution)/shard_map/ppermute | solution.py:333
  30.6 11.7 %collective-permute-start.7 = (f32[6,80,128]{2,1,0:T(8,128)S(1)}, f32[6,80,128]{2,1,0:T(8,128)S(1)}, u32[]{:S(2)}, u32[]{:S(2)}) collective-permute-start(f32[6,80,128]{2,1,0:T(8,128)S(1)} %get-tuple-element.44), channel_id=1, source_target_pairs={{4,0},{8,4},{12,8},{16,12},{20,16},{24,20},{28,24},{5,1},{9,5},{13... | collective-permute-start | bytes 737288 | tf_op jit(solution)/shard_map/ppermute | solution.py:333
  35.4 6.9 %collective-permute-start.8 = (f32[6,16,128]{2,1,0:T(8,128)S(1)}, f32[6,16,128]{2,1,0:T(8,128)S(1)}, u32[]{:S(2)}, u32[]{:S(2)}) collective-permute-start(f32[6,16,128]{2,1,0:T(8,128)S(1)} %get-tuple-element.45), channel_id=1, source_target_pairs={{0,4},{4,8},{8,12},{12,16},{16,20},{20,24},{24,28},{1,5},{5,9},{9,... | collective-permute-start | bytes 147464 | tf_op jit(solution)/shard_map/ppermute | solution.py:333

commit v3 on v2

--- a/solution.py
+++ b/solution.py
@@ -39,6 +39,25 @@
 
 def column(row):
     return jnp.broadcast_to(row, (LANES, LANES)).T
+
+
+def swap_lanes(x, distance):
+    lane = lax.broadcasted_iota(jnp.int32, x.shape, 1)
+    after = pltpu.roll(x, LANES - distance, 1)
+    before = pltpu.roll(x, distance, 1)
+    return jnp.where((lane & distance) == 0, after, before)
+
+
+def order_lists(ids):
+    sub_even = (lax.axis_index("sub") & 1) == 0
+    grp_even = (lax.axis_index("grp") & 1) == 0
+    first, second = ids[:, :LANES], ids[:, LANES:]
+    ids[:, :LANES] = jnp.where(sub_even, swap_lanes(first, NIS), first)
+    lane = lax.broadcasted_iota(jnp.int32, second.shape, 1)
+    groups = jnp.where(grp_even, swap_lanes(second, NIG), second)
+    edges = jnp.where(sub_even, swap_lanes(second, 2 * NED), second)
+    edges = jnp.where(grp_even, swap_lanes(edges, NED), edges)
+    ids[:, LANES:] = jnp.where(lane < 2 * NIG, groups, edges)
 
 
 def prepare_kernel(
@@ -53,7 +72,6 @@
     connect,
     interface,
     volume,
-    coarse,
     inverse,
     coupled,
     loads,
@@ -65,7 +83,6 @@
     count,
     placing,
     inverse_volume,
-    own,
     corner_v,
     panel_v,
     coupling_v,
@@ -89,7 +106,6 @@
         (coupling, coupling_v),
         (force, force_v),
         (panel_inv, inverse),
-        (coarse, own),
     ]
     copies = [pltpu.make_async_copy(src, dst, sems.at[k]) for k, (src, dst) in enumerate(pairs)]
     for copy in copies:
@@ -112,6 +128,7 @@
     copies[1].wait()
     ids[...] = jnp.full(ids.shape, -1.0, F32)
     ids[0:1, 0:NIF] = interface_v[...].astype(F32)
+    order_lists(ids)
     node_of = lax.broadcasted_iota(jnp.int32, (nodes, 2 * LANES), 0)
     placing[...] = jnp.where(ids[0:1, :].astype(jnp.int32) == node_of, 1.0, 0.0).astype(BF16)
     connect_f = connect_v[...].astype(F32)
@@ -129,8 +146,10 @@
     wanted = column(ids[0:1, :LANES])[:TERM]
     lane = lax.broadcasted_iota(jnp.int32, (TERM, LANES), 1)
     entry = lax.broadcasted_iota(jnp.int32, (TERM, LANES), 0)
-    for b in range(3):
-        row = (lax.axis_index("sub") - 1 + b) * blocks + lane
+    s = lax.axis_index("sub")
+    aside = 1 - 2 * (s & 1)
+    for b, owner in enumerate((s, s + aside, s - aside)):
+        row = owner * blocks + lane
         hit = (wanted == row.astype(F32)) & (lane < blocks) & (entry < q)
         select[:, b * LANES : (b + 1) * LANES] = jnp.where(hit, 1.0, 0.0).astype(BF16)
 
@@ -166,7 +185,12 @@
         loads[pl.ds(c, nodes, stride=3), :] = force_v[c].astype(F32)
     loads[...] = loads[...] * live[...]
     copies[9].wait()
-    copies[10].wait()
+
+
+def load_kernel(coarse, own, sem):
+    copy = pltpu.make_async_copy(coarse, own, sem)
+    copy.start()
+    copy.wait()
 
 
 def merge_kernel(bit, own, other, out):
@@ -177,9 +201,9 @@
 
 
 def solve_kernel(
-    below,
     here,
-    above,
+    beside,
+    beyond,
     inverse,
     coupled,
     loads,
@@ -190,7 +214,10 @@
     scaled,
     disp,
     stress,
-    sub_hi,
+    sub_a,
+    sub_b,
+    grp_a,
+    grp_b,
     terms,
     solved,
     disp_t,
@@ -201,7 +228,7 @@
     rows = here.shape[0]
 
     terms[...] = jnp.zeros(terms.shape, BF16)
-    for b, block in enumerate((below, here, above)):
+    for b, block in enumerate((here, beside, beyond)):
         x = block[...]
         high = x.astype(BF16)
         rest = x - high.astype(F32)
@@ -242,31 +269,24 @@
             stress[i * LANES + start : i * LANES + start + step, 0:LANES] = high
             stress[i * LANES + start : i * LANES + start + step, LANES : 2 * LANES] = low
 
-    rows = dot_nt(face[NIS : 2 * NIS, :], stress[...])
-    for i in range(COMPS):
-        sub_hi[i] = rows[:, i * LANES : (i + 1) * LANES]
-
-
-def face_kernel(face, stress, sub_lo, grp_lo, grp_hi):
-    low = dot_nt(face[:NIS, :], stress[...])
-    rows = dot_nt(face[2 * NIS :, :], stress[...])
-    base = EDGES - 2 * NIS
+    rows = dot_nt(face[...], stress[...])
     for i in range(COMPS):
         part = rows[:, i * LANES : (i + 1) * LANES]
-        edge = [part[base + NED * k : base + NED * (k + 1)] for k in range(4)]
-        first = low[:, i * LANES : (i + 1) * LANES]
-        sub_lo[i] = jnp.concatenate([first, edge[0], edge[1]], axis=0)
-        grp_lo[i] = jnp.concatenate([part[:NIG], edge[0], edge[2]], axis=0)
-        grp_hi[i] = jnp.concatenate([part[NIG:base], edge[1], edge[3]], axis=0)
-
-
-def edge_kernel(sub_lo, grp_lo, grp_hi, from_lo, from_hi, _, sub_out, edge_hi):
+        edge = [part[EDGES + NED * k : EDGES + NED * (k + 1)] for k in range(4)]
+        sub_a[i] = part[:NIS]
+        sub_b[i] = part[NIS : 2 * NIS]
+        grp_a[i] = jnp.concatenate([part[2 * NIS : 2 * NIS + NIG], edge[0], edge[2]], axis=0)
+        grp_b[i] = jnp.concatenate([part[2 * NIS + NIG : EDGES], edge[1], edge[3]], axis=0)
+
+
+def edge_kernel(sub_a, sub_b, grp_a, grp_b, from_a, from_b, out_a, out_b):
     split = NIG + NED
-    sub_out[:, :NIS, :] = sub_lo[:, :NIS, :]
-    sub_out[:, NIS : NIS + NED, :] = grp_lo[:, NIG:split, :] + from_lo[:, NIG:split, :]
-    sub_out[:, NIS + NED :, :] = grp_hi[:, NIG:split, :] + from_hi[:, NIG:split, :]
-    edge_hi[:, 0:NED, :] = grp_lo[:, split:, :] + from_lo[:, split:, :]
-    edge_hi[:, NED:, :] = grp_hi[:, split:, :] + from_hi[:, split:, :]
+    out_a[:, :NIS, :] = sub_a[...]
+    out_b[:, :NIS, :] = sub_b[...]
+    out_a[:, NIS : NIS + NED, :] = grp_a[:, NIG:split, :] + from_a[:, NIG:split, :]
+    out_a[:, NIS + NED :, :] = grp_b[:, NIG:split, :] + from_b[:, NIG:split, :]
+    out_b[:, NIS : NIS + NED, :] = grp_a[:, split:, :] + from_a[:, split:, :]
+    out_b[:, NIS + NED :, :] = grp_b[:, split:, :] + from_b[:, split:, :]
 
 
 def partial_kernel(count, stress, disp, partial, disp_out):
@@ -276,21 +296,21 @@
 
 
 def finish_kernel(
-    placing, partial, inverse_volume, sub_lo, sub_hi, grp_lo, grp_hi, edge_lo, out, received
+    placing, partial, inverse_volume, sub_a, sub_b, grp_a, grp_b, out, received
 ):
     split = NIG + NED
     for i in range(COMPS):
-        lo, hi, low_edge, high = grp_lo[i], grp_hi[i], edge_lo[i], sub_hi[i]
+        low, high, sub, last = grp_a[i], grp_b[i], sub_a[i], sub_b[i]
         rows = jnp.concatenate(
             [
-                sub_lo[i],
-                high[:NIS],
-                lo[:NIG],
-                hi[:NIG],
-                lo[NIG:split] + low_edge[:NED],
-                hi[NIG:split] + low_edge[NED:],
-                lo[split:] + high[NIS : NIS + NED],
-                hi[split:] + high[NIS + NED :],
+                sub[:NIS],
+                last[:NIS],
+                low[:NIG],
+                high[:NIG],
+                low[NIG:split] + sub[NIS : NIS + NED],
+                high[NIG:split] + sub[NIS + NED :],
+                low[split:] + last[NIS : NIS + NED],
+                high[split:] + last[NIS + NED :],
                 jnp.zeros((2 * LANES - NIF, LANES), F32),
             ],
             axis=0,
@@ -327,9 +347,11 @@
     )
 
 
-def shift(block, axis, up):
+def exchange(block, axis, first):
     count = lax.axis_size(axis)
-    pairs = [(i, i + 1) if up else (i + 1, i) for i in range(count - 1)]
+    pairs = []
+    for i in range(first, count - 1, 2):
+        pairs += [(i, i + 1), (i + 1, i)]
     return lax.ppermute(block, axis, pairs)
 
 
@@ -389,9 +411,8 @@
             array((nodes, 2 * LANES), BF16),
             array((nodes, 2 * LANES), BF16),
             array((nodes, LANES)),
-            array(coarse.shape),
         ),
-        [pl.BlockSpec(memory_space=pltpu.HBM)] * 11,
+        [pl.BlockSpec(memory_space=pltpu.HBM)] * 10,
         (
             pltpu.VMEM((1, q), jnp.int32),
             pltpu.VMEM(panel_nodes.shape, jnp.int32),
@@ -403,7 +424,7 @@
             pltpu.VMEM(interface.shape, jnp.int32),
             pltpu.VMEM((nodes // LANES, LANES), F32),
             pltpu.VMEM((8, 2 * LANES), F32),
-            pltpu.SemaphoreType.DMA((11,)),
+            pltpu.SemaphoreType.DMA((10,)),
         ),
         flops=200000000,
         moved=8000000,
@@ -419,21 +440,30 @@
             connect,
             interface,
             nodal_volume.reshape(-1, LANES),
-            coarse,
         )
     )
-    *operands, count, placing, inverse_volume, own = prepared
-
+    *operands, count, placing, inverse_volume = prepared
+
+    (own,) = call(
+        load_kernel,
+        "load_own",
+        (array(coarse.shape),),
+        [pl.BlockSpec(memory_space=pltpu.HBM)],
+        (pltpu.SemaphoreType.DMA,),
+    )(*in_hbm(coarse))
     here = gather_group(coarse, own)
-    below = shift(here, "sub", True)
-    above = shift(here, "sub", False)
-    disp, stress, sub_hi = call(
+    beyond = exchange(here, "sub", 1)
+    beside = exchange(here, "sub", 0)
+    disp, stress, sub_a, sub_b, grp_a, grp_b = call(
         solve_kernel,
         "solve_and_stress",
         (
             array((3, nodes, cases), BF16),
             array((COMPS * cases, 2 * LANES), BF16),
             array((COMPS, NIS, cases)),
+            array((COMPS, NIS, cases)),
+            array((COMPS, NIG + 2 * NED, cases)),
+            array((COMPS, NIG + 2 * NED, cases)),
         ),
         vmem(11),
         (
@@ -444,30 +474,17 @@
         ),
         flops=1500000000,
         moved=4000000,
-    )(below, here, above, *operands)
-    from_sub_lo = shift(sub_hi, "sub", True)
-    sub_lo, grp_lo, grp_hi = call(
-        face_kernel,
-        "interface_rows",
-        (
-            array((COMPS, NIS + 2 * NED, cases)),
-            array((COMPS, NIG + 2 * NED, cases)),
-            array((COMPS, NIG + 2 * NED, cases)),
-        ),
-        vmem(2),
-        flops=100000000,
-        moved=1000000,
-    )(operands[6], stress)
-    from_grp_lo = shift(grp_hi, "grp", True)
-    from_grp_hi = shift(grp_lo, "grp", False)
-    sub_lo, edge_hi = call(
+    )(here, beside, beyond, *operands)
+    from_grp_a = exchange(grp_a, "grp", 0)
+    from_grp_b = exchange(grp_b, "grp", 1)
+    sub_a, sub_b = call(
         edge_kernel,
         "sum_edges",
-        (array(sub_lo.shape), array((COMPS, 2 * NED, cases))),
-        vmem(5) + [pl.BlockSpec(memory_space=pl.ANY)],
-    )(sub_lo, grp_lo, grp_hi, from_grp_lo, from_grp_hi, from_sub_lo)
-    from_edge_lo = shift(edge_hi, "sub", True)
-    from_sub_hi = shift(sub_lo, "sub", False)
+        (array((COMPS, NIS + 2 * NED, cases)), array((COMPS, NIS + 2 * NED, cases))),
+        vmem(6),
+    )(sub_a, sub_b, grp_a, grp_b, from_grp_a, from_grp_b)
+    from_sub_a = exchange(sub_a, "sub", 0)
+    from_sub_b = exchange(sub_b, "sub", 1)
     partial, disp = call(
         partial_kernel,
         "assemble_nodes",
@@ -480,7 +497,7 @@
         finish_kernel,
         "add_received",
         (array((COMPS, nodes, cases), BF16),),
-        vmem(8),
+        vmem(7),
         (pltpu.VMEM((2, 2 * LANES, COMPS * cases), BF16),),
         flops=800000000,
         moved=3000000,
@@ -488,11 +505,10 @@
         placing,
         partial,
         inverse_volume,
-        from_sub_lo,
-        from_sub_hi,
-        from_grp_lo,
-        from_grp_hi,
-        from_edge_lo,
+        from_sub_a,
+        from_sub_b,
+        from_grp_a,
+        from_grp_b,
     )
     return jnp.transpose(disp, (1, 0, 2)), jnp.transpose(nodal, (1, 0, 2))
 

time: 44.1 us -> 35.5 us (0.80)
  starting transfers between devices: 19.6 us -> 11.9 us
  waiting for transfers between devices: 15.3 us -> 13.7 us
  Pallas kernels: 8.17 us -> 8.72 us
    ppermute x7 -> x6, starting transfers between devices: 18.9 us -> 11.3 us  [exchange(): return lax.ppermute(block, axis, pairs)]
    ppermute x7 -> x6, waiting for transfers between devices: 12 us -> 9.78 us  [exchange(): return lax.ppermute(block, axis, pairs)]
    ppermute x2, waiting for transfers between devices: 3.29 us -> 3.94 us  [gather_group(): lax.ppermute(block, 'grp', [(i, i ^ 1 << bit) for i in range(count)])]
  transfers between devices with their start and end apart: 9 -> 8, of which waited for: 6 -> 6; matrix products, arithmetic and copies ran while one was open for 0% -> 0% of each run, Pallas kernels for 9% -> 12%
where the time goes in v3:
time: 35.5 us; the launch traced here: 35.1 us
  waiting for transfers between devices  13.7 us (39%)
  starting transfers between devices  11.9 us (34%)
  Pallas kernels  8.72 us (25%)
  between operations  0.71 us (2%)
    ppermute x6, starting transfers between devices, exchange(): return lax.ppermute(block, axis, pairs)  11.3 us
    ppermute x6, waiting for transfers between devices, exchange(): return lax.ppermute(block, axis, pairs)  9.78 us
    ppermute x2, waiting for transfers between devices, gather_group(): lax.ppermute(block, 'grp', [(i, i ^ 1 << bit) for i in range(count)])  3.94 us
    pallas_call x1, Pallas kernels, shards(): call(solve_kernel, 'solve_and_stress', (array((3, nodes, cases), BF16), a...  2.92 us
    pallas_call x1, Pallas kernels, shards(): call(prepare, 'prepare', (array(panel_inv.shape, BF16), array((dofs, LANE...  2.27 us
    pallas_call x1, Pallas kernels, shards(): call(finish_kernel, 'add_received', (array((COMPS, nodes, cases), BF16),)...  1.51 us
    pallas_call x1, Pallas kernels, shards(): call(partial_kernel, 'assemble_nodes', (array((COMPS, nodes, cases)), arr...  1.25 us
    pallas_call x1, Pallas kernels, shards(): call(load_kernel, 'load_own', (array(coarse.shape),), [pl.BlockSpec(memor...  0.72 us
  transfers between devices with their start and end apart: 8, of which 6 were waited for; matrix products, arithmetic and copies ran while one was open for 0% of the time, Pallas kernels for 12%

profile of v3, /device:TPU:10, one launch (start us, length us, event | category | flops | bytes accessed | tf_op | source)
XLA Modules:
  0.0 35.1 jit_solution(10985880585724895401)
XLA Ops:
  0.6 0.1 collective-permute-start
  0.7 0.7 %load_own.1.own = f32[24,128]{1,0:T(8,128)S(1)} custom-call(f32[24,128]{1,0:T(8,128)} %coarse.1), custom_call_target="tpu_custom_call" | custom-call | tf_op jit(solution)/shard_map/load_own/pallas_call | solution.py:447
  1.4 0.7 %collective-permute-done.received = f32[24,128]{1,0:T(8,128)S(1)} collective-permute-done((f32[24,128]{1,0:T(8,128)}, f32[24,128]{1,0:T(8,128)S(1)}, u32[]{:S(2)}, u32[]{:S(2)}) %collective-permute-start) | collective-permute-done | bytes 12320 | tf_op jit(solution)/shard_map/ppermute | solution.py:366
  2.1 0.5 %collective-permute-start.1 = (f32[48,128]{1,0:T(8,128)S(1)}, f32[48,128]{1,0:T(8,128)S(1)}, u32[]{:S(2)}, u32[]{:S(2)}) collective-permute-start(f32[48,128]{1,0:T(8,128)S(1)} %merge_blocks.2.own), channel_id=1, source_target_pairs={{0,2},{1,3},{2,0},{3,1},{4,6},{5,7},{6,4},{7,5},{8,10},{9,11},{10,... | collective-permute-start | bytes 73736 | tf_op jit(solution)/shard_map/ppermute | solution.py:366
  2.6 3.3 %collective-permute-done.1.received = f32[48,128]{1,0:T(8,128)S(1)} collective-permute-done((f32[48,128]{1,0:T(8,128)S(1)}, f32[48,128]{1,0:T(8,128)S(1)}, u32[]{:S(2)}, u32[]{:S(2)}) %collective-permute-start.1) | collective-permute-done | bytes 24608 | tf_op jit(solution)/shard_map/ppermute | solution.py:366
  5.9 3.3 %collective-permute-start.3 = (f32[96,128]{1,0:T(8,128)S(1)}, f32[96,128]{1,0:T(8,128)S(1)}, u32[]{:S(2)}, u32[]{:S(2)}) collective-permute-start(f32[96,128]{1,0:T(8,128)S(1)} %merge_blocks.3.here), channel_id=1, source_target_pairs={{4,8},{8,4},{12,16},{16,12},{20,24},{24,20},{5,9},{9,5},{13,17},{1... | collective-permute-start | bytes 147464 | tf_op jit(solution)/shard_map/ppermute | solution.py:355
  9.2 1.7 %collective-permute-start.2 = (f32[96,128]{1,0:T(8,128)S(1)}, f32[96,128]{1,0:T(8,128)S(1)}, u32[]{:S(2)}, u32[]{:S(2)}) collective-permute-start(f32[96,128]{1,0:T(8,128)S(1)} %merge_blocks.3.here), channel_id=1, source_target_pairs={{0,4},{4,0},{8,12},{12,8},{16,20},{20,16},{24,28},{28,24},{1,5},{5... | collective-permute-start | bytes 147464 | tf_op jit(solution)/shard_map/ppermute | solution.py:355
  10.9 2.3 %prepare.1 = (bf16[4,384,384]{2,1,0:T(8,128)(2,1)S(1)}, bf16[1536,128]{1,0:T(8,128)(2,1)S(1)}, f32[1536,128]{1,0:T(8,128)S(1)}, f32[1536,128]{1,0:T(8,128)S(1)},...) custom-call(s32[1,24]{1,0:T(1,128)} %refs_0_.1, ...), custom_call_target="tpu_custom_call" | custom-call | flops 200000000 | bytes 8000000 | tf_op jit(solution)/shard_map/prepare/pallas_call | solution.py:399
  13.2 0.0 collective-permute-done.3.beyond
  13.2 0.2 collective-permute-done.2.beside
  13.4 2.9 %solve_and_stress.1 = (bf16[3,512,128]{2,1,0:T(8,128)(2,1)S(1)}, bf16[768,256]{1,0:T(8,128)(2,1)S(1)}, f32[6,64,128]{2,1,0:T(8,128)S(1)}, f32[6,64,128]{2,1,0:T(...) custom-call(f32[96,128]{1,0:T(8,128)S(1)} %merge_blocks.3.here, ...), custom_call_target="tpu_custom_call" | custom-call | flops 1500000000 | bytes 4000000 | tf_op jit(solution)/shard_map/solve_and_stress/pallas_call | solution.py:457
  16.3 0.1 collective-permute-start.4
  16.4 2.5 %collective-permute-start.5 = (f32[6,48,128]{2,1,0:T(8,128)S(1)}, f32[6,48,128]{2,1,0:T(8,128)S(1)}, u32[]{:S(2)}, u32[]{:S(2)}) collective-permute-start(f32[6,48,128]{2,1,0:T(8,128)S(1)} %get-tuple-element.41.grp_b), channel_id=1, source_target_pairs={{1,2},{2,1},{5,6},{6,5},{9,10},{10,9},{13,14},{14,13},{17,18},{18,... | collective-permute-start | bytes 442376 | tf_op jit(solution)/shard_map/ppermute | solution.py:355
  18.9 0.0 collective-permute-done.4.from_a.grp_a
  18.9 3.9 %collective-permute-done.5.from_b.grp_b = f32[6,48,128]{2,1,0:T(8,128)S(1)} collective-permute-done((f32[6,48,128]{2,1,0:T(8,128)S(1)}, f32[6,48,128]{2,1,0:T(8,128)S(1)}, u32[]{:S(2)}, u32[]{:S(2)}) %collective-permute-start.5) | collective-permute-done | bytes 147488 | tf_op jit(solution)/shard_map/ppermute | solution.py:355
  22.9 1.7 %collective-permute-start.6 = (f32[6,80,128]{2,1,0:T(8,128)S(1)}, f32[6,80,128]{2,1,0:T(8,128)S(1)}, u32[]{:S(2)}, u32[]{:S(2)}) collective-permute-start(f32[6,80,128]{2,1,0:T(8,128)S(1)} %get-tuple-element.42), channel_id=1, source_target_pairs={{0,4},{4,0},{8,12},{12,8},{16,20},{20,16},{24,28},{28,24},{1,5},{5... | collective-permute-start | bytes 737288 | tf_op jit(solution)/shard_map/ppermute | solution.py:355
  24.6 2.0 %collective-permute-start.7 = (f32[6,80,128]{2,1,0:T(8,128)S(1)}, f32[6,80,128]{2,1,0:T(8,128)S(1)}, u32[]{:S(2)}, u32[]{:S(2)}) collective-permute-start(f32[6,80,128]{2,1,0:T(8,128)S(1)} %get-tuple-element.43), channel_id=1, source_target_pairs={{4,8},{8,4},{12,16},{16,12},{20,24},{24,20},{5,9},{9,5},{13,17},{1... | collective-permute-start | bytes 737288 | tf_op jit(solution)/shard_map/ppermute | solution.py:355
  26.6 1.3 %assemble_nodes.1 = (f32[6,512,128]{2,1,0:T(8,128)S(1)}, bf16[3,512,128]{2,1,0:T(8,128)(2,1)}) custom-call(bf16[512,256]{1,0:T(8,128)(2,1)S(1)} %get-tuple-element.23.count, bf16[768,256]{1,0:T(8,128)(2,1)S(1)} %get-tuple-element.32.stress, bf16[3,512,128]{2,1,0:T(8,128)(2,1)S(1)} %get-tuple-element.33.disp), custom_call_target="tpu_custom_call" | custom-call | flops 400000000 | bytes 2000000 | tf_op jit(solution)/shard_map/assemble_nodes/pallas_call | solution.py:488
  27.9 2.1 %collective-permute-done.6.sub_a = f32[6,80,128]{2,1,0:T(8,128)S(1)} collective-permute-done((f32[6,80,128]{2,1,0:T(8,128)S(1)}, f32[6,80,128]{2,1,0:T(8,128)S(1)}, u32[]{:S(2)}, u32[]{:S(2)}) %collective-permute-start.6) | collective-permute-done | bytes 245792 | tf_op jit(solution)/shard_map/ppermute | solution.py:355
  30.0 3.6 %collective-permute-done.7.sub_b = f32[6,80,128]{2,1,0:T(8,128)S(1)} collective-permute-done((f32[6,80,128]{2,1,0:T(8,128)S(1)}, f32[6,80,128]{2,1,0:T(8,128)S(1)}, u32[]{:S(2)}, u32[]{:S(2)}) %collective-permute-start.7) | collective-permute-done | bytes 245792 | tf_op jit(solution)/shard_map/ppermute | solution.py:355
  33.6 1.5 %add_received.1 = bf16[6,512,128]{2,1,0:T(8,128)(2,1)} custom-call(bf16[512,256]{1,0:T(8,128)(2,1)S(1)} %get-tuple-element.35.placing, f32[6,512,128]{2,1,0:T(8,128)S(1)} %get-tuple-element.36.partial, f32[512,128]{1,0:T(8,128)S(1)} %get-tuple-element.37.inverse_volume, f32[6,80,128]{2,1,0:T(8,128)S(1)} %collective-permute-done.6.sub_a, ...), custom_call_target="tpu_custom_call" | custom-call | flops 800000000 | bytes 3000000 | tf_op jit(solution)/shard_map/add_received/pallas_call | solution.py:496
  (3 shorter events, 0.0 us)
Async XLA Ops:
  0.6 1.5 %collective-permute-start = (f32[24,128]{1,0:T(8,128)}, f32[24,128]{1,0:T(8,128)S(1)}, u32[]{:S(2)}, u32[]{:S(2)}) collective-permute-start(f32[24,128]{1,0:T(8,128)} %coarse.1), channel_id=1, source_target_pairs={{0,1},{1,0},{2,3},{3,2},{4,5},{5,4},{6,7},{7,6},{8,9},{9,8},{10,11... | collective-permute-start | bytes 36872 | tf_op jit(solution)/shard_map/ppermute | solution.py:366
  2.1 3.8 %collective-permute-start.1 = (f32[48,128]{1,0:T(8,128)S(1)}, f32[48,128]{1,0:T(8,128)S(1)}, u32[]{:S(2)}, u32[]{:S(2)}) collective-permute-start(f32[48,128]{1,0:T(8,128)S(1)} %merge_blocks.2.own), channel_id=1, source_target_pairs={{0,2},{1,3},{2,0},{3,1},{4,6},{5,7},{6,4},{7,5},{8,10},{9,11},{10,... | collective-permute-start | bytes 73736 | tf_op jit(solution)/shard_map/ppermute | solution.py:366
  5.9 7.3 %collective-permute-start.3 = (f32[96,128]{1,0:T(8,128)S(1)}, f32[96,128]{1,0:T(8,128)S(1)}, u32[]{:S(2)}, u32[]{:S(2)}) collective-permute-start(f32[96,128]{1,0:T(8,128)S(1)} %merge_blocks.3.here), channel_id=1, source_target_pairs={{4,8},{8,4},{12,16},{16,12},{20,24},{24,20},{5,9},{9,5},{13,17},{1... | collective-permute-start | bytes 147464 | tf_op jit(solution)/shard_map/ppermute | solution.py:355
  9.2 4.2 %collective-permute-start.2 = (f32[96,128]{1,0:T(8,128)S(1)}, f32[96,128]{1,0:T(8,128)S(1)}, u32[]{:S(2)}, u32[]{:S(2)}) collective-permute-start(f32[96,128]{1,0:T(8,128)S(1)} %merge_blocks.3.here), channel_id=1, source_target_pairs={{0,4},{4,0},{8,12},{12,8},{16,20},{20,16},{24,28},{28,24},{1,5},{5... | collective-permute-start | bytes 147464 | tf_op jit(solution)/shard_map/ppermute | solution.py:355
  16.3 2.6 %collective-permute-start.4 = (f32[6,48,128]{2,1,0:T(8,128)S(1)}, f32[6,48,128]{2,1,0:T(8,128)S(1)}, u32[]{:S(2)}, u32[]{:S(2)}) collective-permute-start(f32[6,48,128]{2,1,0:T(8,128)S(1)} %get-tuple-element.40.grp_a), channel_id=1, source_target_pairs={{0,1},{1,0},{2,3},{3,2},{4,5},{5,4},{6,7},{7,6},{8,9},{9,8},{10,11... | collective-permute-start | bytes 442376 | tf_op jit(solution)/shard_map/ppermute | solution.py:355
  16.4 6.5 %collective-permute-start.5 = (f32[6,48,128]{2,1,0:T(8,128)S(1)}, f32[6,48,128]{2,1,0:T(8,128)S(1)}, u32[]{:S(2)}, u32[]{:S(2)}) collective-permute-start(f32[6,48,128]{2,1,0:T(8,128)S(1)} %get-tuple-element.41.grp_b), channel_id=1, source_target_pairs={{1,2},{2,1},{5,6},{6,5},{9,10},{10,9},{13,14},{14,13},{17,18},{18,... | collective-permute-start | bytes 442376 | tf_op jit(solution)/shard_map/ppermute | solution.py:355
  22.9 7.1 %collective-permute-start.6 = (f32[6,80,128]{2,1,0:T(8,128)S(1)}, f32[6,80,128]{2,1,0:T(8,128)S(1)}, u32[]{:S(2)}, u32[]{:S(2)}) collective-permute-start(f32[6,80,128]{2,1,0:T(8,128)S(1)} %get-tuple-element.42), channel_id=1, source_target_pairs={{0,4},{4,0},{8,12},{12,8},{16,20},{20,16},{24,28},{28,24},{1,5},{5... | collective-permute-start | bytes 737288 | tf_op jit(solution)/shard_map/ppermute | solution.py:355
  24.6 9.0 %collective-permute-start.7 = (f32[6,80,128]{2,1,0:T(8,128)S(1)}, f32[6,80,128]{2,1,0:T(8,128)S(1)}, u32[]{:S(2)}, u32[]{:S(2)}) collective-permute-start(f32[6,80,128]{2,1,0:T(8,128)S(1)} %get-tuple-element.43), channel_id=1, source_target_pairs={{4,8},{8,4},{12,16},{16,12},{20,24},{24,20},{5,9},{9,5},{13,17},{1... | collective-permute-start | bytes 737288 | tf_op jit(solution)/shard_map/ppermute | solution.py:355

commit v4 on v3

--- a/solution.py
+++ b/solution.py
@@ -279,14 +279,12 @@
         grp_b[i] = jnp.concatenate([part[2 * NIS + NIG : EDGES], edge[1], edge[3]], axis=0)
 
 
-def edge_kernel(sub_a, sub_b, grp_a, grp_b, from_a, from_b, out_a, out_b):
+def edge_kernel(grp_a, grp_b, from_a, from_b, edge_a, edge_b):
     split = NIG + NED
-    out_a[:, :NIS, :] = sub_a[...]
-    out_b[:, :NIS, :] = sub_b[...]
-    out_a[:, NIS : NIS + NED, :] = grp_a[:, NIG:split, :] + from_a[:, NIG:split, :]
-    out_a[:, NIS + NED :, :] = grp_b[:, NIG:split, :] + from_b[:, NIG:split, :]
-    out_b[:, NIS : NIS + NED, :] = grp_a[:, split:, :] + from_a[:, split:, :]
-    out_b[:, NIS + NED :, :] = grp_b[:, split:, :] + from_b[:, split:, :]
+    edge_a[:, :NED, :] = grp_a[:, NIG:split, :] + from_a[:, NIG:split, :]
+    edge_a[:, NED:, :] = grp_b[:, NIG:split, :] + from_b[:, NIG:split, :]
+    edge_b[:, :NED, :] = grp_a[:, split:, :] + from_a[:, split:, :]
+    edge_b[:, NED:, :] = grp_b[:, split:, :] + from_b[:, split:, :]
 
 
 def partial_kernel(count, stress, disp, partial, disp_out):
@@ -296,21 +294,21 @@
 
 
 def finish_kernel(
-    placing, partial, inverse_volume, sub_a, sub_b, grp_a, grp_b, out, received
+    placing, partial, inverse_volume, sub_a, sub_b, grp_a, grp_b, edge_a, edge_b, out, received
 ):
     split = NIG + NED
     for i in range(COMPS):
-        low, high, sub, last = grp_a[i], grp_b[i], sub_a[i], sub_b[i]
+        low, high, first, second = grp_a[i], grp_b[i], edge_a[i], edge_b[i]
         rows = jnp.concatenate(
             [
-                sub[:NIS],
-                last[:NIS],
+                sub_a[i],
+                sub_b[i],
                 low[:NIG],
                 high[:NIG],
-                low[NIG:split] + sub[NIS : NIS + NED],
-                high[NIG:split] + sub[NIS + NED :],
-                low[split:] + last[NIS : NIS + NED],
-                high[split:] + last[NIS + NED :],
+                low[NIG:split] + first[:NED],
+                high[NIG:split] + first[NED:],
+                low[split:] + second[:NED],
+                high[split:] + second[NED:],
                 jnp.zeros((2 * LANES - NIF, LANES), F32),
             ],
             axis=0,
@@ -477,14 +475,16 @@
     )(here, beside, beyond, *operands)
     from_grp_a = exchange(grp_a, "grp", 0)
     from_grp_b = exchange(grp_b, "grp", 1)
-    sub_a, sub_b = call(
+    edge_a, edge_b = call(
         edge_kernel,
         "sum_edges",
-        (array((COMPS, NIS + 2 * NED, cases)), array((COMPS, NIS + 2 * NED, cases))),
-        vmem(6),
-    )(sub_a, sub_b, grp_a, grp_b, from_grp_a, from_grp_b)
+        (array((COMPS, 2 * NED, cases)), array((COMPS, 2 * NED, cases))),
+        vmem(4),
+    )(grp_a, grp_b, from_grp_a, from_grp_b)
+    from_sub_b = exchange(sub_b, "sub", 1)
     from_sub_a = exchange(sub_a, "sub", 0)
-    from_sub_b = exchange(sub_b, "sub", 1)
+    from_edge_b = exchange(edge_b, "sub", 1)
+    from_edge_a = exchange(edge_a, "sub", 0)
     partial, disp = call(
         partial_kernel,
         "assemble_nodes",
@@ -497,7 +497,7 @@
         finish_kernel,
         "add_received",
         (array((COMPS, nodes, cases), BF16),),
-        vmem(7),
+        vmem(9),
         (pltpu.VMEM((2, 2 * LANES, COMPS * cases), BF16),),
         flops=800000000,
         moved=3000000,
@@ -509,6 +509,8 @@
         from_sub_b,
         from_grp_a,
         from_grp_b,
+        from_edge_a,
+        from_edge_b,
     )
     return jnp.transpose(disp, (1, 0, 2)), jnp.transpose(nodal, (1, 0, 2))
 

time: 35.5 us -> 34.4 us (0.969)
  waiting for transfers between devices: 13.7 us -> 8.01 us
  starting transfers between devices: 11.9 us -> 16.6 us
    ppermute x6 -> x8, waiting for transfers between devices: 9.78 us -> 4.06 us  [exchange(): return lax.ppermute(block, axis, pairs)]
    ppermute x6 -> x8, starting transfers between devices: 11.3 us -> 16 us  [exchange(): return lax.ppermute(block, axis, pairs)]
  transfers between devices with their start and end apart: 8 -> 10, of which waited for: 6 -> 6; matrix products, arithmetic and copies ran while one was open for 0% -> 0% of each run, Pallas kernels for 12% -> 12%
where the time goes in v4:
time: 34.4 us; the launch traced here: 34.1 us
  starting transfers between devices  16.6 us (48%)
  Pallas kernels  8.7 us (25%)
  waiting for transfers between devices  8.01 us (23%)
  between operations  0.72 us (2%)
    ppermute x8, starting transfers between devices, exchange(): return lax.ppermute(block, axis, pairs)  16 us
    ppermute x8, waiting for transfers between devices, exchange(): return lax.ppermute(block, axis, pairs)  4.06 us
    ppermute x2, waiting for transfers between devices, gather_group(): lax.ppermute(block, 'grp', [(i, i ^ 1 << bit) for i in range(count)])  3.94 us
    pallas_call x1, Pallas kernels, shards(): call(solve_kernel, 'solve_and_stress', (array((3, nodes, cases), BF16), a...  2.92 us
    pallas_call x1, Pallas kernels, shards(): call(prepare, 'prepare', (array(panel_inv.shape, BF16), array((dofs, LANE...  2.27 us
    pallas_call x1, Pallas kernels, shards(): call(finish_kernel, 'add_received', (array((COMPS, nodes, cases), BF16),)...  1.51 us
    pallas_call x1, Pallas kernels, shards(): call(partial_kernel, 'assemble_nodes', (array((COMPS, nodes, cases)), arr...  1.25 us
    pallas_call x1, Pallas kernels, shards(): call(load_kernel, 'load_own', (array(coarse.shape),), [pl.BlockSpec(memor...  0.72 us
  transfers between devices with their start and end apart: 10, of which 6 were waited for; matrix products, arithmetic and copies ran while one was open for 0% of the time, Pallas kernels for 12%

profile of v4, /device:TPU:10, one launch (start us, length us, event | category | flops | bytes accessed | tf_op | source)
XLA Modules:
  0.0 34.1 jit_solution(9201851720479564130)
XLA Ops:
  0.6 0.1 collective-permute-start
  0.7 0.7 %load_own.1.own = f32[24,128]{1,0:T(8,128)S(1)} custom-call(f32[24,128]{1,0:T(8,128)} %coarse.1), custom_call_target="tpu_custom_call" | custom-call | tf_op jit(solution)/shard_map/load_own/pallas_call | solution.py:445
  1.4 0.7 %collective-permute-done.received = f32[24,128]{1,0:T(8,128)S(1)} collective-permute-done((f32[24,128]{1,0:T(8,128)}, f32[24,128]{1,0:T(8,128)S(1)}, u32[]{:S(2)}, u32[]{:S(2)}) %collective-permute-start) | collective-permute-done | bytes 12320 | tf_op jit(solution)/shard_map/ppermute | solution.py:364
  2.1 0.5 %collective-permute-start.1 = (f32[48,128]{1,0:T(8,128)S(1)}, f32[48,128]{1,0:T(8,128)S(1)}, u32[]{:S(2)}, u32[]{:S(2)}) collective-permute-start(f32[48,128]{1,0:T(8,128)S(1)} %merge_blocks.2.own), channel_id=1, source_target_pairs={{0,2},{1,3},{2,0},{3,1},{4,6},{5,7},{6,4},{7,5},{8,10},{9,11},{10,... | collective-permute-start | bytes 73736 | tf_op jit(solution)/shard_map/ppermute | solution.py:364
  2.6 3.3 %collective-permute-done.1.received = f32[48,128]{1,0:T(8,128)S(1)} collective-permute-done((f32[48,128]{1,0:T(8,128)S(1)}, f32[48,128]{1,0:T(8,128)S(1)}, u32[]{:S(2)}, u32[]{:S(2)}) %collective-permute-start.1) | collective-permute-done | bytes 24608 | tf_op jit(solution)/shard_map/ppermute | solution.py:364
  5.9 3.3 %collective-permute-start.3 = (f32[96,128]{1,0:T(8,128)S(1)}, f32[96,128]{1,0:T(8,128)S(1)}, u32[]{:S(2)}, u32[]{:S(2)}) collective-permute-start(f32[96,128]{1,0:T(8,128)S(1)} %merge_blocks.3.here), channel_id=1, source_target_pairs={{4,8},{8,4},{12,16},{16,12},{20,24},{24,20},{5,9},{9,5},{13,17},{1... | collective-permute-start | bytes 147464 | tf_op jit(solution)/shard_map/ppermute | solution.py:353
  9.2 1.7 %collective-permute-start.2 = (f32[96,128]{1,0:T(8,128)S(1)}, f32[96,128]{1,0:T(8,128)S(1)}, u32[]{:S(2)}, u32[]{:S(2)}) collective-permute-start(f32[96,128]{1,0:T(8,128)S(1)} %merge_blocks.3.here), channel_id=1, source_target_pairs={{0,4},{4,0},{8,12},{12,8},{16,20},{20,16},{24,28},{28,24},{1,5},{5... | collective-permute-start | bytes 147464 | tf_op jit(solution)/shard_map/ppermute | solution.py:353
  10.9 2.3 %prepare.1 = (bf16[4,384,384]{2,1,0:T(8,128)(2,1)S(1)}, bf16[1536,128]{1,0:T(8,128)(2,1)S(1)}, f32[1536,128]{1,0:T(8,128)S(1)}, f32[1536,128]{1,0:T(8,128)S(1)},...) custom-call(s32[1,24]{1,0:T(1,128)} %refs_0_.1, ...), custom_call_target="tpu_custom_call" | custom-call | flops 200000000 | bytes 8000000 | tf_op jit(solution)/shard_map/prepare/pallas_call | solution.py:397
  13.2 0.0 collective-permute-done.3.beyond
  13.2 0.2 collective-permute-done.2.beside
  13.4 2.9 %solve_and_stress.1 = (bf16[3,512,128]{2,1,0:T(8,128)(2,1)S(1)}, bf16[768,256]{1,0:T(8,128)(2,1)S(1)}, f32[6,64,128]{2,1,0:T(8,128)S(1)}, f32[6,64,128]{2,1,0:T(...) custom-call(f32[96,128]{1,0:T(8,128)S(1)} %merge_blocks.3.here, ...), custom_call_target="tpu_custom_call" | custom-call | flops 1500000000 | bytes 4000000 | tf_op jit(solution)/shard_map/solve_and_stress/pallas_call | solution.py:455
  16.3 0.1 collective-permute-start.6
  16.4 2.5 %collective-permute-start.7 = (f32[6,48,128]{2,1,0:T(8,128)S(1)}, f32[6,48,128]{2,1,0:T(8,128)S(1)}, u32[]{:S(2)}, u32[]{:S(2)}) collective-permute-start(f32[6,48,128]{2,1,0:T(8,128)S(1)} %get-tuple-element.41.grp_b), channel_id=1, source_target_pairs={{1,2},{2,1},{5,6},{6,5},{9,10},{10,9},{13,14},{14,13},{17,18},{18,... | collective-permute-start | bytes 442376 | tf_op jit(solution)/shard_map/ppermute | solution.py:353
  18.9 1.7 %collective-permute-start.4 = (f32[6,64,128]{2,1,0:T(8,128)S(1)}, f32[6,64,128]{2,1,0:T(8,128)S(1)}, u32[]{:S(2)}, u32[]{:S(2)}) collective-permute-start(f32[6,64,128]{2,1,0:T(8,128)S(1)} %get-tuple-element.38), channel_id=1, source_target_pairs={{0,4},{4,0},{8,12},{12,8},{16,20},{20,16},{24,28},{28,24},{1,5},{5... | collective-permute-start | bytes 589832 | tf_op jit(solution)/shard_map/ppermute | solution.py:353
  20.6 2.0 %collective-permute-start.5 = (f32[6,64,128]{2,1,0:T(8,128)S(1)}, f32[6,64,128]{2,1,0:T(8,128)S(1)}, u32[]{:S(2)}, u32[]{:S(2)}) collective-permute-start(f32[6,64,128]{2,1,0:T(8,128)S(1)} %get-tuple-element.39), channel_id=1, source_target_pairs={{4,8},{8,4},{12,16},{16,12},{20,24},{24,20},{5,9},{9,5},{13,17},{1... | collective-permute-start | bytes 589832 | tf_op jit(solution)/shard_map/ppermute | solution.py:353
  22.6 0.0 collective-permute-done.6.from_a.grp_a
  22.7 0.2 collective-permute-done.7.from_b.grp_b
  22.9 2.8 %collective-permute-start.8 = (f32[6,16,128]{2,1,0:T(8,128)S(1)}, f32[6,16,128]{2,1,0:T(8,128)S(1)}, u32[]{:S(2)}, u32[]{:S(2)}) collective-permute-start(f32[6,16,128]{2,1,0:T(8,128)S(1)} %get-tuple-element.42), channel_id=1, source_target_pairs={{0,4},{4,0},{8,12},{12,8},{16,20},{20,16},{24,28},{28,24},{1,5},{5... | collective-permute-start | bytes 147464 | tf_op jit(solution)/shard_map/ppermute | solution.py:353
  25.7 1.9 %collective-permute-start.9 = (f32[6,16,128]{2,1,0:T(8,128)S(1)}, f32[6,16,128]{2,1,0:T(8,128)S(1)}, u32[]{:S(2)}, u32[]{:S(2)}) collective-permute-start(f32[6,16,128]{2,1,0:T(8,128)S(1)} %get-tuple-element.43), channel_id=1, source_target_pairs={{4,8},{8,4},{12,16},{16,12},{20,24},{24,20},{5,9},{9,5},{13,17},{1... | collective-permute-start | bytes 147464 | tf_op jit(solution)/shard_map/ppermute | solution.py:353
  27.6 1.3 %assemble_nodes.1 = (f32[6,512,128]{2,1,0:T(8,128)S(1)}, bf16[3,512,128]{2,1,0:T(8,128)(2,1)}) custom-call(bf16[512,256]{1,0:T(8,128)(2,1)S(1)} %get-tuple-element.23.count, bf16[768,256]{1,0:T(8,128)(2,1)S(1)} %get-tuple-element.32.stress, bf16[3,512,128]{2,1,0:T(8,128)(2,1)S(1)} %get-tuple-element.33.disp), custom_call_target="tpu_custom_call" | custom-call | flops 400000000 | bytes 2000000 | tf_op jit(solution)/shard_map/assemble_nodes/pallas_call | solution.py:488
  28.8 1.6 %collective-permute-done.8.edge_a = f32[6,16,128]{2,1,0:T(8,128)S(1)} collective-permute-done((f32[6,16,128]{2,1,0:T(8,128)S(1)}, f32[6,16,128]{2,1,0:T(8,128)S(1)}, u32[]{:S(2)}, u32[]{:S(2)}) %collective-permute-start.8) | collective-permute-done | bytes 49184 | tf_op jit(solution)/shard_map/ppermute | solution.py:353
  30.4 2.1 %collective-permute-done.9.edge_b = f32[6,16,128]{2,1,0:T(8,128)S(1)} collective-permute-done((f32[6,16,128]{2,1,0:T(8,128)S(1)}, f32[6,16,128]{2,1,0:T(8,128)S(1)}, u32[]{:S(2)}, u32[]{:S(2)}) %collective-permute-start.9) | collective-permute-done | bytes 49184 | tf_op jit(solution)/shard_map/ppermute | solution.py:353
  32.5 0.0 collective-permute-done.4.sub_a
  32.5 0.0 collective-permute-done.5.sub_b
  32.6 1.5 %add_received.1 = bf16[6,512,128]{2,1,0:T(8,128)(2,1)} custom-call(bf16[512,256]{1,0:T(8,128)(2,1)S(1)} %get-tuple-element.35.placing, f32[6,512,128]{2,1,0:T(8,128)S(1)} %get-tuple-element.36.partial, f32[512,128]{1,0:T(8,128)S(1)} %get-tuple-element.37.inverse_volume, f32[6,64,128]{2,1,0:T(8,128)S(1)} %collective-permute-done.4.sub_a, ...), custom_call_target="tpu_custom_call" | custom-call | flops 800000000 | bytes 3000000 | tf_op jit(solution)/shard_map/add_received/pallas_call | solution.py:496
  (3 shorter events, 0.0 us)
Async XLA Ops:
  0.6 1.5 %collective-permute-start = (f32[24,128]{1,0:T(8,128)}, f32[24,128]{1,0:T(8,128)S(1)}, u32[]{:S(2)}, u32[]{:S(2)}) collective-permute-start(f32[24,128]{1,0:T(8,128)} %coarse.1), channel_id=1, source_target_pairs={{0,1},{1,0},{2,3},{3,2},{4,5},{5,4},{6,7},{7,6},{8,9},{9,8},{10,11... | collective-permute-start | bytes 36872 | tf_op jit(solution)/shard_map/ppermute | solution.py:364
  2.1 3.8 %collective-permute-start.1 = (f32[48,128]{1,0:T(8,128)S(1)}, f32[48,128]{1,0:T(8,128)S(1)}, u32[]{:S(2)}, u32[]{:S(2)}) collective-permute-start(f32[48,128]{1,0:T(8,128)S(1)} %merge_blocks.2.own), channel_id=1, source_target_pairs={{0,2},{1,3},{2,0},{3,1},{4,6},{5,7},{6,4},{7,5},{8,10},{9,11},{10,... | collective-permute-start | bytes 73736 | tf_op jit(solution)/shard_map/ppermute | solution.py:364
  5.9 7.3 %collective-permute-start.3 = (f32[96,128]{1,0:T(8,128)S(1)}, f32[96,128]{1,0:T(8,128)S(1)}, u32[]{:S(2)}, u32[]{:S(2)}) collective-permute-start(f32[96,128]{1,0:T(8,128)S(1)} %merge_blocks.3.here), channel_id=1, source_target_pairs={{4,8},{8,4},{12,16},{16,12},{20,24},{24,20},{5,9},{9,5},{13,17},{1... | collective-permute-start | bytes 147464 | tf_op jit(solution)/shard_map/ppermute | solution.py:353
  9.2 4.2 %collective-permute-start.2 = (f32[96,128]{1,0:T(8,128)S(1)}, f32[96,128]{1,0:T(8,128)S(1)}, u32[]{:S(2)}, u32[]{:S(2)}) collective-permute-start(f32[96,128]{1,0:T(8,128)S(1)} %merge_blocks.3.here), channel_id=1, source_target_pairs={{0,4},{4,0},{8,12},{12,8},{16,20},{20,16},{24,28},{28,24},{1,5},{5... | collective-permute-start | bytes 147464 | tf_op jit(solution)/shard_map/ppermute | solution.py:353
  16.3 6.3 %collective-permute-start.6 = (f32[6,48,128]{2,1,0:T(8,128)S(1)}, f32[6,48,128]{2,1,0:T(8,128)S(1)}, u32[]{:S(2)}, u32[]{:S(2)}) collective-permute-start(f32[6,48,128]{2,1,0:T(8,128)S(1)} %get-tuple-element.40.grp_a), channel_id=1, source_target_pairs={{0,1},{1,0},{2,3},{3,2},{4,5},{5,4},{6,7},{7,6},{8,9},{9,8},{10,11... | collective-permute-start | bytes 442376 | tf_op jit(solution)/shard_map/ppermute | solution.py:353
  16.4 6.5 %collective-permute-start.7 = (f32[6,48,128]{2,1,0:T(8,128)S(1)}, f32[6,48,128]{2,1,0:T(8,128)S(1)}, u32[]{:S(2)}, u32[]{:S(2)}) collective-permute-start(f32[6,48,128]{2,1,0:T(8,128)S(1)} %get-tuple-element.41.grp_b), channel_id=1, source_target_pairs={{1,2},{2,1},{5,6},{6,5},{9,10},{10,9},{13,14},{14,13},{17,18},{18,... | collective-permute-start | bytes 442376 | tf_op jit(solution)/shard_map/ppermute | solution.py:353
  18.9 13.6 %collective-permute-start.4 = (f32[6,64,128]{2,1,0:T(8,128)S(1)}, f32[6,64,128]{2,1,0:T(8,128)S(1)}, u32[]{:S(2)}, u32[]{:S(2)}) collective-permute-start(f32[6,64,128]{2,1,0:T(8,128)S(1)} %get-tuple-element.38), channel_id=1, source_target_pairs={{0,4},{4,0},{8,12},{12,8},{16,20},{20,16},{24,28},{28,24},{1,5},{5... | collective-permute-start | bytes 589832 | tf_op jit(solution)/shard_map/ppermute | solution.py:353
  20.6 11.9 %collective-permute-start.5 = (f32[6,64,128]{2,1,0:T(8,128)S(1)}, f32[6,64,128]{2,1,0:T(8,128)S(1)}, u32[]{:S(2)}, u32[]{:S(2)}) collective-permute-start(f32[6,64,128]{2,1,0:T(8,128)S(1)} %get-tuple-element.39), channel_id=1, source_target_pairs={{4,8},{8,4},{12,16},{16,12},{20,24},{24,20},{5,9},{9,5},{13,17},{1... | collective-permute-start | bytes 589832 | tf_op jit(solution)/shard_map/ppermute | solution.py:353
  22.9 7.6 %collective-permute-start.8 = (f32[6,16,128]{2,1,0:T(8,128)S(1)}, f32[6,16,128]{2,1,0:T(8,128)S(1)}, u32[]{:S(2)}, u32[]{:S(2)}) collective-permute-start(f32[6,16,128]{2,1,0:T(8,128)S(1)} %get-tuple-element.42), channel_id=1, source_target_pairs={{0,4},{4,0},{8,12},{12,8},{16,20},{20,16},{24,28},{28,24},{1,5},{5... | collective-permute-start | bytes 147464 | tf_op jit(solution)/shard_map/ppermute | solution.py:353
  25.7 6.9 %collective-permute-start.9 = (f32[6,16,128]{2,1,0:T(8,128)S(1)}, f32[6,16,128]{2,1,0:T(8,128)S(1)}, u32[]{:S(2)}, u32[]{:S(2)}) collective-permute-start(f32[6,16,128]{2,1,0:T(8,128)S(1)} %get-tuple-element.43), channel_id=1, source_target_pairs={{4,8},{8,4},{12,16},{16,12},{20,24},{24,20},{5,9},{9,5},{13,17},{1... | collective-permute-start | bytes 147464 | tf_op jit(solution)/shard_map/ppermute | solution.py:353

commit v5 on v4

--- a/solution.py
+++ b/solution.py
@@ -60,22 +60,22 @@
     ids[:, LANES:] = jnp.where(lane < 2 * NIG, groups, edges)
 
 
-def prepare_kernel(
-    blocks,
+def start_copies(pairs, sems):
+    copies = [pltpu.make_async_copy(src, dst, sems.at[k]) for k, (src, dst) in enumerate(pairs)]
+    for copy in copies:
+        copy.start()
+    return copies
+
+
+def prepare_lists(
+    block_rows,
+    members,
     corner_idx,
-    panel_nodes,
-    coupling,
-    force,
-    panel_inv,
+    connect,
+    interface,
     strain_disp,
     modulus,
-    connect,
-    interface,
     volume,
-    inverse,
-    coupled,
-    loads,
-    live,
     select,
     onehot,
     face,
@@ -84,34 +84,26 @@
     placing,
     inverse_volume,
     corner_v,
-    panel_v,
-    coupling_v,
-    force_v,
+    connect_v,
+    interface_v,
     strain_v,
     modulus_v,
-    connect_v,
-    interface_v,
     volume_v,
     ids,
     sems,
 ):
-    pairs = [
-        (connect, connect_v),
-        (interface, interface_v),
-        (corner_idx, corner_v),
-        (panel_nodes, panel_v),
-        (volume, volume_v),
-        (modulus, modulus_v),
-        (strain_disp, strain_v),
-        (coupling, coupling_v),
-        (force, force_v),
-        (panel_inv, inverse),
-    ]
-    copies = [pltpu.make_async_copy(src, dst, sems.at[k]) for k, (src, dst) in enumerate(pairs)]
-    for copy in copies:
-        copy.start()
-    panels, panel_rows, _ = inverse.shape
-    nodes = force_v.shape[1]
+    copies = start_copies(
+        [
+            (connect, connect_v),
+            (interface, interface_v),
+            (corner_idx, corner_v),
+            (modulus, modulus_v),
+            (strain_disp, strain_v),
+            (volume, volume_v),
+        ],
+        sems,
+    )
+    nodes = onehot.shape[0]
     q = corner_idx.shape[1]
 
     copies[0].wait()
@@ -144,27 +136,28 @@
     copies[2].wait()
     ids[0:1, 0:q] = corner_v[...].astype(F32)
     wanted = column(ids[0:1, :LANES])[:TERM]
-    lane = lax.broadcasted_iota(jnp.int32, (TERM, LANES), 1)
+    lane = lax.broadcasted_iota(jnp.int32, (TERM, 3 * LANES), 1)
     entry = lax.broadcasted_iota(jnp.int32, (TERM, LANES), 0)
-    s = lax.axis_index("sub")
+    s, g = lax.axis_index("sub"), lax.axis_index("grp")
     aside = 1 - 2 * (s & 1)
-    for b, owner in enumerate((s, s + aside, s - aside)):
-        row = owner * blocks + lane
-        hit = (wanted == row.astype(F32)) & (lane < blocks) & (entry < q)
-        select[:, b * LANES : (b + 1) * LANES] = jnp.where(hit, 1.0, 0.0).astype(BF16)
+    row = jnp.full((TERM, 3 * LANES), -1, jnp.int32)
+    base = 0
+    for member in range(members):
+        distance, bits, turn = members // 2, member, 0
+        while distance:
+            turn += (bits & 1) * distance
+            distance, bits = distance // 2, bits >> 1
+        for owner in (s, s + aside, s - aside):
+            first = (owner * members + (g ^ turn)) * block_rows
+            row = jnp.where((lane >= base) & (lane < base + block_rows), first - base + lane, row)
+            base += block_rows
+    for b in range(3):
+        cols = slice(b * LANES, (b + 1) * LANES)
+        hit = (wanted == row[:, cols].astype(F32)) & (entry < q)
+        select[:, cols] = jnp.where(hit, 1.0, 0.0).astype(BF16)
 
     copies[3].wait()
-    row_of = lax.broadcasted_iota(jnp.int32, (panel_rows, LANES), 0)
-    for p in range(panels):
-        alive = row_of < 3 * panel_v[0:1, p : p + 1]
-        live[p * panel_rows : (p + 1) * panel_rows, :] = jnp.where(alive, 1.0, 0.0)
-
     copies[4].wait()
-    for k in range(nodes // LANES):
-        inverse_volume[k * LANES : (k + 1) * LANES, :] = column(1.0 / volume_v[k : k + 1, :])
-
-    copies[5].wait()
-    copies[6].wait()
     factor = modulus_v[...]
     rows = [strain_v[i].astype(F32) for i in range(COMPS)]
     trace = (rows[0] + rows[1] + rows[2]) * LAME
@@ -172,7 +165,45 @@
         value = trace + rows[i] * (2.0 * SHEAR) if i < 3 else rows[i] * SHEAR
         scaled[24 * i : 24 * (i + 1), :] = value * factor
 
-    copies[7].wait()
+    copies[5].wait()
+    for k in range(nodes // LANES):
+        inverse_volume[k * LANES : (k + 1) * LANES, :] = column(1.0 / volume_v[k : k + 1, :])
+
+
+def prepare_panels(
+    panel_nodes,
+    coupling,
+    force,
+    panel_inv,
+    inverse,
+    coupled,
+    loads,
+    live,
+    panel_v,
+    coupling_v,
+    force_v,
+    sems,
+):
+    copies = start_copies(
+        [
+            (panel_nodes, panel_v),
+            (coupling, coupling_v),
+            (force, force_v),
+            (panel_inv, inverse),
+        ],
+        sems,
+    )
+    panels, panel_rows, _ = inverse.shape
+    nodes = force_v.shape[1]
+    q = coupling_v.shape[0]
+
+    copies[0].wait()
+    row_of = lax.broadcasted_iota(jnp.int32, (panel_rows, LANES), 0)
+    for p in range(panels):
+        alive = row_of < 3 * panel_v[0:1, p : p + 1]
+        live[p * panel_rows : (p + 1) * panel_rows, :] = jnp.where(alive, 1.0, 0.0)
+
+    copies[1].wait()
     for k in range(coupling_v.shape[1] // LANES):
         part = coupling_v[:, k * LANES : (k + 1) * LANES].astype(F32)
         gap = jnp.zeros((TERM - q, LANES), F32)
@@ -180,11 +211,11 @@
         rows = slice(k * LANES, (k + 1) * LANES)
         coupled[rows, :] = (stack.T * live[rows, :]).astype(BF16)
 
-    copies[8].wait()
+    copies[2].wait()
     for c in range(3):
         loads[pl.ds(c, nodes, stride=3), :] = force_v[c].astype(F32)
     loads[...] = loads[...] * live[...]
-    copies[9].wait()
+    copies[3].wait()
 
 
 def load_kernel(coarse, own, sem):
@@ -193,17 +224,17 @@
     copy.wait()
 
 
-def merge_kernel(bit, own, other, out):
-    rows = own.shape[0]
-    place = (lax.axis_index("grp") >> bit) & 1
-    out[pl.ds(pl.multiple_of(place * rows, 8), rows), :] = own[...]
-    out[pl.ds(pl.multiple_of((1 - place) * rows, 8), rows), :] = other[...]
+def join_kernel(*refs):
+    *parts, out = refs
+    start = 0
+    for part in parts:
+        out[start : start + part.shape[0], :] = part[...]
+        start += part.shape[0]
 
 
 def solve_kernel(
-    here,
-    beside,
-    beyond,
+    near,
+    across,
     inverse,
     coupled,
     loads,
@@ -215,9 +246,6 @@
     disp,
     stress,
     sub_a,
-    sub_b,
-    grp_a,
-    grp_b,
     terms,
     solved,
     disp_t,
@@ -225,17 +253,17 @@
 ):
     panels, panel_rows, _ = inverse.shape
     panel_size = panel_rows // 3
-    rows = here.shape[0]
-
-    terms[...] = jnp.zeros(terms.shape, BF16)
-    for b, block in enumerate((here, beside, beyond)):
+    rows = near.shape[0]
+
+    terms[:, 2 * rows :, :] = jnp.zeros((3, terms.shape[1] - 2 * rows, terms.shape[2]), BF16)
+    for b, block in enumerate((near, across)):
         x = block[...]
         high = x.astype(BF16)
         rest = x - high.astype(F32)
         middle = rest.astype(BF16)
         low = (rest - middle.astype(F32)).astype(BF16)
         for t, value in enumerate((high, middle, low)):
-            terms[t, b * LANES : b * LANES + rows, :] = value
+            terms[t, b * rows : (b + 1) * rows, :] = value
     picked = [dot(select[...], terms[t]) for t in range(3)]
     picked.append(jnp.zeros((LANES - 3 * TERM, LANES), F32))
     values = jnp.concatenate(picked, axis=0).astype(BF16)
@@ -269,17 +297,23 @@
             stress[i * LANES + start : i * LANES + start + step, 0:LANES] = high
             stress[i * LANES + start : i * LANES + start + step, LANES : 2 * LANES] = low
 
-    rows = dot_nt(face[...], stress[...])
+    rows = dot_nt(face[:NIS, :], stress[...])
+    for i in range(COMPS):
+        sub_a[i] = rows[:, i * LANES : (i + 1) * LANES]
+
+
+def face_kernel(face, stress, sub_b, grp_a, grp_b):
+    base = EDGES - NIS
+    rows = dot_nt(face[NIS:, :], stress[...])
     for i in range(COMPS):
         part = rows[:, i * LANES : (i + 1) * LANES]
-        edge = [part[EDGES + NED * k : EDGES + NED * (k + 1)] for k in range(4)]
-        sub_a[i] = part[:NIS]
-        sub_b[i] = part[NIS : 2 * NIS]
-        grp_a[i] = jnp.concatenate([part[2 * NIS : 2 * NIS + NIG], edge[0], edge[2]], axis=0)
-        grp_b[i] = jnp.concatenate([part[2 * NIS + NIG : EDGES], edge[1], edge[3]], axis=0)
-
-
-def edge_kernel(grp_a, grp_b, from_a, from_b, edge_a, edge_b):
+        edge = [part[base + NED * k : base + NED * (k + 1)] for k in range(4)]
+        sub_b[i] = part[:NIS]
+        grp_a[i] = jnp.concatenate([part[NIS : NIS + NIG], edge[0], edge[2]], axis=0)
+        grp_b[i] = jnp.concatenate([part[NIS + NIG : base], edge[1], edge[3]], axis=0)
+
+
+def edge_kernel(grp_a, grp_b, from_a, from_b, _, edge_a, edge_b):
     split = NIG + NED
     edge_a[:, :NED, :] = grp_a[:, NIG:split, :] + from_a[:, NIG:split, :]
     edge_a[:, NED:, :] = grp_b[:, NIG:split, :] + from_b[:, NIG:split, :]
@@ -328,6 +362,14 @@
     return [pl.BlockSpec(memory_space=pltpu.VMEM)] * count
 
 
+def anywhere(count):
+    return [pl.BlockSpec(memory_space=pl.ANY)] * count
+
+
+def hbm(count):
+    return [pl.BlockSpec(memory_space=pltpu.HBM)] * count
+
+
 def array(shape, dtype=F32):
     return jax.ShapeDtypeStruct(shape, dtype)
 
@@ -357,20 +399,35 @@
     return [pltpu.with_memory_space_constraint(x, pltpu.HBM) for x in arrays]
 
 
-def gather_group(block, own):
-    count = lax.axis_size("grp")
-    bit = 0
-    while 1 << bit < count:
-        other = lax.ppermute(block, "grp", [(i, i ^ (1 << bit)) for i in range(count)])
-        rows, lanes = block.shape
-
-        def merge(own, received, out, bit=bit):
-            merge_kernel(bit, own, received, out)
-
-        (block,) = call(merge, "merge_blocks", (array((2 * rows, lanes)),), vmem(2))(own, other)
-        own = block
-        bit += 1
-    return block
+def gather_near(coarse, ahead):
+    (own,) = call(
+        load_kernel,
+        "load_own",
+        (array(coarse.shape),),
+        [pl.BlockSpec(memory_space=pltpu.HBM)],
+        (pltpu.SemaphoreType.DMA,),
+    )(*in_hbm(coarse))
+    beyond = exchange(coarse, "sub", 1)
+    beside = exchange(coarse, "sub", 0)
+    parts = [own, beside, beyond]
+    distance = lax.axis_size("grp") // 2
+    while distance:
+        rows = sum(x.shape[0] for x in parts)
+        before, ahead = ahead[:1], ahead[1:]
+
+        def join(*refs, skip=len(before)):
+            join_kernel(*refs[: len(refs) - 1 - skip], refs[-1])
+
+        (block,) = call(
+            join,
+            "join_blocks",
+            (array((rows, parts[0].shape[1])),),
+            vmem(len(parts)) + anywhere(len(before)),
+        )(*parts, *before)
+        pairs = [(i, i ^ distance) for i in range(lax.axis_size("grp"))]
+        parts = [block, lax.ppermute(block, "grp", pairs)]
+        distance //= 2
+    return parts
 
 
 def shards(
@@ -389,19 +446,14 @@
     nodes, _, cases = force.shape
     dofs = 3 * nodes
     q = corner_idx.shape[1]
-    blocks = coarse.shape[0] * lax.axis_size("grp")
-
-    def prepare(*refs):
-        prepare_kernel(blocks, *refs)
-
-    prepared = call(
-        prepare,
-        "prepare",
+
+    def lists(*refs):
+        prepare_lists(coarse.shape[0], lax.axis_size("grp"), *refs)
+
+    select, onehot, face, scaled, count, placing, inverse_volume = call(
+        lists,
+        "prepare_lists",
         (
-            array(panel_inv.shape, BF16),
-            array((dofs, LANES), BF16),
-            array((dofs, cases)),
-            array((dofs, LANES)),
             array((TERM, 3 * LANES), BF16),
             array((nodes, CORNERS * LANES), BF16),
             array((NIF, 2 * LANES), BF16),
@@ -410,60 +462,59 @@
             array((nodes, 2 * LANES), BF16),
             array((nodes, LANES)),
         ),
-        [pl.BlockSpec(memory_space=pltpu.HBM)] * 10,
+        hbm(6),
         (
             pltpu.VMEM((1, q), jnp.int32),
+            pltpu.VMEM(connect.shape, jnp.int32),
+            pltpu.VMEM(interface.shape, jnp.int32),
+            pltpu.VMEM(strain_disp.shape, BF16),
+            pltpu.VMEM((1, LANES), F32),
+            pltpu.VMEM((nodes // LANES, LANES), F32),
+            pltpu.VMEM((8, 2 * LANES), F32),
+            pltpu.SemaphoreType.DMA((6,)),
+        ),
+        flops=100000000,
+        moved=4000000,
+    )(
+        *in_hbm(
+            corner_idx,
+            connect,
+            interface,
+            strain_disp,
+            modulus.reshape(1, -1),
+            nodal_volume.reshape(-1, LANES),
+        )
+    )
+    inverse, coupled, loads, live = call(
+        prepare_panels,
+        "prepare_panels",
+        (
+            array(panel_inv.shape, BF16),
+            array((dofs, LANES), BF16),
+            array((dofs, cases)),
+            array((dofs, LANES)),
+        ),
+        hbm(4),
+        (
             pltpu.VMEM(panel_nodes.shape, jnp.int32),
             pltpu.VMEM((q, dofs), BF16),
             pltpu.VMEM((3, nodes, cases), BF16),
-            pltpu.VMEM(strain_disp.shape, BF16),
-            pltpu.VMEM((1, LANES), F32),
-            pltpu.VMEM(connect.shape, jnp.int32),
-            pltpu.VMEM(interface.shape, jnp.int32),
-            pltpu.VMEM((nodes // LANES, LANES), F32),
-            pltpu.VMEM((8, 2 * LANES), F32),
-            pltpu.SemaphoreType.DMA((10,)),
+            pltpu.SemaphoreType.DMA((4,)),
         ),
-        flops=200000000,
-        moved=8000000,
-    )(
-        *in_hbm(
-            corner_idx,
-            panel_nodes,
-            coupling.T,
-            jnp.transpose(force, (1, 0, 2)),
-            panel_inv,
-            strain_disp,
-            modulus.reshape(1, -1),
-            connect,
-            interface,
-            nodal_volume.reshape(-1, LANES),
-        )
-    )
-    *operands, count, placing, inverse_volume = prepared
-
-    (own,) = call(
-        load_kernel,
-        "load_own",
-        (array(coarse.shape),),
-        [pl.BlockSpec(memory_space=pltpu.HBM)],
-        (pltpu.SemaphoreType.DMA,),
-    )(*in_hbm(coarse))
-    here = gather_group(coarse, own)
-    beyond = exchange(here, "sub", 1)
-    beside = exchange(here, "sub", 0)
-    disp, stress, sub_a, sub_b, grp_a, grp_b = call(
+        flops=100000000,
+        moved=4000000,
+    )(*in_hbm(panel_nodes, coupling.T, jnp.transpose(force, (1, 0, 2)), panel_inv))
+
+    near = gather_near(coarse, [select, live])
+    disp, stress, sub_a = call(
         solve_kernel,
         "solve_and_stress",
         (
             array((3, nodes, cases), BF16),
             array((COMPS * cases, 2 * LANES), BF16),
             array((COMPS, NIS, cases)),
-            array((COMPS, NIS, cases)),
-            array((COMPS, NIG + 2 * NED, cases)),
-            array((COMPS, NIG + 2 * NED, cases)),
         ),
-        vmem(11),
+        vmem(10),
         (
             pltpu.VMEM((3, 3 * LANES, cases), BF16),
             pltpu.VMEM((dofs, cases), F32),
@@ -472,17 +523,29 @@
         ),
         flops=1500000000,
         moved=4000000,
-    )(here, beside, beyond, *operands)
+    )(*near, inverse, coupled, loads, live, select, onehot, face, scaled)
+    from_sub_a = exchange(sub_a, "sub", 0)
+    sub_b, grp_a, grp_b = call(
+        face_kernel,
+        "interface_rows",
+        (
+            array((COMPS, NIS, cases)),
+            array((COMPS, NIG + 2 * NED, cases)),
+            array((COMPS, NIG + 2 * NED, cases)),
+        ),
+        vmem(2),
+        flops=100000000,
+        moved=1000000,
+    )(face, stress)
     from_grp_a = exchange(grp_a, "grp", 0)
     from_grp_b = exchange(grp_b, "grp", 1)
     edge_a, edge_b = call(
         edge_kernel,
         "sum_edges",
         (array((COMPS, 2 * NED, cases)), array((COMPS, 2 * NED, cases))),
-        vmem(4),
-    )(grp_a, grp_b, from_grp_a, from_grp_b)
+        vmem(4) + anywhere(1),
+    )(grp_a, grp_b, from_grp_a, from_grp_b, from_sub_a)
     from_sub_b = exchange(sub_b, "sub", 1)
-    from_sub_a = exchange(sub_a, "sub", 0)
     from_edge_b = exchange(edge_b, "sub", 1)
     from_edge_a = exchange(edge_a, "sub", 0)
     partial, disp = call(

time: 34.4 us -> 34.3 us (level)
  Pallas kernels: 8.7 us -> 9.85 us
  starting transfers between devices: 16.6 us -> 16 us
  waiting for transfers between devices: 8.01 us -> 7.45 us
    pallas_call x4 -> x6, Pallas kernels: 3 us -> 4.28 us  [the longest x1 1.74 us: shards(): call(lists, 'prepare_lists', (array((TERM, 3 * LANES), BF16), array((node...]
    ppermute x2, waiting for transfers between devices: 3.94 us -> 3.19 us  [gather_near(): parts = [block, lax.ppermute(block, 'grp', pairs)]]
    ppermute x8, starting transfers between devices: 16 us -> 15.4 us  [exchange(): return lax.ppermute(block, axis, pairs)]
  transfers between devices with their start and end apart: 10 -> 10, of which waited for: 6 -> 5; matrix products, arithmetic and copies ran while one was open for 0% -> 0% of each run, Pallas kernels for 12% -> 16%
where the time goes in v5:
time: 34.3 us; the launch traced here: 34 us
  starting transfers between devices  16 us (47%)
  Pallas kernels  9.85 us (29%)
  waiting for transfers between devices  7.45 us (22%)
  between operations  0.75 us (2%)
    ppermute x8, starting transfers between devices, exchange(): return lax.ppermute(block, axis, pairs)  15.4 us
    ppermute x8, waiting for transfers between devices, exchange(): return lax.ppermute(block, axis, pairs)  4.26 us
    ppermute x2, waiting for transfers between devices, gather_near(): parts = [block, lax.ppermute(block, 'grp', pairs)]  3.19 us
    pallas_call x1, Pallas kernels, shards(): call(solve_kernel, 'solve_and_stress', (array((3, nodes, cases), BF16), a...  2.8 us
    pallas_call x1, Pallas kernels, shards(): call(lists, 'prepare_lists', (array((TERM, 3 * LANES), BF16), array((node...  1.74 us
    pallas_call x1, Pallas kernels, shards(): call(finish_kernel, 'add_received', (array((COMPS, nodes, cases), BF16),)...  1.51 us
    pallas_call x1, Pallas kernels, shards(): call(prepare_panels, 'prepare_panels', (array(panel_inv.shape, BF16), arr...  1.48 us
    pallas_call x1, Pallas kernels, shards(): call(partial_kernel, 'assemble_nodes', (array((COMPS, nodes, cases)), arr...  1.25 us
  transfers between devices with their start and end apart: 10, of which 5 were waited for; matrix products, arithmetic and copies ran while one was open for 0% of the time, Pallas kernels for 16%

profile of v5, /device:TPU:10, one launch (start us, length us, event | category | flops | bytes accessed | tf_op | source)
XLA Modules:
  0.0 34.0 jit_solution(4241724184621414552)
XLA Ops:
  0.6 3.3 %collective-permute-start.1 = (f32[24,128]{1,0:T(8,128)}, f32[24,128]{1,0:T(8,128)S(1)}, u32[]{:S(2)}, u32[]{:S(2)}) collective-permute-start(f32[24,128]{1,0:T(8,128)} %coarse.1), channel_id=1, source_target_pairs={{4,8},{8,4},{12,16},{16,12},{20,24},{24,20},{5,9},{9,5},{13,17},{1... | collective-permute-start | bytes 36872 | tf_op jit(solution)/shard_map/ppermute | solution.py:395
  3.9 1.7 %collective-permute-start = (f32[24,128]{1,0:T(8,128)}, f32[24,128]{1,0:T(8,128)S(1)}, u32[]{:S(2)}, u32[]{:S(2)}) collective-permute-start(f32[24,128]{1,0:T(8,128)} %coarse.1), channel_id=1, source_target_pairs={{0,4},{4,0},{8,12},{12,8},{16,20},{20,16},{24,28},{28,24},{1,5},{5... | collective-permute-start | bytes 36872 | tf_op jit(solution)/shard_map/ppermute | solution.py:395
  5.6 0.7 %load_own.1.refs_0_ = f32[24,128]{1,0:T(8,128)S(1)} custom-call(f32[24,128]{1,0:T(8,128)} %coarse.1), custom_call_target="tpu_custom_call" | custom-call | tf_op jit(solution)/shard_map/load_own/pallas_call | solution.py:403
  6.4 1.7 %prepare_lists.1 = (bf16[32,384]{1,0:T(8,128)(2,1)S(1)}, bf16[512,1024]{1,0:T(8,128)(2,1)S(1)}, bf16[224,256]{1,0:T(8,128)(2,1)S(1)}, f32[144,128]{1,0:T(8,128)S...) custom-call(s32[1,24]{1,0:T(1,128)} %refs_0_.1, s32[8,128]{1,0:T(8,128)} %refs_1_.1, ...), custom_call_target="tpu_custom_call" | custom-call | flops 100000000 | bytes 4000000 | tf_op jit(solution)/shard_map/prepare_lists/pallas_call | solution.py:453
  8.2 0.0 collective-permute-done.1.refs_2_
  8.2 0.0 collective-permute-done.refs_1_
  8.2 0.6 %collective-permute-start.2 = (f32[72,128]{1,0:T(8,128)S(1)}, f32[72,128]{1,0:T(8,128)S(1)}, u32[]{:S(2)}, u32[]{:S(2)}) collective-permute-start(f32[72,128]{1,0:T(8,128)S(1)} %join_blocks.2.refs_0_), channel_id=1, source_target_pairs={{0,2},{1,3},{2,0},{3,1},{4,6},{5,7},{6,4},{7,5},{8,10},{9,11},{10,... | collective-permute-start | bytes 110600 | tf_op jit(solution)/shard_map/ppermute | solution.py:428
  8.8 1.5 %prepare_panels.1 = (bf16[4,384,384]{2,1,0:T(8,128)(2,1)S(1)}, bf16[1536,128]{1,0:T(8,128)(2,1)S(1)}, f32[1536,128]{1,0:T(8,128)S(1)}, f32[1536,128]{1,0:T(8,128)S(1)}) custom-call(s32[1,4]{1,0:T(1,128)} %panel_nodes.1, bf16[24,1536]{1,0:T(8,128)(2,1)} %bitcast.8, bf16[3,512,128]{2,1,0:T(8,128)(2,1)} %bitcast.7, bf16[4,384,384]{2,1,0:T(8,128)(2,1)} %panel_inv.1), custom_call_target="tpu_custom_call" | custom-call | flops 100000000 | bytes 4000000 | tf_op jit(solution)/shard_map/prepare_panels/pallas_call | solution.py:488
  10.3 1.9 %collective-permute-done.2.refs_1_ = f32[72,128]{1,0:T(8,128)S(1)} collective-permute-done((f32[72,128]{1,0:T(8,128)S(1)}, f32[72,128]{1,0:T(8,128)S(1)}, u32[]{:S(2)}, u32[]{:S(2)}) %collective-permute-start.2) | collective-permute-done | bytes 36896 | tf_op jit(solution)/shard_map/ppermute | solution.py:428
  12.2 0.0 collective-permute-start.3
  12.2 1.3 %collective-permute-done.3.across = f32[144,128]{1,0:T(8,128)S(1)} collective-permute-done((f32[144,128]{1,0:T(8,128)S(1)}, f32[144,128]{1,0:T(8,128)S(1)}, u32[]{:S(2)}, u32[]{:S(2)}) %collective-permute-start.3) | collective-permute-done | bytes 73760 | tf_op jit(solution)/shard_map/ppermute | solution.py:428
  13.5 2.8 %solve_and_stress.1 = (bf16[3,512,128]{2,1,0:T(8,128)(2,1)S(1)}, bf16[768,256]{1,0:T(8,128)(2,1)S(1)}, f32[6,64,128]{2,1,0:T(8,128)S(1)}) custom-call(f32[144,128]{1,0:T(8,128)S(1)} %join_blocks.3.near, f32[144,128]{1,0:T(8,128)S(1)} %collective-permute-done.3.across, bf16[4,384,384]{2,1,0:T(8,128)(2,1)S(1)} %get-tuple-element.26.inverse, ...), custom_call_target="tpu_custom_call" | custom-call | flops 1500000000 | bytes 4000000 | tf_op jit(solution)/shard_map/solve_and_stress/pallas_call | solution.py:509
  16.3 1.4 %collective-permute-start.4 = (f32[6,64,128]{2,1,0:T(8,128)S(1)}, f32[6,64,128]{2,1,0:T(8,128)S(1)}, u32[]{:S(2)}, u32[]{:S(2)}) collective-permute-start(f32[6,64,128]{2,1,0:T(8,128)S(1)} %get-tuple-element.38), channel_id=1, source_target_pairs={{0,4},{4,0},{8,12},{12,8},{16,20},{20,16},{24,28},{28,24},{1,5},{5... | collective-permute-start | bytes 589832 | tf_op jit(solution)/shard_map/ppermute | solution.py:395
  17.7 0.3 interface_rows.1
  17.9 0.1 collective-permute-start.6
  18.0 2.5 %collective-permute-start.7 = (f32[6,48,128]{2,1,0:T(8,128)S(1)}, f32[6,48,128]{2,1,0:T(8,128)S(1)}, u32[]{:S(2)}, u32[]{:S(2)}) collective-permute-start(f32[6,48,128]{2,1,0:T(8,128)S(1)} %get-tuple-element.41.grp_b), channel_id=1, source_target_pairs={{1,2},{2,1},{5,6},{6,5},{9,10},{10,9},{13,14},{14,13},{17,18},{18,... | collective-permute-start | bytes 442376 | tf_op jit(solution)/shard_map/ppermute | solution.py:395
  20.6 2.5 %collective-permute-start.5 = (f32[6,64,128]{2,1,0:T(8,128)S(1)}, f32[6,64,128]{2,1,0:T(8,128)S(1)}, u32[]{:S(2)}, u32[]{:S(2)}) collective-permute-start(f32[6,64,128]{2,1,0:T(8,128)S(1)} %get-tuple-element.39), channel_id=1, source_target_pairs={{4,8},{8,4},{12,16},{16,12},{20,24},{24,20},{5,9},{9,5},{13,17},{1... | collective-permute-start | bytes 589832 | tf_op jit(solution)/shard_map/ppermute | solution.py:395
  23.1 0.0 collective-permute-done.6.from_a.grp_a
  23.1 1.4 %collective-permute-done.7.from_b.grp_b = f32[6,48,128]{2,1,0:T(8,128)S(1)} collective-permute-done((f32[6,48,128]{2,1,0:T(8,128)S(1)}, f32[6,48,128]{2,1,0:T(8,128)S(1)}, u32[]{:S(2)}, u32[]{:S(2)}) %collective-permute-start.7) | collective-permute-done | bytes 147488 | tf_op jit(solution)/shard_map/ppermute | solution.py:395
  24.5 0.0 collective-permute-done.4._.sub_a
  24.5 1.1 %collective-permute-start.8 = (f32[6,16,128]{2,1,0:T(8,128)S(1)}, f32[6,16,128]{2,1,0:T(8,128)S(1)}, u32[]{:S(2)}, u32[]{:S(2)}) collective-permute-start(f32[6,16,128]{2,1,0:T(8,128)S(1)} %get-tuple-element.42), channel_id=1, source_target_pairs={{0,4},{4,0},{8,12},{12,8},{16,20},{20,16},{24,28},{28,24},{1,5},{5... | collective-permute-start | bytes 147464 | tf_op jit(solution)/shard_map/ppermute | solution.py:395
  25.6 2.7 %collective-permute-start.9 = (f32[6,16,128]{2,1,0:T(8,128)S(1)}, f32[6,16,128]{2,1,0:T(8,128)S(1)}, u32[]{:S(2)}, u32[]{:S(2)}) collective-permute-start(f32[6,16,128]{2,1,0:T(8,128)S(1)} %get-tuple-element.43), channel_id=1, source_target_pairs={{4,8},{8,4},{12,16},{16,12},{20,24},{24,20},{5,9},{9,5},{13,17},{1... | collective-permute-start | bytes 147464 | tf_op jit(solution)/shard_map/ppermute | solution.py:395
  28.4 1.3 %assemble_nodes.1 = (f32[6,512,128]{2,1,0:T(8,128)S(1)}, bf16[3,512,128]{2,1,0:T(8,128)(2,1)}) custom-call(bf16[512,256]{1,0:T(8,128)(2,1)S(1)} %get-tuple-element.23.count, bf16[768,256]{1,0:T(8,128)(2,1)S(1)} %get-tuple-element.32.stress, bf16[3,512,128]{2,1,0:T(8,128)(2,1)S(1)} %get-tuple-element.33.disp), custom_call_target="tpu_custom_call" | custom-call | flops 400000000 | bytes 2000000 | tf_op jit(solution)/shard_map/assemble_nodes/pallas_call | solution.py:551
  29.6 0.0 collective-permute-done.5.sub_b
  29.6 0.7 %collective-permute-done.8.edge_a = f32[6,16,128]{2,1,0:T(8,128)S(1)} collective-permute-done((f32[6,16,128]{2,1,0:T(8,128)S(1)}, f32[6,16,128]{2,1,0:T(8,128)S(1)}, u32[]{:S(2)}, u32[]{:S(2)}) %collective-permute-start.8) | collective-permute-done | bytes 49184 | tf_op jit(solution)/shard_map/ppermute | solution.py:395
  30.4 2.1 %collective-permute-done.9.edge_b = f32[6,16,128]{2,1,0:T(8,128)S(1)} collective-permute-done((f32[6,16,128]{2,1,0:T(8,128)S(1)}, f32[6,16,128]{2,1,0:T(8,128)S(1)}, u32[]{:S(2)}, u32[]{:S(2)}) %collective-permute-start.9) | collective-permute-done | bytes 49184 | tf_op jit(solution)/shard_map/ppermute | solution.py:395
  32.5 1.5 %add_received.1 = bf16[6,512,128]{2,1,0:T(8,128)(2,1)} custom-call(bf16[512,256]{1,0:T(8,128)(2,1)S(1)} %get-tuple-element.35.placing, f32[6,512,128]{2,1,0:T(8,128)S(1)} %get-tuple-element.36.partial, f32[512,128]{1,0:T(8,128)S(1)} %get-tuple-element.37.inverse_volume, f32[6,64,128]{2,1,0:T(8,128)S(1)} %collective-permute-done.4._.sub_a, ...), custom_call_target="tpu_custom_call" | custom-call | flops 800000000 | bytes 3000000 | tf_op jit(solution)/shard_map/add_received/pallas_call | solution.py:559
  (3 shorter events, 0.0 us)
Async XLA Ops:
  0.6 7.5 %collective-permute-start.1 = (f32[24,128]{1,0:T(8,128)}, f32[24,128]{1,0:T(8,128)S(1)}, u32[]{:S(2)}, u32[]{:S(2)}) collective-permute-start(f32[24,128]{1,0:T(8,128)} %coarse.1), channel_id=1, source_target_pairs={{4,8},{8,4},{12,16},{16,12},{20,24},{24,20},{5,9},{9,5},{13,17},{1... | collective-permute-start | bytes 36872 | tf_op jit(solution)/shard_map/ppermute | solution.py:395
  3.9 4.2 %collective-permute-start = (f32[24,128]{1,0:T(8,128)}, f32[24,128]{1,0:T(8,128)S(1)}, u32[]{:S(2)}, u32[]{:S(2)}) collective-permute-start(f32[24,128]{1,0:T(8,128)} %coarse.1), channel_id=1, source_target_pairs={{0,4},{4,0},{8,12},{12,8},{16,20},{20,16},{24,28},{28,24},{1,5},{5... | collective-permute-start | bytes 36872 | tf_op jit(solution)/shard_map/ppermute | solution.py:395
  8.2 4.0 %collective-permute-start.2 = (f32[72,128]{1,0:T(8,128)S(1)}, f32[72,128]{1,0:T(8,128)S(1)}, u32[]{:S(2)}, u32[]{:S(2)}) collective-permute-start(f32[72,128]{1,0:T(8,128)S(1)} %join_blocks.2.refs_0_), channel_id=1, source_target_pairs={{0,2},{1,3},{2,0},{3,1},{4,6},{5,7},{6,4},{7,5},{8,10},{9,11},{10,... | collective-permute-start | bytes 110600 | tf_op jit(solution)/shard_map/ppermute | solution.py:428
  12.2 1.3 %collective-permute-start.3 = (f32[144,128]{1,0:T(8,128)S(1)}, f32[144,128]{1,0:T(8,128)S(1)}, u32[]{:S(2)}, u32[]{:S(2)}) collective-permute-start(f32[144,128]{1,0:T(8,128)S(1)} %join_blocks.3.near), channel_id=1, source_target_pairs={{0,1},{1,0},{2,3},{3,2},{4,5},{5,4},{6,7},{7,6},{8,9},{9,8},{10,11... | collective-permute-start | bytes 221192 | tf_op jit(solution)/shard_map/ppermute | solution.py:428
  16.3 8.2 %collective-permute-start.4 = (f32[6,64,128]{2,1,0:T(8,128)S(1)}, f32[6,64,128]{2,1,0:T(8,128)S(1)}, u32[]{:S(2)}, u32[]{:S(2)}) collective-permute-start(f32[6,64,128]{2,1,0:T(8,128)S(1)} %get-tuple-element.38), channel_id=1, source_target_pairs={{0,4},{4,0},{8,12},{12,8},{16,20},{20,16},{24,28},{28,24},{1,5},{5... | collective-permute-start | bytes 589832 | tf_op jit(solution)/shard_map/ppermute | solution.py:395
  17.9 5.1 %collective-permute-start.6 = (f32[6,48,128]{2,1,0:T(8,128)S(1)}, f32[6,48,128]{2,1,0:T(8,128)S(1)}, u32[]{:S(2)}, u32[]{:S(2)}) collective-permute-start(f32[6,48,128]{2,1,0:T(8,128)S(1)} %get-tuple-element.40.grp_a), channel_id=1, source_target_pairs={{0,1},{1,0},{2,3},{3,2},{4,5},{5,4},{6,7},{7,6},{8,9},{9,8},{10,11... | collective-permute-start | bytes 442376 | tf_op jit(solution)/shard_map/ppermute | solution.py:395
  18.0 6.5 %collective-permute-start.7 = (f32[6,48,128]{2,1,0:T(8,128)S(1)}, f32[6,48,128]{2,1,0:T(8,128)S(1)}, u32[]{:S(2)}, u32[]{:S(2)}) collective-permute-start(f32[6,48,128]{2,1,0:T(8,128)S(1)} %get-tuple-element.41.grp_b), channel_id=1, source_target_pairs={{1,2},{2,1},{5,6},{6,5},{9,10},{10,9},{13,14},{14,13},{17,18},{18,... | collective-permute-start | bytes 442376 | tf_op jit(solution)/shard_map/ppermute | solution.py:395
  20.6 9.1 %collective-permute-start.5 = (f32[6,64,128]{2,1,0:T(8,128)S(1)}, f32[6,64,128]{2,1,0:T(8,128)S(1)}, u32[]{:S(2)}, u32[]{:S(2)}) collective-permute-start(f32[6,64,128]{2,1,0:T(8,128)S(1)} %get-tuple-element.39), channel_id=1, source_target_pairs={{4,8},{8,4},{12,16},{16,12},{20,24},{24,20},{5,9},{9,5},{13,17},{1... | collective-permute-start | bytes 589832 | tf_op jit(solution)/shard_map/ppermute | solution.py:395
  24.5 5.9 %collective-permute-start.8 = (f32[6,16,128]{2,1,0:T(8,128)S(1)}, f32[6,16,128]{2,1,0:T(8,128)S(1)}, u32[]{:S(2)}, u32[]{:S(2)}) collective-permute-start(f32[6,16,128]{2,1,0:T(8,128)S(1)} %get-tuple-element.42), channel_id=1, source_target_pairs={{0,4},{4,0},{8,12},{12,8},{16,20},{20,16},{24,28},{28,24},{1,5},{5... | collective-permute-start | bytes 147464 | tf_op jit(solution)/shard_map/ppermute | solution.py:395
  25.6 6.9 %collective-permute-start.9 = (f32[6,16,128]{2,1,0:T(8,128)S(1)}, f32[6,16,128]{2,1,0:T(8,128)S(1)}, u32[]{:S(2)}, u32[]{:S(2)}) collective-permute-start(f32[6,16,128]{2,1,0:T(8,128)S(1)} %get-tuple-element.43), channel_id=1, source_target_pairs={{4,8},{8,4},{12,16},{16,12},{20,24},{24,20},{5,9},{9,5},{13,17},{1... | collective-permute-start | bytes 147464 | tf_op jit(solution)/shard_map/ppermute | solution.py:395

commit v6 on v5

--- a/solution.py
+++ b/solution.py
@@ -76,12 +76,15 @@
     strain_disp,
     modulus,
     volume,
+    coarse,
+    own,
     select,
     onehot,
     face,
     scaled,
     count,
     placing,
+    placing_last,
     inverse_volume,
     corner_v,
     connect_v,
@@ -100,6 +103,7 @@
             (modulus, modulus_v),
             (strain_disp, strain_v),
             (volume, volume_v),
+            (coarse, own),
         ],
         sems,
     )
@@ -123,6 +127,12 @@
     order_lists(ids)
     node_of = lax.broadcasted_iota(jnp.int32, (nodes, 2 * LANES), 0)
     placing[...] = jnp.where(ids[0:1, :].astype(jnp.int32) == node_of, 1.0, 0.0).astype(BF16)
+    lane = lax.broadcasted_iota(jnp.int32, (8, LANES), 1)
+    faces = pltpu.roll(ids[:, :LANES], NIS, 1)
+    late = jnp.where(lane < NIS, faces, jnp.where(lane < NIS + 4 * NED, ids[:, LANES:], -1.0))
+    hit = jnp.where(late[0:1, :].astype(jnp.int32) == node_of[:, :LANES], 1.0, 0.0).astype(BF16)
+    placing_last[:, :LANES] = hit
+    placing_last[:, LANES:] = hit
     connect_f = connect_v[...].astype(F32)
     for half in range(2):
         id_col = column(ids[0:1, half * LANES : (half + 1) * LANES])
@@ -163,11 +173,12 @@
     trace = (rows[0] + rows[1] + rows[2]) * LAME
     for i in range(COMPS):
         value = trace + rows[i] * (2.0 * SHEAR) if i < 3 else rows[i] * SHEAR
-        scaled[24 * i : 24 * (i + 1), :] = value * factor
+        scaled[24 * i : 24 * (i + 1)] = jnp.broadcast_to((value * factor)[:, None, :], (24, 8, LANES))
 
     copies[5].wait()
     for k in range(nodes // LANES):
         inverse_volume[k * LANES : (k + 1) * LANES, :] = column(1.0 / volume_v[k : k + 1, :])
+    copies[6].wait()
 
 
 def prepare_panels(
@@ -218,12 +229,6 @@
     copies[3].wait()
 
 
-def load_kernel(coarse, own, sem):
-    copy = pltpu.make_async_copy(coarse, own, sem)
-    copy.start()
-    copy.wait()
-
-
 def join_kernel(*refs):
     *parts, out = refs
     start = 0
@@ -246,6 +251,9 @@
     disp,
     stress,
     sub_a,
+    sub_b,
+    grp_a,
+    grp_b,
     terms,
     solved,
     disp_t,
@@ -280,40 +288,34 @@
                 part.astype(F32).T.astype(BF16)
             )
 
-    for c in range(3):
-        elem_t[c] = dot(disp_t[c * LANES : (c + 1) * LANES, :], onehot[...])
+    elem_t[...] = dot(disp_t[...], onehot[...])
     step = 32
     for start in range(0, LANES, step):
         sums = [None] * COMPS
         for a in range(CORNERS):
             for c in range(3):
-                x = elem_t[c, start : start + step, a * LANES : (a + 1) * LANES]
+                x = elem_t[c * LANES + start : c * LANES + start + step, a * LANES : (a + 1) * LANES]
+                x = x.reshape(step // 8, 8, LANES)
                 for i in range(COMPS):
-                    r = 24 * i + 3 * a + c
-                    term = scaled[r : r + 1, :] * x
+                    term = scaled[24 * i + 3 * a + c] * x
                     sums[i] = term if sums[i] is None else sums[i] + term
+        sums = [x.reshape(step, LANES) for x in sums]
         for i in range(COMPS):
             high, low = split_two(sums[i])
             stress[i * LANES + start : i * LANES + start + step, 0:LANES] = high
             stress[i * LANES + start : i * LANES + start + step, LANES : 2 * LANES] = low
 
-    rows = dot_nt(face[:NIS, :], stress[...])
-    for i in range(COMPS):
-        sub_a[i] = rows[:, i * LANES : (i + 1) * LANES]
-
-
-def face_kernel(face, stress, sub_b, grp_a, grp_b):
-    base = EDGES - NIS
-    rows = dot_nt(face[NIS:, :], stress[...])
+    rows = dot_nt(face[...], stress[...])
     for i in range(COMPS):
         part = rows[:, i * LANES : (i + 1) * LANES]
-        edge = [part[base + NED * k : base + NED * (k + 1)] for k in range(4)]
-        sub_b[i] = part[:NIS]
-        grp_a[i] = jnp.concatenate([part[NIS : NIS + NIG], edge[0], edge[2]], axis=0)
-        grp_b[i] = jnp.concatenate([part[NIS + NIG : base], edge[1], edge[3]], axis=0)
-
-
-def edge_kernel(grp_a, grp_b, from_a, from_b, _, edge_a, edge_b):
+        edge = [part[EDGES + NED * k : EDGES + NED * (k + 1)] for k in range(4)]
+        sub_a[i] = part[:NIS]
+        sub_b[i] = part[NIS : 2 * NIS]
+        grp_a[i] = jnp.concatenate([part[2 * NIS : 2 * NIS + NIG], edge[0], edge[2]], axis=0)
+        grp_b[i] = jnp.concatenate([part[2 * NIS + NIG : EDGES], edge[1], edge[3]], axis=0)
+
+
+def edge_kernel(grp_a, grp_b, from_a, from_b, _, edge_b, edge_a):
     split = NIG + NED
     edge_a[:, :NED, :] = grp_a[:, NIG:split, :] + from_a[:, NIG:split, :]
     edge_a[:, NED:, :] = grp_b[:, NIG:split, :] + from_b[:, NIG:split, :]
@@ -321,41 +323,47 @@
     edge_b[:, NED:, :] = grp_b[:, split:, :] + from_b[:, split:, :]
 
 
-def partial_kernel(count, stress, disp, partial, disp_out):
+def partial_kernel(
+    count, stress, disp, placing, sub_a, grp_a, grp_b, partial, disp_out, received
+):
     disp_out[...] = disp[...]
+    split = NIG + NED
+    gap = jnp.zeros((NIS, LANES), F32)
     for i in range(COMPS):
-        partial[i] = dot_nt(count[...], stress[i * LANES : (i + 1) * LANES, :])
-
-
-def finish_kernel(
-    placing, partial, inverse_volume, sub_a, sub_b, grp_a, grp_b, edge_a, edge_b, out, received
-):
-    split = NIG + NED
-    for i in range(COMPS):
-        low, high, first, second = grp_a[i], grp_b[i], edge_a[i], edge_b[i]
-        rows = jnp.concatenate(
-            [
-                sub_a[i],
-                sub_b[i],
-                low[:NIG],
-                high[:NIG],
-                low[NIG:split] + first[:NED],
-                high[NIG:split] + first[NED:],
-                low[split:] + second[:NED],
-                high[split:] + second[NED:],
-                jnp.zeros((2 * LANES - NIF, LANES), F32),
-            ],
-            axis=0,
-        )
-        first, second = split_two(rows)
-        received[0, :, i * LANES : (i + 1) * LANES] = first
-        received[1, :, i * LANES : (i + 1) * LANES] = second
-    scale = inverse_volume[...]
+        low, high = grp_a[i], grp_b[i]
+        rows = [sub_a[i], gap, low[:NIG], high[:NIG], low[NIG:split], high[NIG:split], low[split:], high[split:]]
+        rows.append(jnp.zeros((2 * LANES - NIF, LANES), F32))
+        first, second = split_two(jnp.concatenate(rows, axis=0))
+        received[: 2 * LANES, i * LANES : (i + 1) * LANES] = first
+        received[2 * LANES :, i * LANES : (i + 1) * LANES] = second
     for i in range(0, COMPS, 2):
         cols = slice(i * LANES, (i + 2) * LANES)
-        added = dot(placing[...], received[0, :, cols]) + dot(placing[...], received[1, :, cols])
-        out[i] = ((partial[i] + added[:, :LANES]) * scale).astype(BF16)
-        out[i + 1] = ((partial[i + 1] + added[:, LANES:]) * scale).astype(BF16)
+        own = dot_nt(count[...], stress[cols, :])
+        added = dot(placing[...], received[: 2 * LANES, cols]) + dot(placing[...], received[2 * LANES :, cols])
+        total = own + added
+        partial[i] = total[:, :LANES]
+        partial[i + 1] = total[:, LANES:]
+
+
+def finish_kernel(placing, partial, inverse_volume, sub_b, edge_b, edge_a, out, received, nodal, sems):
+    rows = NIS + 4 * NED
+    for i in range(COMPS):
+        cols = slice(i * LANES, (i + 1) * LANES)
+        parts = jnp.concatenate([sub_b[i], edge_a[i], edge_b[i], jnp.zeros((LANES - rows, LANES), F32)], axis=0)
+        first, second = split_two(parts)
+        received[:LANES, cols] = first
+        received[LANES:, cols] = second
+    scale = inverse_volume[...]
+    copies = []
+    for i in range(0, COMPS, 2):
+        added = dot(placing[...], received[:, i * LANES : (i + 2) * LANES])
+        nodal[i] = ((partial[i] + added[:, :LANES]) * scale).astype(BF16)
+        nodal[i + 1] = ((partial[i + 1] + added[:, LANES:]) * scale).astype(BF16)
+        copy = pltpu.make_async_copy(nodal.at[pl.ds(i, 2)], out.at[pl.ds(i, 2)], sems.at[i // 2])
+        copy.start()
+        copies.append(copy)
+    for copy in copies:
+        copy.wait()
 
 
 def vmem(count):
@@ -374,13 +382,13 @@
     return jax.ShapeDtypeStruct(shape, dtype)
 
 
-def call(kernel, name, out_shape, in_specs, scratch=(), flops=0, moved=0):
+def call(kernel, name, out_shape, in_specs, scratch=(), flops=0, moved=0, out_specs=None):
     return pl.pallas_call(
         kernel,
         name=name,
         out_shape=out_shape,
         in_specs=in_specs,
-        out_specs=vmem(len(out_shape)),
+        out_specs=out_specs or vmem(len(out_shape)),
         scratch_shapes=list(scratch),
         compiler_params=pltpu.CompilerParams(vmem_limit_bytes=VMEM_LIMIT),
         cost_estimate=pl.CostEstimate(flops=flops, bytes_accessed=moved, transcendentals=0),
@@ -399,14 +407,7 @@
     return [pltpu.with_memory_space_constraint(x, pltpu.HBM) for x in arrays]
 
 
-def gather_near(coarse, ahead):
-    (own,) = call(
-        load_kernel,
-        "load_own",
-        (array(coarse.shape),),
-        [pl.BlockSpec(memory_space=pltpu.HBM)],
-        (pltpu.SemaphoreType.DMA,),
-    )(*in_hbm(coarse))
+def gather_near(coarse, own, ahead):
     beyond = exchange(coarse, "sub", 1)
     beside = exchange(coarse, "sub", 0)
     parts = [own, beside, beyond]
@@ -450,19 +451,21 @@
     def lists(*refs):
         prepare_lists(coarse.shape[0], lax.axis_size("grp"), *refs)
 
-    select, onehot, face, scaled, count, placing, inverse_volume = call(
+    own, select, onehot, face, scaled, count, placing, placing_last, inverse_volume = call(
         lists,
         "prepare_lists",
         (
+            array(coarse.shape),
             array((TERM, 3 * LANES), BF16),
             array((nodes, CORNERS * LANES), BF16),
             array((NIF, 2 * LANES), BF16),
-            array((COMPS * 24, LANES)),
+            array((COMPS * 24, 8, LANES)),
+            array((nodes, 2 * LANES), BF16),
             array((nodes, 2 * LANES), BF16),
             array((nodes, 2 * LANES), BF16),
             array((nodes, LANES)),
         ),
-        hbm(6),
+        hbm(7),
         (
             pltpu.VMEM((1, q), jnp.int32),
             pltpu.VMEM(connect.shape, jnp.int32),
@@ -471,7 +474,7 @@
             pltpu.VMEM((1, LANES), F32),
             pltpu.VMEM((nodes // LANES, LANES), F32),
             pltpu.VMEM((8, 2 * LANES), F32),
-            pltpu.SemaphoreType.DMA((6,)),
+            pltpu.SemaphoreType.DMA((7,)),
         ),
         flops=100000000,
         moved=4000000,
@@ -483,6 +486,7 @@
             strain_disp,
             modulus.reshape(1, -1),
             nodal_volume.reshape(-1, LANES),
+            coarse,
         )
     )
     inverse, coupled, loads, live = call(
@@ -505,41 +509,32 @@
         moved=4000000,
     )(*in_hbm(panel_nodes, coupling.T, jnp.transpose(force, (1, 0, 2)), panel_inv))
 
-    near = gather_near(coarse, [select, live])
-    disp, stress, sub_a = call(
+    near = gather_near(coarse, own, [select, live])
+    disp, stress, sub_a, sub_b, grp_a, grp_b = call(
         solve_kernel,
         "solve_and_stress",
         (
             array((3, nodes, cases), BF16),
             array((COMPS * cases, 2 * LANES), BF16),
             array((COMPS, NIS, cases)),
+            array((COMPS, NIS, cases)),
+            array((COMPS, NIG + 2 * NED, cases)),
+            array((COMPS, NIG + 2 * NED, cases)),
         ),
         vmem(10),
         (
             pltpu.VMEM((3, 3 * LANES, cases), BF16),
             pltpu.VMEM((dofs, cases), F32),
             pltpu.VMEM((3 * cases, nodes), BF16),
-            pltpu.VMEM((3, cases, CORNERS * LANES), F32),
+            pltpu.VMEM((3 * cases, CORNERS * LANES), F32),
         ),
         flops=1500000000,
         moved=4000000,
     )(*near, inverse, coupled, loads, live, select, onehot, face, scaled)
     from_sub_a = exchange(sub_a, "sub", 0)
-    sub_b, grp_a, grp_b = call(
-        face_kernel,
-        "interface_rows",
-        (
-            array((COMPS, NIS, cases)),
-            array((COMPS, NIG + 2 * NED, cases)),
-            array((COMPS, NIG + 2 * NED, cases)),
-        ),
-        vmem(2),
-        flops=100000000,
-        moved=1000000,
-    )(face, stress)
     from_grp_a = exchange(grp_a, "grp", 0)
     from_grp_b = exchange(grp_b, "grp", 1)
-    edge_a, edge_b = call(
+    edge_b, edge_a = call(
         edge_kernel,
         "sum_edges",
         (array((COMPS, 2 * NED, cases)), array((COMPS, 2 * NED, cases))),
@@ -552,29 +547,25 @@
         partial_kernel,
         "assemble_nodes",
         (array((COMPS, nodes, cases)), array(disp.shape, BF16)),
-        vmem(3),
+        vmem(7),
+        (pltpu.VMEM((4 * LANES, COMPS * cases), BF16),),
         flops=400000000,
         moved=2000000,
-    )(count, stress, disp)
+    )(count, stress, disp, placing, from_sub_a, from_grp_a, from_grp_b)
     (nodal,) = call(
         finish_kernel,
-        "add_received",
+        "add_last",
         (array((COMPS, nodes, cases), BF16),),
-        vmem(9),
-        (pltpu.VMEM((2, 2 * LANES, COMPS * cases), BF16),),
-        flops=800000000,
+        vmem(6),
+        (
+            pltpu.VMEM((2 * LANES, COMPS * cases), BF16),
+            pltpu.VMEM((COMPS, nodes, cases), BF16),
+            pltpu.SemaphoreType.DMA((COMPS // 2,)),
+        ),
+        flops=400000000,
         moved=3000000,
-    )(
-        placing,
-        partial,
-        inverse_volume,
-        from_sub_a,
-        from_sub_b,
-        from_grp_a,
-        from_grp_b,
-        from_edge_a,
-        from_edge_b,
-    )
+        out_specs=hbm(1),
+    )(placing_last, partial, inverse_volume, from_sub_b, from_edge_b, from_edge_a)
     return jnp.transpose(disp, (1, 0, 2)), jnp.transpose(nodal, (1, 0, 2))
 
 

time: 34.3 us -> 36.3 us (1.058)
  the two profiles are of different devices: /device:TPU:10 before, /device:TPU:22 now
where the time goes in v6:
time: 36.3 us; the launch traced here: 36.1 us
  starting transfers between devices  18 us (50%)
  Pallas kernels  8.99 us (25%)
  waiting for transfers between devices  8.34 us (23%)
  between operations  0.72 us (2%)
    ppermute x8, starting transfers between devices, exchange(): return lax.ppermute(block, axis, pairs)  17.5 us
    ppermute x8, waiting for transfers between devices, exchange(): return lax.ppermute(block, axis, pairs)  5.15 us
    ppermute x2, waiting for transfers between devices, gather_near(): parts = [block, lax.ppermute(block, 'grp', pairs)]  3.19 us
    pallas_call x1, Pallas kernels, shards(): call(solve_kernel, 'solve_and_stress', (array((3, nodes, cases), BF16), a...  2.83 us
    pallas_call x1, Pallas kernels, shards(): call(lists, 'prepare_lists', (array(coarse.shape), array((TERM, 3 * LANES...  1.86 us
    pallas_call x1, Pallas kernels, shards(): call(partial_kernel, 'assemble_nodes', (array((COMPS, nodes, cases)), arr...  1.57 us
    pallas_call x1, Pallas kernels, shards(): call(prepare_panels, 'prepare_panels', (array(panel_inv.shape, BF16), arr...  1.48 us
    pallas_call x1, Pallas kernels, shards(): call(finish_kernel, 'add_last', (array((COMPS, nodes, cases), BF16),), vm...  1.23 us
  transfers between devices with their start and end apart: 10, of which 8 were waited for; matrix products, arithmetic and copies ran while one was open for 0% of the time, Pallas kernels for 14%

profile of v6, /device:TPU:22, one launch (start us, length us, event | category | flops | bytes accessed | tf_op | source)
XLA Modules:
  0.0 36.1 jit_solution(12786640944101276456)
XLA Ops:
  0.6 3.4 %collective-permute-start.1 = (f32[24,128]{1,0:T(8,128)}, f32[24,128]{1,0:T(8,128)S(1)}, u32[]{:S(2)}, u32[]{:S(2)}) collective-permute-start(f32[24,128]{1,0:T(8,128)} %refs_6_.1), channel_id=1, source_target_pairs={{4,8},{8,4},{12,16},{16,12},{20,24},{24,20},{5,9},{9,5},{13,17},{1... | collective-permute-start | bytes 36872 | tf_op jit(solution)/shard_map/ppermute | solution.py:403
  4.1 0.5 %collective-permute-start = (f32[24,128]{1,0:T(8,128)}, f32[24,128]{1,0:T(8,128)S(1)}, u32[]{:S(2)}, u32[]{:S(2)}) collective-permute-start(f32[24,128]{1,0:T(8,128)} %refs_6_.1), channel_id=1, source_target_pairs={{0,4},{4,0},{8,12},{12,8},{16,20},{20,16},{24,28},{28,24},{1,5},{5... | collective-permute-start | bytes 36872 | tf_op jit(solution)/shard_map/ppermute | solution.py:403
  4.5 1.9 %prepare_lists.1 = (f32[24,128]{1,0:T(8,128)S(1)}, bf16[32,384]{1,0:T(8,128)(2,1)S(1)}, bf16[512,1024]{1,0:T(8,128)(2,1)S(1)}, bf16[224,256]{1,0:T(8,128)(2,1)S(...) custom-call(s32[1,24]{1,0:T(1,128)} %refs_0_.1, ...), custom_call_target="tpu_custom_call" | custom-call | flops 100000000 | bytes 4000000 | tf_op jit(solution)/shard_map/prepare_lists/pallas_call | solution.py:454
  6.4 0.9 %collective-permute-done.1.refs_2_ = f32[24,128]{1,0:T(8,128)S(1)} collective-permute-done((f32[24,128]{1,0:T(8,128)}, f32[24,128]{1,0:T(8,128)S(1)}, u32[]{:S(2)}, u32[]{:S(2)}) %collective-permute-start.1) | collective-permute-done | bytes 12320 | tf_op jit(solution)/shard_map/ppermute | solution.py:403
  7.3 0.7 %collective-permute-done.refs_1_ = f32[24,128]{1,0:T(8,128)S(1)} collective-permute-done((f32[24,128]{1,0:T(8,128)}, f32[24,128]{1,0:T(8,128)S(1)}, u32[]{:S(2)}, u32[]{:S(2)}) %collective-permute-start) | collective-permute-done | bytes 12320 | tf_op jit(solution)/shard_map/ppermute | solution.py:403
  8.0 0.5 %collective-permute-start.2 = (f32[72,128]{1,0:T(8,128)S(1)}, f32[72,128]{1,0:T(8,128)S(1)}, u32[]{:S(2)}, u32[]{:S(2)}) collective-permute-start(f32[72,128]{1,0:T(8,128)S(1)} %join_blocks.2.refs_0_), channel_id=1, source_target_pairs={{0,2},{1,3},{2,0},{3,1},{4,6},{5,7},{6,4},{7,5},{8,10},{9,11},{10,... | collective-permute-start | bytes 110600 | tf_op jit(solution)/shard_map/ppermute | solution.py:429
  8.6 1.5 %prepare_panels.1 = (bf16[4,384,384]{2,1,0:T(8,128)(2,1)S(1)}, bf16[1536,128]{1,0:T(8,128)(2,1)S(1)}, f32[1536,128]{1,0:T(8,128)S(1)}, f32[1536,128]{1,0:T(8,128)S(1)}) custom-call(s32[1,4]{1,0:T(1,128)} %panel_nodes.1, bf16[24,1536]{1,0:T(8,128)(2,1)} %bitcast.8, bf16[3,512,128]{2,1,0:T(8,128)(2,1)} %bitcast.7, bf16[4,384,384]{2,1,0:T(8,128)(2,1)} %panel_inv.1), custom_call_target="tpu_custom_call" | custom-call | flops 100000000 | bytes 4000000 | tf_op jit(solution)/shard_map/prepare_panels/pallas_call | solution.py:492
  10.1 1.9 %collective-permute-done.2.refs_1_ = f32[72,128]{1,0:T(8,128)S(1)} collective-permute-done((f32[72,128]{1,0:T(8,128)S(1)}, f32[72,128]{1,0:T(8,128)S(1)}, u32[]{:S(2)}, u32[]{:S(2)}) %collective-permute-start.2) | collective-permute-done | bytes 36896 | tf_op jit(solution)/shard_map/ppermute | solution.py:429
  12.0 0.0 collective-permute-start.3
  12.0 1.3 %collective-permute-done.3.across = f32[144,128]{1,0:T(8,128)S(1)} collective-permute-done((f32[144,128]{1,0:T(8,128)S(1)}, f32[144,128]{1,0:T(8,128)S(1)}, u32[]{:S(2)}, u32[]{:S(2)}) %collective-permute-start.3) | collective-permute-done | bytes 73760 | tf_op jit(solution)/shard_map/ppermute | solution.py:429
  13.3 2.8 %solve_and_stress.1 = (bf16[3,512,128]{2,1,0:T(8,128)(2,1)S(1)}, bf16[768,256]{1,0:T(8,128)(2,1)S(1)}, f32[6,64,128]{2,1,0:T(8,128)S(1)}, f32[6,64,128]{2,1,0:T(...) custom-call(f32[144,128]{1,0:T(8,128)S(1)} %join_blocks.3.near, ...), custom_call_target="tpu_custom_call" | custom-call | flops 1500000000 | bytes 4000000 | tf_op jit(solution)/shard_map/solve_and_stress/pallas_call | solution.py:513
  16.1 0.5 %collective-permute-start.4 = (f32[6,64,128]{2,1,0:T(8,128)S(1)}, f32[6,64,128]{2,1,0:T(8,128)S(1)}, u32[]{:S(2)}, u32[]{:S(2)}) collective-permute-start(f32[6,64,128]{2,1,0:T(8,128)S(1)} %get-tuple-element.38), channel_id=1, source_target_pairs={{0,4},{4,0},{8,12},{12,8},{16,20},{20,16},{24,28},{28,24},{1,5},{5... | collective-permute-start | bytes 589832 | tf_op jit(solution)/shard_map/ppermute | solution.py:403
  16.6 0.0 collective-permute-start.5
  16.6 2.5 %collective-permute-start.6 = (f32[6,48,128]{2,1,0:T(8,128)S(1)}, f32[6,48,128]{2,1,0:T(8,128)S(1)}, u32[]{:S(2)}, u32[]{:S(2)}) collective-permute-start(f32[6,48,128]{2,1,0:T(8,128)S(1)} %get-tuple-element.40.grp_b), channel_id=1, source_target_pairs={{1,2},{2,1},{5,6},{6,5},{9,10},{10,9},{13,14},{14,13},{17,18},{18,... | collective-permute-start | bytes 442376 | tf_op jit(solution)/shard_map/ppermute | solution.py:403
  19.1 3.0 %collective-permute-start.7 = (f32[6,64,128]{2,1,0:T(8,128)S(1)}, f32[6,64,128]{2,1,0:T(8,128)S(1)}, u32[]{:S(2)}, u32[]{:S(2)}) collective-permute-start(f32[6,64,128]{2,1,0:T(8,128)S(1)} %get-tuple-element.45), channel_id=1, source_target_pairs={{4,8},{8,4},{12,16},{16,12},{20,24},{24,20},{5,9},{9,5},{13,17},{1... | collective-permute-start | bytes 589832 | tf_op jit(solution)/shard_map/ppermute | solution.py:403
  22.1 0.0 collective-permute-done.5.grp_a.from_a
  22.1 0.9 %collective-permute-done.6.grp_b.from_b = f32[6,48,128]{2,1,0:T(8,128)S(1)} collective-permute-done((f32[6,48,128]{2,1,0:T(8,128)S(1)}, f32[6,48,128]{2,1,0:T(8,128)S(1)}, u32[]{:S(2)}, u32[]{:S(2)}) %collective-permute-start.6) | collective-permute-done | bytes 147488 | tf_op jit(solution)/shard_map/ppermute | solution.py:403
  23.0 0.1 collective-permute-done.4.sub_a._
  23.2 7.5 %collective-permute-start.8 = (f32[6,16,128]{2,1,0:T(8,128)S(1)}, f32[6,16,128]{2,1,0:T(8,128)S(1)}, u32[]{:S(2)}, u32[]{:S(2)}) collective-permute-start(f32[6,16,128]{2,1,0:T(8,128)S(1)} %get-tuple-element.46), channel_id=1, source_target_pairs={{4,8},{8,4},{12,16},{16,12},{20,24},{24,20},{5,9},{9,5},{13,17},{1... | collective-permute-start | bytes 147464 | tf_op jit(solution)/shard_map/ppermute | solution.py:403
  30.7 0.1 collective-permute-start.9
  30.8 1.6 %assemble_nodes.1 = (f32[6,512,128]{2,1,0:T(8,128)S(1)}, bf16[3,512,128]{2,1,0:T(8,128)(2,1)}) custom-call(bf16[512,256]{1,0:T(8,128)(2,1)S(1)} %get-tuple-element.25.count, bf16[768,256]{1,0:T(8,128)(2,1)S(1)} %get-tuple-element.35.stress, bf16[3,512,128]{2,1,0:T(8,128)(2,1)S(1)} %get-tuple-element.36.disp, bf16[512,256]{1,0:T(8,128)(2,1)S(1)} %get-tuple-element.37.placing, ...), custom_call_target="tpu_custom_call" | custom-call | flops 400000000 | bytes 2000000 | tf_op jit(solution)/shard_map/assemble_nodes/pallas_call | solution.py:546
  32.3 0.0 collective-permute-done.7.sub_b
  32.3 0.4 %collective-permute-done.8.edge_b = f32[6,16,128]{2,1,0:T(8,128)S(1)} collective-permute-done((f32[6,16,128]{2,1,0:T(8,128)S(1)}, f32[6,16,128]{2,1,0:T(8,128)S(1)}, u32[]{:S(2)}, u32[]{:S(2)}) %collective-permute-start.8) | collective-permute-done | bytes 49184 | tf_op jit(solution)/shard_map/ppermute | solution.py:403
  32.7 2.1 %collective-permute-done.9.edge_a = f32[6,16,128]{2,1,0:T(8,128)S(1)} collective-permute-done((f32[6,16,128]{2,1,0:T(8,128)S(1)}, f32[6,16,128]{2,1,0:T(8,128)S(1)}, u32[]{:S(2)}, u32[]{:S(2)}) %collective-permute-start.9) | collective-permute-done | bytes 49184 | tf_op jit(solution)/shard_map/ppermute | solution.py:403
  34.8 1.2 %add_last.1 = bf16[6,512,128]{2,1,0:T(8,128)(2,1)} custom-call(bf16[512,256]{1,0:T(8,128)(2,1)S(1)} %get-tuple-element.42.placing, f32[6,512,128]{2,1,0:T(8,128)S(1)} %get-tuple-element.43.partial, f32[512,128]{1,0:T(8,128)S(1)} %get-tuple-element.44.inverse_volume, f32[6,64,128]{2,1,0:T(8,128)S(1)} %collective-permute-done.7.sub_b, ...), custom_call_target="tpu_custom_call" | custom-call | flops 400000000 | bytes 3000000 | tf_op jit(solution)/shard_map/add_last/pallas_call | solution.py:555
  (3 shorter events, 0.0 us)
Async XLA Ops:
  0.6 6.7 %collective-permute-start.1 = (f32[24,128]{1,0:T(8,128)}, f32[24,128]{1,0:T(8,128)S(1)}, u32[]{:S(2)}, u32[]{:S(2)}) collective-permute-start(f32[24,128]{1,0:T(8,128)} %refs_6_.1), channel_id=1, source_target_pairs={{4,8},{8,4},{12,16},{16,12},{20,24},{24,20},{5,9},{9,5},{13,17},{1... | collective-permute-start | bytes 36872 | tf_op jit(solution)/shard_map/ppermute | solution.py:403
  4.1 4.0 %collective-permute-start = (f32[24,128]{1,0:T(8,128)}, f32[24,128]{1,0:T(8,128)S(1)}, u32[]{:S(2)}, u32[]{:S(2)}) collective-permute-start(f32[24,128]{1,0:T(8,128)} %refs_6_.1), channel_id=1, source_target_pairs={{0,4},{4,0},{8,12},{12,8},{16,20},{20,16},{24,28},{28,24},{1,5},{5... | collective-permute-start | bytes 36872 | tf_op jit(solution)/shard_map/ppermute | solution.py:403
  8.0 4.0 %collective-permute-start.2 = (f32[72,128]{1,0:T(8,128)S(1)}, f32[72,128]{1,0:T(8,128)S(1)}, u32[]{:S(2)}, u32[]{:S(2)}) collective-permute-start(f32[72,128]{1,0:T(8,128)S(1)} %join_blocks.2.refs_0_), channel_id=1, source_target_pairs={{0,2},{1,3},{2,0},{3,1},{4,6},{5,7},{6,4},{7,5},{8,10},{9,11},{10,... | collective-permute-start | bytes 110600 | tf_op jit(solution)/shard_map/ppermute | solution.py:429
  12.0 1.3 %collective-permute-start.3 = (f32[144,128]{1,0:T(8,128)S(1)}, f32[144,128]{1,0:T(8,128)S(1)}, u32[]{:S(2)}, u32[]{:S(2)}) collective-permute-start(f32[144,128]{1,0:T(8,128)S(1)} %join_blocks.3.near), channel_id=1, source_target_pairs={{0,1},{1,0},{2,3},{3,2},{4,5},{5,4},{6,7},{7,6},{8,9},{9,8},{10,11... | collective-permute-start | bytes 221192 | tf_op jit(solution)/shard_map/ppermute | solution.py:429
  16.1 7.0 %collective-permute-start.4 = (f32[6,64,128]{2,1,0:T(8,128)S(1)}, f32[6,64,128]{2,1,0:T(8,128)S(1)}, u32[]{:S(2)}, u32[]{:S(2)}) collective-permute-start(f32[6,64,128]{2,1,0:T(8,128)S(1)} %get-tuple-element.38), channel_id=1, source_target_pairs={{0,4},{4,0},{8,12},{12,8},{16,20},{20,16},{24,28},{28,24},{1,5},{5... | collective-permute-start | bytes 589832 | tf_op jit(solution)/shard_map/ppermute | solution.py:403
  16.6 5.6 %collective-permute-start.5 = (f32[6,48,128]{2,1,0:T(8,128)S(1)}, f32[6,48,128]{2,1,0:T(8,128)S(1)}, u32[]{:S(2)}, u32[]{:S(2)}) collective-permute-start(f32[6,48,128]{2,1,0:T(8,128)S(1)} %get-tuple-element.39.grp_a), channel_id=1, source_target_pairs={{0,1},{1,0},{2,3},{3,2},{4,5},{5,4},{6,7},{7,6},{8,9},{9,8},{10,11... | collective-permute-start | bytes 442376 | tf_op jit(solution)/shard_map/ppermute | solution.py:403
  16.6 6.5 %collective-permute-start.6 = (f32[6,48,128]{2,1,0:T(8,128)S(1)}, f32[6,48,128]{2,1,0:T(8,128)S(1)}, u32[]{:S(2)}, u32[]{:S(2)}) collective-permute-start(f32[6,48,128]{2,1,0:T(8,128)S(1)} %get-tuple-element.40.grp_b), channel_id=1, source_target_pairs={{1,2},{2,1},{5,6},{6,5},{9,10},{10,9},{13,14},{14,13},{17,18},{18,... | collective-permute-start | bytes 442376 | tf_op jit(solution)/shard_map/ppermute | solution.py:403
  19.1 13.2 %collective-permute-start.7 = (f32[6,64,128]{2,1,0:T(8,128)S(1)}, f32[6,64,128]{2,1,0:T(8,128)S(1)}, u32[]{:S(2)}, u32[]{:S(2)}) collective-permute-start(f32[6,64,128]{2,1,0:T(8,128)S(1)} %get-tuple-element.45), channel_id=1, source_target_pairs={{4,8},{8,4},{12,16},{16,12},{20,24},{24,20},{5,9},{9,5},{13,17},{1... | collective-permute-start | bytes 589832 | tf_op jit(solution)/shard_map/ppermute | solution.py:403
  23.2 9.6 %collective-permute-start.8 = (f32[6,16,128]{2,1,0:T(8,128)S(1)}, f32[6,16,128]{2,1,0:T(8,128)S(1)}, u32[]{:S(2)}, u32[]{:S(2)}) collective-permute-start(f32[6,16,128]{2,1,0:T(8,128)S(1)} %get-tuple-element.46), channel_id=1, source_target_pairs={{4,8},{8,4},{12,16},{16,12},{20,24},{24,20},{5,9},{9,5},{13,17},{1... | collective-permute-start | bytes 147464 | tf_op jit(solution)/shard_map/ppermute | solution.py:403
  30.7 4.2 %collective-permute-start.9 = (f32[6,16,128]{2,1,0:T(8,128)S(1)}, f32[6,16,128]{2,1,0:T(8,128)S(1)}, u32[]{:S(2)}, u32[]{:S(2)}) collective-permute-start(f32[6,16,128]{2,1,0:T(8,128)S(1)} %get-tuple-element.47), channel_id=1, source_target_pairs={{0,4},{4,0},{8,12},{12,8},{16,20},{20,16},{24,28},{28,24},{1,5},{5... | collective-permute-start | bytes 147464 | tf_op jit(solution)/shard_map/ppermute | solution.py:403

commit v7 on v6

--- a/solution.py
+++ b/solution.py
@@ -315,7 +315,7 @@
         grp_b[i] = jnp.concatenate([part[2 * NIS + NIG : EDGES], edge[1], edge[3]], axis=0)
 
 
-def edge_kernel(grp_a, grp_b, from_a, from_b, _, edge_b, edge_a):
+def edge_kernel(grp_a, grp_b, from_a, from_b, edge_b, edge_a):
     split = NIG + NED
     edge_a[:, :NED, :] = grp_a[:, NIG:split, :] + from_a[:, NIG:split, :]
     edge_a[:, NED:, :] = grp_b[:, NIG:split, :] + from_b[:, NIG:split, :]
@@ -538,8 +538,8 @@
         edge_kernel,
         "sum_edges",
         (array((COMPS, 2 * NED, cases)), array((COMPS, 2 * NED, cases))),
-        vmem(4) + anywhere(1),
-    )(grp_a, grp_b, from_grp_a, from_grp_b, from_sub_a)
+        vmem(4),
+    )(grp_a, grp_b, from_grp_a, from_grp_b)
     from_sub_b = exchange(sub_b, "sub", 1)
     from_edge_b = exchange(edge_b, "sub", 1)
     from_edge_a = exchange(edge_a, "sub", 0)

time: 36.3 us -> 33.5 us (0.923)
  the two profiles are of different devices: /device:TPU:22 before, /device:TPU:1 now
where the time goes in v7:
time: 33.5 us; the launch traced here: 33.2 us
  starting transfers between devices  19.7 us (59%)
  Pallas kernels  8.98 us (27%)
  waiting for transfers between devices  3.8 us (11%)
  between operations  0.73 us (2%)
    ppermute x8, starting transfers between devices, exchange(): return lax.ppermute(block, axis, pairs)  16.1 us
    ppermute x2, starting transfers between devices, gather_near(): parts = [block, lax.ppermute(block, 'grp', pairs)]  3.66 us
    pallas_call x1, Pallas kernels, shards(): call(solve_kernel, 'solve_and_stress', (array((3, nodes, cases), BF16), a...  2.83 us
    ppermute x8, waiting for transfers between devices, exchange(): return lax.ppermute(block, axis, pairs)  2.78 us
    pallas_call x1, Pallas kernels, shards(): call(lists, 'prepare_lists', (array(coarse.shape), array((TERM, 3 * LANES...  1.86 us
    pallas_call x1, Pallas kernels, shards(): call(partial_kernel, 'assemble_nodes', (array((COMPS, nodes, cases)), arr...  1.57 us
    pallas_call x1, Pallas kernels, shards(): call(prepare_panels, 'prepare_panels', (array(panel_inv.shape, BF16), arr...  1.48 us
    pallas_call x1, Pallas kernels, shards(): call(finish_kernel, 'add_last', (array((COMPS, nodes, cases), BF16),), vm...  1.22 us
  transfers between devices with their start and end apart: 10, of which 3 were waited for; matrix products, arithmetic and copies ran while one was open for 0% of the time, Pallas kernels for 15%

profile of v7, /device:TPU:1, one launch (start us, length us, event | category | flops | bytes accessed | tf_op | source)
XLA Modules:
  0.0 33.2 jit_solution(9723086264999882161)
XLA Ops:
  0.6 0.7 %collective-permute-start.1 = (f32[24,128]{1,0:T(8,128)}, f32[24,128]{1,0:T(8,128)S(1)}, u32[]{:S(2)}, u32[]{:S(2)}) collective-permute-start(f32[24,128]{1,0:T(8,128)} %refs_6_.1), channel_id=1, source_target_pairs={{4,8},{8,4},{12,16},{16,12},{20,24},{24,20},{5,9},{9,5},{13,17},{1... | collective-permute-start | bytes 36872 | tf_op jit(solution)/shard_map/ppermute | solution.py:403
  1.3 4.6 %collective-permute-start = (f32[24,128]{1,0:T(8,128)}, f32[24,128]{1,0:T(8,128)S(1)}, u32[]{:S(2)}, u32[]{:S(2)}) collective-permute-start(f32[24,128]{1,0:T(8,128)} %refs_6_.1), channel_id=1, source_target_pairs={{0,4},{4,0},{8,12},{12,8},{16,20},{20,16},{24,28},{28,24},{1,5},{5... | collective-permute-start | bytes 36872 | tf_op jit(solution)/shard_map/ppermute | solution.py:403
  5.9 1.9 %prepare_lists.1 = (f32[24,128]{1,0:T(8,128)S(1)}, bf16[32,384]{1,0:T(8,128)(2,1)S(1)}, bf16[512,1024]{1,0:T(8,128)(2,1)S(1)}, bf16[224,256]{1,0:T(8,128)(2,1)S(...) custom-call(s32[1,24]{1,0:T(1,128)} %refs_0_.1, ...), custom_call_target="tpu_custom_call" | custom-call | flops 100000000 | bytes 4000000 | tf_op jit(solution)/shard_map/prepare_lists/pallas_call | solution.py:454
  7.8 0.0 collective-permute-done.1.refs_2_
  7.8 0.0 collective-permute-done.refs_1_
  7.8 1.3 %collective-permute-start.2 = (f32[72,128]{1,0:T(8,128)S(1)}, f32[72,128]{1,0:T(8,128)S(1)}, u32[]{:S(2)}, u32[]{:S(2)}) collective-permute-start(f32[72,128]{1,0:T(8,128)S(1)} %join_blocks.2.refs_0_), channel_id=1, source_target_pairs={{0,2},{1,3},{2,0},{3,1},{4,6},{5,7},{6,4},{7,5},{8,10},{9,11},{10,... | collective-permute-start | bytes 110600 | tf_op jit(solution)/shard_map/ppermute | solution.py:429
  9.1 1.5 %prepare_panels.1 = (bf16[4,384,384]{2,1,0:T(8,128)(2,1)S(1)}, bf16[1536,128]{1,0:T(8,128)(2,1)S(1)}, f32[1536,128]{1,0:T(8,128)S(1)}, f32[1536,128]{1,0:T(8,128)S(1)}) custom-call(s32[1,4]{1,0:T(1,128)} %panel_nodes.1, bf16[24,1536]{1,0:T(8,128)(2,1)} %bitcast.8, bf16[3,512,128]{2,1,0:T(8,128)(2,1)} %bitcast.7, bf16[4,384,384]{2,1,0:T(8,128)(2,1)} %panel_inv.1), custom_call_target="tpu_custom_call" | custom-call | flops 100000000 | bytes 4000000 | tf_op jit(solution)/shard_map/prepare_panels/pallas_call | solution.py:492
  10.6 0.1 collective-permute-done.2.refs_1_
  10.7 2.4 %collective-permute-start.3 = (f32[144,128]{1,0:T(8,128)S(1)}, f32[144,128]{1,0:T(8,128)S(1)}, u32[]{:S(2)}, u32[]{:S(2)}) collective-permute-start(f32[144,128]{1,0:T(8,128)S(1)} %join_blocks.3.near), channel_id=1, source_target_pairs={{0,1},{1,0},{2,3},{3,2},{4,5},{5,4},{6,7},{7,6},{8,9},{9,8},{10,11... | collective-permute-start | bytes 221192 | tf_op jit(solution)/shard_map/ppermute | solution.py:429
  13.1 0.9 %collective-permute-done.3.across = f32[144,128]{1,0:T(8,128)S(1)} collective-permute-done((f32[144,128]{1,0:T(8,128)S(1)}, f32[144,128]{1,0:T(8,128)S(1)}, u32[]{:S(2)}, u32[]{:S(2)}) %collective-permute-start.3) | collective-permute-done | bytes 73760 | tf_op jit(solution)/shard_map/ppermute | solution.py:429
  14.0 2.8 %solve_and_stress.1 = (bf16[3,512,128]{2,1,0:T(8,128)(2,1)S(1)}, bf16[768,256]{1,0:T(8,128)(2,1)S(1)}, f32[6,64,128]{2,1,0:T(8,128)S(1)}, f32[6,64,128]{2,1,0:T(...) custom-call(f32[144,128]{1,0:T(8,128)S(1)} %join_blocks.3.near, ...), custom_call_target="tpu_custom_call" | custom-call | flops 1500000000 | bytes 4000000 | tf_op jit(solution)/shard_map/solve_and_stress/pallas_call | solution.py:513
  16.8 1.7 %collective-permute-start.4 = (f32[6,64,128]{2,1,0:T(8,128)S(1)}, f32[6,64,128]{2,1,0:T(8,128)S(1)}, u32[]{:S(2)}, u32[]{:S(2)}) collective-permute-start(f32[6,64,128]{2,1,0:T(8,128)S(1)} %get-tuple-element.38), channel_id=1, source_target_pairs={{0,4},{4,0},{8,12},{12,8},{16,20},{20,16},{24,28},{28,24},{1,5},{5... | collective-permute-start | bytes 589832 | tf_op jit(solution)/shard_map/ppermute | solution.py:403
  18.6 0.6 %collective-permute-start.5 = (f32[6,48,128]{2,1,0:T(8,128)S(1)}, f32[6,48,128]{2,1,0:T(8,128)S(1)}, u32[]{:S(2)}, u32[]{:S(2)}) collective-permute-start(f32[6,48,128]{2,1,0:T(8,128)S(1)} %get-tuple-element.39.grp_a), channel_id=1, source_target_pairs={{0,1},{1,0},{2,3},{3,2},{4,5},{5,4},{6,7},{7,6},{8,9},{9,8},{10,11... | collective-permute-start | bytes 442376 | tf_op jit(solution)/shard_map/ppermute | solution.py:403
  19.2 3.0 %collective-permute-start.6 = (f32[6,48,128]{2,1,0:T(8,128)S(1)}, f32[6,48,128]{2,1,0:T(8,128)S(1)}, u32[]{:S(2)}, u32[]{:S(2)}) collective-permute-start(f32[6,48,128]{2,1,0:T(8,128)S(1)} %get-tuple-element.40.grp_b), channel_id=1, source_target_pairs={{1,2},{2,1},{5,6},{6,5},{9,10},{10,9},{13,14},{14,13},{17,18},{18,... | collective-permute-start | bytes 442376 | tf_op jit(solution)/shard_map/ppermute | solution.py:403
  22.2 0.7 %collective-permute-start.7 = (f32[6,64,128]{2,1,0:T(8,128)S(1)}, f32[6,64,128]{2,1,0:T(8,128)S(1)}, u32[]{:S(2)}, u32[]{:S(2)}) collective-permute-start(f32[6,64,128]{2,1,0:T(8,128)S(1)} %get-tuple-element.45), channel_id=1, source_target_pairs={{4,8},{8,4},{12,16},{16,12},{20,24},{24,20},{5,9},{9,5},{13,17},{1... | collective-permute-start | bytes 589832 | tf_op jit(solution)/shard_map/ppermute | solution.py:403
  22.9 0.0 collective-permute-done.5.grp_a.from_a
  22.9 2.8 %collective-permute-done.6.grp_b.from_b = f32[6,48,128]{2,1,0:T(8,128)S(1)} collective-permute-done((f32[6,48,128]{2,1,0:T(8,128)S(1)}, f32[6,48,128]{2,1,0:T(8,128)S(1)}, u32[]{:S(2)}, u32[]{:S(2)}) %collective-permute-start.6) | collective-permute-done | bytes 147488 | tf_op jit(solution)/shard_map/ppermute | solution.py:403
  25.7 0.7 %collective-permute-start.8 = (f32[6,16,128]{2,1,0:T(8,128)S(1)}, f32[6,16,128]{2,1,0:T(8,128)S(1)}, u32[]{:S(2)}, u32[]{:S(2)}) collective-permute-start(f32[6,16,128]{2,1,0:T(8,128)S(1)} %get-tuple-element.46), channel_id=1, source_target_pairs={{4,8},{8,4},{12,16},{16,12},{20,24},{24,20},{5,9},{9,5},{13,17},{1... | collective-permute-start | bytes 147464 | tf_op jit(solution)/shard_map/ppermute | solution.py:403
  26.3 4.1 %collective-permute-start.9 = (f32[6,16,128]{2,1,0:T(8,128)S(1)}, f32[6,16,128]{2,1,0:T(8,128)S(1)}, u32[]{:S(2)}, u32[]{:S(2)}) collective-permute-start(f32[6,16,128]{2,1,0:T(8,128)S(1)} %get-tuple-element.47), channel_id=1, source_target_pairs={{0,4},{4,0},{8,12},{12,8},{16,20},{20,16},{24,28},{28,24},{1,5},{5... | collective-permute-start | bytes 147464 | tf_op jit(solution)/shard_map/ppermute | solution.py:403
  30.4 0.0 collective-permute-done.4.sub_a
  30.4 1.6 %assemble_nodes.1 = (f32[6,512,128]{2,1,0:T(8,128)S(1)}, bf16[3,512,128]{2,1,0:T(8,128)(2,1)}) custom-call(bf16[512,256]{1,0:T(8,128)(2,1)S(1)} %get-tuple-element.25.count, bf16[768,256]{1,0:T(8,128)(2,1)S(1)} %get-tuple-element.35.stress, bf16[3,512,128]{2,1,0:T(8,128)(2,1)S(1)} %get-tuple-element.36.disp, bf16[512,256]{1,0:T(8,128)(2,1)S(1)} %get-tuple-element.37.placing, ...), custom_call_target="tpu_custom_call" | custom-call | flops 400000000 | bytes 2000000 | tf_op jit(solution)/shard_map/assemble_nodes/pallas_call | solution.py:546
  32.0 0.0 collective-permute-done.7.sub_b
  32.0 0.0 collective-permute-done.8.edge_b
  32.0 0.0 collective-permute-done.9.edge_a
  32.0 1.2 %add_last.1 = bf16[6,512,128]{2,1,0:T(8,128)(2,1)} custom-call(bf16[512,256]{1,0:T(8,128)(2,1)S(1)} %get-tuple-element.42.placing, f32[6,512,128]{2,1,0:T(8,128)S(1)} %get-tuple-element.43.partial, f32[512,128]{1,0:T(8,128)S(1)} %get-tuple-element.44.inverse_volume, f32[6,64,128]{2,1,0:T(8,128)S(1)} %collective-permute-done.7.sub_b, ...), custom_call_target="tpu_custom_call" | custom-call | flops 400000000 | bytes 3000000 | tf_op jit(solution)/shard_map/add_last/pallas_call | solution.py:555
  (3 shorter events, 0.0 us)
Async XLA Ops:
  0.6 7.2 %collective-permute-start.1 = (f32[24,128]{1,0:T(8,128)}, f32[24,128]{1,0:T(8,128)S(1)}, u32[]{:S(2)}, u32[]{:S(2)}) collective-permute-start(f32[24,128]{1,0:T(8,128)} %refs_6_.1), channel_id=1, source_target_pairs={{4,8},{8,4},{12,16},{16,12},{20,24},{24,20},{5,9},{9,5},{13,17},{1... | collective-permute-start | bytes 36872 | tf_op jit(solution)/shard_map/ppermute | solution.py:403
  1.3 6.5 %collective-permute-start = (f32[24,128]{1,0:T(8,128)}, f32[24,128]{1,0:T(8,128)S(1)}, u32[]{:S(2)}, u32[]{:S(2)}) collective-permute-start(f32[24,128]{1,0:T(8,128)} %refs_6_.1), channel_id=1, source_target_pairs={{0,4},{4,0},{8,12},{12,8},{16,20},{20,16},{24,28},{28,24},{1,5},{5... | collective-permute-start | bytes 36872 | tf_op jit(solution)/shard_map/ppermute | solution.py:403
  7.8 2.9 %collective-permute-start.2 = (f32[72,128]{1,0:T(8,128)S(1)}, f32[72,128]{1,0:T(8,128)S(1)}, u32[]{:S(2)}, u32[]{:S(2)}) collective-permute-start(f32[72,128]{1,0:T(8,128)S(1)} %join_blocks.2.refs_0_), channel_id=1, source_target_pairs={{0,2},{1,3},{2,0},{3,1},{4,6},{5,7},{6,4},{7,5},{8,10},{9,11},{10,... | collective-permute-start | bytes 110600 | tf_op jit(solution)/shard_map/ppermute | solution.py:429
  10.7 3.3 %collective-permute-start.3 = (f32[144,128]{1,0:T(8,128)S(1)}, f32[144,128]{1,0:T(8,128)S(1)}, u32[]{:S(2)}, u32[]{:S(2)}) collective-permute-start(f32[144,128]{1,0:T(8,128)S(1)} %join_blocks.3.near), channel_id=1, source_target_pairs={{0,1},{1,0},{2,3},{3,2},{4,5},{5,4},{6,7},{7,6},{8,9},{9,8},{10,11... | collective-permute-start | bytes 221192 | tf_op jit(solution)/shard_map/ppermute | solution.py:429
  16.8 13.6 %collective-permute-start.4 = (f32[6,64,128]{2,1,0:T(8,128)S(1)}, f32[6,64,128]{2,1,0:T(8,128)S(1)}, u32[]{:S(2)}, u32[]{:S(2)}) collective-permute-start(f32[6,64,128]{2,1,0:T(8,128)S(1)} %get-tuple-element.38), channel_id=1, source_target_pairs={{0,4},{4,0},{8,12},{12,8},{16,20},{20,16},{24,28},{28,24},{1,5},{5... | collective-permute-start | bytes 589832 | tf_op jit(solution)/shard_map/ppermute | solution.py:403
  18.6 4.3 %collective-permute-start.5 = (f32[6,48,128]{2,1,0:T(8,128)S(1)}, f32[6,48,128]{2,1,0:T(8,128)S(1)}, u32[]{:S(2)}, u32[]{:S(2)}) collective-permute-start(f32[6,48,128]{2,1,0:T(8,128)S(1)} %get-tuple-element.39.grp_a), channel_id=1, source_target_pairs={{0,1},{1,0},{2,3},{3,2},{4,5},{5,4},{6,7},{7,6},{8,9},{9,8},{10,11... | collective-permute-start | bytes 442376 | tf_op jit(solution)/shard_map/ppermute | solution.py:403
  19.2 6.5 %collective-permute-start.6 = (f32[6,48,128]{2,1,0:T(8,128)S(1)}, f32[6,48,128]{2,1,0:T(8,128)S(1)}, u32[]{:S(2)}, u32[]{:S(2)}) collective-permute-start(f32[6,48,128]{2,1,0:T(8,128)S(1)} %get-tuple-element.40.grp_b), channel_id=1, source_target_pairs={{1,2},{2,1},{5,6},{6,5},{9,10},{10,9},{13,14},{14,13},{17,18},{18,... | collective-permute-start | bytes 442376 | tf_op jit(solution)/shard_map/ppermute | solution.py:403
  22.2 9.8 %collective-permute-start.7 = (f32[6,64,128]{2,1,0:T(8,128)S(1)}, f32[6,64,128]{2,1,0:T(8,128)S(1)}, u32[]{:S(2)}, u32[]{:S(2)}) collective-permute-start(f32[6,64,128]{2,1,0:T(8,128)S(1)} %get-tuple-element.45), channel_id=1, source_target_pairs={{4,8},{8,4},{12,16},{16,12},{20,24},{24,20},{5,9},{9,5},{13,17},{1... | collective-permute-start | bytes 589832 | tf_op jit(solution)/shard_map/ppermute | solution.py:403
  25.7 6.3 %collective-permute-start.8 = (f32[6,16,128]{2,1,0:T(8,128)S(1)}, f32[6,16,128]{2,1,0:T(8,128)S(1)}, u32[]{:S(2)}, u32[]{:S(2)}) collective-permute-start(f32[6,16,128]{2,1,0:T(8,128)S(1)} %get-tuple-element.46), channel_id=1, source_target_pairs={{4,8},{8,4},{12,16},{16,12},{20,24},{24,20},{5,9},{9,5},{13,17},{1... | collective-permute-start | bytes 147464 | tf_op jit(solution)/shard_map/ppermute | solution.py:403
  26.3 5.7 %collective-permute-start.9 = (f32[6,16,128]{2,1,0:T(8,128)S(1)}, f32[6,16,128]{2,1,0:T(8,128)S(1)}, u32[]{:S(2)}, u32[]{:S(2)}) collective-permute-start(f32[6,16,128]{2,1,0:T(8,128)S(1)} %get-tuple-element.47), channel_id=1, source_target_pairs={{0,4},{4,0},{8,12},{12,8},{16,20},{20,16},{24,28},{28,24},{1,5},{5... | collective-permute-start | bytes 147464 | tf_op jit(solution)/shard_map/ppermute | solution.py:403

commit v8 on v7

--- a/solution.py
+++ b/solution.py
@@ -125,14 +125,15 @@
     ids[...] = jnp.full(ids.shape, -1.0, F32)
     ids[0:1, 0:NIF] = interface_v[...].astype(F32)
     order_lists(ids)
-    node_of = lax.broadcasted_iota(jnp.int32, (nodes, 2 * LANES), 0)
-    placing[...] = jnp.where(ids[0:1, :].astype(jnp.int32) == node_of, 1.0, 0.0).astype(BF16)
     lane = lax.broadcasted_iota(jnp.int32, (8, LANES), 1)
-    faces = pltpu.roll(ids[:, :LANES], NIS, 1)
-    late = jnp.where(lane < NIS, faces, jnp.where(lane < NIS + 4 * NED, ids[:, LANES:], -1.0))
-    hit = jnp.where(late[0:1, :].astype(jnp.int32) == node_of[:, :LANES], 1.0, 0.0).astype(BF16)
-    placing_last[:, :LANES] = hit
-    placing_last[:, LANES:] = hit
+    last = jnp.where((lane >= NIS) & (lane < NIS + 4 * NED), ids[:, LANES:], -1.0)
+    for index, (row, target) in enumerate(((ids[0:1, LANES:], placing), (ids[0:1, :LANES], placing_last), (last[0:1], placing_last))):
+        hit = jnp.where(row.astype(jnp.int32) == node_of, 1.0, 0.0).astype(BF16)
+        if index == 0:
+            target[:, :LANES] = hit
+            target[:, LANES:] = hit
+        else:
+            target[:, (index - 1) * LANES : index * LANES] = hit
     connect_f = connect_v[...].astype(F32)
     for half in range(2):
         id_col = column(ids[0:1, half * LANES : (half + 1) * LANES])
@@ -324,39 +325,41 @@
 
 
 def partial_kernel(
-    count, stress, disp, placing, sub_a, grp_a, grp_b, partial, disp_out, received
+    count, stress, disp, placing, grp_a, grp_b, partial, disp_out, received
 ):
     disp_out[...] = disp[...]
     split = NIG + NED
-    gap = jnp.zeros((NIS, LANES), F32)
     for i in range(COMPS):
         low, high = grp_a[i], grp_b[i]
-        rows = [sub_a[i], gap, low[:NIG], high[:NIG], low[NIG:split], high[NIG:split], low[split:], high[split:]]
+        rows = [low[:NIG], high[:NIG], low[NIG:split], high[NIG:split], low[split:], high[split:]]
         rows.append(jnp.zeros((2 * LANES - NIF, LANES), F32))
         first, second = split_two(jnp.concatenate(rows, axis=0))
-        received[: 2 * LANES, i * LANES : (i + 1) * LANES] = first
-        received[2 * LANES :, i * LANES : (i + 1) * LANES] = second
+        received[:LANES, i * LANES : (i + 1) * LANES] = first
+        received[LANES:, i * LANES : (i + 1) * LANES] = second
     for i in range(0, COMPS, 2):
         cols = slice(i * LANES, (i + 2) * LANES)
         own = dot_nt(count[...], stress[cols, :])
-        added = dot(placing[...], received[: 2 * LANES, cols]) + dot(placing[...], received[2 * LANES :, cols])
-        total = own + added
+        total = own + dot(placing[...], received[:, cols])
         partial[i] = total[:, :LANES]
         partial[i + 1] = total[:, LANES:]
 
 
-def finish_kernel(placing, partial, inverse_volume, sub_b, edge_b, edge_a, out, received, nodal, sems):
-    rows = NIS + 4 * NED
+def finish_kernel(
+    placing, partial, inverse_volume, sub_a, sub_b, edge_b, edge_a, out, received, nodal, sems
+):
+    gap = jnp.zeros((NIS, LANES), F32)
     for i in range(COMPS):
         cols = slice(i * LANES, (i + 1) * LANES)
-        parts = jnp.concatenate([sub_b[i], edge_a[i], edge_b[i], jnp.zeros((LANES - rows, LANES), F32)], axis=0)
-        first, second = split_two(parts)
-        received[:LANES, cols] = first
-        received[LANES:, cols] = second
+        tail = jnp.zeros((2 * LANES - NIF, LANES), F32)
+        rows = jnp.concatenate([sub_a[i], sub_b[i], gap, edge_a[i], edge_b[i], tail], axis=0)
+        first, second = split_two(rows)
+        received[: 2 * LANES, cols] = first
+        received[2 * LANES :, cols] = second
     scale = inverse_volume[...]
     copies = []
     for i in range(0, COMPS, 2):
-        added = dot(placing[...], received[:, i * LANES : (i + 2) * LANES])
+        cols = slice(i * LANES, (i + 2) * LANES)
+        added = dot(placing[...], received[: 2 * LANES, cols]) + dot(placing[...], received[2 * LANES :, cols])
         nodal[i] = ((partial[i] + added[:, :LANES]) * scale).astype(BF16)
         nodal[i + 1] = ((partial[i + 1] + added[:, LANES:]) * scale).astype(BF16)
         copy = pltpu.make_async_copy(nodal.at[pl.ds(i, 2)], out.at[pl.ds(i, 2)], sems.at[i // 2])
@@ -547,25 +550,25 @@
         partial_kernel,
         "assemble_nodes",
         (array((COMPS, nodes, cases)), array(disp.shape, BF16)),
-        vmem(7),
-        (pltpu.VMEM((4 * LANES, COMPS * cases), BF16),),
+        vmem(6),
+        (pltpu.VMEM((2 * LANES, COMPS * cases), BF16),),
         flops=400000000,
         moved=2000000,
-    )(count, stress, disp, placing, from_sub_a, from_grp_a, from_grp_b)
+    )(count, stress, disp, placing, from_grp_a, from_grp_b)
     (nodal,) = call(
         finish_kernel,
         "add_last",
         (array((COMPS, nodes, cases), BF16),),
-        vmem(6),
-        (
-            pltpu.VMEM((2 * LANES, COMPS * cases), BF16),
+        vmem(7),
+        (
+            pltpu.VMEM((4 * LANES, COMPS * cases), BF16),
             pltpu.VMEM((COMPS, nodes, cases), BF16),
             pltpu.SemaphoreType.DMA((COMPS // 2,)),
         ),
         flops=400000000,
         moved=3000000,
         out_specs=hbm(1),
-    )(placing_last, partial, inverse_volume, from_sub_b, from_edge_b, from_edge_a)
+    )(placing_last, partial, inverse_volume, from_sub_a, from_sub_b, from_edge_b, from_edge_a)
     return jnp.transpose(disp, (1, 0, 2)), jnp.transpose(nodal, (1, 0, 2))
 
 

time: 33.5 us -> 33.1 us (0.988)
  the two profiles are of different devices: /device:TPU:1 before, /device:TPU:10 now
where the time goes in v8:
time: 33.1 us; the launch traced here: 32.7 us
  starting transfers between devices  16.8 us (51%)
  Pallas kernels  8.92 us (27%)
  waiting for transfers between devices  6.29 us (19%)
  between operations  0.72 us (2%)
    ppermute x8, starting transfers between devices, exchange(): return lax.ppermute(block, axis, pairs)  16.2 us
    ppermute x2, waiting for transfers between devices, gather_near(): parts = [block, lax.ppermute(block, 'grp', pairs)]  3.19 us
    ppermute x8, waiting for transfers between devices, exchange(): return lax.ppermute(block, axis, pairs)  3.1 us
    pallas_call x1, Pallas kernels, shards(): call(solve_kernel, 'solve_and_stress', (array((3, nodes, cases), BF16), a...  2.82 us
    pallas_call x1, Pallas kernels, shards(): call(lists, 'prepare_lists', (array(coarse.shape), array((TERM, 3 * LANES...  1.81 us
    pallas_call x1, Pallas kernels, shards(): call(prepare_panels, 'prepare_panels', (array(panel_inv.shape, BF16), arr...  1.48 us
    pallas_call x1, Pallas kernels, shards(): call(finish_kernel, 'add_last', (array((COMPS, nodes, cases), BF16),), vm...  1.46 us
    pallas_call x1, Pallas kernels, shards(): call(partial_kernel, 'assemble_nodes', (array((COMPS, nodes, cases)), arr...  1.32 us
  transfers between devices with their start and end apart: 10, of which 6 were waited for; matrix products, arithmetic and copies ran while one was open for 0% of the time, Pallas kernels for 14%

profile of v8, /device:TPU:10, one launch (start us, length us, event | category | flops | bytes accessed | tf_op | source)
XLA Modules:
  0.0 32.7 jit_solution(565443336211915901)
XLA Ops:
  0.6 3.3 %collective-permute-start.1 = (f32[24,128]{1,0:T(8,128)}, f32[24,128]{1,0:T(8,128)S(1)}, u32[]{:S(2)}, u32[]{:S(2)}) collective-permute-start(f32[24,128]{1,0:T(8,128)} %refs_6_.1), channel_id=1, source_target_pairs={{4,8},{8,4},{12,16},{16,12},{20,24},{24,20},{5,9},{9,5},{13,17},{1... | collective-permute-start | bytes 36872 | tf_op jit(solution)/shard_map/ppermute | solution.py:406
  4.0 1.7 %collective-permute-start = (f32[24,128]{1,0:T(8,128)}, f32[24,128]{1,0:T(8,128)S(1)}, u32[]{:S(2)}, u32[]{:S(2)}) collective-permute-start(f32[24,128]{1,0:T(8,128)} %refs_6_.1), channel_id=1, source_target_pairs={{0,4},{4,0},{8,12},{12,8},{16,20},{20,16},{24,28},{28,24},{1,5},{5... | collective-permute-start | bytes 36872 | tf_op jit(solution)/shard_map/ppermute | solution.py:406
  5.7 1.8 %prepare_lists.1 = (f32[24,128]{1,0:T(8,128)S(1)}, bf16[32,384]{1,0:T(8,128)(2,1)S(1)}, bf16[512,1024]{1,0:T(8,128)(2,1)S(1)}, bf16[224,256]{1,0:T(8,128)(2,1)S(...) custom-call(s32[1,24]{1,0:T(1,128)} %refs_0_.1, ...), custom_call_target="tpu_custom_call" | custom-call | flops 100000000 | bytes 4000000 | tf_op jit(solution)/shard_map/prepare_lists/pallas_call | solution.py:457
  7.5 0.0 collective-permute-done.1.refs_2_
  7.5 0.4 %collective-permute-done.refs_1_ = f32[24,128]{1,0:T(8,128)S(1)} collective-permute-done((f32[24,128]{1,0:T(8,128)}, f32[24,128]{1,0:T(8,128)S(1)}, u32[]{:S(2)}, u32[]{:S(2)}) %collective-permute-start) | collective-permute-done | bytes 12320 | tf_op jit(solution)/shard_map/ppermute | solution.py:406
  7.9 0.5 %collective-permute-start.2 = (f32[72,128]{1,0:T(8,128)S(1)}, f32[72,128]{1,0:T(8,128)S(1)}, u32[]{:S(2)}, u32[]{:S(2)}) collective-permute-start(f32[72,128]{1,0:T(8,128)S(1)} %join_blocks.2.refs_0_), channel_id=1, source_target_pairs={{0,2},{1,3},{2,0},{3,1},{4,6},{5,7},{6,4},{7,5},{8,10},{9,11},{10,... | collective-permute-start | bytes 110600 | tf_op jit(solution)/shard_map/ppermute | solution.py:432
  8.5 1.5 %prepare_panels.1 = (bf16[4,384,384]{2,1,0:T(8,128)(2,1)S(1)}, bf16[1536,128]{1,0:T(8,128)(2,1)S(1)}, f32[1536,128]{1,0:T(8,128)S(1)}, f32[1536,128]{1,0:T(8,128)S(1)}) custom-call(s32[1,4]{1,0:T(1,128)} %panel_nodes.1, bf16[24,1536]{1,0:T(8,128)(2,1)} %bitcast.8, bf16[3,512,128]{2,1,0:T(8,128)(2,1)} %bitcast.7, bf16[4,384,384]{2,1,0:T(8,128)(2,1)} %panel_inv.1), custom_call_target="tpu_custom_call" | custom-call | flops 100000000 | bytes 4000000 | tf_op jit(solution)/shard_map/prepare_panels/pallas_call | solution.py:495
  10.0 1.9 %collective-permute-done.2.refs_1_ = f32[72,128]{1,0:T(8,128)S(1)} collective-permute-done((f32[72,128]{1,0:T(8,128)S(1)}, f32[72,128]{1,0:T(8,128)S(1)}, u32[]{:S(2)}, u32[]{:S(2)}) %collective-permute-start.2) | collective-permute-done | bytes 36896 | tf_op jit(solution)/shard_map/ppermute | solution.py:432
  11.9 0.0 collective-permute-start.3
  11.9 1.3 %collective-permute-done.3.across = f32[144,128]{1,0:T(8,128)S(1)} collective-permute-done((f32[144,128]{1,0:T(8,128)S(1)}, f32[144,128]{1,0:T(8,128)S(1)}, u32[]{:S(2)}, u32[]{:S(2)}) %collective-permute-start.3) | collective-permute-done | bytes 73760 | tf_op jit(solution)/shard_map/ppermute | solution.py:432
  13.2 2.8 %solve_and_stress.1 = (bf16[3,512,128]{2,1,0:T(8,128)(2,1)S(1)}, bf16[768,256]{1,0:T(8,128)(2,1)S(1)}, f32[6,64,128]{2,1,0:T(8,128)S(1)}, f32[6,64,128]{2,1,0:T(...) custom-call(f32[144,128]{1,0:T(8,128)S(1)} %join_blocks.3.near, ...), custom_call_target="tpu_custom_call" | custom-call | flops 1500000000 | bytes 4000000 | tf_op jit(solution)/shard_map/solve_and_stress/pallas_call | solution.py:516
  16.0 0.2 collective-permute-start.4
  16.2 2.4 %collective-permute-start.5 = (f32[6,48,128]{2,1,0:T(8,128)S(1)}, f32[6,48,128]{2,1,0:T(8,128)S(1)}, u32[]{:S(2)}, u32[]{:S(2)}) collective-permute-start(f32[6,48,128]{2,1,0:T(8,128)S(1)} %get-tuple-element.39.grp_b), channel_id=1, source_target_pairs={{1,2},{2,1},{5,6},{6,5},{9,10},{10,9},{13,14},{14,13},{17,18},{18,... | collective-permute-start | bytes 442376 | tf_op jit(solution)/shard_map/ppermute | solution.py:406
  18.6 1.7 %collective-permute-start.6 = (f32[6,64,128]{2,1,0:T(8,128)S(1)}, f32[6,64,128]{2,1,0:T(8,128)S(1)}, u32[]{:S(2)}, u32[]{:S(2)}) collective-permute-start(f32[6,64,128]{2,1,0:T(8,128)S(1)} %get-tuple-element.44), channel_id=1, source_target_pairs={{0,4},{4,0},{8,12},{12,8},{16,20},{20,16},{24,28},{28,24},{1,5},{5... | collective-permute-start | bytes 589832 | tf_op jit(solution)/shard_map/ppermute | solution.py:406
  20.3 1.9 %collective-permute-start.7 = (f32[6,64,128]{2,1,0:T(8,128)S(1)}, f32[6,64,128]{2,1,0:T(8,128)S(1)}, u32[]{:S(2)}, u32[]{:S(2)}) collective-permute-start(f32[6,64,128]{2,1,0:T(8,128)S(1)} %get-tuple-element.45), channel_id=1, source_target_pairs={{4,8},{8,4},{12,16},{16,12},{20,24},{24,20},{5,9},{9,5},{13,17},{1... | collective-permute-start | bytes 589832 | tf_op jit(solution)/shard_map/ppermute | solution.py:406
  22.2 0.0 collective-permute-done.4.grp_a.from_a
  22.2 0.4 %collective-permute-done.5.grp_b.from_b = f32[6,48,128]{2,1,0:T(8,128)S(1)} collective-permute-done((f32[6,48,128]{2,1,0:T(8,128)S(1)}, f32[6,48,128]{2,1,0:T(8,128)S(1)}, u32[]{:S(2)}, u32[]{:S(2)}) %collective-permute-start.5) | collective-permute-done | bytes 147488 | tf_op jit(solution)/shard_map/ppermute | solution.py:406
  22.7 4.4 %collective-permute-start.8 = (f32[6,16,128]{2,1,0:T(8,128)S(1)}, f32[6,16,128]{2,1,0:T(8,128)S(1)}, u32[]{:S(2)}, u32[]{:S(2)}) collective-permute-start(f32[6,16,128]{2,1,0:T(8,128)S(1)} %get-tuple-element.46), channel_id=1, source_target_pairs={{4,8},{8,4},{12,16},{16,12},{20,24},{24,20},{5,9},{9,5},{13,17},{1... | collective-permute-start | bytes 147464 | tf_op jit(solution)/shard_map/ppermute | solution.py:406
  27.1 0.6 %collective-permute-start.9 = (f32[6,16,128]{2,1,0:T(8,128)S(1)}, f32[6,16,128]{2,1,0:T(8,128)S(1)}, u32[]{:S(2)}, u32[]{:S(2)}) collective-permute-start(f32[6,16,128]{2,1,0:T(8,128)S(1)} %get-tuple-element.47), channel_id=1, source_target_pairs={{0,4},{4,0},{8,12},{12,8},{16,20},{20,16},{24,28},{28,24},{1,5},{5... | collective-permute-start | bytes 147464 | tf_op jit(solution)/shard_map/ppermute | solution.py:406
  27.7 1.3 %assemble_nodes.1 = (f32[6,512,128]{2,1,0:T(8,128)S(1)}, bf16[3,512,128]{2,1,0:T(8,128)(2,1)}) custom-call(bf16[512,256]{1,0:T(8,128)(2,1)S(1)} %get-tuple-element.25.count, bf16[768,256]{1,0:T(8,128)(2,1)S(1)} %get-tuple-element.35.stress, bf16[3,512,128]{2,1,0:T(8,128)(2,1)S(1)} %get-tuple-element.36.disp, bf16[512,256]{1,0:T(8,128)(2,1)S(1)} %get-tuple-element.37.placing, ...), custom_call_target="tpu_custom_call" | custom-call | flops 400000000 | bytes 2000000 | tf_op jit(solution)/shard_map/assemble_nodes/pallas_call | solution.py:549
  29.0 0.7 %collective-permute-done.6.sub_a = f32[6,64,128]{2,1,0:T(8,128)S(1)} collective-permute-done((f32[6,64,128]{2,1,0:T(8,128)S(1)}, f32[6,64,128]{2,1,0:T(8,128)S(1)}, u32[]{:S(2)}, u32[]{:S(2)}) %collective-permute-start.6) | collective-permute-done | bytes 196640 | tf_op jit(solution)/shard_map/ppermute | solution.py:406
  29.8 0.0 collective-permute-done.7.sub_b
  29.8 0.0 collective-permute-done.8.edge_b
  29.8 1.5 %collective-permute-done.9.edge_a = f32[6,16,128]{2,1,0:T(8,128)S(1)} collective-permute-done((f32[6,16,128]{2,1,0:T(8,128)S(1)}, f32[6,16,128]{2,1,0:T(8,128)S(1)}, u32[]{:S(2)}, u32[]{:S(2)}) %collective-permute-start.9) | collective-permute-done | bytes 49184 | tf_op jit(solution)/shard_map/ppermute | solution.py:406
  31.3 1.5 %add_last.1 = bf16[6,512,128]{2,1,0:T(8,128)(2,1)} custom-call(bf16[512,256]{1,0:T(8,128)(2,1)S(1)} %get-tuple-element.41.placing, f32[6,512,128]{2,1,0:T(8,128)S(1)} %get-tuple-element.42.partial, f32[512,128]{1,0:T(8,128)S(1)} %get-tuple-element.43.inverse_volume, f32[6,64,128]{2,1,0:T(8,128)S(1)} %collective-permute-done.6.sub_a, ...), custom_call_target="tpu_custom_call" | custom-call | flops 400000000 | bytes 3000000 | tf_op jit(solution)/shard_map/add_last/pallas_call | solution.py:558
  (3 shorter events, 0.0 us)
Async XLA Ops:
  0.6 6.8 %collective-permute-start.1 = (f32[24,128]{1,0:T(8,128)}, f32[24,128]{1,0:T(8,128)S(1)}, u32[]{:S(2)}, u32[]{:S(2)}) collective-permute-start(f32[24,128]{1,0:T(8,128)} %refs_6_.1), channel_id=1, source_target_pairs={{4,8},{8,4},{12,16},{16,12},{20,24},{24,20},{5,9},{9,5},{13,17},{1... | collective-permute-start | bytes 36872 | tf_op jit(solution)/shard_map/ppermute | solution.py:406
  4.0 4.0 %collective-permute-start = (f32[24,128]{1,0:T(8,128)}, f32[24,128]{1,0:T(8,128)S(1)}, u32[]{:S(2)}, u32[]{:S(2)}) collective-permute-start(f32[24,128]{1,0:T(8,128)} %refs_6_.1), channel_id=1, source_target_pairs={{0,4},{4,0},{8,12},{12,8},{16,20},{20,16},{24,28},{28,24},{1,5},{5... | collective-permute-start | bytes 36872 | tf_op jit(solution)/shard_map/ppermute | solution.py:406
  7.9 4.0 %collective-permute-start.2 = (f32[72,128]{1,0:T(8,128)S(1)}, f32[72,128]{1,0:T(8,128)S(1)}, u32[]{:S(2)}, u32[]{:S(2)}) collective-permute-start(f32[72,128]{1,0:T(8,128)S(1)} %join_blocks.2.refs_0_), channel_id=1, source_target_pairs={{0,2},{1,3},{2,0},{3,1},{4,6},{5,7},{6,4},{7,5},{8,10},{9,11},{10,... | collective-permute-start | bytes 110600 | tf_op jit(solution)/shard_map/ppermute | solution.py:432
  11.9 1.3 %collective-permute-start.3 = (f32[144,128]{1,0:T(8,128)S(1)}, f32[144,128]{1,0:T(8,128)S(1)}, u32[]{:S(2)}, u32[]{:S(2)}) collective-permute-start(f32[144,128]{1,0:T(8,128)S(1)} %join_blocks.3.near), channel_id=1, source_target_pairs={{0,1},{1,0},{2,3},{3,2},{4,5},{5,4},{6,7},{7,6},{8,9},{9,8},{10,11... | collective-permute-start | bytes 221192 | tf_op jit(solution)/shard_map/ppermute | solution.py:432
  16.0 6.2 %collective-permute-start.4 = (f32[6,48,128]{2,1,0:T(8,128)S(1)}, f32[6,48,128]{2,1,0:T(8,128)S(1)}, u32[]{:S(2)}, u32[]{:S(2)}) collective-permute-start(f32[6,48,128]{2,1,0:T(8,128)S(1)} %get-tuple-element.38.grp_a), channel_id=1, source_target_pairs={{0,1},{1,0},{2,3},{3,2},{4,5},{5,4},{6,7},{7,6},{8,9},{9,8},{10,11... | collective-permute-start | bytes 442376 | tf_op jit(solution)/shard_map/ppermute | solution.py:406
  16.2 6.5 %collective-permute-start.5 = (f32[6,48,128]{2,1,0:T(8,128)S(1)}, f32[6,48,128]{2,1,0:T(8,128)S(1)}, u32[]{:S(2)}, u32[]{:S(2)}) collective-permute-start(f32[6,48,128]{2,1,0:T(8,128)S(1)} %get-tuple-element.39.grp_b), channel_id=1, source_target_pairs={{1,2},{2,1},{5,6},{6,5},{9,10},{10,9},{13,14},{14,13},{17,18},{18,... | collective-permute-start | bytes 442376 | tf_op jit(solution)/shard_map/ppermute | solution.py:406
  18.6 11.2 %collective-permute-start.6 = (f32[6,64,128]{2,1,0:T(8,128)S(1)}, f32[6,64,128]{2,1,0:T(8,128)S(1)}, u32[]{:S(2)}, u32[]{:S(2)}) collective-permute-start(f32[6,64,128]{2,1,0:T(8,128)S(1)} %get-tuple-element.44), channel_id=1, source_target_pairs={{0,4},{4,0},{8,12},{12,8},{16,20},{20,16},{24,28},{28,24},{1,5},{5... | collective-permute-start | bytes 589832 | tf_op jit(solution)/shard_map/ppermute | solution.py:406
  20.3 9.5 %collective-permute-start.7 = (f32[6,64,128]{2,1,0:T(8,128)S(1)}, f32[6,64,128]{2,1,0:T(8,128)S(1)}, u32[]{:S(2)}, u32[]{:S(2)}) collective-permute-start(f32[6,64,128]{2,1,0:T(8,128)S(1)} %get-tuple-element.45), channel_id=1, source_target_pairs={{4,8},{8,4},{12,16},{16,12},{20,24},{24,20},{5,9},{9,5},{13,17},{1... | collective-permute-start | bytes 589832 | tf_op jit(solution)/shard_map/ppermute | solution.py:406
  22.7 7.1 %collective-permute-start.8 = (f32[6,16,128]{2,1,0:T(8,128)S(1)}, f32[6,16,128]{2,1,0:T(8,128)S(1)}, u32[]{:S(2)}, u32[]{:S(2)}) collective-permute-start(f32[6,16,128]{2,1,0:T(8,128)S(1)} %get-tuple-element.46), channel_id=1, source_target_pairs={{4,8},{8,4},{12,16},{16,12},{20,24},{24,20},{5,9},{9,5},{13,17},{1... | collective-permute-start | bytes 147464 | tf_op jit(solution)/shard_map/ppermute | solution.py:406
  27.1 4.2 %collective-permute-start.9 = (f32[6,16,128]{2,1,0:T(8,128)S(1)}, f32[6,16,128]{2,1,0:T(8,128)S(1)}, u32[]{:S(2)}, u32[]{:S(2)}) collective-permute-start(f32[6,16,128]{2,1,0:T(8,128)S(1)} %get-tuple-element.47), channel_id=1, source_target_pairs={{0,4},{4,0},{8,12},{12,8},{16,20},{20,16},{24,28},{28,24},{1,5},{5... | collective-permute-start | bytes 147464 | tf_op jit(solution)/shard_map/ppermute | solution.py:406

commit v9 on v8

--- a/solution.py
+++ b/solution.py
@@ -14,6 +14,7 @@
 COMPS = 6
 LANES = 128
 TERM = 32
+TERMS = ((0, 0), (0, 1), (0, 2), (1, 0), (1, 1), (2, 0))
 
 POISSON = 0.3
 LAME = POISSON / ((1.0 + POISSON) * (1.0 - 2.0 * POISSON))
@@ -27,6 +28,13 @@
 def split_two(x):
     high = x.astype(BF16)
     return high, (x - high.astype(F32)).astype(BF16)
+
+
+def split_three(x):
+    high = x.astype(BF16)
+    rest = x - high.astype(F32)
+    middle = rest.astype(BF16)
+    return high, middle, (rest - middle.astype(F32)).astype(BF16)
 
 
 def dot(a, b):
@@ -187,13 +195,14 @@
     coupling,
     force,
     panel_inv,
-    inverse,
-    coupled,
-    loads,
-    live,
+    free_t,
+    corner_t,
     panel_v,
     coupling_v,
     force_v,
+    inverse,
+    loads,
+    solved,
     sems,
 ):
     copies = start_copies(
@@ -206,28 +215,38 @@
         sems,
     )
     panels, panel_rows, _ = inverse.shape
+    panel_size = panel_rows // 3
     nodes = force_v.shape[1]
     q = coupling_v.shape[0]
 
     copies[0].wait()
-    row_of = lax.broadcasted_iota(jnp.int32, (panel_rows, LANES), 0)
-    for p in range(panels):
-        alive = row_of < 3 * panel_v[0:1, p : p + 1]
-        live[p * panel_rows : (p + 1) * panel_rows, :] = jnp.where(alive, 1.0, 0.0)
-
     copies[1].wait()
-    for k in range(coupling_v.shape[1] // LANES):
-        part = coupling_v[:, k * LANES : (k + 1) * LANES].astype(F32)
-        gap = jnp.zeros((TERM - q, LANES), F32)
-        stack = jnp.concatenate([part, gap] * 3 + [jnp.zeros((LANES - 3 * TERM, LANES), F32)], axis=0)
-        rows = slice(k * LANES, (k + 1) * LANES)
-        coupled[rows, :] = (stack.T * live[rows, :]).astype(BF16)
-
     copies[2].wait()
     for c in range(3):
         loads[pl.ds(c, nodes, stride=3), :] = force_v[c].astype(F32)
-    loads[...] = loads[...] * live[...]
+    corner_t[len(TERMS) * TERM :, :] = jnp.zeros((corner_t.shape[0] - len(TERMS) * TERM, 3 * nodes), BF16)
+    row_of = lax.broadcasted_iota(jnp.int32, (panel_rows, LANES), 0)
+    lane = lax.broadcasted_iota(jnp.int32, (panel_rows, LANES), 1)
     copies[3].wait()
+    for p in range(panels):
+        start = p * panel_rows
+        live = row_of < 3 * panel_v[0:1, p : p + 1]
+        columns = []
+        for k in range(panel_rows // LANES):
+            part = coupling_v[:, start + k * LANES : start + (k + 1) * LANES].astype(F32)
+            columns.append(jnp.concatenate([part, jnp.zeros((LANES - q, LANES), F32)], axis=0).T)
+        sides = [loads[start : start + panel_rows, :], jnp.concatenate(columns, axis=0)]
+        sides = jnp.concatenate([jnp.where(live, x, 0.0).astype(BF16) for x in sides], axis=1)
+        result = dot(inverse[p], sides)
+        for side in range(2):
+            solved[side] = jnp.where(live, result[:, side * LANES : (side + 1) * LANES], 0.0)
+        for c in range(3):
+            cols = slice(c * nodes + p * panel_size, c * nodes + (p + 1) * panel_size)
+            free_t[:, cols] = solved[0, pl.ds(c, panel_size, stride=3), :].T
+            value = solved[1, pl.ds(c, panel_size, stride=3), :].T[:TERM]
+            pieces = split_three(value)
+            for k, (piece, _) in enumerate(TERMS):
+                corner_t[k * TERM : (k + 1) * TERM, cols] = pieces[piece]
 
 
 def join_kernel(*refs):
@@ -241,53 +260,37 @@
 def solve_kernel(
     near,
     across,
-    inverse,
-    coupled,
-    loads,
-    live,
+    free_t,
+    corner_t,
     select,
     onehot,
     face,
     scaled,
-    disp,
+    disp_t,
     stress,
     sub_a,
     sub_b,
     grp_a,
     grp_b,
     terms,
-    solved,
-    disp_t,
     elem_t,
 ):
-    panels, panel_rows, _ = inverse.shape
-    panel_size = panel_rows // 3
     rows = near.shape[0]
-
     terms[:, 2 * rows :, :] = jnp.zeros((3, terms.shape[1] - 2 * rows, terms.shape[2]), BF16)
     for b, block in enumerate((near, across)):
-        x = block[...]
-        high = x.astype(BF16)
-        rest = x - high.astype(F32)
-        middle = rest.astype(BF16)
-        low = (rest - middle.astype(F32)).astype(BF16)
-        for t, value in enumerate((high, middle, low)):
+        for t, value in enumerate(split_three(block[...])):
             terms[t, b * rows : (b + 1) * rows, :] = value
     picked = [dot(select[...], terms[t]) for t in range(3)]
-    picked.append(jnp.zeros((LANES - 3 * TERM, LANES), F32))
-    values = jnp.concatenate(picked, axis=0).astype(BF16)
-
-    for p in range(panels):
-        start = p * panel_rows
-        span = slice(start, start + panel_rows)
-        reduced = (loads[span, :] - dot(coupled[span, :], values)).astype(BF16)
-        solved[span, :] = dot(inverse[p], reduced) * live[span, :]
-        for c in range(3):
-            part = solved[pl.ds(start + c, panel_size, stride=3), :].astype(BF16)
-            disp[c, p * panel_size : (p + 1) * panel_size, :] = part
-            disp_t[c * LANES : (c + 1) * LANES, p * panel_size : (p + 1) * panel_size] = (
-                part.astype(F32).T.astype(BF16)
-            )
+    values = [picked[term] for _, term in TERMS]
+    values += [jnp.zeros_like(picked[0])] * (corner_t.shape[0] // TERM - len(values))
+    per = LANES // TERM
+    values = [jnp.concatenate(values[k : k + per], axis=0).T for k in range(0, len(values), per)]
+    values = jnp.concatenate(values, axis=1).astype(BF16)
+    nodes = disp_t.shape[1]
+    for c in range(3):
+        cols = slice(c * nodes, (c + 1) * nodes)
+        part = free_t[:, cols] - dot(values, corner_t[:, cols])
+        disp_t[c * LANES : (c + 1) * LANES, :] = part.astype(BF16)
 
     elem_t[...] = dot(disp_t[...], onehot[...])
     step = 32
@@ -325,9 +328,12 @@
 
 
 def partial_kernel(
-    count, stress, disp, placing, grp_a, grp_b, partial, disp_out, received
+    count, stress, disp_t, placing, grp_a, grp_b, partial, disp_out, received
 ):
-    disp_out[...] = disp[...]
+    for c in range(3):
+        for k in range(0, disp_out.shape[1], LANES):
+            part = disp_t[c * LANES : (c + 1) * LANES, k : k + LANES].astype(F32).T
+            disp_out[c, k : k + LANES, :] = part.astype(BF16)
     split = NIG + NED
     for i in range(COMPS):
         low, high = grp_a[i], grp_b[i]
@@ -492,48 +498,45 @@
             coarse,
         )
     )
-    inverse, coupled, loads, live = call(
+    panel_rows = panel_inv.shape[1]
+    free_t, corner_t = call(
         prepare_panels,
         "prepare_panels",
-        (
-            array(panel_inv.shape, BF16),
-            array((dofs, LANES), BF16),
-            array((dofs, cases)),
-            array((dofs, LANES)),
-        ),
+        (array((cases, dofs)), array((2 * LANES, dofs), BF16)),
         hbm(4),
         (
             pltpu.VMEM(panel_nodes.shape, jnp.int32),
             pltpu.VMEM((q, dofs), BF16),
             pltpu.VMEM((3, nodes, cases), BF16),
+            pltpu.VMEM(panel_inv.shape, BF16),
+            pltpu.VMEM((dofs, cases), F32),
+            pltpu.VMEM((2, panel_rows, LANES), F32),
             pltpu.SemaphoreType.DMA((4,)),
         ),
-        flops=100000000,
+        flops=400000000,
         moved=4000000,
     )(*in_hbm(panel_nodes, coupling.T, jnp.transpose(force, (1, 0, 2)), panel_inv))
 
-    near = gather_near(coarse, own, [select, live])
-    disp, stress, sub_a, sub_b, grp_a, grp_b = call(
+    near = gather_near(coarse, own, [select, corner_t])
+    disp_t, stress, sub_a, sub_b, grp_a, grp_b = call(
         solve_kernel,
         "solve_and_stress",
         (
-            array((3, nodes, cases), BF16),
+            array((3 * cases, nodes), BF16),
             array((COMPS * cases, 2 * LANES), BF16),
             array((COMPS, NIS, cases)),
             array((COMPS, NIS, cases)),
             array((COMPS, NIG + 2 * NED, cases)),
             array((COMPS, NIG + 2 * NED, cases)),
         ),
-        vmem(10),
+        vmem(8),
         (
             pltpu.VMEM((3, 3 * LANES, cases), BF16),
-            pltpu.VMEM((dofs, cases), F32),
-            pltpu.VMEM((3 * cases, nodes), BF16),
             pltpu.VMEM((3 * cases, CORNERS * LANES), F32),
         ),
-        flops=1500000000,
+        flops=1000000000,
         moved=4000000,
-    )(*near, inverse, coupled, loads, live, select, onehot, face, scaled)
+    )(*near, free_t, corner_t, select, onehot, face, scaled)
     from_sub_a = exchange(sub_a, "sub", 0)
     from_grp_a = exchange(grp_a, "grp", 0)
     from_grp_b = exchange(grp_b, "grp", 1)
@@ -549,12 +552,12 @@
     partial, disp = call(
         partial_kernel,
         "assemble_nodes",
-        (array((COMPS, nodes, cases)), array(disp.shape, BF16)),
+        (array((COMPS, nodes, cases)), array((3, nodes, cases), BF16)),
         vmem(6),
         (pltpu.VMEM((2 * LANES, COMPS * cases), BF16),),
         flops=400000000,
         moved=2000000,
-    )(count, stress, disp, placing, from_grp_a, from_grp_b)
+    )(count, stress, disp_t, placing, from_grp_a, from_grp_b)
     (nodal,) = call(
         finish_kernel,
         "add_last",

time: 33.1 us -> 32.3 us (0.976)
  waiting for transfers between devices: 6.29 us -> 5.27 us
    ppermute x2, waiting for transfers between devices: 3.19 us -> 2.21 us  [gather_near(): parts = [block, lax.ppermute(block, 'grp', pairs)]]
  transfers between devices with their start and end apart: 10 -> 10, of which waited for: 6 -> 6; matrix products, arithmetic and copies ran while one was open for 0% -> 0% of each run, Pallas kernels for 14% -> 18%
where the time goes in v9:
time: 32.3 us; the launch traced here: 31.8 us
  starting transfers between devices  16.9 us (52%)
  Pallas kernels  8.99 us (28%)
  waiting for transfers between devices  5.27 us (16%)
  between operations  0.72 us (2%)
    ppermute x8, starting transfers between devices, exchange(): return lax.ppermute(block, axis, pairs)  16.3 us
    ppermute x8, waiting for transfers between devices, exchange(): return lax.ppermute(block, axis, pairs)  3.05 us
    pallas_call x1, Pallas kernels, shards(): call(prepare_panels, 'prepare_panels', (array((cases, dofs)), array((2 *...  2.46 us
    ppermute x2, waiting for transfers between devices, gather_near(): parts = [block, lax.ppermute(block, 'grp', pairs)]  2.21 us
    pallas_call x1, Pallas kernels, shards(): call(solve_kernel, 'solve_and_stress', (array((3 * cases, nodes), BF16),...  1.84 us
    pallas_call x1, Pallas kernels, shards(): call(lists, 'prepare_lists', (array(coarse.shape), array((TERM, 3 * LANES...  1.81 us
    pallas_call x1, Pallas kernels, shards(): call(finish_kernel, 'add_last', (array((COMPS, nodes, cases), BF16),), vm...  1.49 us
    pallas_call x1, Pallas kernels, shards(): call(partial_kernel, 'assemble_nodes', (array((COMPS, nodes, cases)), arr...  1.37 us
  transfers between devices with their start and end apart: 10, of which 6 were waited for; matrix products, arithmetic and copies ran while one was open for 0% of the time, Pallas kernels for 18%

profile of v9, /device:TPU:10, one launch (start us, length us, event | category | flops | bytes accessed | tf_op | source)
XLA Modules:
  0.0 31.8 jit_solution(2967333051071935459)
XLA Ops:
  0.6 3.3 %collective-permute-start.1 = (f32[24,128]{1,0:T(8,128)}, f32[24,128]{1,0:T(8,128)S(1)}, u32[]{:S(2)}, u32[]{:S(2)}) collective-permute-start(f32[24,128]{1,0:T(8,128)} %refs_6_.1), channel_id=1, source_target_pairs={{4,8},{8,4},{12,16},{16,12},{20,24},{24,20},{5,9},{9,5},{13,17},{1... | collective-permute-start | bytes 36872 | tf_op jit(solution)/shard_map/ppermute | solution.py:412
  4.0 1.7 %collective-permute-start = (f32[24,128]{1,0:T(8,128)}, f32[24,128]{1,0:T(8,128)S(1)}, u32[]{:S(2)}, u32[]{:S(2)}) collective-permute-start(f32[24,128]{1,0:T(8,128)} %refs_6_.1), channel_id=1, source_target_pairs={{0,4},{4,0},{8,12},{12,8},{16,20},{20,16},{24,28},{28,24},{1,5},{5... | collective-permute-start | bytes 36872 | tf_op jit(solution)/shard_map/ppermute | solution.py:412
  5.7 1.8 %prepare_lists.1 = (f32[24,128]{1,0:T(8,128)S(1)}, bf16[32,384]{1,0:T(8,128)(2,1)S(1)}, bf16[512,1024]{1,0:T(8,128)(2,1)S(1)}, bf16[224,256]{1,0:T(8,128)(2,1)S(...) custom-call(s32[1,24]{1,0:T(1,128)} %refs_0_.1, ...), custom_call_target="tpu_custom_call" | custom-call | flops 100000000 | bytes 4000000 | tf_op jit(solution)/shard_map/prepare_lists/pallas_call | solution.py:463
  7.5 0.0 collective-permute-done.1.refs_2_
  7.5 0.4 %collective-permute-done.refs_1_ = f32[24,128]{1,0:T(8,128)S(1)} collective-permute-done((f32[24,128]{1,0:T(8,128)}, f32[24,128]{1,0:T(8,128)S(1)}, u32[]{:S(2)}, u32[]{:S(2)}) %collective-permute-start) | collective-permute-done | bytes 12320 | tf_op jit(solution)/shard_map/ppermute | solution.py:412
  7.9 0.5 %collective-permute-start.2 = (f32[72,128]{1,0:T(8,128)S(1)}, f32[72,128]{1,0:T(8,128)S(1)}, u32[]{:S(2)}, u32[]{:S(2)}) collective-permute-start(f32[72,128]{1,0:T(8,128)S(1)} %join_blocks.2.refs_0_), channel_id=1, source_target_pairs={{0,2},{1,3},{2,0},{3,1},{4,6},{5,7},{6,4},{7,5},{8,10},{9,11},{10,... | collective-permute-start | bytes 110600 | tf_op jit(solution)/shard_map/ppermute | solution.py:438
  8.5 2.5 %prepare_panels.1 = (f32[128,1536]{1,0:T(8,128)S(1)}, bf16[256,1536]{1,0:T(8,128)(2,1)S(1)}) custom-call(s32[1,4]{1,0:T(1,128)} %panel_nodes.1, bf16[24,1536]{1,0:T(8,128)(2,1)} %bitcast.8, bf16[3,512,128]{2,1,0:T(8,128)(2,1)} %bitcast.7, bf16[4,384,384]{2,1,0:T(8,128)(2,1)} %panel_inv.1), custom_call_target="tpu_custom_call" | custom-call | flops 400000000 | bytes 4000000 | tf_op jit(solution)/shard_map/prepare_panels/pallas_call | solution.py:502
  10.9 1.0 %collective-permute-done.2.refs_1_ = f32[72,128]{1,0:T(8,128)S(1)} collective-permute-done((f32[72,128]{1,0:T(8,128)S(1)}, f32[72,128]{1,0:T(8,128)S(1)}, u32[]{:S(2)}, u32[]{:S(2)}) %collective-permute-start.2) | collective-permute-done | bytes 36896 | tf_op jit(solution)/shard_map/ppermute | solution.py:438
  11.9 0.0 collective-permute-start.3
  11.9 1.3 %collective-permute-done.3.across = f32[144,128]{1,0:T(8,128)S(1)} collective-permute-done((f32[144,128]{1,0:T(8,128)S(1)}, f32[144,128]{1,0:T(8,128)S(1)}, u32[]{:S(2)}, u32[]{:S(2)}) %collective-permute-start.3) | collective-permute-done | bytes 73760 | tf_op jit(solution)/shard_map/ppermute | solution.py:438
  13.2 1.8 %solve_and_stress.1 = (bf16[384,512]{1,0:T(8,128)(2,1)S(1)}, bf16[768,256]{1,0:T(8,128)(2,1)S(1)}, f32[6,64,128]{2,1,0:T(8,128)S(1)}, f32[6,64,128]{2,1,0:T(8,12...) custom-call(f32[144,128]{1,0:T(8,128)S(1)} %join_blocks.3.near, ...), custom_call_target="tpu_custom_call" | custom-call | flops 1000000000 | bytes 4000000 | tf_op jit(solution)/shard_map/solve_and_stress/pallas_call | solution.py:521
  15.0 0.2 collective-permute-start.4
  15.2 2.5 %collective-permute-start.5 = (f32[6,48,128]{2,1,0:T(8,128)S(1)}, f32[6,48,128]{2,1,0:T(8,128)S(1)}, u32[]{:S(2)}, u32[]{:S(2)}) collective-permute-start(f32[6,48,128]{2,1,0:T(8,128)S(1)} %get-tuple-element.35.grp_b), channel_id=1, source_target_pairs={{1,2},{2,1},{5,6},{6,5},{9,10},{10,9},{13,14},{14,13},{17,18},{18,... | collective-permute-start | bytes 442376 | tf_op jit(solution)/shard_map/ppermute | solution.py:412
  17.7 1.7 %collective-permute-start.6 = (f32[6,64,128]{2,1,0:T(8,128)S(1)}, f32[6,64,128]{2,1,0:T(8,128)S(1)}, u32[]{:S(2)}, u32[]{:S(2)}) collective-permute-start(f32[6,64,128]{2,1,0:T(8,128)S(1)} %get-tuple-element.40), channel_id=1, source_target_pairs={{0,4},{4,0},{8,12},{12,8},{16,20},{20,16},{24,28},{28,24},{1,5},{5... | collective-permute-start | bytes 589832 | tf_op jit(solution)/shard_map/ppermute | solution.py:412
  19.4 1.9 %collective-permute-start.7 = (f32[6,64,128]{2,1,0:T(8,128)S(1)}, f32[6,64,128]{2,1,0:T(8,128)S(1)}, u32[]{:S(2)}, u32[]{:S(2)}) collective-permute-start(f32[6,64,128]{2,1,0:T(8,128)S(1)} %get-tuple-element.41), channel_id=1, source_target_pairs={{4,8},{8,4},{12,16},{16,12},{20,24},{24,20},{5,9},{9,5},{13,17},{1... | collective-permute-start | bytes 589832 | tf_op jit(solution)/shard_map/ppermute | solution.py:412
  21.3 0.0 collective-permute-done.4.grp_a.from_a
  21.3 0.3 %collective-permute-done.5.grp_b.from_b = f32[6,48,128]{2,1,0:T(8,128)S(1)} collective-permute-done((f32[6,48,128]{2,1,0:T(8,128)S(1)}, f32[6,48,128]{2,1,0:T(8,128)S(1)}, u32[]{:S(2)}, u32[]{:S(2)}) %collective-permute-start.5) | collective-permute-done | bytes 147488 | tf_op jit(solution)/shard_map/ppermute | solution.py:412
  21.7 4.5 %collective-permute-start.8 = (f32[6,16,128]{2,1,0:T(8,128)S(1)}, f32[6,16,128]{2,1,0:T(8,128)S(1)}, u32[]{:S(2)}, u32[]{:S(2)}) collective-permute-start(f32[6,16,128]{2,1,0:T(8,128)S(1)} %get-tuple-element.42), channel_id=1, source_target_pairs={{4,8},{8,4},{12,16},{16,12},{20,24},{24,20},{5,9},{9,5},{13,17},{1... | collective-permute-start | bytes 147464 | tf_op jit(solution)/shard_map/ppermute | solution.py:412
  26.2 0.5 %collective-permute-start.9 = (f32[6,16,128]{2,1,0:T(8,128)S(1)}, f32[6,16,128]{2,1,0:T(8,128)S(1)}, u32[]{:S(2)}, u32[]{:S(2)}) collective-permute-start(f32[6,16,128]{2,1,0:T(8,128)S(1)} %get-tuple-element.43), channel_id=1, source_target_pairs={{0,4},{4,0},{8,12},{12,8},{16,20},{20,16},{24,28},{28,24},{1,5},{5... | collective-permute-start | bytes 147464 | tf_op jit(solution)/shard_map/ppermute | solution.py:412
  26.7 1.4 %assemble_nodes.1 = (f32[6,512,128]{2,1,0:T(8,128)S(1)}, bf16[3,512,128]{2,1,0:T(8,128)(2,1)}) custom-call(bf16[512,256]{1,0:T(8,128)(2,1)S(1)} %get-tuple-element.23.count, bf16[768,256]{1,0:T(8,128)(2,1)S(1)} %get-tuple-element.31.stress, bf16[384,512]{1,0:T(8,128)(2,1)S(1)} %get-tuple-element.32.disp_t, bf16[512,256]{1,0:T(8,128)(2,1)S(1)} %get-tuple-element.33.placing, ...), custom_call_target="tpu_custom_call" | custom-call | flops 400000000 | bytes 2000000 | tf_op jit(solution)/shard_map/assemble_nodes/pallas_call | solution.py:552
  28.1 0.8 %collective-permute-done.6.sub_a = f32[6,64,128]{2,1,0:T(8,128)S(1)} collective-permute-done((f32[6,64,128]{2,1,0:T(8,128)S(1)}, f32[6,64,128]{2,1,0:T(8,128)S(1)}, u32[]{:S(2)}, u32[]{:S(2)}) %collective-permute-start.6) | collective-permute-done | bytes 196640 | tf_op jit(solution)/shard_map/ppermute | solution.py:412
  28.9 0.0 collective-permute-done.7.sub_b
  28.9 0.0 collective-permute-done.8.edge_b
  28.9 1.4 %collective-permute-done.9.edge_a = f32[6,16,128]{2,1,0:T(8,128)S(1)} collective-permute-done((f32[6,16,128]{2,1,0:T(8,128)S(1)}, f32[6,16,128]{2,1,0:T(8,128)S(1)}, u32[]{:S(2)}, u32[]{:S(2)}) %collective-permute-start.9) | collective-permute-done | bytes 49184 | tf_op jit(solution)/shard_map/ppermute | solution.py:412
  30.3 1.5 %add_last.1 = bf16[6,512,128]{2,1,0:T(8,128)(2,1)} custom-call(bf16[512,256]{1,0:T(8,128)(2,1)S(1)} %get-tuple-element.37.placing, f32[6,512,128]{2,1,0:T(8,128)S(1)} %get-tuple-element.38.partial, f32[512,128]{1,0:T(8,128)S(1)} %get-tuple-element.39.inverse_volume, f32[6,64,128]{2,1,0:T(8,128)S(1)} %collective-permute-done.6.sub_a, ...), custom_call_target="tpu_custom_call" | custom-call | flops 400000000 | bytes 3000000 | tf_op jit(solution)/shard_map/add_last/pallas_call | solution.py:561
  (3 shorter events, 0.0 us)
Async XLA Ops:
  0.6 6.8 %collective-permute-start.1 = (f32[24,128]{1,0:T(8,128)}, f32[24,128]{1,0:T(8,128)S(1)}, u32[]{:S(2)}, u32[]{:S(2)}) collective-permute-start(f32[24,128]{1,0:T(8,128)} %refs_6_.1), channel_id=1, source_target_pairs={{4,8},{8,4},{12,16},{16,12},{20,24},{24,20},{5,9},{9,5},{13,17},{1... | collective-permute-start | bytes 36872 | tf_op jit(solution)/shard_map/ppermute | solution.py:412
  4.0 4.0 %collective-permute-start = (f32[24,128]{1,0:T(8,128)}, f32[24,128]{1,0:T(8,128)S(1)}, u32[]{:S(2)}, u32[]{:S(2)}) collective-permute-start(f32[24,128]{1,0:T(8,128)} %refs_6_.1), channel_id=1, source_target_pairs={{0,4},{4,0},{8,12},{12,8},{16,20},{20,16},{24,28},{28,24},{1,5},{5... | collective-permute-start | bytes 36872 | tf_op jit(solution)/shard_map/ppermute | solution.py:412
  7.9 4.0 %collective-permute-start.2 = (f32[72,128]{1,0:T(8,128)S(1)}, f32[72,128]{1,0:T(8,128)S(1)}, u32[]{:S(2)}, u32[]{:S(2)}) collective-permute-start(f32[72,128]{1,0:T(8,128)S(1)} %join_blocks.2.refs_0_), channel_id=1, source_target_pairs={{0,2},{1,3},{2,0},{3,1},{4,6},{5,7},{6,4},{7,5},{8,10},{9,11},{10,... | collective-permute-start | bytes 110600 | tf_op jit(solution)/shard_map/ppermute | solution.py:438
  11.9 1.3 %collective-permute-start.3 = (f32[144,128]{1,0:T(8,128)S(1)}, f32[144,128]{1,0:T(8,128)S(1)}, u32[]{:S(2)}, u32[]{:S(2)}) collective-permute-start(f32[144,128]{1,0:T(8,128)S(1)} %join_blocks.3.near), channel_id=1, source_target_pairs={{0,1},{1,0},{2,3},{3,2},{4,5},{5,4},{6,7},{7,6},{8,9},{9,8},{10,11... | collective-permute-start | bytes 221192 | tf_op jit(solution)/shard_map/ppermute | solution.py:438
  15.0 6.3 %collective-permute-start.4 = (f32[6,48,128]{2,1,0:T(8,128)S(1)}, f32[6,48,128]{2,1,0:T(8,128)S(1)}, u32[]{:S(2)}, u32[]{:S(2)}) collective-permute-start(f32[6,48,128]{2,1,0:T(8,128)S(1)} %get-tuple-element.34.grp_a), channel_id=1, source_target_pairs={{0,1},{1,0},{2,3},{3,2},{4,5},{5,4},{6,7},{7,6},{8,9},{9,8},{10,11... | collective-permute-start | bytes 442376 | tf_op jit(solution)/shard_map/ppermute | solution.py:412
  15.2 6.5 %collective-permute-start.5 = (f32[6,48,128]{2,1,0:T(8,128)S(1)}, f32[6,48,128]{2,1,0:T(8,128)S(1)}, u32[]{:S(2)}, u32[]{:S(2)}) collective-permute-start(f32[6,48,128]{2,1,0:T(8,128)S(1)} %get-tuple-element.35.grp_b), channel_id=1, source_target_pairs={{1,2},{2,1},{5,6},{6,5},{9,10},{10,9},{13,14},{14,13},{17,18},{18,... | collective-permute-start | bytes 442376 | tf_op jit(solution)/shard_map/ppermute | solution.py:412
  17.7 11.2 %collective-permute-start.6 = (f32[6,64,128]{2,1,0:T(8,128)S(1)}, f32[6,64,128]{2,1,0:T(8,128)S(1)}, u32[]{:S(2)}, u32[]{:S(2)}) collective-permute-start(f32[6,64,128]{2,1,0:T(8,128)S(1)} %get-tuple-element.40), channel_id=1, source_target_pairs={{0,4},{4,0},{8,12},{12,8},{16,20},{20,16},{24,28},{28,24},{1,5},{5... | collective-permute-start | bytes 589832 | tf_op jit(solution)/shard_map/ppermute | solution.py:412
  19.4 9.5 %collective-permute-start.7 = (f32[6,64,128]{2,1,0:T(8,128)S(1)}, f32[6,64,128]{2,1,0:T(8,128)S(1)}, u32[]{:S(2)}, u32[]{:S(2)}) collective-permute-start(f32[6,64,128]{2,1,0:T(8,128)S(1)} %get-tuple-element.41), channel_id=1, source_target_pairs={{4,8},{8,4},{12,16},{16,12},{20,24},{24,20},{5,9},{9,5},{13,17},{1... | collective-permute-start | bytes 589832 | tf_op jit(solution)/shard_map/ppermute | solution.py:412
  21.7 7.2 %collective-permute-start.8 = (f32[6,16,128]{2,1,0:T(8,128)S(1)}, f32[6,16,128]{2,1,0:T(8,128)S(1)}, u32[]{:S(2)}, u32[]{:S(2)}) collective-permute-start(f32[6,16,128]{2,1,0:T(8,128)S(1)} %get-tuple-element.42), channel_id=1, source_target_pairs={{4,8},{8,4},{12,16},{16,12},{20,24},{24,20},{5,9},{9,5},{13,17},{1... | collective-permute-start | bytes 147464 | tf_op jit(solution)/shard_map/ppermute | solution.py:412
  26.2 4.2 %collective-permute-start.9 = (f32[6,16,128]{2,1,0:T(8,128)S(1)}, f32[6,16,128]{2,1,0:T(8,128)S(1)}, u32[]{:S(2)}, u32[]{:S(2)}) collective-permute-start(f32[6,16,128]{2,1,0:T(8,128)S(1)} %get-tuple-element.43), channel_id=1, source_target_pairs={{0,4},{4,0},{8,12},{12,8},{16,20},{20,16},{24,28},{28,24},{1,5},{5... | collective-permute-start | bytes 147464 | tf_op jit(solution)/shard_map/ppermute | solution.py:412

commit v10 on v9

--- a/solution.py
+++ b/solution.py
@@ -10,6 +10,7 @@
 NED = 8
 EDGES = 2 * NIS + 2 * NIG
 NIF = EDGES + 4 * NED
+LATE = NIS + 4 * NED
 CORNERS = 8
 COMPS = 6
 LANES = 128
@@ -134,14 +135,17 @@
     ids[0:1, 0:NIF] = interface_v[...].astype(F32)
     order_lists(ids)
     lane = lax.broadcasted_iota(jnp.int32, (8, LANES), 1)
-    last = jnp.where((lane >= NIS) & (lane < NIS + 4 * NED), ids[:, LANES:], -1.0)
-    for index, (row, target) in enumerate(((ids[0:1, LANES:], placing), (ids[0:1, :LANES], placing_last), (last[0:1], placing_last))):
+    edges = pltpu.roll(ids[:, LANES:], LANES - NIS, 1)
+    again = pltpu.roll(ids[:, :LANES], LANES - NIS + 4 * NED, 1)
+    last = jnp.where(lane < 4 * NED, edges, again)
+    last = jnp.where(lane < LATE, last, pltpu.roll(edges, LATE, 1))
+    for row, target in ((ids[0:1, LANES:], 0), (ids[0:1, :LANES], 1), (last[0:1], 2)):
         hit = jnp.where(row.astype(jnp.int32) == node_of, 1.0, 0.0).astype(BF16)
-        if index == 0:
-            target[:, :LANES] = hit
-            target[:, LANES:] = hit
+        if target == 0:
+            placing[:, :LANES] = hit
+            placing[:, LANES:] = hit
         else:
-            target[:, (index - 1) * LANES : index * LANES] = hit
+            placing_last[:, (target - 1) * LANES : target * LANES] = hit
     connect_f = connect_v[...].astype(F32)
     for half in range(2):
         id_col = column(ids[0:1, half * LANES : (half + 1) * LANES])
@@ -273,7 +277,7 @@
     grp_a,
     grp_b,
     terms,
-    elem_t,
+    sofar,
 ):
     rows = near.shape[0]
     terms[:, 2 * rows :, :] = jnp.zeros((3, terms.shape[1] - 2 * rows, terms.shape[2]), BF16)
@@ -292,22 +296,27 @@
         part = free_t[:, cols] - dot(values, corner_t[:, cols])
         disp_t[c * LANES : (c + 1) * LANES, :] = part.astype(BF16)
 
-    elem_t[...] = dot(disp_t[...], onehot[...])
     step = 32
-    for start in range(0, LANES, step):
-        sums = [None] * COMPS
-        for a in range(CORNERS):
-            for c in range(3):
-                x = elem_t[c * LANES + start : c * LANES + start + step, a * LANES : (a + 1) * LANES]
-                x = x.reshape(step // 8, 8, LANES)
-                for i in range(COMPS):
-                    term = scaled[24 * i + 3 * a + c] * x
-                    sums[i] = term if sums[i] is None else sums[i] + term
-        sums = [x.reshape(step, LANES) for x in sums]
-        for i in range(COMPS):
-            high, low = split_two(sums[i])
-            stress[i * LANES + start : i * LANES + start + step, 0:LANES] = high
-            stress[i * LANES + start : i * LANES + start + step, LANES : 2 * LANES] = low
+    pairs = onehot.shape[1] // (2 * LANES)
+    for pair in range(pairs):
+        elem_t = dot(disp_t[...], onehot[:, 2 * LANES * pair : 2 * LANES * (pair + 1)])
+        for start in range(0, LANES, step):
+            sums = [None] * COMPS if pair == 0 else [sofar[i, start : start + step, :] for i in range(COMPS)]
+            for half in range(2):
+                for c in range(3):
+                    x = elem_t[c * LANES + start : c * LANES + start + step, half * LANES : (half + 1) * LANES]
+                    x = x.reshape(step // 8, 8, LANES)
+                    for i in range(COMPS):
+                        term = scaled[24 * i + 3 * (2 * pair + half) + c] * x
+                        term = term.reshape(step, LANES)
+                        sums[i] = term if sums[i] is None else sums[i] + term
+            for i in range(COMPS):
+                if pair < pairs - 1:
+                    sofar[i, start : start + step, :] = sums[i]
+                else:
+                    high, low = split_two(sums[i])
+                    stress[i * LANES + start : i * LANES + start + step, 0:LANES] = high
+                    stress[i * LANES + start : i * LANES + start + step, LANES : 2 * LANES] = low
 
     rows = dot_nt(face[...], stress[...])
     for i in range(COMPS):
@@ -353,19 +362,18 @@
 def finish_kernel(
     placing, partial, inverse_volume, sub_a, sub_b, edge_b, edge_a, out, received, nodal, sems
 ):
-    gap = jnp.zeros((NIS, LANES), F32)
     for i in range(COMPS):
         cols = slice(i * LANES, (i + 1) * LANES)
-        tail = jnp.zeros((2 * LANES - NIF, LANES), F32)
-        rows = jnp.concatenate([sub_a[i], sub_b[i], gap, edge_a[i], edge_b[i], tail], axis=0)
-        first, second = split_two(rows)
-        received[: 2 * LANES, cols] = first
-        received[2 * LANES :, cols] = second
+        late = jnp.concatenate([sub_b[i], edge_a[i], edge_b[i]], axis=0)
+        first, second = split_two(late)
+        received[:NIS, cols] = sub_a[i].astype(BF16)
+        received[NIS : NIS + LATE, cols] = first
+        received[NIS + LATE :, cols] = second
     scale = inverse_volume[...]
     copies = []
     for i in range(0, COMPS, 2):
         cols = slice(i * LANES, (i + 2) * LANES)
-        added = dot(placing[...], received[: 2 * LANES, cols]) + dot(placing[...], received[2 * LANES :, cols])
+        added = dot(placing[...], received[:, cols])
         nodal[i] = ((partial[i] + added[:, :LANES]) * scale).astype(BF16)
         nodal[i + 1] = ((partial[i + 1] + added[:, LANES:]) * scale).astype(BF16)
         copy = pltpu.make_async_copy(nodal.at[pl.ds(i, 2)], out.at[pl.ds(i, 2)], sems.at[i // 2])
@@ -532,7 +540,7 @@
         vmem(8),
         (
             pltpu.VMEM((3, 3 * LANES, cases), BF16),
-            pltpu.VMEM((3 * cases, CORNERS * LANES), F32),
+            pltpu.VMEM((COMPS, cases, LANES), F32),
         ),
         flops=1000000000,
         moved=4000000,
@@ -564,7 +572,7 @@
         (array((COMPS, nodes, cases), BF16),),
         vmem(7),
         (
-            pltpu.VMEM((4 * LANES, COMPS * cases), BF16),
+            pltpu.VMEM((NIS + 2 * LATE, COMPS * cases), BF16),
             pltpu.VMEM((COMPS, nodes, cases), BF16),
             pltpu.SemaphoreType.DMA((COMPS // 2,)),
         ),

time: 32.3 us -> 32 us (level)
  no operation moved by 1% of the time
where the time goes in v10:
time: 32 us; the launch traced here: 31.6 us
  starting transfers between devices  16.9 us (53%)
  Pallas kernels  8.79 us (27%)
  waiting for transfers between devices  5.19 us (16%)
  between operations  0.72 us (2%)
    ppermute x8, starting transfers between devices, exchange(): return lax.ppermute(block, axis, pairs)  16.3 us
    ppermute x8, waiting for transfers between devices, exchange(): return lax.ppermute(block, axis, pairs)  2.98 us
    pallas_call x1, Pallas kernels, shards(): call(prepare_panels, 'prepare_panels', (array((cases, dofs)), array((2 *...  2.46 us
    ppermute x2, waiting for transfers between devices, gather_near(): parts = [block, lax.ppermute(block, 'grp', pairs)]  2.21 us
    pallas_call x1, Pallas kernels, shards(): call(lists, 'prepare_lists', (array(coarse.shape), array((TERM, 3 * LANES...  1.88 us
    pallas_call x1, Pallas kernels, shards(): call(solve_kernel, 'solve_and_stress', (array((3 * cases, nodes), BF16),...  1.84 us
    pallas_call x1, Pallas kernels, shards(): call(partial_kernel, 'assemble_nodes', (array((COMPS, nodes, cases)), arr...  1.37 us
    pallas_call x1, Pallas kernels, shards(): call(finish_kernel, 'add_last', (array((COMPS, nodes, cases), BF16),), vm...  1.22 us
  transfers between devices with their start and end apart: 10, of which 6 were waited for; matrix products, arithmetic and copies ran while one was open for 0% of the time, Pallas kernels for 18%

profile of v10, /device:TPU:10, one launch (start us, length us, event | category | flops | bytes accessed | tf_op | source)
XLA Modules:
  0.0 31.6 jit_solution(7057205459056852717)
XLA Ops:
  0.6 3.3 %collective-permute-start.1 = (f32[24,128]{1,0:T(8,128)}, f32[24,128]{1,0:T(8,128)S(1)}, u32[]{:S(2)}, u32[]{:S(2)}) collective-permute-start(f32[24,128]{1,0:T(8,128)} %refs_6_.1), channel_id=1, source_target_pairs={{4,8},{8,4},{12,16},{16,12},{20,24},{24,20},{5,9},{9,5},{13,17},{1... | collective-permute-start | bytes 36872 | tf_op jit(solution)/shard_map/ppermute | solution.py:420
  4.0 1.7 %collective-permute-start = (f32[24,128]{1,0:T(8,128)}, f32[24,128]{1,0:T(8,128)S(1)}, u32[]{:S(2)}, u32[]{:S(2)}) collective-permute-start(f32[24,128]{1,0:T(8,128)} %refs_6_.1), channel_id=1, source_target_pairs={{0,4},{4,0},{8,12},{12,8},{16,20},{20,16},{24,28},{28,24},{1,5},{5... | collective-permute-start | bytes 36872 | tf_op jit(solution)/shard_map/ppermute | solution.py:420
  5.7 1.9 %prepare_lists.1 = (f32[24,128]{1,0:T(8,128)S(1)}, bf16[32,384]{1,0:T(8,128)(2,1)S(1)}, bf16[512,1024]{1,0:T(8,128)(2,1)S(1)}, bf16[224,256]{1,0:T(8,128)(2,1)S(...) custom-call(s32[1,24]{1,0:T(1,128)} %refs_0_.1, ...), custom_call_target="tpu_custom_call" | custom-call | flops 100000000 | bytes 4000000 | tf_op jit(solution)/shard_map/prepare_lists/pallas_call | solution.py:471
  7.5 0.0 collective-permute-done.1.refs_2_
  7.6 0.4 %collective-permute-done.refs_1_ = f32[24,128]{1,0:T(8,128)S(1)} collective-permute-done((f32[24,128]{1,0:T(8,128)}, f32[24,128]{1,0:T(8,128)S(1)}, u32[]{:S(2)}, u32[]{:S(2)}) %collective-permute-start) | collective-permute-done | bytes 12320 | tf_op jit(solution)/shard_map/ppermute | solution.py:420
  7.9 0.5 %collective-permute-start.2 = (f32[72,128]{1,0:T(8,128)S(1)}, f32[72,128]{1,0:T(8,128)S(1)}, u32[]{:S(2)}, u32[]{:S(2)}) collective-permute-start(f32[72,128]{1,0:T(8,128)S(1)} %join_blocks.2.refs_0_), channel_id=1, source_target_pairs={{0,2},{1,3},{2,0},{3,1},{4,6},{5,7},{6,4},{7,5},{8,10},{9,11},{10,... | collective-permute-start | bytes 110600 | tf_op jit(solution)/shard_map/ppermute | solution.py:446
  8.5 2.5 %prepare_panels.1 = (f32[128,1536]{1,0:T(8,128)S(1)}, bf16[256,1536]{1,0:T(8,128)(2,1)S(1)}) custom-call(s32[1,4]{1,0:T(1,128)} %panel_nodes.1, bf16[24,1536]{1,0:T(8,128)(2,1)} %bitcast.8, bf16[3,512,128]{2,1,0:T(8,128)(2,1)} %bitcast.7, bf16[4,384,384]{2,1,0:T(8,128)(2,1)} %panel_inv.1), custom_call_target="tpu_custom_call" | custom-call | flops 400000000 | bytes 4000000 | tf_op jit(solution)/shard_map/prepare_panels/pallas_call | solution.py:510
  10.9 1.0 %collective-permute-done.2.refs_1_ = f32[72,128]{1,0:T(8,128)S(1)} collective-permute-done((f32[72,128]{1,0:T(8,128)S(1)}, f32[72,128]{1,0:T(8,128)S(1)}, u32[]{:S(2)}, u32[]{:S(2)}) %collective-permute-start.2) | collective-permute-done | bytes 36896 | tf_op jit(solution)/shard_map/ppermute | solution.py:446
  11.9 0.0 collective-permute-start.3
  11.9 1.3 %collective-permute-done.3.across = f32[144,128]{1,0:T(8,128)S(1)} collective-permute-done((f32[144,128]{1,0:T(8,128)S(1)}, f32[144,128]{1,0:T(8,128)S(1)}, u32[]{:S(2)}, u32[]{:S(2)}) %collective-permute-start.3) | collective-permute-done | bytes 73760 | tf_op jit(solution)/shard_map/ppermute | solution.py:446
  13.2 1.8 %solve_and_stress.1 = (bf16[384,512]{1,0:T(8,128)(2,1)S(1)}, bf16[768,256]{1,0:T(8,128)(2,1)S(1)}, f32[6,64,128]{2,1,0:T(8,128)S(1)}, f32[6,64,128]{2,1,0:T(8,12...) custom-call(f32[144,128]{1,0:T(8,128)S(1)} %join_blocks.3.near, ...), custom_call_target="tpu_custom_call" | custom-call | flops 1000000000 | bytes 4000000 | tf_op jit(solution)/shard_map/solve_and_stress/pallas_call | solution.py:529
  15.0 0.2 collective-permute-start.4
  15.2 2.5 %collective-permute-start.5 = (f32[6,48,128]{2,1,0:T(8,128)S(1)}, f32[6,48,128]{2,1,0:T(8,128)S(1)}, u32[]{:S(2)}, u32[]{:S(2)}) collective-permute-start(f32[6,48,128]{2,1,0:T(8,128)S(1)} %get-tuple-element.35.grp_b), channel_id=1, source_target_pairs={{1,2},{2,1},{5,6},{6,5},{9,10},{10,9},{13,14},{14,13},{17,18},{18,... | collective-permute-start | bytes 442376 | tf_op jit(solution)/shard_map/ppermute | solution.py:420
  17.7 1.7 %collective-permute-start.6 = (f32[6,64,128]{2,1,0:T(8,128)S(1)}, f32[6,64,128]{2,1,0:T(8,128)S(1)}, u32[]{:S(2)}, u32[]{:S(2)}) collective-permute-start(f32[6,64,128]{2,1,0:T(8,128)S(1)} %get-tuple-element.40), channel_id=1, source_target_pairs={{0,4},{4,0},{8,12},{12,8},{16,20},{20,16},{24,28},{28,24},{1,5},{5... | collective-permute-start | bytes 589832 | tf_op jit(solution)/shard_map/ppermute | solution.py:420
  19.4 1.9 %collective-permute-start.7 = (f32[6,64,128]{2,1,0:T(8,128)S(1)}, f32[6,64,128]{2,1,0:T(8,128)S(1)}, u32[]{:S(2)}, u32[]{:S(2)}) collective-permute-start(f32[6,64,128]{2,1,0:T(8,128)S(1)} %get-tuple-element.41), channel_id=1, source_target_pairs={{4,8},{8,4},{12,16},{16,12},{20,24},{24,20},{5,9},{9,5},{13,17},{1... | collective-permute-start | bytes 589832 | tf_op jit(solution)/shard_map/ppermute | solution.py:420
  21.3 0.0 collective-permute-done.4.grp_a.from_a
  21.3 0.3 %collective-permute-done.5.grp_b.from_b = f32[6,48,128]{2,1,0:T(8,128)S(1)} collective-permute-done((f32[6,48,128]{2,1,0:T(8,128)S(1)}, f32[6,48,128]{2,1,0:T(8,128)S(1)}, u32[]{:S(2)}, u32[]{:S(2)}) %collective-permute-start.5) | collective-permute-done | bytes 147488 | tf_op jit(solution)/shard_map/ppermute | solution.py:420
  21.7 4.5 %collective-permute-start.8 = (f32[6,16,128]{2,1,0:T(8,128)S(1)}, f32[6,16,128]{2,1,0:T(8,128)S(1)}, u32[]{:S(2)}, u32[]{:S(2)}) collective-permute-start(f32[6,16,128]{2,1,0:T(8,128)S(1)} %get-tuple-element.42), channel_id=1, source_target_pairs={{4,8},{8,4},{12,16},{16,12},{20,24},{24,20},{5,9},{9,5},{13,17},{1... | collective-permute-start | bytes 147464 | tf_op jit(solution)/shard_map/ppermute | solution.py:420
  26.2 0.5 %collective-permute-start.9 = (f32[6,16,128]{2,1,0:T(8,128)S(1)}, f32[6,16,128]{2,1,0:T(8,128)S(1)}, u32[]{:S(2)}, u32[]{:S(2)}) collective-permute-start(f32[6,16,128]{2,1,0:T(8,128)S(1)} %get-tuple-element.43), channel_id=1, source_target_pairs={{0,4},{4,0},{8,12},{12,8},{16,20},{20,16},{24,28},{28,24},{1,5},{5... | collective-permute-start | bytes 147464 | tf_op jit(solution)/shard_map/ppermute | solution.py:420
  26.7 1.4 %assemble_nodes.1 = (f32[6,512,128]{2,1,0:T(8,128)S(1)}, bf16[3,512,128]{2,1,0:T(8,128)(2,1)}) custom-call(bf16[512,256]{1,0:T(8,128)(2,1)S(1)} %get-tuple-element.23.count, bf16[768,256]{1,0:T(8,128)(2,1)S(1)} %get-tuple-element.31.stress, bf16[384,512]{1,0:T(8,128)(2,1)S(1)} %get-tuple-element.32.disp_t, bf16[512,256]{1,0:T(8,128)(2,1)S(1)} %get-tuple-element.33.placing, ...), custom_call_target="tpu_custom_call" | custom-call | flops 400000000 | bytes 2000000 | tf_op jit(solution)/shard_map/assemble_nodes/pallas_call | solution.py:560
  28.1 0.8 %collective-permute-done.6.sub_a = f32[6,64,128]{2,1,0:T(8,128)S(1)} collective-permute-done((f32[6,64,128]{2,1,0:T(8,128)S(1)}, f32[6,64,128]{2,1,0:T(8,128)S(1)}, u32[]{:S(2)}, u32[]{:S(2)}) %collective-permute-start.6) | collective-permute-done | bytes 196640 | tf_op jit(solution)/shard_map/ppermute | solution.py:420
  28.9 0.0 collective-permute-done.7.sub_b
  28.9 0.0 collective-permute-done.8.edge_b
  28.9 1.4 %collective-permute-done.9.edge_a = f32[6,16,128]{2,1,0:T(8,128)S(1)} collective-permute-done((f32[6,16,128]{2,1,0:T(8,128)S(1)}, f32[6,16,128]{2,1,0:T(8,128)S(1)}, u32[]{:S(2)}, u32[]{:S(2)}) %collective-permute-start.9) | collective-permute-done | bytes 49184 | tf_op jit(solution)/shard_map/ppermute | solution.py:420
  30.4 1.2 %add_last.1 = bf16[6,512,128]{2,1,0:T(8,128)(2,1)} custom-call(bf16[512,256]{1,0:T(8,128)(2,1)S(1)} %get-tuple-element.37.placing, f32[6,512,128]{2,1,0:T(8,128)S(1)} %get-tuple-element.38.partial, f32[512,128]{1,0:T(8,128)S(1)} %get-tuple-element.39.inverse_volume, f32[6,64,128]{2,1,0:T(8,128)S(1)} %collective-permute-done.6.sub_a, ...), custom_call_target="tpu_custom_call" | custom-call | flops 400000000 | bytes 3000000 | tf_op jit(solution)/shard_map/add_last/pallas_call | solution.py:569
  (3 shorter events, 0.0 us)
Async XLA Ops:
  0.6 6.9 %collective-permute-start.1 = (f32[24,128]{1,0:T(8,128)}, f32[24,128]{1,0:T(8,128)S(1)}, u32[]{:S(2)}, u32[]{:S(2)}) collective-permute-start(f32[24,128]{1,0:T(8,128)} %refs_6_.1), channel_id=1, source_target_pairs={{4,8},{8,4},{12,16},{16,12},{20,24},{24,20},{5,9},{9,5},{13,17},{1... | collective-permute-start | bytes 36872 | tf_op jit(solution)/shard_map/ppermute | solution.py:420
  4.0 4.0 %collective-permute-start = (f32[24,128]{1,0:T(8,128)}, f32[24,128]{1,0:T(8,128)S(1)}, u32[]{:S(2)}, u32[]{:S(2)}) collective-permute-start(f32[24,128]{1,0:T(8,128)} %refs_6_.1), channel_id=1, source_target_pairs={{0,4},{4,0},{8,12},{12,8},{16,20},{20,16},{24,28},{28,24},{1,5},{5... | collective-permute-start | bytes 36872 | tf_op jit(solution)/shard_map/ppermute | solution.py:420
  7.9 4.0 %collective-permute-start.2 = (f32[72,128]{1,0:T(8,128)S(1)}, f32[72,128]{1,0:T(8,128)S(1)}, u32[]{:S(2)}, u32[]{:S(2)}) collective-permute-start(f32[72,128]{1,0:T(8,128)S(1)} %join_blocks.2.refs_0_), channel_id=1, source_target_pairs={{0,2},{1,3},{2,0},{3,1},{4,6},{5,7},{6,4},{7,5},{8,10},{9,11},{10,... | collective-permute-start | bytes 110600 | tf_op jit(solution)/shard_map/ppermute | solution.py:446
  11.9 1.3 %collective-permute-start.3 = (f32[144,128]{1,0:T(8,128)S(1)}, f32[144,128]{1,0:T(8,128)S(1)}, u32[]{:S(2)}, u32[]{:S(2)}) collective-permute-start(f32[144,128]{1,0:T(8,128)S(1)} %join_blocks.3.near), channel_id=1, source_target_pairs={{0,1},{1,0},{2,3},{3,2},{4,5},{5,4},{6,7},{7,6},{8,9},{9,8},{10,11... | collective-permute-start | bytes 221192 | tf_op jit(solution)/shard_map/ppermute | solution.py:446
  15.0 6.3 %collective-permute-start.4 = (f32[6,48,128]{2,1,0:T(8,128)S(1)}, f32[6,48,128]{2,1,0:T(8,128)S(1)}, u32[]{:S(2)}, u32[]{:S(2)}) collective-permute-start(f32[6,48,128]{2,1,0:T(8,128)S(1)} %get-tuple-element.34.grp_a), channel_id=1, source_target_pairs={{0,1},{1,0},{2,3},{3,2},{4,5},{5,4},{6,7},{7,6},{8,9},{9,8},{10,11... | collective-permute-start | bytes 442376 | tf_op jit(solution)/shard_map/ppermute | solution.py:420
  15.2 6.5 %collective-permute-start.5 = (f32[6,48,128]{2,1,0:T(8,128)S(1)}, f32[6,48,128]{2,1,0:T(8,128)S(1)}, u32[]{:S(2)}, u32[]{:S(2)}) collective-permute-start(f32[6,48,128]{2,1,0:T(8,128)S(1)} %get-tuple-element.35.grp_b), channel_id=1, source_target_pairs={{1,2},{2,1},{5,6},{6,5},{9,10},{10,9},{13,14},{14,13},{17,18},{18,... | collective-permute-start | bytes 442376 | tf_op jit(solution)/shard_map/ppermute | solution.py:420
  17.7 11.2 %collective-permute-start.6 = (f32[6,64,128]{2,1,0:T(8,128)S(1)}, f32[6,64,128]{2,1,0:T(8,128)S(1)}, u32[]{:S(2)}, u32[]{:S(2)}) collective-permute-start(f32[6,64,128]{2,1,0:T(8,128)S(1)} %get-tuple-element.40), channel_id=1, source_target_pairs={{0,4},{4,0},{8,12},{12,8},{16,20},{20,16},{24,28},{28,24},{1,5},{5... | collective-permute-start | bytes 589832 | tf_op jit(solution)/shard_map/ppermute | solution.py:420
  19.4 9.5 %collective-permute-start.7 = (f32[6,64,128]{2,1,0:T(8,128)S(1)}, f32[6,64,128]{2,1,0:T(8,128)S(1)}, u32[]{:S(2)}, u32[]{:S(2)}) collective-permute-start(f32[6,64,128]{2,1,0:T(8,128)S(1)} %get-tuple-element.41), channel_id=1, source_target_pairs={{4,8},{8,4},{12,16},{16,12},{20,24},{24,20},{5,9},{9,5},{13,17},{1... | collective-permute-start | bytes 589832 | tf_op jit(solution)/shard_map/ppermute | solution.py:420
  21.7 7.2 %collective-permute-start.8 = (f32[6,16,128]{2,1,0:T(8,128)S(1)}, f32[6,16,128]{2,1,0:T(8,128)S(1)}, u32[]{:S(2)}, u32[]{:S(2)}) collective-permute-start(f32[6,16,128]{2,1,0:T(8,128)S(1)} %get-tuple-element.42), channel_id=1, source_target_pairs={{4,8},{8,4},{12,16},{16,12},{20,24},{24,20},{5,9},{9,5},{13,17},{1... | collective-permute-start | bytes 147464 | tf_op jit(solution)/shard_map/ppermute | solution.py:420
  26.2 4.2 %collective-permute-start.9 = (f32[6,16,128]{2,1,0:T(8,128)S(1)}, f32[6,16,128]{2,1,0:T(8,128)S(1)}, u32[]{:S(2)}, u32[]{:S(2)}) collective-permute-start(f32[6,16,128]{2,1,0:T(8,128)S(1)} %get-tuple-element.43), channel_id=1, source_target_pairs={{0,4},{4,0},{8,12},{12,8},{16,20},{20,16},{24,28},{28,24},{1,5},{5... | collective-permute-start | bytes 147464 | tf_op jit(solution)/shard_map/ppermute | solution.py:420

commit v11 on v10

--- a/solution.py
+++ b/solution.py
@@ -328,7 +328,7 @@
         grp_b[i] = jnp.concatenate([part[2 * NIS + NIG : EDGES], edge[1], edge[3]], axis=0)
 
 
-def edge_kernel(grp_a, grp_b, from_a, from_b, edge_b, edge_a):
+def edge_kernel(grp_b, grp_a, from_b, from_a, edge_b, edge_a):
     split = NIG + NED
     edge_a[:, :NED, :] = grp_a[:, NIG:split, :] + from_a[:, NIG:split, :]
     edge_a[:, NED:, :] = grp_b[:, NIG:split, :] + from_b[:, NIG:split, :]
@@ -337,7 +337,7 @@
 
 
 def partial_kernel(
-    count, stress, disp_t, placing, grp_a, grp_b, partial, disp_out, received
+    count, stress, disp_t, placing, grp_b, grp_a, partial, disp_out, received
 ):
     for c in range(3):
         for k in range(0, disp_out.shape[1], LANES):
@@ -546,14 +546,14 @@
         moved=4000000,
     )(*near, free_t, corner_t, select, onehot, face, scaled)
     from_sub_a = exchange(sub_a, "sub", 0)
+    from_grp_b = exchange(grp_b, "grp", 1)
     from_grp_a = exchange(grp_a, "grp", 0)
-    from_grp_b = exchange(grp_b, "grp", 1)
     edge_b, edge_a = call(
         edge_kernel,
         "sum_edges",
         (array((COMPS, 2 * NED, cases)), array((COMPS, 2 * NED, cases))),
         vmem(4),
-    )(grp_a, grp_b, from_grp_a, from_grp_b)
+    )(grp_b, grp_a, from_grp_b, from_grp_a)
     from_sub_b = exchange(sub_b, "sub", 1)
     from_edge_b = exchange(edge_b, "sub", 1)
     from_edge_a = exchange(edge_a, "sub", 0)
@@ -565,7 +565,7 @@
         (pltpu.VMEM((2 * LANES, COMPS * cases), BF16),),
         flops=400000000,
         moved=2000000,
-    )(count, stress, disp_t, placing, from_grp_a, from_grp_b)
+    )(count, stress, disp_t, placing, from_grp_b, from_grp_a)
     (nodal,) = call(
         finish_kernel,
         "add_last",

time: 32 us -> 33.9 us (1.059)
  the two profiles are of different devices: /device:TPU:10 before, /device:TPU:0 now
where the time goes in v11:
time: 33.9 us; the launch traced here: 33.6 us
  starting transfers between devices  20.4 us (60%)
  Pallas kernels  8.8 us (26%)
  waiting for transfers between devices  3.63 us (11%)
  between operations  0.76 us (2%)
    ppermute x8, starting transfers between devices, exchange(): return lax.ppermute(block, axis, pairs)  18.8 us
    pallas_call x1, Pallas kernels, shards(): call(prepare_panels, 'prepare_panels', (array((cases, dofs)), array((2 *...  2.46 us
    ppermute x8, waiting for transfers between devices, exchange(): return lax.ppermute(block, axis, pairs)  2.38 us
    pallas_call x1, Pallas kernels, shards(): call(lists, 'prepare_lists', (array(coarse.shape), array((TERM, 3 * LANES...  1.88 us
    pallas_call x1, Pallas kernels, shards(): call(solve_kernel, 'solve_and_stress', (array((3 * cases, nodes), BF16),...  1.84 us
    ppermute x2, starting transfers between devices, gather_near(): parts = [block, lax.ppermute(block, 'grp', pairs)]  1.63 us
    pallas_call x1, Pallas kernels, shards(): call(partial_kernel, 'assemble_nodes', (array((COMPS, nodes, cases)), arr...  1.37 us
    ppermute x2, waiting for transfers between devices, gather_near(): parts = [block, lax.ppermute(block, 'grp', pairs)]  1.26 us
  transfers between devices with their start and end apart: 10, of which 3 were waited for; matrix products, arithmetic and copies ran while one was open for 0% of the time, Pallas kernels for 17%

profile of v11, /device:TPU:0, one launch (start us, length us, event | category | flops | bytes accessed | tf_op | source)
XLA Modules:
  0.0 33.6 jit_solution(17986170035533231471)
XLA Ops:
  0.6 0.7 %collective-permute-start.1 = (f32[24,128]{1,0:T(8,128)}, f32[24,128]{1,0:T(8,128)S(1)}, u32[]{:S(2)}, u32[]{:S(2)}) collective-permute-start(f32[24,128]{1,0:T(8,128)} %refs_6_.1), channel_id=1, source_target_pairs={{4,8},{8,4},{12,16},{16,12},{20,24},{24,20},{5,9},{9,5},{13,17},{1... | collective-permute-start | bytes 36872 | tf_op jit(solution)/shard_map/ppermute | solution.py:420
  1.3 5.8 %collective-permute-start = (f32[24,128]{1,0:T(8,128)}, f32[24,128]{1,0:T(8,128)S(1)}, u32[]{:S(2)}, u32[]{:S(2)}) collective-permute-start(f32[24,128]{1,0:T(8,128)} %refs_6_.1), channel_id=1, source_target_pairs={{0,4},{4,0},{8,12},{12,8},{16,20},{20,16},{24,28},{28,24},{1,5},{5... | collective-permute-start | bytes 36872 | tf_op jit(solution)/shard_map/ppermute | solution.py:420
  7.1 1.9 %prepare_lists.1 = (f32[24,128]{1,0:T(8,128)S(1)}, bf16[32,384]{1,0:T(8,128)(2,1)S(1)}, bf16[512,1024]{1,0:T(8,128)(2,1)S(1)}, bf16[224,256]{1,0:T(8,128)(2,1)S(...) custom-call(s32[1,24]{1,0:T(1,128)} %refs_0_.1, ...), custom_call_target="tpu_custom_call" | custom-call | flops 100000000 | bytes 4000000 | tf_op jit(solution)/shard_map/prepare_lists/pallas_call | solution.py:471
  9.0 0.0 collective-permute-done.1.refs_2_
  9.0 0.0 collective-permute-done.refs_1_
  9.0 1.6 %collective-permute-start.2 = (f32[72,128]{1,0:T(8,128)S(1)}, f32[72,128]{1,0:T(8,128)S(1)}, u32[]{:S(2)}, u32[]{:S(2)}) collective-permute-start(f32[72,128]{1,0:T(8,128)S(1)} %join_blocks.2.refs_0_), channel_id=1, source_target_pairs={{0,2},{1,3},{2,0},{3,1},{4,6},{5,7},{6,4},{7,5},{8,10},{9,11},{10,... | collective-permute-start | bytes 110600 | tf_op jit(solution)/shard_map/ppermute | solution.py:446
  10.6 2.5 %prepare_panels.1 = (f32[128,1536]{1,0:T(8,128)S(1)}, bf16[256,1536]{1,0:T(8,128)(2,1)S(1)}) custom-call(s32[1,4]{1,0:T(1,128)} %panel_nodes.1, bf16[24,1536]{1,0:T(8,128)(2,1)} %bitcast.8, bf16[3,512,128]{2,1,0:T(8,128)(2,1)} %bitcast.7, bf16[4,384,384]{2,1,0:T(8,128)(2,1)} %panel_inv.1), custom_call_target="tpu_custom_call" | custom-call | flops 400000000 | bytes 4000000 | tf_op jit(solution)/shard_map/prepare_panels/pallas_call | solution.py:510
  13.0 0.0 collective-permute-done.2.refs_1_
  13.1 0.1 collective-permute-start.3
  13.2 1.3 %collective-permute-done.3.across = f32[144,128]{1,0:T(8,128)S(1)} collective-permute-done((f32[144,128]{1,0:T(8,128)S(1)}, f32[144,128]{1,0:T(8,128)S(1)}, u32[]{:S(2)}, u32[]{:S(2)}) %collective-permute-start.3) | collective-permute-done | bytes 73760 | tf_op jit(solution)/shard_map/ppermute | solution.py:446
  14.4 1.8 %solve_and_stress.1 = (bf16[384,512]{1,0:T(8,128)(2,1)S(1)}, bf16[768,256]{1,0:T(8,128)(2,1)S(1)}, f32[6,64,128]{2,1,0:T(8,128)S(1)}, f32[6,64,128]{2,1,0:T(8,12...) custom-call(f32[144,128]{1,0:T(8,128)S(1)} %join_blocks.3.near, ...), custom_call_target="tpu_custom_call" | custom-call | flops 1000000000 | bytes 4000000 | tf_op jit(solution)/shard_map/solve_and_stress/pallas_call | solution.py:529
  16.2 0.7 %collective-permute-start.4 = (f32[6,48,128]{2,1,0:T(8,128)S(1)}, f32[6,48,128]{2,1,0:T(8,128)S(1)}, u32[]{:S(2)}, u32[]{:S(2)}) collective-permute-start(f32[6,48,128]{2,1,0:T(8,128)S(1)} %get-tuple-element.34.grp_b), channel_id=1, source_target_pairs={{1,2},{2,1},{5,6},{6,5},{9,10},{10,9},{13,14},{14,13},{17,18},{18,... | collective-permute-start | bytes 442376 | tf_op jit(solution)/shard_map/ppermute | solution.py:420
  16.9 2.8 %collective-permute-start.5 = (f32[6,48,128]{2,1,0:T(8,128)S(1)}, f32[6,48,128]{2,1,0:T(8,128)S(1)}, u32[]{:S(2)}, u32[]{:S(2)}) collective-permute-start(f32[6,48,128]{2,1,0:T(8,128)S(1)} %get-tuple-element.35.grp_a), channel_id=1, source_target_pairs={{0,1},{1,0},{2,3},{3,2},{4,5},{5,4},{6,7},{7,6},{8,9},{9,8},{10,11... | collective-permute-start | bytes 442376 | tf_op jit(solution)/shard_map/ppermute | solution.py:420
  19.7 1.9 %collective-permute-start.6 = (f32[6,64,128]{2,1,0:T(8,128)S(1)}, f32[6,64,128]{2,1,0:T(8,128)S(1)}, u32[]{:S(2)}, u32[]{:S(2)}) collective-permute-start(f32[6,64,128]{2,1,0:T(8,128)S(1)} %get-tuple-element.40), channel_id=1, source_target_pairs={{0,4},{4,0},{8,12},{12,8},{16,20},{20,16},{24,28},{28,24},{1,5},{5... | collective-permute-start | bytes 589832 | tf_op jit(solution)/shard_map/ppermute | solution.py:420
  21.7 0.7 %collective-permute-start.7 = (f32[6,64,128]{2,1,0:T(8,128)S(1)}, f32[6,64,128]{2,1,0:T(8,128)S(1)}, u32[]{:S(2)}, u32[]{:S(2)}) collective-permute-start(f32[6,64,128]{2,1,0:T(8,128)S(1)} %get-tuple-element.41), channel_id=1, source_target_pairs={{4,8},{8,4},{12,16},{16,12},{20,24},{24,20},{5,9},{9,5},{13,17},{1... | collective-permute-start | bytes 589832 | tf_op jit(solution)/shard_map/ppermute | solution.py:420
  22.3 0.0 collective-permute-done.4.grp_b.from_b
  22.4 0.0 collective-permute-done.5.grp_a.from_a
  22.4 0.7 %collective-permute-start.8 = (f32[6,16,128]{2,1,0:T(8,128)S(1)}, f32[6,16,128]{2,1,0:T(8,128)S(1)}, u32[]{:S(2)}, u32[]{:S(2)}) collective-permute-start(f32[6,16,128]{2,1,0:T(8,128)S(1)} %get-tuple-element.42), channel_id=1, source_target_pairs={{4,8},{8,4},{12,16},{16,12},{20,24},{24,20},{5,9},{9,5},{13,17},{1... | collective-permute-start | bytes 147464 | tf_op jit(solution)/shard_map/ppermute | solution.py:420
  23.1 5.6 %collective-permute-start.9 = (f32[6,16,128]{2,1,0:T(8,128)S(1)}, f32[6,16,128]{2,1,0:T(8,128)S(1)}, u32[]{:S(2)}, u32[]{:S(2)}) collective-permute-start(f32[6,16,128]{2,1,0:T(8,128)S(1)} %get-tuple-element.43), channel_id=1, source_target_pairs={{0,4},{4,0},{8,12},{12,8},{16,20},{20,16},{24,28},{28,24},{1,5},{5... | collective-permute-start | bytes 147464 | tf_op jit(solution)/shard_map/ppermute | solution.py:420
  28.7 1.4 %assemble_nodes.1 = (f32[6,512,128]{2,1,0:T(8,128)S(1)}, bf16[3,512,128]{2,1,0:T(8,128)(2,1)}) custom-call(bf16[512,256]{1,0:T(8,128)(2,1)S(1)} %get-tuple-element.23.count, bf16[768,256]{1,0:T(8,128)(2,1)S(1)} %get-tuple-element.31.stress, bf16[384,512]{1,0:T(8,128)(2,1)S(1)} %get-tuple-element.32.disp_t, bf16[512,256]{1,0:T(8,128)(2,1)S(1)} %get-tuple-element.33.placing, ...), custom_call_target="tpu_custom_call" | custom-call | flops 400000000 | bytes 2000000 | tf_op jit(solution)/shard_map/assemble_nodes/pallas_call | solution.py:560
  30.0 1.8 %collective-permute-done.6.sub_a = f32[6,64,128]{2,1,0:T(8,128)S(1)} collective-permute-done((f32[6,64,128]{2,1,0:T(8,128)S(1)}, f32[6,64,128]{2,1,0:T(8,128)S(1)}, u32[]{:S(2)}, u32[]{:S(2)}) %collective-permute-start.6) | collective-permute-done | bytes 196640 | tf_op jit(solution)/shard_map/ppermute | solution.py:420
  31.9 0.0 collective-permute-done.7.sub_b
  31.9 0.0 collective-permute-done.8.edge_b
  31.9 0.5 %collective-permute-done.9.edge_a = f32[6,16,128]{2,1,0:T(8,128)S(1)} collective-permute-done((f32[6,16,128]{2,1,0:T(8,128)S(1)}, f32[6,16,128]{2,1,0:T(8,128)S(1)}, u32[]{:S(2)}, u32[]{:S(2)}) %collective-permute-start.9) | collective-permute-done | bytes 49184 | tf_op jit(solution)/shard_map/ppermute | solution.py:420
  32.4 1.2 %add_last.1 = bf16[6,512,128]{2,1,0:T(8,128)(2,1)} custom-call(bf16[512,256]{1,0:T(8,128)(2,1)S(1)} %get-tuple-element.37.placing, f32[6,512,128]{2,1,0:T(8,128)S(1)} %get-tuple-element.38.partial, f32[512,128]{1,0:T(8,128)S(1)} %get-tuple-element.39.inverse_volume, f32[6,64,128]{2,1,0:T(8,128)S(1)} %collective-permute-done.6.sub_a, ...), custom_call_target="tpu_custom_call" | custom-call | flops 400000000 | bytes 3000000 | tf_op jit(solution)/shard_map/add_last/pallas_call | solution.py:569
  (3 shorter events, 0.0 us)
Async XLA Ops:
  0.6 8.4 %collective-permute-start.1 = (f32[24,128]{1,0:T(8,128)}, f32[24,128]{1,0:T(8,128)S(1)}, u32[]{:S(2)}, u32[]{:S(2)}) collective-permute-start(f32[24,128]{1,0:T(8,128)} %refs_6_.1), channel_id=1, source_target_pairs={{4,8},{8,4},{12,16},{16,12},{20,24},{24,20},{5,9},{9,5},{13,17},{1... | collective-permute-start | bytes 36872 | tf_op jit(solution)/shard_map/ppermute | solution.py:420
  1.3 7.7 %collective-permute-start = (f32[24,128]{1,0:T(8,128)}, f32[24,128]{1,0:T(8,128)S(1)}, u32[]{:S(2)}, u32[]{:S(2)}) collective-permute-start(f32[24,128]{1,0:T(8,128)} %refs_6_.1), channel_id=1, source_target_pairs={{0,4},{4,0},{8,12},{12,8},{16,20},{20,16},{24,28},{28,24},{1,5},{5... | collective-permute-start | bytes 36872 | tf_op jit(solution)/shard_map/ppermute | solution.py:420
  9.0 4.0 %collective-permute-start.2 = (f32[72,128]{1,0:T(8,128)S(1)}, f32[72,128]{1,0:T(8,128)S(1)}, u32[]{:S(2)}, u32[]{:S(2)}) collective-permute-start(f32[72,128]{1,0:T(8,128)S(1)} %join_blocks.2.refs_0_), channel_id=1, source_target_pairs={{0,2},{1,3},{2,0},{3,1},{4,6},{5,7},{6,4},{7,5},{8,10},{9,11},{10,... | collective-permute-start | bytes 110600 | tf_op jit(solution)/shard_map/ppermute | solution.py:446
  13.1 1.3 %collective-permute-start.3 = (f32[144,128]{1,0:T(8,128)S(1)}, f32[144,128]{1,0:T(8,128)S(1)}, u32[]{:S(2)}, u32[]{:S(2)}) collective-permute-start(f32[144,128]{1,0:T(8,128)S(1)} %join_blocks.3.near), channel_id=1, source_target_pairs={{0,1},{1,0},{2,3},{3,2},{4,5},{5,4},{6,7},{7,6},{8,9},{9,8},{10,11... | collective-permute-start | bytes 221192 | tf_op jit(solution)/shard_map/ppermute | solution.py:446
  16.2 6.1 %collective-permute-start.4 = (f32[6,48,128]{2,1,0:T(8,128)S(1)}, f32[6,48,128]{2,1,0:T(8,128)S(1)}, u32[]{:S(2)}, u32[]{:S(2)}) collective-permute-start(f32[6,48,128]{2,1,0:T(8,128)S(1)} %get-tuple-element.34.grp_b), channel_id=1, source_target_pairs={{1,2},{2,1},{5,6},{6,5},{9,10},{10,9},{13,14},{14,13},{17,18},{18,... | collective-permute-start | bytes 442376 | tf_op jit(solution)/shard_map/ppermute | solution.py:420
  16.9 5.4 %collective-permute-start.5 = (f32[6,48,128]{2,1,0:T(8,128)S(1)}, f32[6,48,128]{2,1,0:T(8,128)S(1)}, u32[]{:S(2)}, u32[]{:S(2)}) collective-permute-start(f32[6,48,128]{2,1,0:T(8,128)S(1)} %get-tuple-element.35.grp_a), channel_id=1, source_target_pairs={{0,1},{1,0},{2,3},{3,2},{4,5},{5,4},{6,7},{7,6},{8,9},{9,8},{10,11... | collective-permute-start | bytes 442376 | tf_op jit(solution)/shard_map/ppermute | solution.py:420
  19.7 12.1 %collective-permute-start.6 = (f32[6,64,128]{2,1,0:T(8,128)S(1)}, f32[6,64,128]{2,1,0:T(8,128)S(1)}, u32[]{:S(2)}, u32[]{:S(2)}) collective-permute-start(f32[6,64,128]{2,1,0:T(8,128)S(1)} %get-tuple-element.40), channel_id=1, source_target_pairs={{0,4},{4,0},{8,12},{12,8},{16,20},{20,16},{24,28},{28,24},{1,5},{5... | collective-permute-start | bytes 589832 | tf_op jit(solution)/shard_map/ppermute | solution.py:420
  21.7 10.2 %collective-permute-start.7 = (f32[6,64,128]{2,1,0:T(8,128)S(1)}, f32[6,64,128]{2,1,0:T(8,128)S(1)}, u32[]{:S(2)}, u32[]{:S(2)}) collective-permute-start(f32[6,64,128]{2,1,0:T(8,128)S(1)} %get-tuple-element.41), channel_id=1, source_target_pairs={{4,8},{8,4},{12,16},{16,12},{20,24},{24,20},{5,9},{9,5},{13,17},{1... | collective-permute-start | bytes 589832 | tf_op jit(solution)/shard_map/ppermute | solution.py:420
  22.4 9.5 %collective-permute-start.8 = (f32[6,16,128]{2,1,0:T(8,128)S(1)}, f32[6,16,128]{2,1,0:T(8,128)S(1)}, u32[]{:S(2)}, u32[]{:S(2)}) collective-permute-start(f32[6,16,128]{2,1,0:T(8,128)S(1)} %get-tuple-element.42), channel_id=1, source_target_pairs={{4,8},{8,4},{12,16},{16,12},{20,24},{24,20},{5,9},{9,5},{13,17},{1... | collective-permute-start | bytes 147464 | tf_op jit(solution)/shard_map/ppermute | solution.py:420
  23.1 9.3 %collective-permute-start.9 = (f32[6,16,128]{2,1,0:T(8,128)S(1)}, f32[6,16,128]{2,1,0:T(8,128)S(1)}, u32[]{:S(2)}, u32[]{:S(2)}) collective-permute-start(f32[6,16,128]{2,1,0:T(8,128)S(1)} %get-tuple-element.43), channel_id=1, source_target_pairs={{0,4},{4,0},{8,12},{12,8},{16,20},{20,16},{24,28},{28,24},{1,5},{5... | collective-permute-start | bytes 147464 | tf_op jit(solution)/shard_map/ppermute | solution.py:420

commit v12 on v10

--- a/solution.py
+++ b/solution.py
@@ -69,6 +69,41 @@
     ids[:, LANES:] = jnp.where(lane < 2 * NIG, groups, edges)
 
 
+def element_stress(terms, rows, onehot, scaled, sofar, store):
+    step = 32
+    pairs = onehot.shape[1] // (2 * LANES)
+    for pair in range(pairs):
+        operand = onehot[:, 2 * LANES * pair : 2 * LANES * (pair + 1)]
+        elem = dot(terms[0], operand)
+        for term in terms[1:]:
+            elem = elem + dot(term, operand)
+        for start in range(0, rows, step):
+            sums = [None] * COMPS if pair == 0 else [sofar[i, start : start + step, :] for i in range(COMPS)]
+            for half in range(2):
+                for c in range(3):
+                    x = elem[c * rows + start : c * rows + start + step, half * LANES : (half + 1) * LANES]
+                    x = x.reshape(step // 8, 8, LANES)
+                    for i in range(COMPS):
+                        term = scaled[24 * i + 3 * (2 * pair + half) + c] * x
+                        term = term.reshape(step, LANES)
+                        sums[i] = term if sums[i] is None else sums[i] + term
+            for i in range(COMPS):
+                if pair < pairs - 1:
+                    sofar[i, start : start + step, :] = sums[i]
+                else:
+                    store(i, start, sums[i])
+
+
+def free_stress(free_t, first, rows, onehot, scaled, sofar, out):
+    nodes = onehot.shape[0]
+    parts = [free_t[first : first + rows, c * nodes : (c + 1) * nodes] for c in range(3)]
+
+    def store(i, start, value):
+        out[i, start : start + value.shape[0], :] = value
+
+    element_stress(split_two(jnp.concatenate(parts, axis=0)), rows, onehot, scaled, sofar, store)
+
+
 def start_copies(pairs, sems):
     copies = [pltpu.make_async_copy(src, dst, sems.at[k]) for k, (src, dst) in enumerate(pairs)]
     for copy in copies:
@@ -86,7 +121,15 @@
     modulus,
     volume,
     coarse,
+    panel_nodes,
+    coupling,
+    force,
+    panel_inv,
     own,
+    panel_v,
+    coupling_v,
+    force_v,
+    inverse,
     select,
     onehot,
     face,
@@ -113,6 +156,10 @@
             (strain_disp, strain_v),
             (volume, volume_v),
             (coarse, own),
+            (panel_nodes, panel_v),
+            (coupling, coupling_v),
+            (force, force_v),
+            (panel_inv, inverse),
         ],
         sems,
     )
@@ -170,7 +217,7 @@
         while distance:
             turn += (bits & 1) * distance
             distance, bits = distance // 2, bits >> 1
-        for owner in (s, s + aside, s - aside):
+        for owner in (s, s - aside, s + aside):
             first = (owner * members + (g ^ turn)) * block_rows
             row = jnp.where((lane >= base) & (lane < base + block_rows), first - base + lane, row)
             base += block_rows
@@ -191,47 +238,36 @@
     copies[5].wait()
     for k in range(nodes // LANES):
         inverse_volume[k * LANES : (k + 1) * LANES, :] = column(1.0 / volume_v[k : k + 1, :])
-    copies[6].wait()
+    for copy in copies[6:]:
+        copy.wait()
 
 
 def prepare_panels(
-    panel_nodes,
-    coupling,
-    force,
-    panel_inv,
-    free_t,
-    corner_t,
     panel_v,
     coupling_v,
     force_v,
     inverse,
+    onehot,
+    scaled,
+    free_t,
+    corner_t,
+    stress_first,
+    stress_corner,
     loads,
     solved,
-    sems,
+    whole,
+    sofar,
 ):
-    copies = start_copies(
-        [
-            (panel_nodes, panel_v),
-            (coupling, coupling_v),
-            (force, force_v),
-            (panel_inv, inverse),
-        ],
-        sems,
-    )
     panels, panel_rows, _ = inverse.shape
     panel_size = panel_rows // 3
     nodes = force_v.shape[1]
     q = coupling_v.shape[0]
-
-    copies[0].wait()
-    copies[1].wait()
-    copies[2].wait()
     for c in range(3):
         loads[pl.ds(c, nodes, stride=3), :] = force_v[c].astype(F32)
-    corner_t[len(TERMS) * TERM :, :] = jnp.zeros((corner_t.shape[0] - len(TERMS) * TERM, 3 * nodes), BF16)
+    spare = corner_t.shape[0] - len(TERMS) * TERM
+    stress_corner[len(TERMS) * TERM :, :] = jnp.zeros((spare, stress_corner.shape[1]), BF16)
+    corner_t[len(TERMS) * TERM :, :] = jnp.zeros((spare, 3 * nodes), BF16)
     row_of = lax.broadcasted_iota(jnp.int32, (panel_rows, LANES), 0)
-    lane = lax.broadcasted_iota(jnp.int32, (panel_rows, LANES), 1)
-    copies[3].wait()
     for p in range(panels):
         start = p * panel_rows
         live = row_of < 3 * panel_v[0:1, p : p + 1]
@@ -248,9 +284,24 @@
             cols = slice(c * nodes + p * panel_size, c * nodes + (p + 1) * panel_size)
             free_t[:, cols] = solved[0, pl.ds(c, panel_size, stride=3), :].T
             value = solved[1, pl.ds(c, panel_size, stride=3), :].T[:TERM]
+            whole[:, cols] = value
             pieces = split_three(value)
             for k, (piece, _) in enumerate(TERMS):
                 corner_t[k * TERM : (k + 1) * TERM, cols] = pieces[piece]
+
+    def store(i, start, value):
+        pieces = split_three(value)
+        for k, (piece, _) in enumerate(TERMS):
+            stress_corner[k * TERM : (k + 1) * TERM, i * LANES : (i + 1) * LANES] = pieces[piece]
+
+    parts = jnp.concatenate([whole[:, c * nodes : (c + 1) * nodes] for c in range(3)], axis=0)
+    element_stress(split_two(parts), TERM, onehot, scaled, sofar, store)
+    free_stress(free_t, 0, stress_first.shape[1], onehot, scaled, sofar, stress_first)
+
+
+def stress_kernel(free_t, onehot, scaled, out, sofar):
+    rows = out.shape[1]
+    free_stress(free_t, free_t.shape[0] - rows, rows, onehot, scaled, sofar, out)
 
 
 def join_kernel(*refs):
@@ -264,20 +315,18 @@
 def solve_kernel(
     near,
     across,
-    free_t,
-    corner_t,
     select,
-    onehot,
+    stress_first,
+    stress_rest,
+    stress_corner,
     face,
-    scaled,
-    disp_t,
+    values,
     stress,
     sub_a,
     sub_b,
     grp_a,
     grp_b,
     terms,
-    sofar,
 ):
     rows = near.shape[0]
     terms[:, 2 * rows :, :] = jnp.zeros((3, terms.shape[1] - 2 * rows, terms.shape[2]), BF16)
@@ -285,38 +334,19 @@
         for t, value in enumerate(split_three(block[...])):
             terms[t, b * rows : (b + 1) * rows, :] = value
     picked = [dot(select[...], terms[t]) for t in range(3)]
-    values = [picked[term] for _, term in TERMS]
-    values += [jnp.zeros_like(picked[0])] * (corner_t.shape[0] // TERM - len(values))
+    ordered = [picked[term] for _, term in TERMS]
+    ordered += [jnp.zeros_like(picked[0])] * (stress_corner.shape[0] // TERM - len(ordered))
     per = LANES // TERM
-    values = [jnp.concatenate(values[k : k + per], axis=0).T for k in range(0, len(values), per)]
-    values = jnp.concatenate(values, axis=1).astype(BF16)
-    nodes = disp_t.shape[1]
-    for c in range(3):
-        cols = slice(c * nodes, (c + 1) * nodes)
-        part = free_t[:, cols] - dot(values, corner_t[:, cols])
-        disp_t[c * LANES : (c + 1) * LANES, :] = part.astype(BF16)
-
-    step = 32
-    pairs = onehot.shape[1] // (2 * LANES)
-    for pair in range(pairs):
-        elem_t = dot(disp_t[...], onehot[:, 2 * LANES * pair : 2 * LANES * (pair + 1)])
-        for start in range(0, LANES, step):
-            sums = [None] * COMPS if pair == 0 else [sofar[i, start : start + step, :] for i in range(COMPS)]
-            for half in range(2):
-                for c in range(3):
-                    x = elem_t[c * LANES + start : c * LANES + start + step, half * LANES : (half + 1) * LANES]
-                    x = x.reshape(step // 8, 8, LANES)
-                    for i in range(COMPS):
-                        term = scaled[24 * i + 3 * (2 * pair + half) + c] * x
-                        term = term.reshape(step, LANES)
-                        sums[i] = term if sums[i] is None else sums[i] + term
-            for i in range(COMPS):
-                if pair < pairs - 1:
-                    sofar[i, start : start + step, :] = sums[i]
-                else:
-                    high, low = split_two(sums[i])
-                    stress[i * LANES + start : i * LANES + start + step, 0:LANES] = high
-                    stress[i * LANES + start : i * LANES + start + step, LANES : 2 * LANES] = low
+    for k in range(0, len(ordered), per):
+        block = jnp.concatenate(ordered[k : k + per], axis=0).T.astype(BF16)
+        values[:, k * TERM : (k + per) * TERM] = block
+    moved = dot(values[...], stress_corner[...])
+    for i in range(COMPS):
+        cols = slice(i * LANES, (i + 1) * LANES)
+        free = jnp.concatenate([stress_first[i], stress_rest[i]], axis=0)
+        high, low = split_two(free - moved[:, cols])
+        stress[cols, 0:LANES] = high
+        stress[cols, LANES : 2 * LANES] = low
 
     rows = dot_nt(face[...], stress[...])
     for i in range(COMPS):
@@ -337,12 +367,14 @@
 
 
 def partial_kernel(
-    count, stress, disp_t, placing, grp_a, grp_b, partial, disp_out, received
+    count, stress, free_t, corner_t, values, placing, grp_a, grp_b, partial, disp_out, received
 ):
+    nodes = disp_out.shape[1]
     for c in range(3):
-        for k in range(0, disp_out.shape[1], LANES):
-            part = disp_t[c * LANES : (c + 1) * LANES, k : k + LANES].astype(F32).T
-            disp_out[c, k : k + LANES, :] = part.astype(BF16)
+        cols = slice(c * nodes, (c + 1) * nodes)
+        part = free_t[:, cols] - dot(values[...], corner_t[:, cols])
+        for k in range(0, nodes, LANES):
+            disp_out[c, k : k + LANES, :] = part[:, k : k + LANES].T.astype(BF16)
     split = NIG + NED
     for i in range(COMPS):
         low, high = grp_a[i], grp_b[i]
@@ -427,7 +459,7 @@
 def gather_near(coarse, own, ahead):
     beyond = exchange(coarse, "sub", 1)
     beside = exchange(coarse, "sub", 0)
-    parts = [own, beside, beyond]
+    parts = [own, beyond, beside]
     distance = lax.axis_size("grp") // 2
     while distance:
         rows = sum(x.shape[0] for x in parts)
@@ -468,11 +500,15 @@
     def lists(*refs):
         prepare_lists(coarse.shape[0], lax.axis_size("grp"), *refs)
 
-    own, select, onehot, face, scaled, count, placing, placing_last, inverse_volume = call(
+    own, *panels, select, onehot, face, scaled, count, placing, placing_last, inverse_volume = call(
         lists,
         "prepare_lists",
         (
             array(coarse.shape),
+            array(panel_nodes.shape, jnp.int32),
+            array((q, dofs), BF16),
+            array((3, nodes, cases), BF16),
+            array(panel_inv.shape, BF16),
             array((TERM, 3 * LANES), BF16),
             array((nodes, CORNERS * LANES), BF16),
             array((NIF, 2 * LANES), BF16),
@@ -482,7 +518,7 @@
             array((nodes, 2 * LANES), BF16),
             array((nodes, LANES)),
         ),
-        hbm(7),
+        hbm(11),
         (
             pltpu.VMEM((1, q), jnp.int32),
             pltpu.VMEM(connect.shape, jnp.int32),
@@ -491,7 +527,7 @@
             pltpu.VMEM((1, LANES), F32),
             pltpu.VMEM((nodes // LANES, LANES), F32),
             pltpu.VMEM((8, 2 * LANES), F32),
-            pltpu.SemaphoreType.DMA((7,)),
+            pltpu.SemaphoreType.DMA((11,)),
         ),
         flops=100000000,
         moved=4000000,
@@ -504,47 +540,59 @@
             modulus.reshape(1, -1),
             nodal_volume.reshape(-1, LANES),
             coarse,
+            panel_nodes,
+            coupling.T,
+            jnp.transpose(force, (1, 0, 2)),
+            panel_inv,
         )
     )
-    panel_rows = panel_inv.shape[1]
-    free_t, corner_t = call(
+    first = 32
+    free_t, corner_t, stress_first, stress_corner = call(
         prepare_panels,
         "prepare_panels",
-        (array((cases, dofs)), array((2 * LANES, dofs), BF16)),
-        hbm(4),
         (
-            pltpu.VMEM(panel_nodes.shape, jnp.int32),
-            pltpu.VMEM((q, dofs), BF16),
-            pltpu.VMEM((3, nodes, cases), BF16),
-            pltpu.VMEM(panel_inv.shape, BF16),
+            array((cases, dofs)),
+            array((2 * LANES, dofs), BF16),
+            array((COMPS, first, LANES)),
+            array((2 * LANES, COMPS * LANES), BF16),
+        ),
+        vmem(6),
+        (
             pltpu.VMEM((dofs, cases), F32),
-            pltpu.VMEM((2, panel_rows, LANES), F32),
-            pltpu.SemaphoreType.DMA((4,)),
+            pltpu.VMEM((2, panel_inv.shape[1], LANES), F32),
+            pltpu.VMEM((TERM, dofs), F32),
+            pltpu.VMEM((COMPS, max(first, TERM), LANES), F32),
         ),
         flops=400000000,
         moved=4000000,
-    )(*in_hbm(panel_nodes, coupling.T, jnp.transpose(force, (1, 0, 2)), panel_inv))
+    )(*panels, onehot, scaled)
+    (stress_rest,) = call(
+        stress_kernel,
+        "stress_of_loads",
+        (array((COMPS, cases - first, LANES)),),
+        vmem(3),
+        (pltpu.VMEM((COMPS, cases - first, LANES), F32),),
+        flops=400000000,
+        moved=4000000,
+    )(free_t, onehot, scaled)
 
     near = gather_near(coarse, own, [select, corner_t])
-    disp_t, stress, sub_a, sub_b, grp_a, grp_b = call(
+    values, stress, sub_a, sub_b, grp_a, grp_b = call(
         solve_kernel,
-        "solve_and_stress",
+        "stress_and_rows",
         (
-            array((3 * cases, nodes), BF16),
+            array((cases, 2 * LANES), BF16),
             array((COMPS * cases, 2 * LANES), BF16),
             array((COMPS, NIS, cases)),
             array((COMPS, NIS, cases)),
             array((COMPS, NIG + 2 * NED, cases)),
             array((COMPS, NIG + 2 * NED, cases)),
         ),
-        vmem(8),
-        (
-            pltpu.VMEM((3, 3 * LANES, cases), BF16),
-            pltpu.VMEM((COMPS, cases, LANES), F32),
-        ),
-        flops=1000000000,
-        moved=4000000,
-    )(*near, free_t, corner_t, select, onehot, face, scaled)
+        vmem(7),
+        (pltpu.VMEM((3, 3 * LANES, cases), BF16),),
+        flops=300000000,
+        moved=3000000,
+    )(*near, select, stress_first, stress_rest, stress_corner, face)
     from_sub_a = exchange(sub_a, "sub", 0)
     from_grp_a = exchange(grp_a, "grp", 0)
     from_grp_b = exchange(grp_b, "grp", 1)
@@ -561,11 +609,11 @@
         partial_kernel,
         "assemble_nodes",
         (array((COMPS, nodes, cases)), array((3, nodes, cases), BF16)),
-        vmem(6),
+        vmem(8),
         (pltpu.VMEM((2 * LANES, COMPS * cases), BF16),),
         flops=400000000,
         moved=2000000,
-    )(count, stress, disp_t, placing, from_grp_a, from_grp_b)
+    )(count, stress, free_t, corner_t, values, placing, from_grp_a, from_grp_b)
     (nodal,) = call(
         finish_kernel,
         "add_last",

time: 32 us -> 31 us (0.969)
  waiting for transfers between devices: 5.19 us -> 4.45 us
  Pallas kernels: 8.79 us -> 8.42 us
    ppermute x2, waiting for transfers between devices: 2.21 us -> 1.62 us  [gather_near(): parts = [block, lax.ppermute(block, 'grp', pairs)]]
    pallas_call x1, Pallas kernels: 2.46 us -> 1.94 us  [shards(): call(prepare_panels, 'prepare_panels', (array((cases, dofs)), array((2 *...]
    pallas_call x2 -> x3, Pallas kernels: 3.72 us -> 3.8 us  [the longest x1 1.93 us: shards(): call(lists, 'prepare_lists', (array(coarse.shape), array(panel_nodes.shap...]
  transfers between devices with their start and end apart: 10 -> 10, of which waited for: 6 -> 6; matrix products, arithmetic and copies ran while one was open for 0% -> 0% of each run, Pallas kernels for 18% -> 21%
where the time goes in v12:
time: 31 us; the launch traced here: 30.4 us
  starting transfers between devices  16.8 us (54%)
  Pallas kernels  8.42 us (27%)
  waiting for transfers between devices  4.45 us (14%)
  between operations  0.72 us (2%)
    ppermute x8, starting transfers between devices, exchange(): return lax.ppermute(block, axis, pairs)  16.3 us
    ppermute x8, waiting for transfers between devices, exchange(): return lax.ppermute(block, axis, pairs)  2.83 us
    pallas_call x1, Pallas kernels, shards(): call(prepare_panels, 'prepare_panels', (array((cases, dofs)), array((2 *...  1.94 us
    pallas_call x1, Pallas kernels, shards(): call(lists, 'prepare_lists', (array(coarse.shape), array(panel_nodes.shap...  1.93 us
    ppermute x2, waiting for transfers between devices, gather_near(): parts = [block, lax.ppermute(block, 'grp', pairs)]  1.62 us
    pallas_call x1, Pallas kernels, shards(): call(partial_kernel, 'assemble_nodes', (array((COMPS, nodes, cases)), arr...  1.46 us
    pallas_call x1, Pallas kernels, shards(): call(finish_kernel, 'add_last', (array((COMPS, nodes, cases), BF16),), vm...  1.21 us
    pallas_call x1, Pallas kernels, shards(): call(stress_kernel, 'stress_of_loads', (array((COMPS, cases - first, LANE...  1.11 us
  transfers between devices with their start and end apart: 10, of which 6 were waited for; matrix products, arithmetic and copies ran while one was open for 0% of the time, Pallas kernels for 21%

profile of v12, /device:TPU:10, one launch (start us, length us, event | category | flops | bytes accessed | tf_op | source)
XLA Modules:
  0.0 30.4 jit_solution(4818961486529662842)
XLA Ops:
  0.6 3.3 %collective-permute-start = (f32[24,128]{1,0:T(8,128)}, f32[24,128]{1,0:T(8,128)S(1)}, u32[]{:S(2)}, u32[]{:S(2)}) collective-permute-start(f32[24,128]{1,0:T(8,128)} %refs_6_.1), channel_id=1, source_target_pairs={{4,8},{8,4},{12,16},{16,12},{20,24},{24,20},{5,9},{9,5},{13,17},{1... | collective-permute-start | bytes 36872 | tf_op jit(solution)/shard_map/ppermute | solution.py:452
  4.0 1.7 %collective-permute-start.1 = (f32[24,128]{1,0:T(8,128)}, f32[24,128]{1,0:T(8,128)S(1)}, u32[]{:S(2)}, u32[]{:S(2)}) collective-permute-start(f32[24,128]{1,0:T(8,128)} %refs_6_.1), channel_id=1, source_target_pairs={{0,4},{4,0},{8,12},{12,8},{16,20},{20,16},{24,28},{28,24},{1,5},{5... | collective-permute-start | bytes 36872 | tf_op jit(solution)/shard_map/ppermute | solution.py:452
  5.7 1.9 %prepare_lists.1 = (f32[24,128]{1,0:T(8,128)S(1)}, s32[1,4]{1,0:T(1,128)S(1)}, bf16[24,1536]{1,0:T(8,128)(2,1)S(1)}, bf16[3,512,128]{2,1,0:T(8,128)(2,1)S(1)}, b...) custom-call(s32[1,24]{1,0:T(1,128)} %refs_0_.1, ...), custom_call_target="tpu_custom_call" | custom-call | flops 100000000 | bytes 4000000 | tf_op jit(solution)/shard_map/prepare_lists/pallas_call | solution.py:503
  7.6 0.0 collective-permute-done.refs_1_
  7.6 0.3 %collective-permute-done.1.refs_2_ = f32[24,128]{1,0:T(8,128)S(1)} collective-permute-done((f32[24,128]{1,0:T(8,128)}, f32[24,128]{1,0:T(8,128)S(1)}, u32[]{:S(2)}, u32[]{:S(2)}) %collective-permute-start.1) | collective-permute-done | bytes 12320 | tf_op jit(solution)/shard_map/ppermute | solution.py:452
  7.9 0.5 %collective-permute-start.2 = (f32[72,128]{1,0:T(8,128)S(1)}, f32[72,128]{1,0:T(8,128)S(1)}, u32[]{:S(2)}, u32[]{:S(2)}) collective-permute-start(f32[72,128]{1,0:T(8,128)S(1)} %join_blocks.2.refs_0_), channel_id=1, source_target_pairs={{0,2},{1,3},{2,0},{3,1},{4,6},{5,7},{6,4},{7,5},{8,10},{9,11},{10,... | collective-permute-start | bytes 110600 | tf_op jit(solution)/shard_map/ppermute | solution.py:478
  8.5 1.9 %prepare_panels.1 = (f32[128,1536]{1,0:T(8,128)S(1)}, bf16[256,1536]{1,0:T(8,128)(2,1)S(1)}, f32[6,32,128]{2,1,0:T(8,128)S(1)}, bf16[256,768]{1,0:T(8,128)(2,1)S(1)}) custom-call(s32[1,4]{1,0:T(1,128)S(1)} %get-tuple-element.32.panel_v, bf16[24,1536]{1,0:T(8,128)(2,1)S(1)} %get-tuple-element.33.coupling_v, ...), custom_call_target="tpu_custom_call" | custom-call | flops 400000000 | bytes 4000000 | tf_op jit(solution)/shard_map/prepare_panels/pallas_call | solution.py:550
  10.4 1.5 %collective-permute-done.2.refs_1_ = f32[72,128]{1,0:T(8,128)S(1)} collective-permute-done((f32[72,128]{1,0:T(8,128)S(1)}, f32[72,128]{1,0:T(8,128)S(1)}, u32[]{:S(2)}, u32[]{:S(2)}) %collective-permute-start.2) | collective-permute-done | bytes 36896 | tf_op jit(solution)/shard_map/ppermute | solution.py:478
  11.9 0.0 collective-permute-start.3
  11.9 1.1 %stress_of_loads.1.stress_rest = f32[6,96,128]{2,1,0:T(8,128)S(1)} custom-call(f32[128,1536]{1,0:T(8,128)S(1)} %get-tuple-element.40.free_t, bf16[512,1024]{1,0:T(8,128)(2,1)S(1)} %get-tuple-element.36.onehot, f32[144,8,128]{2,1,0:T(8,128)S(1)} %get-tuple-element.37.scaled), custom_call_target="tpu_custom_call" | custom-call | flops 400000000 | bytes 4000000 | tf_op jit(solution)/shard_map/stress_of_loads/pallas_call | solution.py:569
  13.0 0.1 collective-permute-done.3.across
  13.2 0.8 %stress_and_rows.1 = (bf16[128,256]{1,0:T(8,128)(2,1)S(1)}, bf16[768,256]{1,0:T(8,128)(2,1)S(1)}, f32[6,64,128]{2,1,0:T(8,128)S(1)}, f32[6,64,128]{2,1,0:T(8,128...) custom-call(f32[144,128]{1,0:T(8,128)S(1)} %join_blocks.3.near, ...), custom_call_target="tpu_custom_call" | custom-call | flops 300000000 | bytes 3000000 | tf_op jit(solution)/shard_map/stress_and_rows/pallas_call | solution.py:580
  13.9 0.4 %collective-permute-start.4 = (f32[6,48,128]{2,1,0:T(8,128)S(1)}, f32[6,48,128]{2,1,0:T(8,128)S(1)}, u32[]{:S(2)}, u32[]{:S(2)}) collective-permute-start(f32[6,48,128]{2,1,0:T(8,128)S(1)} %get-tuple-element.46.grp_a), channel_id=1, source_target_pairs={{0,1},{1,0},{2,3},{3,2},{4,5},{5,4},{6,7},{7,6},{8,9},{9,8},{10,11... | collective-permute-start | bytes 442376 | tf_op jit(solution)/shard_map/ppermute | solution.py:452
  14.4 2.2 %collective-permute-start.5 = (f32[6,48,128]{2,1,0:T(8,128)S(1)}, f32[6,48,128]{2,1,0:T(8,128)S(1)}, u32[]{:S(2)}, u32[]{:S(2)}) collective-permute-start(f32[6,48,128]{2,1,0:T(8,128)S(1)} %get-tuple-element.47.grp_b), channel_id=1, source_target_pairs={{1,2},{2,1},{5,6},{6,5},{9,10},{10,9},{13,14},{14,13},{17,18},{18,... | collective-permute-start | bytes 442376 | tf_op jit(solution)/shard_map/ppermute | solution.py:452
  16.6 1.7 %collective-permute-start.6 = (f32[6,64,128]{2,1,0:T(8,128)S(1)}, f32[6,64,128]{2,1,0:T(8,128)S(1)}, u32[]{:S(2)}, u32[]{:S(2)}) collective-permute-start(f32[6,64,128]{2,1,0:T(8,128)S(1)} %get-tuple-element.52), channel_id=1, source_target_pairs={{0,4},{4,0},{8,12},{12,8},{16,20},{20,16},{24,28},{28,24},{1,5},{5... | collective-permute-start | bytes 589832 | tf_op jit(solution)/shard_map/ppermute | solution.py:452
  18.2 1.9 %collective-permute-start.7 = (f32[6,64,128]{2,1,0:T(8,128)S(1)}, f32[6,64,128]{2,1,0:T(8,128)S(1)}, u32[]{:S(2)}, u32[]{:S(2)}) collective-permute-start(f32[6,64,128]{2,1,0:T(8,128)S(1)} %get-tuple-element.53), channel_id=1, source_target_pairs={{4,8},{8,4},{12,16},{16,12},{20,24},{24,20},{5,9},{9,5},{13,17},{1... | collective-permute-start | bytes 589832 | tf_op jit(solution)/shard_map/ppermute | solution.py:452
  20.2 0.0 collective-permute-done.4.grp_a.from_a
  20.2 0.6 %collective-permute-done.5.grp_b.from_b = f32[6,48,128]{2,1,0:T(8,128)S(1)} collective-permute-done((f32[6,48,128]{2,1,0:T(8,128)S(1)}, f32[6,48,128]{2,1,0:T(8,128)S(1)}, u32[]{:S(2)}, u32[]{:S(2)}) %collective-permute-start.5) | collective-permute-done | bytes 147488 | tf_op jit(solution)/shard_map/ppermute | solution.py:452
  20.8 4.2 %collective-permute-start.8 = (f32[6,16,128]{2,1,0:T(8,128)S(1)}, f32[6,16,128]{2,1,0:T(8,128)S(1)}, u32[]{:S(2)}, u32[]{:S(2)}) collective-permute-start(f32[6,16,128]{2,1,0:T(8,128)S(1)} %get-tuple-element.54), channel_id=1, source_target_pairs={{4,8},{8,4},{12,16},{16,12},{20,24},{24,20},{5,9},{9,5},{13,17},{1... | collective-permute-start | bytes 147464 | tf_op jit(solution)/shard_map/ppermute | solution.py:452
  25.0 0.8 %collective-permute-start.9 = (f32[6,16,128]{2,1,0:T(8,128)S(1)}, f32[6,16,128]{2,1,0:T(8,128)S(1)}, u32[]{:S(2)}, u32[]{:S(2)}) collective-permute-start(f32[6,16,128]{2,1,0:T(8,128)S(1)} %get-tuple-element.55), channel_id=1, source_target_pairs={{0,4},{4,0},{8,12},{12,8},{16,20},{20,16},{24,28},{28,24},{1,5},{5... | collective-permute-start | bytes 147464 | tf_op jit(solution)/shard_map/ppermute | solution.py:452
  25.9 1.5 %assemble_nodes.1 = (f32[6,512,128]{2,1,0:T(8,128)S(1)}, bf16[3,512,128]{2,1,0:T(8,128)(2,1)}) custom-call(bf16[512,256]{1,0:T(8,128)(2,1)S(1)} %get-tuple-element.29.count, bf16[768,256]{1,0:T(8,128)(2,1)S(1)} %get-tuple-element.43.stress, f32[128,1536]{1,0:T(8,128)S(1)} %get-tuple-element.40.free_t, ...), custom_call_target="tpu_custom_call" | custom-call | flops 400000000 | bytes 2000000 | tf_op jit(solution)/shard_map/assemble_nodes/pallas_call | solution.py:608
  27.3 0.0 collective-permute-done.6.sub_a
  27.3 0.0 collective-permute-done.7.sub_b
  27.3 0.5 %collective-permute-done.8.edge_b = f32[6,16,128]{2,1,0:T(8,128)S(1)} collective-permute-done((f32[6,16,128]{2,1,0:T(8,128)S(1)}, f32[6,16,128]{2,1,0:T(8,128)S(1)}, u32[]{:S(2)}, u32[]{:S(2)}) %collective-permute-start.8) | collective-permute-done | bytes 49184 | tf_op jit(solution)/shard_map/ppermute | solution.py:452
  27.8 1.4 %collective-permute-done.9.edge_a = f32[6,16,128]{2,1,0:T(8,128)S(1)} collective-permute-done((f32[6,16,128]{2,1,0:T(8,128)S(1)}, f32[6,16,128]{2,1,0:T(8,128)S(1)}, u32[]{:S(2)}, u32[]{:S(2)}) %collective-permute-start.9) | collective-permute-done | bytes 49184 | tf_op jit(solution)/shard_map/ppermute | solution.py:452
  29.2 1.2 %add_last.1 = bf16[6,512,128]{2,1,0:T(8,128)(2,1)} custom-call(bf16[512,256]{1,0:T(8,128)(2,1)S(1)} %get-tuple-element.49.placing, f32[6,512,128]{2,1,0:T(8,128)S(1)} %get-tuple-element.50.partial, f32[512,128]{1,0:T(8,128)S(1)} %get-tuple-element.51.inverse_volume, f32[6,64,128]{2,1,0:T(8,128)S(1)} %collective-permute-done.6.sub_a, ...), custom_call_target="tpu_custom_call" | custom-call | flops 400000000 | bytes 3000000 | tf_op jit(solution)/shard_map/add_last/pallas_call | solution.py:617
  (3 shorter events, 0.0 us)
Async XLA Ops:
  0.6 7.0 %collective-permute-start = (f32[24,128]{1,0:T(8,128)}, f32[24,128]{1,0:T(8,128)S(1)}, u32[]{:S(2)}, u32[]{:S(2)}) collective-permute-start(f32[24,128]{1,0:T(8,128)} %refs_6_.1), channel_id=1, source_target_pairs={{4,8},{8,4},{12,16},{16,12},{20,24},{24,20},{5,9},{9,5},{13,17},{1... | collective-permute-start | bytes 36872 | tf_op jit(solution)/shard_map/ppermute | solution.py:452
  4.0 4.0 %collective-permute-start.1 = (f32[24,128]{1,0:T(8,128)}, f32[24,128]{1,0:T(8,128)S(1)}, u32[]{:S(2)}, u32[]{:S(2)}) collective-permute-start(f32[24,128]{1,0:T(8,128)} %refs_6_.1), channel_id=1, source_target_pairs={{0,4},{4,0},{8,12},{12,8},{16,20},{20,16},{24,28},{28,24},{1,5},{5... | collective-permute-start | bytes 36872 | tf_op jit(solution)/shard_map/ppermute | solution.py:452
  7.9 4.0 %collective-permute-start.2 = (f32[72,128]{1,0:T(8,128)S(1)}, f32[72,128]{1,0:T(8,128)S(1)}, u32[]{:S(2)}, u32[]{:S(2)}) collective-permute-start(f32[72,128]{1,0:T(8,128)S(1)} %join_blocks.2.refs_0_), channel_id=1, source_target_pairs={{0,2},{1,3},{2,0},{3,1},{4,6},{5,7},{6,4},{7,5},{8,10},{9,11},{10,... | collective-permute-start | bytes 110600 | tf_op jit(solution)/shard_map/ppermute | solution.py:478
  11.9 1.3 %collective-permute-start.3 = (f32[144,128]{1,0:T(8,128)S(1)}, f32[144,128]{1,0:T(8,128)S(1)}, u32[]{:S(2)}, u32[]{:S(2)}) collective-permute-start(f32[144,128]{1,0:T(8,128)S(1)} %join_blocks.3.near), channel_id=1, source_target_pairs={{0,1},{1,0},{2,3},{3,2},{4,5},{5,4},{6,7},{7,6},{8,9},{9,8},{10,11... | collective-permute-start | bytes 221192 | tf_op jit(solution)/shard_map/ppermute | solution.py:478
  13.9 6.3 %collective-permute-start.4 = (f32[6,48,128]{2,1,0:T(8,128)S(1)}, f32[6,48,128]{2,1,0:T(8,128)S(1)}, u32[]{:S(2)}, u32[]{:S(2)}) collective-permute-start(f32[6,48,128]{2,1,0:T(8,128)S(1)} %get-tuple-element.46.grp_a), channel_id=1, source_target_pairs={{0,1},{1,0},{2,3},{3,2},{4,5},{5,4},{6,7},{7,6},{8,9},{9,8},{10,11... | collective-permute-start | bytes 442376 | tf_op jit(solution)/shard_map/ppermute | solution.py:452
  14.4 6.5 %collective-permute-start.5 = (f32[6,48,128]{2,1,0:T(8,128)S(1)}, f32[6,48,128]{2,1,0:T(8,128)S(1)}, u32[]{:S(2)}, u32[]{:S(2)}) collective-permute-start(f32[6,48,128]{2,1,0:T(8,128)S(1)} %get-tuple-element.47.grp_b), channel_id=1, source_target_pairs={{1,2},{2,1},{5,6},{6,5},{9,10},{10,9},{13,14},{14,13},{17,18},{18,... | collective-permute-start | bytes 442376 | tf_op jit(solution)/shard_map/ppermute | solution.py:452
  16.6 10.8 %collective-permute-start.6 = (f32[6,64,128]{2,1,0:T(8,128)S(1)}, f32[6,64,128]{2,1,0:T(8,128)S(1)}, u32[]{:S(2)}, u32[]{:S(2)}) collective-permute-start(f32[6,64,128]{2,1,0:T(8,128)S(1)} %get-tuple-element.52), channel_id=1, source_target_pairs={{0,4},{4,0},{8,12},{12,8},{16,20},{20,16},{24,28},{28,24},{1,5},{5... | collective-permute-start | bytes 589832 | tf_op jit(solution)/shard_map/ppermute | solution.py:452
  18.2 9.1 %collective-permute-start.7 = (f32[6,64,128]{2,1,0:T(8,128)S(1)}, f32[6,64,128]{2,1,0:T(8,128)S(1)}, u32[]{:S(2)}, u32[]{:S(2)}) collective-permute-start(f32[6,64,128]{2,1,0:T(8,128)S(1)} %get-tuple-element.53), channel_id=1, source_target_pairs={{4,8},{8,4},{12,16},{16,12},{20,24},{24,20},{5,9},{9,5},{13,17},{1... | collective-permute-start | bytes 589832 | tf_op jit(solution)/shard_map/ppermute | solution.py:452
  20.8 6.9 %collective-permute-start.8 = (f32[6,16,128]{2,1,0:T(8,128)S(1)}, f32[6,16,128]{2,1,0:T(8,128)S(1)}, u32[]{:S(2)}, u32[]{:S(2)}) collective-permute-start(f32[6,16,128]{2,1,0:T(8,128)S(1)} %get-tuple-element.54), channel_id=1, source_target_pairs={{4,8},{8,4},{12,16},{16,12},{20,24},{24,20},{5,9},{9,5},{13,17},{1... | collective-permute-start | bytes 147464 | tf_op jit(solution)/shard_map/ppermute | solution.py:452
  25.0 4.2 %collective-permute-start.9 = (f32[6,16,128]{2,1,0:T(8,128)S(1)}, f32[6,16,128]{2,1,0:T(8,128)S(1)}, u32[]{:S(2)}, u32[]{:S(2)}) collective-permute-start(f32[6,16,128]{2,1,0:T(8,128)S(1)} %get-tuple-element.55), channel_id=1, source_target_pairs={{0,4},{4,0},{8,12},{12,8},{16,20},{20,16},{24,28},{28,24},{1,5},{5... | collective-permute-start | bytes 147464 | tf_op jit(solution)/shard_map/ppermute | solution.py:452

commit v13 on v12

--- a/solution.py
+++ b/solution.py
@@ -182,17 +182,33 @@
     ids[0:1, 0:NIF] = interface_v[...].astype(F32)
     order_lists(ids)
     lane = lax.broadcasted_iota(jnp.int32, (8, LANES), 1)
-    edges = pltpu.roll(ids[:, LANES:], LANES - NIS, 1)
-    again = pltpu.roll(ids[:, :LANES], LANES - NIS + 4 * NED, 1)
-    last = jnp.where(lane < 4 * NED, edges, again)
-    last = jnp.where(lane < LATE, last, pltpu.roll(edges, LATE, 1))
-    for row, target in ((ids[0:1, LANES:], 0), (ids[0:1, :LANES], 1), (last[0:1], 2)):
-        hit = jnp.where(row.astype(jnp.int32) == node_of, 1.0, 0.0).astype(BF16)
-        if target == 0:
-            placing[:, :LANES] = hit
-            placing[:, LANES:] = hit
-        else:
-            placing_last[:, (target - 1) * LANES : target * LANES] = hit
+    faces, others = ids[:, :LANES], ids[:, LANES:]
+    turned = pltpu.roll(others, NIS, 1)
+    lists = (
+        (placing, 0, jnp.where(lane < NIS, faces, turned)),
+        (placing, 1, jnp.where(lane < 4 * NED, turned, pltpu.roll(others, 4 * NED, 1))),
+        (
+            placing_last,
+            0,
+            jnp.where(
+                lane < NIS,
+                pltpu.roll(faces, NIS, 1),
+                jnp.where(lane < LATE, others, pltpu.roll(faces, 4 * NED, 1)),
+            ),
+        ),
+        (
+            placing_last,
+            1,
+            jnp.where(
+                lane < 4 * NED,
+                pltpu.roll(faces, 4 * NED, 1),
+                jnp.where(lane < 8 * NED, pltpu.roll(others, LATE, 1), -1.0),
+            ),
+        ),
+    )
+    for target, half, row in lists:
+        hit = jnp.where(row[0:1].astype(jnp.int32) == node_of, 1.0, 0.0).astype(BF16)
+        target[:, half * LANES : (half + 1) * LANES] = hit
     connect_f = connect_v[...].astype(F32)
     for half in range(2):
         id_col = column(ids[0:1, half * LANES : (half + 1) * LANES])
@@ -367,7 +383,7 @@
 
 
 def partial_kernel(
-    count, stress, free_t, corner_t, values, placing, grp_a, grp_b, partial, disp_out, received
+    count, stress, free_t, corner_t, values, placing, sub_a, grp_a, grp_b, partial, disp_out, received
 ):
     nodes = disp_out.shape[1]
     for c in range(3):
@@ -379,10 +395,11 @@
     for i in range(COMPS):
         low, high = grp_a[i], grp_b[i]
         rows = [low[:NIG], high[:NIG], low[NIG:split], high[NIG:split], low[split:], high[split:]]
-        rows.append(jnp.zeros((2 * LANES - NIF, LANES), F32))
         first, second = split_two(jnp.concatenate(rows, axis=0))
-        received[:LANES, i * LANES : (i + 1) * LANES] = first
-        received[LANES:, i * LANES : (i + 1) * LANES] = second
+        cols = slice(i * LANES, (i + 1) * LANES)
+        received[:NIS, cols] = sub_a[i].astype(BF16)
+        received[NIS : NIS + LATE, cols] = first
+        received[NIS + LATE :, cols] = second
     for i in range(0, COMPS, 2):
         cols = slice(i * LANES, (i + 2) * LANES)
         own = dot_nt(count[...], stress[cols, :])
@@ -392,15 +409,15 @@
 
 
 def finish_kernel(
-    placing, partial, inverse_volume, sub_a, sub_b, edge_b, edge_a, out, received, nodal, sems
+    placing, partial, inverse_volume, sub_b, edge_b, edge_a, out, received, nodal, sems
 ):
+    received[2 * LATE :, :] = jnp.zeros((received.shape[0] - 2 * LATE, received.shape[1]), BF16)
     for i in range(COMPS):
         cols = slice(i * LANES, (i + 1) * LANES)
         late = jnp.concatenate([sub_b[i], edge_a[i], edge_b[i]], axis=0)
         first, second = split_two(late)
-        received[:NIS, cols] = sub_a[i].astype(BF16)
-        received[NIS : NIS + LATE, cols] = first
-        received[NIS + LATE :, cols] = second
+        received[:LATE, cols] = first
+        received[LATE : 2 * LATE, cols] = second
     scale = inverse_volume[...]
     copies = []
     for i in range(0, COMPS, 2):
@@ -546,7 +563,7 @@
             panel_inv,
         )
     )
-    first = 32
+    first = 64
     free_t, corner_t, stress_first, stress_corner = call(
         prepare_panels,
         "prepare_panels",
@@ -609,25 +626,25 @@
         partial_kernel,
         "assemble_nodes",
         (array((COMPS, nodes, cases)), array((3, nodes, cases), BF16)),
-        vmem(8),
-        (pltpu.VMEM((2 * LANES, COMPS * cases), BF16),),
+        vmem(9),
+        (pltpu.VMEM((NIS + 2 * LATE, COMPS * cases), BF16),),
         flops=400000000,
         moved=2000000,
-    )(count, stress, free_t, corner_t, values, placing, from_grp_a, from_grp_b)
+    )(count, stress, free_t, corner_t, values, placing, from_sub_a, from_grp_a, from_grp_b)
     (nodal,) = call(
         finish_kernel,
         "add_last",
         (array((COMPS, nodes, cases), BF16),),
-        vmem(7),
-        (
-            pltpu.VMEM((NIS + 2 * LATE, COMPS * cases), BF16),
+        vmem(6),
+        (
+            pltpu.VMEM((2 * LANES, COMPS * cases), BF16),
             pltpu.VMEM((COMPS, nodes, cases), BF16),
             pltpu.SemaphoreType.DMA((COMPS // 2,)),
         ),
         flops=400000000,
         moved=3000000,
         out_specs=hbm(1),
-    )(placing_last, partial, inverse_volume, from_sub_a, from_sub_b, from_edge_b, from_edge_a)
+    )(placing_last, partial, inverse_volume, from_sub_b, from_edge_b, from_edge_a)
     return jnp.transpose(disp, (1, 0, 2)), jnp.transpose(nodal, (1, 0, 2))
 
 

time: 31 us -> 31.3 us (level)
  waiting for transfers between devices: 4.45 us -> 4.81 us
where the time goes in v13:
time: 31.3 us; the launch traced here: 30.7 us
  starting transfers between devices  16.8 us (54%)
  Pallas kernels  8.38 us (27%)
  waiting for transfers between devices  4.81 us (15%)
  between operations  0.72 us (2%)
    ppermute x8, starting transfers between devices, exchange(): return lax.ppermute(block, axis, pairs)  16.3 us
    ppermute x8, waiting for transfers between devices, exchange(): return lax.ppermute(block, axis, pairs)  3.12 us
    pallas_call x1, Pallas kernels, shards(): call(prepare_panels, 'prepare_panels', (array((cases, dofs)), array((2 *...  2.16 us
    pallas_call x1, Pallas kernels, shards(): call(lists, 'prepare_lists', (array(coarse.shape), array(panel_nodes.shap...  1.96 us
    ppermute x2, waiting for transfers between devices, gather_near(): parts = [block, lax.ppermute(block, 'grp', pairs)]  1.69 us
    pallas_call x1, Pallas kernels, shards(): call(partial_kernel, 'assemble_nodes', (array((COMPS, nodes, cases)), arr...  1.46 us
    pallas_call x1, Pallas kernels, shards(): call(finish_kernel, 'add_last', (array((COMPS, nodes, cases), BF16),), vm...  1.2 us
    pallas_call x1, Pallas kernels, shards(): call(stress_kernel, 'stress_of_loads', (array((COMPS, cases - first, LANE...  0.81 us
  transfers between devices with their start and end apart: 10, of which 6 were waited for; matrix products, arithmetic and copies ran while one was open for 0% of the time, Pallas kernels for 21%

profile of v13, /device:TPU:10, one launch (start us, length us, event | category | flops | bytes accessed | tf_op | source)
XLA Modules:
  0.0 30.7 jit_solution(5156355643845290886)
XLA Ops:
  0.6 3.3 %collective-permute-start = (f32[24,128]{1,0:T(8,128)}, f32[24,128]{1,0:T(8,128)S(1)}, u32[]{:S(2)}, u32[]{:S(2)}) collective-permute-start(f32[24,128]{1,0:T(8,128)} %refs_6_.1), channel_id=1, source_target_pairs={{4,8},{8,4},{12,16},{16,12},{20,24},{24,20},{5,9},{9,5},{13,17},{1... | collective-permute-start | bytes 36872 | tf_op jit(solution)/shard_map/ppermute | solution.py:469
  4.0 1.7 %collective-permute-start.1 = (f32[24,128]{1,0:T(8,128)}, f32[24,128]{1,0:T(8,128)S(1)}, u32[]{:S(2)}, u32[]{:S(2)}) collective-permute-start(f32[24,128]{1,0:T(8,128)} %refs_6_.1), channel_id=1, source_target_pairs={{0,4},{4,0},{8,12},{12,8},{16,20},{20,16},{24,28},{28,24},{1,5},{5... | collective-permute-start | bytes 36872 | tf_op jit(solution)/shard_map/ppermute | solution.py:469
  5.7 2.0 %prepare_lists.1 = (f32[24,128]{1,0:T(8,128)S(1)}, s32[1,4]{1,0:T(1,128)S(1)}, bf16[24,1536]{1,0:T(8,128)(2,1)S(1)}, bf16[3,512,128]{2,1,0:T(8,128)(2,1)S(1)}, b...) custom-call(s32[1,24]{1,0:T(1,128)} %refs_0_.1, ...), custom_call_target="tpu_custom_call" | custom-call | flops 100000000 | bytes 4000000 | tf_op jit(solution)/shard_map/prepare_lists/pallas_call | solution.py:520
  7.6 0.0 collective-permute-done.refs_1_
  7.6 0.3 collective-permute-done.1.refs_2_
  7.9 0.5 %collective-permute-start.2 = (f32[72,128]{1,0:T(8,128)S(1)}, f32[72,128]{1,0:T(8,128)S(1)}, u32[]{:S(2)}, u32[]{:S(2)}) collective-permute-start(f32[72,128]{1,0:T(8,128)S(1)} %join_blocks.2.refs_0_), channel_id=1, source_target_pairs={{0,2},{1,3},{2,0},{3,1},{4,6},{5,7},{6,4},{7,5},{8,10},{9,11},{10,... | collective-permute-start | bytes 110600 | tf_op jit(solution)/shard_map/ppermute | solution.py:495
  8.5 2.2 %prepare_panels.1 = (f32[128,1536]{1,0:T(8,128)S(1)}, bf16[256,1536]{1,0:T(8,128)(2,1)S(1)}, f32[6,64,128]{2,1,0:T(8,128)S(1)}, bf16[256,768]{1,0:T(8,128)(2,1)S(1)}) custom-call(s32[1,4]{1,0:T(1,128)S(1)} %get-tuple-element.32.panel_v, bf16[24,1536]{1,0:T(8,128)(2,1)S(1)} %get-tuple-element.33.coupling_v, ...), custom_call_target="tpu_custom_call" | custom-call | flops 400000000 | bytes 4000000 | tf_op jit(solution)/shard_map/prepare_panels/pallas_call | solution.py:567
  10.6 1.3 %collective-permute-done.2.refs_1_ = f32[72,128]{1,0:T(8,128)S(1)} collective-permute-done((f32[72,128]{1,0:T(8,128)S(1)}, f32[72,128]{1,0:T(8,128)S(1)}, u32[]{:S(2)}, u32[]{:S(2)}) %collective-permute-start.2) | collective-permute-done | bytes 36896 | tf_op jit(solution)/shard_map/ppermute | solution.py:495
  11.9 0.0 collective-permute-start.3
  11.9 0.8 %stress_of_loads.1.stress_rest = f32[6,64,128]{2,1,0:T(8,128)S(1)} custom-call(f32[128,1536]{1,0:T(8,128)S(1)} %get-tuple-element.40.free_t, bf16[512,1024]{1,0:T(8,128)(2,1)S(1)} %get-tuple-element.36.onehot, f32[144,8,128]{2,1,0:T(8,128)S(1)} %get-tuple-element.37.scaled), custom_call_target="tpu_custom_call" | custom-call | flops 400000000 | bytes 4000000 | tf_op jit(solution)/shard_map/stress_of_loads/pallas_call | solution.py:586
  12.7 0.4 %collective-permute-done.3.across = f32[144,128]{1,0:T(8,128)S(1)} collective-permute-done((f32[144,128]{1,0:T(8,128)S(1)}, f32[144,128]{1,0:T(8,128)S(1)}, u32[]{:S(2)}, u32[]{:S(2)}) %collective-permute-start.3) | collective-permute-done | bytes 73760 | tf_op jit(solution)/shard_map/ppermute | solution.py:495
  13.2 0.8 %stress_and_rows.1 = (bf16[128,256]{1,0:T(8,128)(2,1)S(1)}, bf16[768,256]{1,0:T(8,128)(2,1)S(1)}, f32[6,64,128]{2,1,0:T(8,128)S(1)}, f32[6,64,128]{2,1,0:T(8,128...) custom-call(f32[144,128]{1,0:T(8,128)S(1)} %join_blocks.3.near, ...), custom_call_target="tpu_custom_call" | custom-call | flops 300000000 | bytes 3000000 | tf_op jit(solution)/shard_map/stress_and_rows/pallas_call | solution.py:597
  13.9 1.7 %collective-permute-start.4 = (f32[6,64,128]{2,1,0:T(8,128)S(1)}, f32[6,64,128]{2,1,0:T(8,128)S(1)}, u32[]{:S(2)}, u32[]{:S(2)}) collective-permute-start(f32[6,64,128]{2,1,0:T(8,128)S(1)} %get-tuple-element.46), channel_id=1, source_target_pairs={{0,4},{4,0},{8,12},{12,8},{16,20},{20,16},{24,28},{28,24},{1,5},{5... | collective-permute-start | bytes 589832 | tf_op jit(solution)/shard_map/ppermute | solution.py:469
  15.6 0.0 collective-permute-start.5
  15.6 2.5 %collective-permute-start.6 = (f32[6,48,128]{2,1,0:T(8,128)S(1)}, f32[6,48,128]{2,1,0:T(8,128)S(1)}, u32[]{:S(2)}, u32[]{:S(2)}) collective-permute-start(f32[6,48,128]{2,1,0:T(8,128)S(1)} %get-tuple-element.48.grp_b), channel_id=1, source_target_pairs={{1,2},{2,1},{5,6},{6,5},{9,10},{10,9},{13,14},{14,13},{17,18},{18,... | collective-permute-start | bytes 442376 | tf_op jit(solution)/shard_map/ppermute | solution.py:469
  18.2 2.0 %collective-permute-start.7 = (f32[6,64,128]{2,1,0:T(8,128)S(1)}, f32[6,64,128]{2,1,0:T(8,128)S(1)}, u32[]{:S(2)}, u32[]{:S(2)}) collective-permute-start(f32[6,64,128]{2,1,0:T(8,128)S(1)} %get-tuple-element.53), channel_id=1, source_target_pairs={{4,8},{8,4},{12,16},{16,12},{20,24},{24,20},{5,9},{9,5},{13,17},{1... | collective-permute-start | bytes 589832 | tf_op jit(solution)/shard_map/ppermute | solution.py:469
  20.2 0.0 collective-permute-done.5.grp_a.from_a
  20.2 1.9 %collective-permute-done.6.grp_b.from_b = f32[6,48,128]{2,1,0:T(8,128)S(1)} collective-permute-done((f32[6,48,128]{2,1,0:T(8,128)S(1)}, f32[6,48,128]{2,1,0:T(8,128)S(1)}, u32[]{:S(2)}, u32[]{:S(2)}) %collective-permute-start.6) | collective-permute-done | bytes 147488 | tf_op jit(solution)/shard_map/ppermute | solution.py:469
  22.1 2.9 %collective-permute-start.8 = (f32[6,16,128]{2,1,0:T(8,128)S(1)}, f32[6,16,128]{2,1,0:T(8,128)S(1)}, u32[]{:S(2)}, u32[]{:S(2)}) collective-permute-start(f32[6,16,128]{2,1,0:T(8,128)S(1)} %get-tuple-element.54), channel_id=1, source_target_pairs={{4,8},{8,4},{12,16},{16,12},{20,24},{24,20},{5,9},{9,5},{13,17},{1... | collective-permute-start | bytes 147464 | tf_op jit(solution)/shard_map/ppermute | solution.py:469
  25.0 2.1 %collective-permute-start.9 = (f32[6,16,128]{2,1,0:T(8,128)S(1)}, f32[6,16,128]{2,1,0:T(8,128)S(1)}, u32[]{:S(2)}, u32[]{:S(2)}) collective-permute-start(f32[6,16,128]{2,1,0:T(8,128)S(1)} %get-tuple-element.55), channel_id=1, source_target_pairs={{0,4},{4,0},{8,12},{12,8},{16,20},{20,16},{24,28},{28,24},{1,5},{5... | collective-permute-start | bytes 147464 | tf_op jit(solution)/shard_map/ppermute | solution.py:469
  27.1 0.0 collective-permute-done.4.sub_a
  27.1 1.5 %assemble_nodes.1 = (f32[6,512,128]{2,1,0:T(8,128)S(1)}, bf16[3,512,128]{2,1,0:T(8,128)(2,1)}) custom-call(bf16[512,256]{1,0:T(8,128)(2,1)S(1)} %get-tuple-element.29.count, bf16[768,256]{1,0:T(8,128)(2,1)S(1)} %get-tuple-element.43.stress, f32[128,1536]{1,0:T(8,128)S(1)} %get-tuple-element.40.free_t, ...), custom_call_target="tpu_custom_call" | custom-call | flops 400000000 | bytes 2000000 | tf_op jit(solution)/shard_map/assemble_nodes/pallas_call | solution.py:625
  28.6 0.0 collective-permute-done.7.sub_b
  28.6 0.4 %collective-permute-done.8.edge_b = f32[6,16,128]{2,1,0:T(8,128)S(1)} collective-permute-done((f32[6,16,128]{2,1,0:T(8,128)S(1)}, f32[6,16,128]{2,1,0:T(8,128)S(1)}, u32[]{:S(2)}, u32[]{:S(2)}) %collective-permute-start.8) | collective-permute-done | bytes 49184 | tf_op jit(solution)/shard_map/ppermute | solution.py:469
  29.0 0.5 %collective-permute-done.9.edge_a = f32[6,16,128]{2,1,0:T(8,128)S(1)} collective-permute-done((f32[6,16,128]{2,1,0:T(8,128)S(1)}, f32[6,16,128]{2,1,0:T(8,128)S(1)}, u32[]{:S(2)}, u32[]{:S(2)}) %collective-permute-start.9) | collective-permute-done | bytes 49184 | tf_op jit(solution)/shard_map/ppermute | solution.py:469
  29.5 1.2 %add_last.1 = bf16[6,512,128]{2,1,0:T(8,128)(2,1)} custom-call(bf16[512,256]{1,0:T(8,128)(2,1)S(1)} %get-tuple-element.50.placing, f32[6,512,128]{2,1,0:T(8,128)S(1)} %get-tuple-element.51.partial, f32[512,128]{1,0:T(8,128)S(1)} %get-tuple-element.52.inverse_volume, f32[6,64,128]{2,1,0:T(8,128)S(1)} %collective-permute-done.7.sub_b, ...), custom_call_target="tpu_custom_call" | custom-call | flops 400000000 | bytes 3000000 | tf_op jit(solution)/shard_map/add_last/pallas_call | solution.py:634
  (3 shorter events, 0.0 us)
Async XLA Ops:
  0.6 7.0 %collective-permute-start = (f32[24,128]{1,0:T(8,128)}, f32[24,128]{1,0:T(8,128)S(1)}, u32[]{:S(2)}, u32[]{:S(2)}) collective-permute-start(f32[24,128]{1,0:T(8,128)} %refs_6_.1), channel_id=1, source_target_pairs={{4,8},{8,4},{12,16},{16,12},{20,24},{24,20},{5,9},{9,5},{13,17},{1... | collective-permute-start | bytes 36872 | tf_op jit(solution)/shard_map/ppermute | solution.py:469
  4.0 4.0 %collective-permute-start.1 = (f32[24,128]{1,0:T(8,128)}, f32[24,128]{1,0:T(8,128)S(1)}, u32[]{:S(2)}, u32[]{:S(2)}) collective-permute-start(f32[24,128]{1,0:T(8,128)} %refs_6_.1), channel_id=1, source_target_pairs={{0,4},{4,0},{8,12},{12,8},{16,20},{20,16},{24,28},{28,24},{1,5},{5... | collective-permute-start | bytes 36872 | tf_op jit(solution)/shard_map/ppermute | solution.py:469
  7.9 4.0 %collective-permute-start.2 = (f32[72,128]{1,0:T(8,128)S(1)}, f32[72,128]{1,0:T(8,128)S(1)}, u32[]{:S(2)}, u32[]{:S(2)}) collective-permute-start(f32[72,128]{1,0:T(8,128)S(1)} %join_blocks.2.refs_0_), channel_id=1, source_target_pairs={{0,2},{1,3},{2,0},{3,1},{4,6},{5,7},{6,4},{7,5},{8,10},{9,11},{10,... | collective-permute-start | bytes 110600 | tf_op jit(solution)/shard_map/ppermute | solution.py:495
  11.9 1.3 %collective-permute-start.3 = (f32[144,128]{1,0:T(8,128)S(1)}, f32[144,128]{1,0:T(8,128)S(1)}, u32[]{:S(2)}, u32[]{:S(2)}) collective-permute-start(f32[144,128]{1,0:T(8,128)S(1)} %join_blocks.3.near), channel_id=1, source_target_pairs={{0,1},{1,0},{2,3},{3,2},{4,5},{5,4},{6,7},{7,6},{8,9},{9,8},{10,11... | collective-permute-start | bytes 221192 | tf_op jit(solution)/shard_map/ppermute | solution.py:495
  13.9 13.2 %collective-permute-start.4 = (f32[6,64,128]{2,1,0:T(8,128)S(1)}, f32[6,64,128]{2,1,0:T(8,128)S(1)}, u32[]{:S(2)}, u32[]{:S(2)}) collective-permute-start(f32[6,64,128]{2,1,0:T(8,128)S(1)} %get-tuple-element.46), channel_id=1, source_target_pairs={{0,4},{4,0},{8,12},{12,8},{16,20},{20,16},{24,28},{28,24},{1,5},{5... | collective-permute-start | bytes 589832 | tf_op jit(solution)/shard_map/ppermute | solution.py:469
  15.6 4.5 %collective-permute-start.5 = (f32[6,48,128]{2,1,0:T(8,128)S(1)}, f32[6,48,128]{2,1,0:T(8,128)S(1)}, u32[]{:S(2)}, u32[]{:S(2)}) collective-permute-start(f32[6,48,128]{2,1,0:T(8,128)S(1)} %get-tuple-element.47.grp_a), channel_id=1, source_target_pairs={{0,1},{1,0},{2,3},{3,2},{4,5},{5,4},{6,7},{7,6},{8,9},{9,8},{10,11... | collective-permute-start | bytes 442376 | tf_op jit(solution)/shard_map/ppermute | solution.py:469
  15.6 6.5 %collective-permute-start.6 = (f32[6,48,128]{2,1,0:T(8,128)S(1)}, f32[6,48,128]{2,1,0:T(8,128)S(1)}, u32[]{:S(2)}, u32[]{:S(2)}) collective-permute-start(f32[6,48,128]{2,1,0:T(8,128)S(1)} %get-tuple-element.48.grp_b), channel_id=1, source_target_pairs={{1,2},{2,1},{5,6},{6,5},{9,10},{10,9},{13,14},{14,13},{17,18},{18,... | collective-permute-start | bytes 442376 | tf_op jit(solution)/shard_map/ppermute | solution.py:469
  18.2 10.4 %collective-permute-start.7 = (f32[6,64,128]{2,1,0:T(8,128)S(1)}, f32[6,64,128]{2,1,0:T(8,128)S(1)}, u32[]{:S(2)}, u32[]{:S(2)}) collective-permute-start(f32[6,64,128]{2,1,0:T(8,128)S(1)} %get-tuple-element.53), channel_id=1, source_target_pairs={{4,8},{8,4},{12,16},{16,12},{20,24},{24,20},{5,9},{9,5},{13,17},{1... | collective-permute-start | bytes 589832 | tf_op jit(solution)/shard_map/ppermute | solution.py:469
  22.1 6.9 %collective-permute-start.8 = (f32[6,16,128]{2,1,0:T(8,128)S(1)}, f32[6,16,128]{2,1,0:T(8,128)S(1)}, u32[]{:S(2)}, u32[]{:S(2)}) collective-permute-start(f32[6,16,128]{2,1,0:T(8,128)S(1)} %get-tuple-element.54), channel_id=1, source_target_pairs={{4,8},{8,4},{12,16},{16,12},{20,24},{24,20},{5,9},{9,5},{13,17},{1... | collective-permute-start | bytes 147464 | tf_op jit(solution)/shard_map/ppermute | solution.py:469
  25.0 4.5 %collective-permute-start.9 = (f32[6,16,128]{2,1,0:T(8,128)S(1)}, f32[6,16,128]{2,1,0:T(8,128)S(1)}, u32[]{:S(2)}, u32[]{:S(2)}) collective-permute-start(f32[6,16,128]{2,1,0:T(8,128)S(1)} %get-tuple-element.55), channel_id=1, source_target_pairs={{0,4},{4,0},{8,12},{12,8},{16,20},{20,16},{24,28},{28,24},{1,5},{5... | collective-permute-start | bytes 147464 | tf_op jit(solution)/shard_map/ppermute | solution.py:469

commit v14 on v12

--- a/solution.py
+++ b/solution.py
@@ -1,3 +1,5 @@
+import functools
+
 import jax
 import jax.numpy as jnp
 from jax import lax
@@ -358,16 +360,22 @@
         grp_b[i] = jnp.concatenate([part[2 * NIS + NIG : EDGES], edge[1], edge[3]], axis=0)
 
 
-def edge_kernel(grp_a, grp_b, from_a, from_b, edge_b, edge_a):
+def grp_b_rows(members, rows):
+    g = lax.axis_index("grp")
+    partner = g - 1 + 2 * (g & 1)
+    return jnp.where((partner >= 0) & (partner < members), rows, 0.0)
+
+
+def edge_kernel(members, grp_a, grp_b, from_a, from_b, edge_b, edge_a):
     split = NIG + NED
     edge_a[:, :NED, :] = grp_a[:, NIG:split, :] + from_a[:, NIG:split, :]
-    edge_a[:, NED:, :] = grp_b[:, NIG:split, :] + from_b[:, NIG:split, :]
+    edge_a[:, NED:, :] = grp_b[:, NIG:split, :] + grp_b_rows(members, from_b[:, NIG:split, :])
     edge_b[:, :NED, :] = grp_a[:, split:, :] + from_a[:, split:, :]
-    edge_b[:, NED:, :] = grp_b[:, split:, :] + from_b[:, split:, :]
+    edge_b[:, NED:, :] = grp_b[:, split:, :] + grp_b_rows(members, from_b[:, split:, :])
 
 
 def partial_kernel(
-    count, stress, free_t, corner_t, values, placing, grp_a, grp_b, partial, disp_out, received
+    members, count, stress, free_t, corner_t, values, placing, grp_a, grp_b, partial, disp_out, received
 ):
     nodes = disp_out.shape[1]
     for c in range(3):
@@ -377,7 +385,7 @@
             disp_out[c, k : k + LANES, :] = part[:, k : k + LANES].T.astype(BF16)
     split = NIG + NED
     for i in range(COMPS):
-        low, high = grp_a[i], grp_b[i]
+        low, high = grp_a[i], grp_b_rows(members, grp_b[i])
         rows = [low[:NIG], high[:NIG], low[NIG:split], high[NIG:split], low[split:], high[split:]]
         rows.append(jnp.zeros((2 * LANES - NIF, LANES), F32))
         first, second = split_two(jnp.concatenate(rows, axis=0))
@@ -444,11 +452,14 @@
     )
 
 
-def exchange(block, axis, first):
+def exchange(block, axis, first, keep=False):
     count = lax.axis_size(axis)
     pairs = []
     for i in range(first, count - 1, 2):
         pairs += [(i, i + 1), (i + 1, i)]
+    if keep:
+        alone = set(range(count)) - {i for i, _ in pairs}
+        pairs += [(i, i) for i in sorted(alone)]
     return lax.ppermute(block, axis, pairs)
 
 
@@ -595,9 +606,10 @@
     )(*near, select, stress_first, stress_rest, stress_corner, face)
     from_sub_a = exchange(sub_a, "sub", 0)
     from_grp_a = exchange(grp_a, "grp", 0)
-    from_grp_b = exchange(grp_b, "grp", 1)
+    from_grp_b = exchange(grp_b, "grp", 1, keep=True)
+    members = lax.axis_size("grp")
     edge_b, edge_a = call(
-        edge_kernel,
+        functools.partial(edge_kernel, members),
         "sum_edges",
         (array((COMPS, 2 * NED, cases)), array((COMPS, 2 * NED, cases))),
         vmem(4),
@@ -606,7 +618,7 @@
     from_edge_b = exchange(edge_b, "sub", 1)
     from_edge_a = exchange(edge_a, "sub", 0)
     partial, disp = call(
-        partial_kernel,
+        functools.partial(partial_kernel, members),
         "assemble_nodes",
         (array((COMPS, nodes, cases)), array((3, nodes, cases), BF16)),
         vmem(8),

time: 31 us -> 31 us (level)
  no operation moved by 1% of the time
where the time goes in v14:
time: 31 us; the launch traced here: 30.4 us
  starting transfers between devices  16.8 us (54%)
  Pallas kernels  8.42 us (27%)
  waiting for transfers between devices  4.45 us (14%)
  between operations  0.73 us (2%)
    ppermute x8, starting transfers between devices, exchange(): return lax.ppermute(block, axis, pairs)  16.3 us
    ppermute x8, waiting for transfers between devices, exchange(): return lax.ppermute(block, axis, pairs)  2.84 us
    pallas_call x1, Pallas kernels, shards(): call(prepare_panels, 'prepare_panels', (array((cases, dofs)), array((2 *...  1.94 us
    pallas_call x1, Pallas kernels, shards(): call(lists, 'prepare_lists', (array(coarse.shape), array(panel_nodes.shap...  1.93 us
    ppermute x2, waiting for transfers between devices, gather_near(): parts = [block, lax.ppermute(block, 'grp', pairs)]  1.62 us
    pallas_call x1, Pallas kernels, shards(): call(functools.partial(partial_kernel, members), 'assemble_nodes', (array...  1.45 us
    pallas_call x1, Pallas kernels, shards(): call(finish_kernel, 'add_last', (array((COMPS, nodes, cases), BF16),), vm...  1.21 us
    pallas_call x1, Pallas kernels, shards(): call(stress_kernel, 'stress_of_loads', (array((COMPS, cases - first, LANE...  1.11 us
  transfers between devices with their start and end apart: 10, of which 6 were waited for; matrix products, arithmetic and copies ran while one was open for 0% of the time, Pallas kernels for 21%

profile of v14, /device:TPU:10, one launch (start us, length us, event | category | flops | bytes accessed | tf_op | source)
XLA Modules:
  0.0 30.4 jit_solution(14329280436264062862)
XLA Ops:
  0.6 3.3 %collective-permute-start = (f32[24,128]{1,0:T(8,128)}, f32[24,128]{1,0:T(8,128)S(1)}, u32[]{:S(2)}, u32[]{:S(2)}) collective-permute-start(f32[24,128]{1,0:T(8,128)} %refs_6_.1), channel_id=1, source_target_pairs={{4,8},{8,4},{12,16},{16,12},{20,24},{24,20},{5,9},{9,5},{13,17},{1... | collective-permute-start | bytes 36872 | tf_op jit(solution)/shard_map/ppermute | solution.py:463
  4.0 1.7 %collective-permute-start.1 = (f32[24,128]{1,0:T(8,128)}, f32[24,128]{1,0:T(8,128)S(1)}, u32[]{:S(2)}, u32[]{:S(2)}) collective-permute-start(f32[24,128]{1,0:T(8,128)} %refs_6_.1), channel_id=1, source_target_pairs={{0,4},{4,0},{8,12},{12,8},{16,20},{20,16},{24,28},{28,24},{1,5},{5... | collective-permute-start | bytes 36872 | tf_op jit(solution)/shard_map/ppermute | solution.py:463
  5.7 1.9 %prepare_lists.1 = (f32[24,128]{1,0:T(8,128)S(1)}, s32[1,4]{1,0:T(1,128)S(1)}, bf16[24,1536]{1,0:T(8,128)(2,1)S(1)}, bf16[3,512,128]{2,1,0:T(8,128)(2,1)S(1)}, b...) custom-call(s32[1,24]{1,0:T(1,128)} %refs_0_.1, ...), custom_call_target="tpu_custom_call" | custom-call | flops 100000000 | bytes 4000000 | tf_op jit(solution)/shard_map/prepare_lists/pallas_call | solution.py:514
  7.6 0.0 collective-permute-done.refs_1_
  7.6 0.3 %collective-permute-done.1.refs_2_ = f32[24,128]{1,0:T(8,128)S(1)} collective-permute-done((f32[24,128]{1,0:T(8,128)}, f32[24,128]{1,0:T(8,128)S(1)}, u32[]{:S(2)}, u32[]{:S(2)}) %collective-permute-start.1) | collective-permute-done | bytes 12320 | tf_op jit(solution)/shard_map/ppermute | solution.py:463
  7.9 0.5 %collective-permute-start.2 = (f32[72,128]{1,0:T(8,128)S(1)}, f32[72,128]{1,0:T(8,128)S(1)}, u32[]{:S(2)}, u32[]{:S(2)}) collective-permute-start(f32[72,128]{1,0:T(8,128)S(1)} %join_blocks.2.refs_0_), channel_id=1, source_target_pairs={{0,2},{1,3},{2,0},{3,1},{4,6},{5,7},{6,4},{7,5},{8,10},{9,11},{10,... | collective-permute-start | bytes 110600 | tf_op jit(solution)/shard_map/ppermute | solution.py:489
  8.5 1.9 %prepare_panels.1 = (f32[128,1536]{1,0:T(8,128)S(1)}, bf16[256,1536]{1,0:T(8,128)(2,1)S(1)}, f32[6,32,128]{2,1,0:T(8,128)S(1)}, bf16[256,768]{1,0:T(8,128)(2,1)S(1)}) custom-call(s32[1,4]{1,0:T(1,128)S(1)} %get-tuple-element.32.panel_v, bf16[24,1536]{1,0:T(8,128)(2,1)S(1)} %get-tuple-element.33.coupling_v, ...), custom_call_target="tpu_custom_call" | custom-call | flops 400000000 | bytes 4000000 | tf_op jit(solution)/shard_map/prepare_panels/pallas_call | solution.py:561
  10.4 1.5 %collective-permute-done.2.refs_1_ = f32[72,128]{1,0:T(8,128)S(1)} collective-permute-done((f32[72,128]{1,0:T(8,128)S(1)}, f32[72,128]{1,0:T(8,128)S(1)}, u32[]{:S(2)}, u32[]{:S(2)}) %collective-permute-start.2) | collective-permute-done | bytes 36896 | tf_op jit(solution)/shard_map/ppermute | solution.py:489
  11.9 0.0 collective-permute-start.3
  11.9 1.1 %stress_of_loads.1.stress_rest = f32[6,96,128]{2,1,0:T(8,128)S(1)} custom-call(f32[128,1536]{1,0:T(8,128)S(1)} %get-tuple-element.40.free_t, bf16[512,1024]{1,0:T(8,128)(2,1)S(1)} %get-tuple-element.36.onehot, f32[144,8,128]{2,1,0:T(8,128)S(1)} %get-tuple-element.37.scaled), custom_call_target="tpu_custom_call" | custom-call | flops 400000000 | bytes 4000000 | tf_op jit(solution)/shard_map/stress_of_loads/pallas_call | solution.py:580
  13.0 0.1 collective-permute-done.3.across
  13.2 0.8 %stress_and_rows.1 = (bf16[128,256]{1,0:T(8,128)(2,1)S(1)}, bf16[768,256]{1,0:T(8,128)(2,1)S(1)}, f32[6,64,128]{2,1,0:T(8,128)S(1)}, f32[6,64,128]{2,1,0:T(8,128...) custom-call(f32[144,128]{1,0:T(8,128)S(1)} %join_blocks.3.near, ...), custom_call_target="tpu_custom_call" | custom-call | flops 300000000 | bytes 3000000 | tf_op jit(solution)/shard_map/stress_and_rows/pallas_call | solution.py:591
  13.9 0.4 %collective-permute-start.4 = (f32[6,48,128]{2,1,0:T(8,128)S(1)}, f32[6,48,128]{2,1,0:T(8,128)S(1)}, u32[]{:S(2)}, u32[]{:S(2)}) collective-permute-start(f32[6,48,128]{2,1,0:T(8,128)S(1)} %get-tuple-element.46.grp_a), channel_id=1, source_target_pairs={{0,1},{1,0},{2,3},{3,2},{4,5},{5,4},{6,7},{7,6},{8,9},{9,8},{10,11... | collective-permute-start | bytes 442376 | tf_op jit(solution)/shard_map/ppermute | solution.py:463
  14.4 2.2 %collective-permute-start.5 = (f32[6,48,128]{2,1,0:T(8,128)S(1)}, f32[6,48,128]{2,1,0:T(8,128)S(1)}, u32[]{:S(2)}, u32[]{:S(2)}) collective-permute-start(f32[6,48,128]{2,1,0:T(8,128)S(1)} %get-tuple-element.47.grp_b), channel_id=1, source_target_pairs={{1,2},{2,1},{0,0},{3,3},{5,6},{6,5},{4,4},{7,7},{9,10},{10,9},{8,8... | collective-permute-start | bytes 442376 | tf_op jit(solution)/shard_map/ppermute | solution.py:463
  16.6 1.7 %collective-permute-start.6 = (f32[6,64,128]{2,1,0:T(8,128)S(1)}, f32[6,64,128]{2,1,0:T(8,128)S(1)}, u32[]{:S(2)}, u32[]{:S(2)}) collective-permute-start(f32[6,64,128]{2,1,0:T(8,128)S(1)} %get-tuple-element.52), channel_id=1, source_target_pairs={{0,4},{4,0},{8,12},{12,8},{16,20},{20,16},{24,28},{28,24},{1,5},{5... | collective-permute-start | bytes 589832 | tf_op jit(solution)/shard_map/ppermute | solution.py:463
  18.2 1.9 %collective-permute-start.7 = (f32[6,64,128]{2,1,0:T(8,128)S(1)}, f32[6,64,128]{2,1,0:T(8,128)S(1)}, u32[]{:S(2)}, u32[]{:S(2)}) collective-permute-start(f32[6,64,128]{2,1,0:T(8,128)S(1)} %get-tuple-element.53), channel_id=1, source_target_pairs={{4,8},{8,4},{12,16},{16,12},{20,24},{24,20},{5,9},{9,5},{13,17},{1... | collective-permute-start | bytes 589832 | tf_op jit(solution)/shard_map/ppermute | solution.py:463
  20.2 0.0 collective-permute-done.4.grp_a.from_a
  20.2 0.6 %collective-permute-done.5.grp_b.from_b = f32[6,48,128]{2,1,0:T(8,128)S(1)} collective-permute-done((f32[6,48,128]{2,1,0:T(8,128)S(1)}, f32[6,48,128]{2,1,0:T(8,128)S(1)}, u32[]{:S(2)}, u32[]{:S(2)}) %collective-permute-start.5) | collective-permute-done | bytes 147488 | tf_op jit(solution)/shard_map/ppermute | solution.py:463
  20.8 4.2 %collective-permute-start.8 = (f32[6,16,128]{2,1,0:T(8,128)S(1)}, f32[6,16,128]{2,1,0:T(8,128)S(1)}, u32[]{:S(2)}, u32[]{:S(2)}) collective-permute-start(f32[6,16,128]{2,1,0:T(8,128)S(1)} %get-tuple-element.54), channel_id=1, source_target_pairs={{4,8},{8,4},{12,16},{16,12},{20,24},{24,20},{5,9},{9,5},{13,17},{1... | collective-permute-start | bytes 147464 | tf_op jit(solution)/shard_map/ppermute | solution.py:463
  25.0 0.8 %collective-permute-start.9 = (f32[6,16,128]{2,1,0:T(8,128)S(1)}, f32[6,16,128]{2,1,0:T(8,128)S(1)}, u32[]{:S(2)}, u32[]{:S(2)}) collective-permute-start(f32[6,16,128]{2,1,0:T(8,128)S(1)} %get-tuple-element.55), channel_id=1, source_target_pairs={{0,4},{4,0},{8,12},{12,8},{16,20},{20,16},{24,28},{28,24},{1,5},{5... | collective-permute-start | bytes 147464 | tf_op jit(solution)/shard_map/ppermute | solution.py:463
  25.9 1.5 %assemble_nodes.1 = (f32[6,512,128]{2,1,0:T(8,128)S(1)}, bf16[3,512,128]{2,1,0:T(8,128)(2,1)}) custom-call(bf16[512,256]{1,0:T(8,128)(2,1)S(1)} %get-tuple-element.29.count, bf16[768,256]{1,0:T(8,128)(2,1)S(1)} %get-tuple-element.43.stress, f32[128,1536]{1,0:T(8,128)S(1)} %get-tuple-element.40.free_t, ...), custom_call_target="tpu_custom_call" | custom-call | flops 400000000 | bytes 2000000 | tf_op jit(solution)/shard_map/assemble_nodes/pallas_call | solution.py:620
  27.3 0.0 collective-permute-done.6.sub_a
  27.3 0.0 collective-permute-done.7.sub_b
  27.3 0.5 %collective-permute-done.8.edge_b = f32[6,16,128]{2,1,0:T(8,128)S(1)} collective-permute-done((f32[6,16,128]{2,1,0:T(8,128)S(1)}, f32[6,16,128]{2,1,0:T(8,128)S(1)}, u32[]{:S(2)}, u32[]{:S(2)}) %collective-permute-start.8) | collective-permute-done | bytes 49184 | tf_op jit(solution)/shard_map/ppermute | solution.py:463
  27.8 1.4 %collective-permute-done.9.edge_a = f32[6,16,128]{2,1,0:T(8,128)S(1)} collective-permute-done((f32[6,16,128]{2,1,0:T(8,128)S(1)}, f32[6,16,128]{2,1,0:T(8,128)S(1)}, u32[]{:S(2)}, u32[]{:S(2)}) %collective-permute-start.9) | collective-permute-done | bytes 49184 | tf_op jit(solution)/shard_map/ppermute | solution.py:463
  29.2 1.2 %add_last.1 = bf16[6,512,128]{2,1,0:T(8,128)(2,1)} custom-call(bf16[512,256]{1,0:T(8,128)(2,1)S(1)} %get-tuple-element.49.placing, f32[6,512,128]{2,1,0:T(8,128)S(1)} %get-tuple-element.50.partial, f32[512,128]{1,0:T(8,128)S(1)} %get-tuple-element.51.inverse_volume, f32[6,64,128]{2,1,0:T(8,128)S(1)} %collective-permute-done.6.sub_a, ...), custom_call_target="tpu_custom_call" | custom-call | flops 400000000 | bytes 3000000 | tf_op jit(solution)/shard_map/add_last/pallas_call | solution.py:629
  (3 shorter events, 0.0 us)
Async XLA Ops:
  0.6 7.0 %collective-permute-start = (f32[24,128]{1,0:T(8,128)}, f32[24,128]{1,0:T(8,128)S(1)}, u32[]{:S(2)}, u32[]{:S(2)}) collective-permute-start(f32[24,128]{1,0:T(8,128)} %refs_6_.1), channel_id=1, source_target_pairs={{4,8},{8,4},{12,16},{16,12},{20,24},{24,20},{5,9},{9,5},{13,17},{1... | collective-permute-start | bytes 36872 | tf_op jit(solution)/shard_map/ppermute | solution.py:463
  4.0 4.0 %collective-permute-start.1 = (f32[24,128]{1,0:T(8,128)}, f32[24,128]{1,0:T(8,128)S(1)}, u32[]{:S(2)}, u32[]{:S(2)}) collective-permute-start(f32[24,128]{1,0:T(8,128)} %refs_6_.1), channel_id=1, source_target_pairs={{0,4},{4,0},{8,12},{12,8},{16,20},{20,16},{24,28},{28,24},{1,5},{5... | collective-permute-start | bytes 36872 | tf_op jit(solution)/shard_map/ppermute | solution.py:463
  7.9 4.0 %collective-permute-start.2 = (f32[72,128]{1,0:T(8,128)S(1)}, f32[72,128]{1,0:T(8,128)S(1)}, u32[]{:S(2)}, u32[]{:S(2)}) collective-permute-start(f32[72,128]{1,0:T(8,128)S(1)} %join_blocks.2.refs_0_), channel_id=1, source_target_pairs={{0,2},{1,3},{2,0},{3,1},{4,6},{5,7},{6,4},{7,5},{8,10},{9,11},{10,... | collective-permute-start | bytes 110600 | tf_op jit(solution)/shard_map/ppermute | solution.py:489
  11.9 1.3 %collective-permute-start.3 = (f32[144,128]{1,0:T(8,128)S(1)}, f32[144,128]{1,0:T(8,128)S(1)}, u32[]{:S(2)}, u32[]{:S(2)}) collective-permute-start(f32[144,128]{1,0:T(8,128)S(1)} %join_blocks.3.near), channel_id=1, source_target_pairs={{0,1},{1,0},{2,3},{3,2},{4,5},{5,4},{6,7},{7,6},{8,9},{9,8},{10,11... | collective-permute-start | bytes 221192 | tf_op jit(solution)/shard_map/ppermute | solution.py:489
  13.9 6.3 %collective-permute-start.4 = (f32[6,48,128]{2,1,0:T(8,128)S(1)}, f32[6,48,128]{2,1,0:T(8,128)S(1)}, u32[]{:S(2)}, u32[]{:S(2)}) collective-permute-start(f32[6,48,128]{2,1,0:T(8,128)S(1)} %get-tuple-element.46.grp_a), channel_id=1, source_target_pairs={{0,1},{1,0},{2,3},{3,2},{4,5},{5,4},{6,7},{7,6},{8,9},{9,8},{10,11... | collective-permute-start | bytes 442376 | tf_op jit(solution)/shard_map/ppermute | solution.py:463
  14.4 6.5 %collective-permute-start.5 = (f32[6,48,128]{2,1,0:T(8,128)S(1)}, f32[6,48,128]{2,1,0:T(8,128)S(1)}, u32[]{:S(2)}, u32[]{:S(2)}) collective-permute-start(f32[6,48,128]{2,1,0:T(8,128)S(1)} %get-tuple-element.47.grp_b), channel_id=1, source_target_pairs={{1,2},{2,1},{0,0},{3,3},{5,6},{6,5},{4,4},{7,7},{9,10},{10,9},{8,8... | collective-permute-start | bytes 442376 | tf_op jit(solution)/shard_map/ppermute | solution.py:463
  16.6 10.8 %collective-permute-start.6 = (f32[6,64,128]{2,1,0:T(8,128)S(1)}, f32[6,64,128]{2,1,0:T(8,128)S(1)}, u32[]{:S(2)}, u32[]{:S(2)}) collective-permute-start(f32[6,64,128]{2,1,0:T(8,128)S(1)} %get-tuple-element.52), channel_id=1, source_target_pairs={{0,4},{4,0},{8,12},{12,8},{16,20},{20,16},{24,28},{28,24},{1,5},{5... | collective-permute-start | bytes 589832 | tf_op jit(solution)/shard_map/ppermute | solution.py:463
  18.2 9.1 %collective-permute-start.7 = (f32[6,64,128]{2,1,0:T(8,128)S(1)}, f32[6,64,128]{2,1,0:T(8,128)S(1)}, u32[]{:S(2)}, u32[]{:S(2)}) collective-permute-start(f32[6,64,128]{2,1,0:T(8,128)S(1)} %get-tuple-element.53), channel_id=1, source_target_pairs={{4,8},{8,4},{12,16},{16,12},{20,24},{24,20},{5,9},{9,5},{13,17},{1... | collective-permute-start | bytes 589832 | tf_op jit(solution)/shard_map/ppermute | solution.py:463
  20.8 6.9 %collective-permute-start.8 = (f32[6,16,128]{2,1,0:T(8,128)S(1)}, f32[6,16,128]{2,1,0:T(8,128)S(1)}, u32[]{:S(2)}, u32[]{:S(2)}) collective-permute-start(f32[6,16,128]{2,1,0:T(8,128)S(1)} %get-tuple-element.54), channel_id=1, source_target_pairs={{4,8},{8,4},{12,16},{16,12},{20,24},{24,20},{5,9},{9,5},{13,17},{1... | collective-permute-start | bytes 147464 | tf_op jit(solution)/shard_map/ppermute | solution.py:463
  25.0 4.2 %collective-permute-start.9 = (f32[6,16,128]{2,1,0:T(8,128)S(1)}, f32[6,16,128]{2,1,0:T(8,128)S(1)}, u32[]{:S(2)}, u32[]{:S(2)}) collective-permute-start(f32[6,16,128]{2,1,0:T(8,128)S(1)} %get-tuple-element.55), channel_id=1, source_target_pairs={{0,4},{4,0},{8,12},{12,8},{16,20},{20,16},{24,28},{28,24},{1,5},{5... | collective-permute-start | bytes 147464 | tf_op jit(solution)/shard_map/ppermute | solution.py:463

commit v15 on v12

--- a/solution.py
+++ b/solution.py
@@ -229,7 +229,8 @@
     copies[3].wait()
     copies[4].wait()
     factor = modulus_v[...]
-    rows = [strain_v[i].astype(F32) for i in range(COMPS)]
+    whole = strain_v[...].astype(F32)
+    rows = [whole[24 * i : 24 * (i + 1)] for i in range(COMPS)]
     trace = (rows[0] + rows[1] + rows[2]) * LAME
     for i in range(COMPS):
         value = trace + rows[i] * (2.0 * SHEAR) if i < 3 else rows[i] * SHEAR
@@ -523,7 +524,7 @@
             pltpu.VMEM((1, q), jnp.int32),
             pltpu.VMEM(connect.shape, jnp.int32),
             pltpu.VMEM(interface.shape, jnp.int32),
-            pltpu.VMEM(strain_disp.shape, BF16),
+            pltpu.VMEM((COMPS * 24, LANES), BF16),
             pltpu.VMEM((1, LANES), F32),
             pltpu.VMEM((nodes // LANES, LANES), F32),
             pltpu.VMEM((8, 2 * LANES), F32),
@@ -536,7 +537,7 @@
             corner_idx,
             connect,
             interface,
-            strain_disp,
+            strain_disp.reshape(COMPS * 24, LANES),
             modulus.reshape(1, -1),
             nodal_volume.reshape(-1, LANES),
             coarse,
@@ -546,7 +547,7 @@
             panel_inv,
         )
     )
-    first = 32
+    first = 64
     free_t, corner_t, stress_first, stress_corner = call(
         prepare_panels,
         "prepare_panels",

time: 31 us -> 30.8 us (level)
  no operation moved by 1% of the time
where the time goes in v15:
time: 30.8 us; the launch traced here: 30.4 us
  starting transfers between devices  16.8 us (55%)
  Pallas kernels  8.36 us (27%)
  waiting for transfers between devices  4.52 us (15%)
  between operations  0.72 us (2%)
    ppermute x8, starting transfers between devices, exchange(): return lax.ppermute(block, axis, pairs)  16.3 us
    ppermute x8, waiting for transfers between devices, exchange(): return lax.ppermute(block, axis, pairs)  2.83 us
    pallas_call x1, Pallas kernels, shards(): call(prepare_panels, 'prepare_panels', (array((cases, dofs)), array((2 *...  2.16 us
    pallas_call x1, Pallas kernels, shards(): call(lists, 'prepare_lists', (array(coarse.shape), array(panel_nodes.shap...  1.93 us
    ppermute x2, waiting for transfers between devices, gather_near(): parts = [block, lax.ppermute(block, 'grp', pairs)]  1.69 us
    pallas_call x1, Pallas kernels, shards(): call(partial_kernel, 'assemble_nodes', (array((COMPS, nodes, cases)), arr...  1.46 us
    pallas_call x1, Pallas kernels, shards(): call(finish_kernel, 'add_last', (array((COMPS, nodes, cases), BF16),), vm...  1.21 us
    pallas_call x1, Pallas kernels, shards(): call(stress_kernel, 'stress_of_loads', (array((COMPS, cases - first, LANE...  0.81 us
  transfers between devices with their start and end apart: 10, of which 6 were waited for; matrix products, arithmetic and copies ran while one was open for 0% of the time, Pallas kernels for 21%

profile of v15, /device:TPU:10, one launch (start us, length us, event | category | flops | bytes accessed | tf_op | source)
XLA Modules:
  0.0 30.4 jit_solution(14152206916330539638)
XLA Ops:
  0.6 3.3 %collective-permute-start = (f32[24,128]{1,0:T(8,128)}, f32[24,128]{1,0:T(8,128)S(1)}, u32[]{:S(2)}, u32[]{:S(2)}) collective-permute-start(f32[24,128]{1,0:T(8,128)} %refs_6_.1), channel_id=1, source_target_pairs={{4,8},{8,4},{12,16},{16,12},{20,24},{24,20},{5,9},{9,5},{13,17},{1... | collective-permute-start | bytes 36872 | tf_op jit(solution)/shard_map/ppermute | solution.py:453
  4.0 1.7 %collective-permute-start.1 = (f32[24,128]{1,0:T(8,128)}, f32[24,128]{1,0:T(8,128)S(1)}, u32[]{:S(2)}, u32[]{:S(2)}) collective-permute-start(f32[24,128]{1,0:T(8,128)} %refs_6_.1), channel_id=1, source_target_pairs={{0,4},{4,0},{8,12},{12,8},{16,20},{20,16},{24,28},{28,24},{1,5},{5... | collective-permute-start | bytes 36872 | tf_op jit(solution)/shard_map/ppermute | solution.py:453
  5.7 1.9 %prepare_lists.1 = (f32[24,128]{1,0:T(8,128)S(1)}, s32[1,4]{1,0:T(1,128)S(1)}, bf16[24,1536]{1,0:T(8,128)(2,1)S(1)}, bf16[3,512,128]{2,1,0:T(8,128)(2,1)S(1)}, b...) custom-call(s32[1,24]{1,0:T(1,128)} %refs_0_.1, ...), custom_call_target="tpu_custom_call" | custom-call | flops 100000000 | bytes 4000000 | tf_op jit(solution)/shard_map/prepare_lists/pallas_call | solution.py:504
  7.6 0.0 collective-permute-done.refs_1_
  7.6 0.3 %collective-permute-done.1.refs_2_ = f32[24,128]{1,0:T(8,128)S(1)} collective-permute-done((f32[24,128]{1,0:T(8,128)}, f32[24,128]{1,0:T(8,128)S(1)}, u32[]{:S(2)}, u32[]{:S(2)}) %collective-permute-start.1) | collective-permute-done | bytes 12320 | tf_op jit(solution)/shard_map/ppermute | solution.py:453
  7.9 0.5 %collective-permute-start.2 = (f32[72,128]{1,0:T(8,128)S(1)}, f32[72,128]{1,0:T(8,128)S(1)}, u32[]{:S(2)}, u32[]{:S(2)}) collective-permute-start(f32[72,128]{1,0:T(8,128)S(1)} %join_blocks.2.refs_0_), channel_id=1, source_target_pairs={{0,2},{1,3},{2,0},{3,1},{4,6},{5,7},{6,4},{7,5},{8,10},{9,11},{10,... | collective-permute-start | bytes 110600 | tf_op jit(solution)/shard_map/ppermute | solution.py:479
  8.5 2.2 %prepare_panels.1 = (f32[128,1536]{1,0:T(8,128)S(1)}, bf16[256,1536]{1,0:T(8,128)(2,1)S(1)}, f32[6,64,128]{2,1,0:T(8,128)S(1)}, bf16[256,768]{1,0:T(8,128)(2,1)S(1)}) custom-call(s32[1,4]{1,0:T(1,128)S(1)} %get-tuple-element.32.panel_v, bf16[24,1536]{1,0:T(8,128)(2,1)S(1)} %get-tuple-element.33.coupling_v, ...), custom_call_target="tpu_custom_call" | custom-call | flops 400000000 | bytes 4000000 | tf_op jit(solution)/shard_map/prepare_panels/pallas_call | solution.py:551
  10.6 1.3 %collective-permute-done.2.refs_1_ = f32[72,128]{1,0:T(8,128)S(1)} collective-permute-done((f32[72,128]{1,0:T(8,128)S(1)}, f32[72,128]{1,0:T(8,128)S(1)}, u32[]{:S(2)}, u32[]{:S(2)}) %collective-permute-start.2) | collective-permute-done | bytes 36896 | tf_op jit(solution)/shard_map/ppermute | solution.py:479
  11.9 0.0 collective-permute-start.3
  11.9 0.8 %stress_of_loads.1.stress_rest = f32[6,64,128]{2,1,0:T(8,128)S(1)} custom-call(f32[128,1536]{1,0:T(8,128)S(1)} %get-tuple-element.40.free_t, bf16[512,1024]{1,0:T(8,128)(2,1)S(1)} %get-tuple-element.36.onehot, f32[144,8,128]{2,1,0:T(8,128)S(1)} %get-tuple-element.37.scaled), custom_call_target="tpu_custom_call" | custom-call | flops 400000000 | bytes 4000000 | tf_op jit(solution)/shard_map/stress_of_loads/pallas_call | solution.py:570
  12.7 0.4 %collective-permute-done.3.across = f32[144,128]{1,0:T(8,128)S(1)} collective-permute-done((f32[144,128]{1,0:T(8,128)S(1)}, f32[144,128]{1,0:T(8,128)S(1)}, u32[]{:S(2)}, u32[]{:S(2)}) %collective-permute-start.3) | collective-permute-done | bytes 73760 | tf_op jit(solution)/shard_map/ppermute | solution.py:479
  13.2 0.8 %stress_and_rows.1 = (bf16[128,256]{1,0:T(8,128)(2,1)S(1)}, bf16[768,256]{1,0:T(8,128)(2,1)S(1)}, f32[6,64,128]{2,1,0:T(8,128)S(1)}, f32[6,64,128]{2,1,0:T(8,128...) custom-call(f32[144,128]{1,0:T(8,128)S(1)} %join_blocks.3.near, ...), custom_call_target="tpu_custom_call" | custom-call | flops 300000000 | bytes 3000000 | tf_op jit(solution)/shard_map/stress_and_rows/pallas_call | solution.py:581
  13.9 0.2 collective-permute-start.4
  14.1 2.4 %collective-permute-start.5 = (f32[6,48,128]{2,1,0:T(8,128)S(1)}, f32[6,48,128]{2,1,0:T(8,128)S(1)}, u32[]{:S(2)}, u32[]{:S(2)}) collective-permute-start(f32[6,48,128]{2,1,0:T(8,128)S(1)} %get-tuple-element.47.grp_b), channel_id=1, source_target_pairs={{1,2},{2,1},{5,6},{6,5},{9,10},{10,9},{13,14},{14,13},{17,18},{18,... | collective-permute-start | bytes 442376 | tf_op jit(solution)/shard_map/ppermute | solution.py:453
  16.6 1.7 %collective-permute-start.6 = (f32[6,64,128]{2,1,0:T(8,128)S(1)}, f32[6,64,128]{2,1,0:T(8,128)S(1)}, u32[]{:S(2)}, u32[]{:S(2)}) collective-permute-start(f32[6,64,128]{2,1,0:T(8,128)S(1)} %get-tuple-element.52), channel_id=1, source_target_pairs={{0,4},{4,0},{8,12},{12,8},{16,20},{20,16},{24,28},{28,24},{1,5},{5... | collective-permute-start | bytes 589832 | tf_op jit(solution)/shard_map/ppermute | solution.py:453
  18.2 1.9 %collective-permute-start.7 = (f32[6,64,128]{2,1,0:T(8,128)S(1)}, f32[6,64,128]{2,1,0:T(8,128)S(1)}, u32[]{:S(2)}, u32[]{:S(2)}) collective-permute-start(f32[6,64,128]{2,1,0:T(8,128)S(1)} %get-tuple-element.53), channel_id=1, source_target_pairs={{4,8},{8,4},{12,16},{16,12},{20,24},{24,20},{5,9},{9,5},{13,17},{1... | collective-permute-start | bytes 589832 | tf_op jit(solution)/shard_map/ppermute | solution.py:453
  20.2 0.0 collective-permute-done.4.grp_a.from_a
  20.2 0.4 %collective-permute-done.5.grp_b.from_b = f32[6,48,128]{2,1,0:T(8,128)S(1)} collective-permute-done((f32[6,48,128]{2,1,0:T(8,128)S(1)}, f32[6,48,128]{2,1,0:T(8,128)S(1)}, u32[]{:S(2)}, u32[]{:S(2)}) %collective-permute-start.5) | collective-permute-done | bytes 147488 | tf_op jit(solution)/shard_map/ppermute | solution.py:453
  20.6 4.4 %collective-permute-start.8 = (f32[6,16,128]{2,1,0:T(8,128)S(1)}, f32[6,16,128]{2,1,0:T(8,128)S(1)}, u32[]{:S(2)}, u32[]{:S(2)}) collective-permute-start(f32[6,16,128]{2,1,0:T(8,128)S(1)} %get-tuple-element.54), channel_id=1, source_target_pairs={{4,8},{8,4},{12,16},{16,12},{20,24},{24,20},{5,9},{9,5},{13,17},{1... | collective-permute-start | bytes 147464 | tf_op jit(solution)/shard_map/ppermute | solution.py:453
  25.0 0.6 %collective-permute-start.9 = (f32[6,16,128]{2,1,0:T(8,128)S(1)}, f32[6,16,128]{2,1,0:T(8,128)S(1)}, u32[]{:S(2)}, u32[]{:S(2)}) collective-permute-start(f32[6,16,128]{2,1,0:T(8,128)S(1)} %get-tuple-element.55), channel_id=1, source_target_pairs={{0,4},{4,0},{8,12},{12,8},{16,20},{20,16},{24,28},{28,24},{1,5},{5... | collective-permute-start | bytes 147464 | tf_op jit(solution)/shard_map/ppermute | solution.py:453
  25.6 1.5 %assemble_nodes.1 = (f32[6,512,128]{2,1,0:T(8,128)S(1)}, bf16[3,512,128]{2,1,0:T(8,128)(2,1)}) custom-call(bf16[512,256]{1,0:T(8,128)(2,1)S(1)} %get-tuple-element.29.count, bf16[768,256]{1,0:T(8,128)(2,1)S(1)} %get-tuple-element.43.stress, f32[128,1536]{1,0:T(8,128)S(1)} %get-tuple-element.40.free_t, ...), custom_call_target="tpu_custom_call" | custom-call | flops 400000000 | bytes 2000000 | tf_op jit(solution)/shard_map/assemble_nodes/pallas_call | solution.py:609
  27.1 0.6 %collective-permute-done.6.sub_a = f32[6,64,128]{2,1,0:T(8,128)S(1)} collective-permute-done((f32[6,64,128]{2,1,0:T(8,128)S(1)}, f32[6,64,128]{2,1,0:T(8,128)S(1)}, u32[]{:S(2)}, u32[]{:S(2)}) %collective-permute-start.6) | collective-permute-done | bytes 196640 | tf_op jit(solution)/shard_map/ppermute | solution.py:453
  27.7 0.0 collective-permute-done.7.sub_b
  27.7 0.0 collective-permute-done.8.edge_b
  27.7 1.5 %collective-permute-done.9.edge_a = f32[6,16,128]{2,1,0:T(8,128)S(1)} collective-permute-done((f32[6,16,128]{2,1,0:T(8,128)S(1)}, f32[6,16,128]{2,1,0:T(8,128)S(1)}, u32[]{:S(2)}, u32[]{:S(2)}) %collective-permute-start.9) | collective-permute-done | bytes 49184 | tf_op jit(solution)/shard_map/ppermute | solution.py:453
  29.2 1.2 %add_last.1 = bf16[6,512,128]{2,1,0:T(8,128)(2,1)} custom-call(bf16[512,256]{1,0:T(8,128)(2,1)S(1)} %get-tuple-element.49.placing, f32[6,512,128]{2,1,0:T(8,128)S(1)} %get-tuple-element.50.partial, f32[512,128]{1,0:T(8,128)S(1)} %get-tuple-element.51.inverse_volume, f32[6,64,128]{2,1,0:T(8,128)S(1)} %collective-permute-done.6.sub_a, ...), custom_call_target="tpu_custom_call" | custom-call | flops 400000000 | bytes 3000000 | tf_op jit(solution)/shard_map/add_last/pallas_call | solution.py:618
  (3 shorter events, 0.0 us)
Async XLA Ops:
  0.6 7.0 %collective-permute-start = (f32[24,128]{1,0:T(8,128)}, f32[24,128]{1,0:T(8,128)S(1)}, u32[]{:S(2)}, u32[]{:S(2)}) collective-permute-start(f32[24,128]{1,0:T(8,128)} %refs_6_.1), channel_id=1, source_target_pairs={{4,8},{8,4},{12,16},{16,12},{20,24},{24,20},{5,9},{9,5},{13,17},{1... | collective-permute-start | bytes 36872 | tf_op jit(solution)/shard_map/ppermute | solution.py:453
  4.0 4.0 %collective-permute-start.1 = (f32[24,128]{1,0:T(8,128)}, f32[24,128]{1,0:T(8,128)S(1)}, u32[]{:S(2)}, u32[]{:S(2)}) collective-permute-start(f32[24,128]{1,0:T(8,128)} %refs_6_.1), channel_id=1, source_target_pairs={{0,4},{4,0},{8,12},{12,8},{16,20},{20,16},{24,28},{28,24},{1,5},{5... | collective-permute-start | bytes 36872 | tf_op jit(solution)/shard_map/ppermute | solution.py:453
  7.9 4.0 %collective-permute-start.2 = (f32[72,128]{1,0:T(8,128)S(1)}, f32[72,128]{1,0:T(8,128)S(1)}, u32[]{:S(2)}, u32[]{:S(2)}) collective-permute-start(f32[72,128]{1,0:T(8,128)S(1)} %join_blocks.2.refs_0_), channel_id=1, source_target_pairs={{0,2},{1,3},{2,0},{3,1},{4,6},{5,7},{6,4},{7,5},{8,10},{9,11},{10,... | collective-permute-start | bytes 110600 | tf_op jit(solution)/shard_map/ppermute | solution.py:479
  11.9 1.3 %collective-permute-start.3 = (f32[144,128]{1,0:T(8,128)S(1)}, f32[144,128]{1,0:T(8,128)S(1)}, u32[]{:S(2)}, u32[]{:S(2)}) collective-permute-start(f32[144,128]{1,0:T(8,128)S(1)} %join_blocks.3.near), channel_id=1, source_target_pairs={{0,1},{1,0},{2,3},{3,2},{4,5},{5,4},{6,7},{7,6},{8,9},{9,8},{10,11... | collective-permute-start | bytes 221192 | tf_op jit(solution)/shard_map/ppermute | solution.py:479
  13.9 6.3 %collective-permute-start.4 = (f32[6,48,128]{2,1,0:T(8,128)S(1)}, f32[6,48,128]{2,1,0:T(8,128)S(1)}, u32[]{:S(2)}, u32[]{:S(2)}) collective-permute-start(f32[6,48,128]{2,1,0:T(8,128)S(1)} %get-tuple-element.46.grp_a), channel_id=1, source_target_pairs={{0,1},{1,0},{2,3},{3,2},{4,5},{5,4},{6,7},{7,6},{8,9},{9,8},{10,11... | collective-permute-start | bytes 442376 | tf_op jit(solution)/shard_map/ppermute | solution.py:453
  14.1 6.5 %collective-permute-start.5 = (f32[6,48,128]{2,1,0:T(8,128)S(1)}, f32[6,48,128]{2,1,0:T(8,128)S(1)}, u32[]{:S(2)}, u32[]{:S(2)}) collective-permute-start(f32[6,48,128]{2,1,0:T(8,128)S(1)} %get-tuple-element.47.grp_b), channel_id=1, source_target_pairs={{1,2},{2,1},{5,6},{6,5},{9,10},{10,9},{13,14},{14,13},{17,18},{18,... | collective-permute-start | bytes 442376 | tf_op jit(solution)/shard_map/ppermute | solution.py:453
  16.6 11.2 %collective-permute-start.6 = (f32[6,64,128]{2,1,0:T(8,128)S(1)}, f32[6,64,128]{2,1,0:T(8,128)S(1)}, u32[]{:S(2)}, u32[]{:S(2)}) collective-permute-start(f32[6,64,128]{2,1,0:T(8,128)S(1)} %get-tuple-element.52), channel_id=1, source_target_pairs={{0,4},{4,0},{8,12},{12,8},{16,20},{20,16},{24,28},{28,24},{1,5},{5... | collective-permute-start | bytes 589832 | tf_op jit(solution)/shard_map/ppermute | solution.py:453
  18.2 9.5 %collective-permute-start.7 = (f32[6,64,128]{2,1,0:T(8,128)S(1)}, f32[6,64,128]{2,1,0:T(8,128)S(1)}, u32[]{:S(2)}, u32[]{:S(2)}) collective-permute-start(f32[6,64,128]{2,1,0:T(8,128)S(1)} %get-tuple-element.53), channel_id=1, source_target_pairs={{4,8},{8,4},{12,16},{16,12},{20,24},{24,20},{5,9},{9,5},{13,17},{1... | collective-permute-start | bytes 589832 | tf_op jit(solution)/shard_map/ppermute | solution.py:453
  20.6 7.1 %collective-permute-start.8 = (f32[6,16,128]{2,1,0:T(8,128)S(1)}, f32[6,16,128]{2,1,0:T(8,128)S(1)}, u32[]{:S(2)}, u32[]{:S(2)}) collective-permute-start(f32[6,16,128]{2,1,0:T(8,128)S(1)} %get-tuple-element.54), channel_id=1, source_target_pairs={{4,8},{8,4},{12,16},{16,12},{20,24},{24,20},{5,9},{9,5},{13,17},{1... | collective-permute-start | bytes 147464 | tf_op jit(solution)/shard_map/ppermute | solution.py:453
  25.0 4.2 %collective-permute-start.9 = (f32[6,16,128]{2,1,0:T(8,128)S(1)}, f32[6,16,128]{2,1,0:T(8,128)S(1)}, u32[]{:S(2)}, u32[]{:S(2)}) collective-permute-start(f32[6,16,128]{2,1,0:T(8,128)S(1)} %get-tuple-element.55), channel_id=1, source_target_pairs={{0,4},{4,0},{8,12},{12,8},{16,20},{20,16},{24,28},{28,24},{1,5},{5... | collective-permute-start | bytes 147464 | tf_op jit(solution)/shard_map/ppermute | solution.py:453

commit v16 on v15

--- a/solution.py
+++ b/solution.py
@@ -15,6 +15,7 @@
 COMPS = 6
 LANES = 128
 TERM = 32
+SPARE = 8
 TERMS = ((0, 0), (0, 1), (0, 2), (1, 0), (1, 1), (2, 0))
 
 POISSON = 0.3
@@ -280,7 +281,7 @@
         sides = jnp.concatenate([jnp.where(live, x, 0.0).astype(BF16) for x in sides], axis=1)
         result = dot(inverse[p], sides)
         for side in range(2):
-            solved[side] = jnp.where(live, result[:, side * LANES : (side + 1) * LANES], 0.0)
+            solved[side, :panel_rows, :] = jnp.where(live, result[:, side * LANES : (side + 1) * LANES], 0.0)
         for c in range(3):
             cols = slice(c * nodes + p * panel_size, c * nodes + (p + 1) * panel_size)
             free_t[:, cols] = solved[0, pl.ds(c, panel_size, stride=3), :].T
@@ -395,18 +396,17 @@
 def finish_kernel(
     placing, partial, inverse_volume, sub_a, sub_b, edge_b, edge_a, out, received, nodal, sems
 ):
-    for i in range(COMPS):
-        cols = slice(i * LANES, (i + 1) * LANES)
-        late = jnp.concatenate([sub_b[i], edge_a[i], edge_b[i]], axis=0)
-        first, second = split_two(late)
-        received[:NIS, cols] = sub_a[i].astype(BF16)
-        received[NIS : NIS + LATE, cols] = first
-        received[NIS + LATE :, cols] = second
     scale = inverse_volume[...]
     copies = []
     for i in range(0, COMPS, 2):
-        cols = slice(i * LANES, (i + 2) * LANES)
-        added = dot(placing[...], received[:, cols])
+        for k in (i, i + 1):
+            cols = slice(k * LANES, (k + 1) * LANES)
+            late = jnp.concatenate([sub_b[k], edge_a[k], edge_b[k]], axis=0)
+            first, second = split_two(late)
+            received[:NIS, cols] = sub_a[k].astype(BF16)
+            received[NIS : NIS + LATE, cols] = first
+            received[NIS + LATE :, cols] = second
+        added = dot(placing[...], received[:, i * LANES : (i + 2) * LANES])
         nodal[i] = ((partial[i] + added[:, :LANES]) * scale).astype(BF16)
         nodal[i + 1] = ((partial[i + 1] + added[:, LANES:]) * scale).astype(BF16)
         copy = pltpu.make_async_copy(nodal.at[pl.ds(i, 2)], out.at[pl.ds(i, 2)], sems.at[i // 2])
@@ -559,8 +559,8 @@
         ),
         vmem(6),
         (
-            pltpu.VMEM((dofs, cases), F32),
-            pltpu.VMEM((2, panel_inv.shape[1], LANES), F32),
+            pltpu.VMEM((dofs + SPARE, cases), F32),
+            pltpu.VMEM((2, panel_inv.shape[1] + SPARE, LANES), F32),
             pltpu.VMEM((TERM, dofs), F32),
             pltpu.VMEM((COMPS, max(first, TERM), LANES), F32),
         ),

time: 30.8 us -> 30.8 us (level)
  no operation moved by 1% of the time
where the time goes in v16:
time: 30.8 us; the launch traced here: 30.4 us
  starting transfers between devices  16.8 us (55%)
  Pallas kernels  8.34 us (27%)
  waiting for transfers between devices  4.53 us (15%)
  between operations  0.72 us (2%)
    ppermute x8, starting transfers between devices, exchange(): return lax.ppermute(block, axis, pairs)  16.3 us
    ppermute x8, waiting for transfers between devices, exchange(): return lax.ppermute(block, axis, pairs)  2.83 us
    pallas_call x1, Pallas kernels, shards(): call(prepare_panels, 'prepare_panels', (array((cases, dofs)), array((2 *...  2.15 us
    pallas_call x1, Pallas kernels, shards(): call(lists, 'prepare_lists', (array(coarse.shape), array(panel_nodes.shap...  1.93 us
    ppermute x2, waiting for transfers between devices, gather_near(): parts = [block, lax.ppermute(block, 'grp', pairs)]  1.71 us
    pallas_call x1, Pallas kernels, shards(): call(partial_kernel, 'assemble_nodes', (array((COMPS, nodes, cases)), arr...  1.46 us
    pallas_call x1, Pallas kernels, shards(): call(finish_kernel, 'add_last', (array((COMPS, nodes, cases), BF16),), vm...  1.21 us
    pallas_call x1, Pallas kernels, shards(): call(stress_kernel, 'stress_of_loads', (array((COMPS, cases - first, LANE...  0.81 us
  transfers between devices with their start and end apart: 10, of which 6 were waited for; matrix products, arithmetic and copies ran while one was open for 0% of the time, Pallas kernels for 21%

profile of v16, /device:TPU:10, one launch (start us, length us, event | category | flops | bytes accessed | tf_op | source)
XLA Modules:
  0.0 30.4 jit_solution(2387629286672364362)
XLA Ops:
  0.6 3.3 %collective-permute-start = (f32[24,128]{1,0:T(8,128)}, f32[24,128]{1,0:T(8,128)S(1)}, u32[]{:S(2)}, u32[]{:S(2)}) collective-permute-start(f32[24,128]{1,0:T(8,128)} %refs_6_.1), channel_id=1, source_target_pairs={{4,8},{8,4},{12,16},{16,12},{20,24},{24,20},{5,9},{9,5},{13,17},{1... | collective-permute-start | bytes 36872 | tf_op jit(solution)/shard_map/ppermute | solution.py:453
  4.0 1.7 %collective-permute-start.1 = (f32[24,128]{1,0:T(8,128)}, f32[24,128]{1,0:T(8,128)S(1)}, u32[]{:S(2)}, u32[]{:S(2)}) collective-permute-start(f32[24,128]{1,0:T(8,128)} %refs_6_.1), channel_id=1, source_target_pairs={{0,4},{4,0},{8,12},{12,8},{16,20},{20,16},{24,28},{28,24},{1,5},{5... | collective-permute-start | bytes 36872 | tf_op jit(solution)/shard_map/ppermute | solution.py:453
  5.7 1.9 %prepare_lists.1 = (f32[24,128]{1,0:T(8,128)S(1)}, s32[1,4]{1,0:T(1,128)S(1)}, bf16[24,1536]{1,0:T(8,128)(2,1)S(1)}, bf16[3,512,128]{2,1,0:T(8,128)(2,1)S(1)}, b...) custom-call(s32[1,24]{1,0:T(1,128)} %refs_0_.1, ...), custom_call_target="tpu_custom_call" | custom-call | flops 100000000 | bytes 4000000 | tf_op jit(solution)/shard_map/prepare_lists/pallas_call | solution.py:504
  7.6 0.0 collective-permute-done.refs_1_
  7.6 0.3 %collective-permute-done.1.refs_2_ = f32[24,128]{1,0:T(8,128)S(1)} collective-permute-done((f32[24,128]{1,0:T(8,128)}, f32[24,128]{1,0:T(8,128)S(1)}, u32[]{:S(2)}, u32[]{:S(2)}) %collective-permute-start.1) | collective-permute-done | bytes 12320 | tf_op jit(solution)/shard_map/ppermute | solution.py:453
  7.9 0.5 %collective-permute-start.2 = (f32[72,128]{1,0:T(8,128)S(1)}, f32[72,128]{1,0:T(8,128)S(1)}, u32[]{:S(2)}, u32[]{:S(2)}) collective-permute-start(f32[72,128]{1,0:T(8,128)S(1)} %join_blocks.2.refs_0_), channel_id=1, source_target_pairs={{0,2},{1,3},{2,0},{3,1},{4,6},{5,7},{6,4},{7,5},{8,10},{9,11},{10,... | collective-permute-start | bytes 110600 | tf_op jit(solution)/shard_map/ppermute | solution.py:479
  8.5 2.1 %prepare_panels.1 = (f32[128,1536]{1,0:T(8,128)S(1)}, bf16[256,1536]{1,0:T(8,128)(2,1)S(1)}, f32[6,64,128]{2,1,0:T(8,128)S(1)}, bf16[256,768]{1,0:T(8,128)(2,1)S(1)}) custom-call(s32[1,4]{1,0:T(1,128)S(1)} %get-tuple-element.32.panel_v, bf16[24,1536]{1,0:T(8,128)(2,1)S(1)} %get-tuple-element.33.coupling_v, ...), custom_call_target="tpu_custom_call" | custom-call | flops 400000000 | bytes 4000000 | tf_op jit(solution)/shard_map/prepare_panels/pallas_call | solution.py:551
  10.6 1.3 %collective-permute-done.2.refs_1_ = f32[72,128]{1,0:T(8,128)S(1)} collective-permute-done((f32[72,128]{1,0:T(8,128)S(1)}, f32[72,128]{1,0:T(8,128)S(1)}, u32[]{:S(2)}, u32[]{:S(2)}) %collective-permute-start.2) | collective-permute-done | bytes 36896 | tf_op jit(solution)/shard_map/ppermute | solution.py:479
  11.9 0.0 collective-permute-start.3
  11.9 0.8 %stress_of_loads.1.stress_rest = f32[6,64,128]{2,1,0:T(8,128)S(1)} custom-call(f32[128,1536]{1,0:T(8,128)S(1)} %get-tuple-element.40.free_t, bf16[512,1024]{1,0:T(8,128)(2,1)S(1)} %get-tuple-element.36.onehot, f32[144,8,128]{2,1,0:T(8,128)S(1)} %get-tuple-element.37.scaled), custom_call_target="tpu_custom_call" | custom-call | flops 400000000 | bytes 4000000 | tf_op jit(solution)/shard_map/stress_of_loads/pallas_call | solution.py:570
  12.7 0.4 %collective-permute-done.3.across = f32[144,128]{1,0:T(8,128)S(1)} collective-permute-done((f32[144,128]{1,0:T(8,128)S(1)}, f32[144,128]{1,0:T(8,128)S(1)}, u32[]{:S(2)}, u32[]{:S(2)}) %collective-permute-start.3) | collective-permute-done | bytes 73760 | tf_op jit(solution)/shard_map/ppermute | solution.py:479
  13.2 0.8 %stress_and_rows.1 = (bf16[128,256]{1,0:T(8,128)(2,1)S(1)}, bf16[768,256]{1,0:T(8,128)(2,1)S(1)}, f32[6,64,128]{2,1,0:T(8,128)S(1)}, f32[6,64,128]{2,1,0:T(8,128...) custom-call(f32[144,128]{1,0:T(8,128)S(1)} %join_blocks.3.near, ...), custom_call_target="tpu_custom_call" | custom-call | flops 300000000 | bytes 3000000 | tf_op jit(solution)/shard_map/stress_and_rows/pallas_call | solution.py:581
  13.9 0.2 collective-permute-start.4
  14.1 2.4 %collective-permute-start.5 = (f32[6,48,128]{2,1,0:T(8,128)S(1)}, f32[6,48,128]{2,1,0:T(8,128)S(1)}, u32[]{:S(2)}, u32[]{:S(2)}) collective-permute-start(f32[6,48,128]{2,1,0:T(8,128)S(1)} %get-tuple-element.47.grp_b), channel_id=1, source_target_pairs={{1,2},{2,1},{5,6},{6,5},{9,10},{10,9},{13,14},{14,13},{17,18},{18,... | collective-permute-start | bytes 442376 | tf_op jit(solution)/shard_map/ppermute | solution.py:453
  16.6 1.7 %collective-permute-start.6 = (f32[6,64,128]{2,1,0:T(8,128)S(1)}, f32[6,64,128]{2,1,0:T(8,128)S(1)}, u32[]{:S(2)}, u32[]{:S(2)}) collective-permute-start(f32[6,64,128]{2,1,0:T(8,128)S(1)} %get-tuple-element.52), channel_id=1, source_target_pairs={{0,4},{4,0},{8,12},{12,8},{16,20},{20,16},{24,28},{28,24},{1,5},{5... | collective-permute-start | bytes 589832 | tf_op jit(solution)/shard_map/ppermute | solution.py:453
  18.2 1.9 %collective-permute-start.7 = (f32[6,64,128]{2,1,0:T(8,128)S(1)}, f32[6,64,128]{2,1,0:T(8,128)S(1)}, u32[]{:S(2)}, u32[]{:S(2)}) collective-permute-start(f32[6,64,128]{2,1,0:T(8,128)S(1)} %get-tuple-element.53), channel_id=1, source_target_pairs={{4,8},{8,4},{12,16},{16,12},{20,24},{24,20},{5,9},{9,5},{13,17},{1... | collective-permute-start | bytes 589832 | tf_op jit(solution)/shard_map/ppermute | solution.py:453
  20.2 0.0 collective-permute-done.4.grp_a.from_a
  20.2 0.4 %collective-permute-done.5.grp_b.from_b = f32[6,48,128]{2,1,0:T(8,128)S(1)} collective-permute-done((f32[6,48,128]{2,1,0:T(8,128)S(1)}, f32[6,48,128]{2,1,0:T(8,128)S(1)}, u32[]{:S(2)}, u32[]{:S(2)}) %collective-permute-start.5) | collective-permute-done | bytes 147488 | tf_op jit(solution)/shard_map/ppermute | solution.py:453
  20.6 4.4 %collective-permute-start.8 = (f32[6,16,128]{2,1,0:T(8,128)S(1)}, f32[6,16,128]{2,1,0:T(8,128)S(1)}, u32[]{:S(2)}, u32[]{:S(2)}) collective-permute-start(f32[6,16,128]{2,1,0:T(8,128)S(1)} %get-tuple-element.54), channel_id=1, source_target_pairs={{4,8},{8,4},{12,16},{16,12},{20,24},{24,20},{5,9},{9,5},{13,17},{1... | collective-permute-start | bytes 147464 | tf_op jit(solution)/shard_map/ppermute | solution.py:453
  25.0 0.6 %collective-permute-start.9 = (f32[6,16,128]{2,1,0:T(8,128)S(1)}, f32[6,16,128]{2,1,0:T(8,128)S(1)}, u32[]{:S(2)}, u32[]{:S(2)}) collective-permute-start(f32[6,16,128]{2,1,0:T(8,128)S(1)} %get-tuple-element.55), channel_id=1, source_target_pairs={{0,4},{4,0},{8,12},{12,8},{16,20},{20,16},{24,28},{28,24},{1,5},{5... | collective-permute-start | bytes 147464 | tf_op jit(solution)/shard_map/ppermute | solution.py:453
  25.6 1.5 %assemble_nodes.1 = (f32[6,512,128]{2,1,0:T(8,128)S(1)}, bf16[3,512,128]{2,1,0:T(8,128)(2,1)}) custom-call(bf16[512,256]{1,0:T(8,128)(2,1)S(1)} %get-tuple-element.29.count, bf16[768,256]{1,0:T(8,128)(2,1)S(1)} %get-tuple-element.43.stress, f32[128,1536]{1,0:T(8,128)S(1)} %get-tuple-element.40.free_t, ...), custom_call_target="tpu_custom_call" | custom-call | flops 400000000 | bytes 2000000 | tf_op jit(solution)/shard_map/assemble_nodes/pallas_call | solution.py:609
  27.1 0.6 %collective-permute-done.6.sub_a = f32[6,64,128]{2,1,0:T(8,128)S(1)} collective-permute-done((f32[6,64,128]{2,1,0:T(8,128)S(1)}, f32[6,64,128]{2,1,0:T(8,128)S(1)}, u32[]{:S(2)}, u32[]{:S(2)}) %collective-permute-start.6) | collective-permute-done | bytes 196640 | tf_op jit(solution)/shard_map/ppermute | solution.py:453
  27.7 0.0 collective-permute-done.7.sub_b
  27.7 0.0 collective-permute-done.8.edge_b
  27.7 1.5 %collective-permute-done.9.edge_a = f32[6,16,128]{2,1,0:T(8,128)S(1)} collective-permute-done((f32[6,16,128]{2,1,0:T(8,128)S(1)}, f32[6,16,128]{2,1,0:T(8,128)S(1)}, u32[]{:S(2)}, u32[]{:S(2)}) %collective-permute-start.9) | collective-permute-done | bytes 49184 | tf_op jit(solution)/shard_map/ppermute | solution.py:453
  29.2 1.2 %add_last.1 = bf16[6,512,128]{2,1,0:T(8,128)(2,1)} custom-call(bf16[512,256]{1,0:T(8,128)(2,1)S(1)} %get-tuple-element.49.placing, f32[6,512,128]{2,1,0:T(8,128)S(1)} %get-tuple-element.50.partial, f32[512,128]{1,0:T(8,128)S(1)} %get-tuple-element.51.inverse_volume, f32[6,64,128]{2,1,0:T(8,128)S(1)} %collective-permute-done.6.sub_a, ...), custom_call_target="tpu_custom_call" | custom-call | flops 400000000 | bytes 3000000 | tf_op jit(solution)/shard_map/add_last/pallas_call | solution.py:618
  (3 shorter events, 0.0 us)
Async XLA Ops:
  0.6 7.0 %collective-permute-start = (f32[24,128]{1,0:T(8,128)}, f32[24,128]{1,0:T(8,128)S(1)}, u32[]{:S(2)}, u32[]{:S(2)}) collective-permute-start(f32[24,128]{1,0:T(8,128)} %refs_6_.1), channel_id=1, source_target_pairs={{4,8},{8,4},{12,16},{16,12},{20,24},{24,20},{5,9},{9,5},{13,17},{1... | collective-permute-start | bytes 36872 | tf_op jit(solution)/shard_map/ppermute | solution.py:453
  4.0 4.0 %collective-permute-start.1 = (f32[24,128]{1,0:T(8,128)}, f32[24,128]{1,0:T(8,128)S(1)}, u32[]{:S(2)}, u32[]{:S(2)}) collective-permute-start(f32[24,128]{1,0:T(8,128)} %refs_6_.1), channel_id=1, source_target_pairs={{0,4},{4,0},{8,12},{12,8},{16,20},{20,16},{24,28},{28,24},{1,5},{5... | collective-permute-start | bytes 36872 | tf_op jit(solution)/shard_map/ppermute | solution.py:453
  7.9 4.0 %collective-permute-start.2 = (f32[72,128]{1,0:T(8,128)S(1)}, f32[72,128]{1,0:T(8,128)S(1)}, u32[]{:S(2)}, u32[]{:S(2)}) collective-permute-start(f32[72,128]{1,0:T(8,128)S(1)} %join_blocks.2.refs_0_), channel_id=1, source_target_pairs={{0,2},{1,3},{2,0},{3,1},{4,6},{5,7},{6,4},{7,5},{8,10},{9,11},{10,... | collective-permute-start | bytes 110600 | tf_op jit(solution)/shard_map/ppermute | solution.py:479
  11.9 1.3 %collective-permute-start.3 = (f32[144,128]{1,0:T(8,128)S(1)}, f32[144,128]{1,0:T(8,128)S(1)}, u32[]{:S(2)}, u32[]{:S(2)}) collective-permute-start(f32[144,128]{1,0:T(8,128)S(1)} %join_blocks.3.near), channel_id=1, source_target_pairs={{0,1},{1,0},{2,3},{3,2},{4,5},{5,4},{6,7},{7,6},{8,9},{9,8},{10,11... | collective-permute-start | bytes 221192 | tf_op jit(solution)/shard_map/ppermute | solution.py:479
  13.9 6.3 %collective-permute-start.4 = (f32[6,48,128]{2,1,0:T(8,128)S(1)}, f32[6,48,128]{2,1,0:T(8,128)S(1)}, u32[]{:S(2)}, u32[]{:S(2)}) collective-permute-start(f32[6,48,128]{2,1,0:T(8,128)S(1)} %get-tuple-element.46.grp_a), channel_id=1, source_target_pairs={{0,1},{1,0},{2,3},{3,2},{4,5},{5,4},{6,7},{7,6},{8,9},{9,8},{10,11... | collective-permute-start | bytes 442376 | tf_op jit(solution)/shard_map/ppermute | solution.py:453
  14.1 6.5 %collective-permute-start.5 = (f32[6,48,128]{2,1,0:T(8,128)S(1)}, f32[6,48,128]{2,1,0:T(8,128)S(1)}, u32[]{:S(2)}, u32[]{:S(2)}) collective-permute-start(f32[6,48,128]{2,1,0:T(8,128)S(1)} %get-tuple-element.47.grp_b), channel_id=1, source_target_pairs={{1,2},{2,1},{5,6},{6,5},{9,10},{10,9},{13,14},{14,13},{17,18},{18,... | collective-permute-start | bytes 442376 | tf_op jit(solution)/shard_map/ppermute | solution.py:453
  16.6 11.2 %collective-permute-start.6 = (f32[6,64,128]{2,1,0:T(8,128)S(1)}, f32[6,64,128]{2,1,0:T(8,128)S(1)}, u32[]{:S(2)}, u32[]{:S(2)}) collective-permute-start(f32[6,64,128]{2,1,0:T(8,128)S(1)} %get-tuple-element.52), channel_id=1, source_target_pairs={{0,4},{4,0},{8,12},{12,8},{16,20},{20,16},{24,28},{28,24},{1,5},{5... | collective-permute-start | bytes 589832 | tf_op jit(solution)/shard_map/ppermute | solution.py:453
  18.2 9.5 %collective-permute-start.7 = (f32[6,64,128]{2,1,0:T(8,128)S(1)}, f32[6,64,128]{2,1,0:T(8,128)S(1)}, u32[]{:S(2)}, u32[]{:S(2)}) collective-permute-start(f32[6,64,128]{2,1,0:T(8,128)S(1)} %get-tuple-element.53), channel_id=1, source_target_pairs={{4,8},{8,4},{12,16},{16,12},{20,24},{24,20},{5,9},{9,5},{13,17},{1... | collective-permute-start | bytes 589832 | tf_op jit(solution)/shard_map/ppermute | solution.py:453
  20.6 7.1 %collective-permute-start.8 = (f32[6,16,128]{2,1,0:T(8,128)S(1)}, f32[6,16,128]{2,1,0:T(8,128)S(1)}, u32[]{:S(2)}, u32[]{:S(2)}) collective-permute-start(f32[6,16,128]{2,1,0:T(8,128)S(1)} %get-tuple-element.54), channel_id=1, source_target_pairs={{4,8},{8,4},{12,16},{16,12},{20,24},{24,20},{5,9},{9,5},{13,17},{1... | collective-permute-start | bytes 147464 | tf_op jit(solution)/shard_map/ppermute | solution.py:453
  25.0 4.2 %collective-permute-start.9 = (f32[6,16,128]{2,1,0:T(8,128)S(1)}, f32[6,16,128]{2,1,0:T(8,128)S(1)}, u32[]{:S(2)}, u32[]{:S(2)}) collective-permute-start(f32[6,16,128]{2,1,0:T(8,128)S(1)} %get-tuple-element.55), channel_id=1, source_target_pairs={{0,4},{4,0},{8,12},{12,8},{16,20},{20,16},{24,28},{28,24},{1,5},{5... | collective-permute-start | bytes 147464 | tf_op jit(solution)/shard_map/ppermute | solution.py:453

commit v17 on v16

--- a/solution.py
+++ b/solution.py
@@ -123,12 +123,10 @@
     volume,
     coarse,
     panel_nodes,
-    coupling,
     force,
     panel_inv,
     own,
     panel_v,
-    coupling_v,
     force_v,
     inverse,
     select,
@@ -158,7 +156,6 @@
             (volume, volume_v),
             (coarse, own),
             (panel_nodes, panel_v),
-            (coupling, coupling_v),
             (force, force_v),
             (panel_inv, inverse),
         ],
@@ -245,8 +242,8 @@
 
 
 def prepare_panels(
+    coupling_v,
     panel_v,
-    coupling_v,
     force_v,
     inverse,
     onehot,
@@ -507,7 +504,6 @@
         (
             array(coarse.shape),
             array(panel_nodes.shape, jnp.int32),
-            array((q, dofs), BF16),
             array((3, nodes, cases), BF16),
             array(panel_inv.shape, BF16),
             array((TERM, 3 * LANES), BF16),
@@ -519,7 +515,7 @@
             array((nodes, 2 * LANES), BF16),
             array((nodes, LANES)),
         ),
-        hbm(11),
+        hbm(10),
         (
             pltpu.VMEM((1, q), jnp.int32),
             pltpu.VMEM(connect.shape, jnp.int32),
@@ -528,7 +524,7 @@
             pltpu.VMEM((1, LANES), F32),
             pltpu.VMEM((nodes // LANES, LANES), F32),
             pltpu.VMEM((8, 2 * LANES), F32),
-            pltpu.SemaphoreType.DMA((11,)),
+            pltpu.SemaphoreType.DMA((10,)),
         ),
         flops=100000000,
         moved=4000000,
@@ -542,7 +538,6 @@
             nodal_volume.reshape(-1, LANES),
             coarse,
             panel_nodes,
-            coupling.T,
             jnp.transpose(force, (1, 0, 2)),
             panel_inv,
         )
@@ -566,7 +561,7 @@
         ),
         flops=400000000,
         moved=4000000,
-    )(*panels, onehot, scaled)
+    )(coupling.T, *panels, onehot, scaled)
     (stress_rest,) = call(
         stress_kernel,
         "stress_of_loads",

time: 30.8 us -> 30.9 us (level)
  no operation moved by 1% of the time
where the time goes in v17:
time: 30.9 us; the launch traced here: 30.5 us
  starting transfers between devices  16.9 us (55%)
  Pallas kernels  8.32 us (27%)
  waiting for transfers between devices  4.56 us (15%)
  between operations  0.73 us (2%)
    ppermute x8, starting transfers between devices, exchange(): return lax.ppermute(block, axis, pairs)  16.4 us
    ppermute x8, waiting for transfers between devices, exchange(): return lax.ppermute(block, axis, pairs)  2.84 us
    pallas_call x1, Pallas kernels, shards(): call(prepare_panels, 'prepare_panels', (array((cases, dofs)), array((2 *...  2.13 us
    pallas_call x1, Pallas kernels, shards(): call(lists, 'prepare_lists', (array(coarse.shape), array(panel_nodes.shap...  1.91 us
    ppermute x2, waiting for transfers between devices, gather_near(): parts = [block, lax.ppermute(block, 'grp', pairs)]  1.72 us
    pallas_call x1, Pallas kernels, shards(): call(partial_kernel, 'assemble_nodes', (array((COMPS, nodes, cases)), arr...  1.47 us
    pallas_call x1, Pallas kernels, shards(): call(finish_kernel, 'add_last', (array((COMPS, nodes, cases), BF16),), vm...  1.22 us
    pallas_call x1, Pallas kernels, shards(): call(stress_kernel, 'stress_of_loads', (array((COMPS, cases - first, LANE...  0.81 us
  transfers between devices with their start and end apart: 10, of which 6 were waited for; matrix products, arithmetic and copies ran while one was open for 0% of the time, Pallas kernels for 21%

profile of v17, /device:TPU:10, one launch (start us, length us, event | category | flops | bytes accessed | tf_op | source)
XLA Modules:
  0.0 30.5 jit_solution(18424207542589208119)
XLA Ops:
  0.6 0.0 copy-start
  0.6 3.4 %collective-permute-start = (f32[24,128]{1,0:T(8,128)}, f32[24,128]{1,0:T(8,128)S(1)}, u32[]{:S(2)}, u32[]{:S(2)}) collective-permute-start(f32[24,128]{1,0:T(8,128)} %refs_6_.1), channel_id=1, source_target_pairs={{4,8},{8,4},{12,16},{16,12},{20,24},{24,20},{5,9},{9,5},{13,17},{1... | collective-permute-start | bytes 36872 | tf_op jit(solution)/shard_map/ppermute | solution.py:450
  4.1 1.7 %collective-permute-start.1 = (f32[24,128]{1,0:T(8,128)}, f32[24,128]{1,0:T(8,128)S(1)}, u32[]{:S(2)}, u32[]{:S(2)}) collective-permute-start(f32[24,128]{1,0:T(8,128)} %refs_6_.1), channel_id=1, source_target_pairs={{0,4},{4,0},{8,12},{12,8},{16,20},{20,16},{24,28},{28,24},{1,5},{5... | collective-permute-start | bytes 36872 | tf_op jit(solution)/shard_map/ppermute | solution.py:450
  5.8 1.9 %prepare_lists.1 = (f32[24,128]{1,0:T(8,128)S(1)}, s32[1,4]{1,0:T(1,128)S(1)}, bf16[3,512,128]{2,1,0:T(8,128)(2,1)S(1)}, bf16[4,384,384]{2,1,0:T(8,128)(2,1)S(1)...) custom-call(s32[1,24]{1,0:T(1,128)} %refs_0_.1, ...), custom_call_target="tpu_custom_call" | custom-call | flops 100000000 | bytes 4000000 | tf_op jit(solution)/shard_map/prepare_lists/pallas_call | solution.py:501
  7.7 0.0 collective-permute-done.refs_1_
  7.7 0.3 %collective-permute-done.1.refs_2_ = f32[24,128]{1,0:T(8,128)S(1)} collective-permute-done((f32[24,128]{1,0:T(8,128)}, f32[24,128]{1,0:T(8,128)S(1)}, u32[]{:S(2)}, u32[]{:S(2)}) %collective-permute-start.1) | collective-permute-done | bytes 12320 | tf_op jit(solution)/shard_map/ppermute | solution.py:450
  8.1 0.5 %collective-permute-start.2 = (f32[72,128]{1,0:T(8,128)S(1)}, f32[72,128]{1,0:T(8,128)S(1)}, u32[]{:S(2)}, u32[]{:S(2)}) collective-permute-start(f32[72,128]{1,0:T(8,128)S(1)} %join_blocks.2.refs_0_), channel_id=1, source_target_pairs={{0,2},{1,3},{2,0},{3,1},{4,6},{5,7},{6,4},{7,5},{8,10},{9,11},{10,... | collective-permute-start | bytes 110600 | tf_op jit(solution)/shard_map/ppermute | solution.py:476
  8.6 0.0 copy-done
  8.6 2.1 %prepare_panels.1 = (f32[128,1536]{1,0:T(8,128)S(1)}, bf16[256,1536]{1,0:T(8,128)(2,1)S(1)}, f32[6,64,128]{2,1,0:T(8,128)S(1)}, bf16[256,768]{1,0:T(8,128)(2,1)S(1)}) custom-call(bf16[24,1536]{1,0:T(8,128)(2,1)S(1)} %bitcast.7, s32[1,4]{1,0:T(1,128)S(1)} %get-tuple-element.31.panel_v, bf16[3,512,128]{2,1,0:T(8,128)(2,1)S(1)} %get-tuple-element.32.force_v, ...), custom_call_target="tpu_custom_call" | custom-call | flops 400000000 | bytes 4000000 | tf_op jit(solution)/shard_map/prepare_panels/pallas_call | solution.py:546
  10.7 1.3 %collective-permute-done.2.refs_1_ = f32[72,128]{1,0:T(8,128)S(1)} collective-permute-done((f32[72,128]{1,0:T(8,128)S(1)}, f32[72,128]{1,0:T(8,128)S(1)}, u32[]{:S(2)}, u32[]{:S(2)}) %collective-permute-start.2) | collective-permute-done | bytes 36896 | tf_op jit(solution)/shard_map/ppermute | solution.py:476
  12.0 0.0 collective-permute-start.3
  12.0 0.8 %stress_of_loads.1.stress_rest = f32[6,64,128]{2,1,0:T(8,128)S(1)} custom-call(f32[128,1536]{1,0:T(8,128)S(1)} %get-tuple-element.38.free_t, bf16[512,1024]{1,0:T(8,128)(2,1)S(1)} %get-tuple-element.34.onehot, f32[144,8,128]{2,1,0:T(8,128)S(1)} %get-tuple-element.35.scaled), custom_call_target="tpu_custom_call" | custom-call | flops 400000000 | bytes 4000000 | tf_op jit(solution)/shard_map/stress_of_loads/pallas_call | solution.py:565
  12.9 0.4 %collective-permute-done.3.across = f32[144,128]{1,0:T(8,128)S(1)} collective-permute-done((f32[144,128]{1,0:T(8,128)S(1)}, f32[144,128]{1,0:T(8,128)S(1)}, u32[]{:S(2)}, u32[]{:S(2)}) %collective-permute-start.3) | collective-permute-done | bytes 73760 | tf_op jit(solution)/shard_map/ppermute | solution.py:476
  13.3 0.8 %stress_and_rows.1 = (bf16[128,256]{1,0:T(8,128)(2,1)S(1)}, bf16[768,256]{1,0:T(8,128)(2,1)S(1)}, f32[6,64,128]{2,1,0:T(8,128)S(1)}, f32[6,64,128]{2,1,0:T(8,128...) custom-call(f32[144,128]{1,0:T(8,128)S(1)} %join_blocks.3.near, ...), custom_call_target="tpu_custom_call" | custom-call | flops 300000000 | bytes 3000000 | tf_op jit(solution)/shard_map/stress_and_rows/pallas_call | solution.py:576
  14.1 0.2 collective-permute-start.4
  14.3 2.4 %collective-permute-start.5 = (f32[6,48,128]{2,1,0:T(8,128)S(1)}, f32[6,48,128]{2,1,0:T(8,128)S(1)}, u32[]{:S(2)}, u32[]{:S(2)}) collective-permute-start(f32[6,48,128]{2,1,0:T(8,128)S(1)} %get-tuple-element.45.grp_b), channel_id=1, source_target_pairs={{1,2},{2,1},{5,6},{6,5},{9,10},{10,9},{13,14},{14,13},{17,18},{18,... | collective-permute-start | bytes 442376 | tf_op jit(solution)/shard_map/ppermute | solution.py:450
  16.7 1.7 %collective-permute-start.6 = (f32[6,64,128]{2,1,0:T(8,128)S(1)}, f32[6,64,128]{2,1,0:T(8,128)S(1)}, u32[]{:S(2)}, u32[]{:S(2)}) collective-permute-start(f32[6,64,128]{2,1,0:T(8,128)S(1)} %get-tuple-element.50), channel_id=1, source_target_pairs={{0,4},{4,0},{8,12},{12,8},{16,20},{20,16},{24,28},{28,24},{1,5},{5... | collective-permute-start | bytes 589832 | tf_op jit(solution)/shard_map/ppermute | solution.py:450
  18.4 1.9 %collective-permute-start.7 = (f32[6,64,128]{2,1,0:T(8,128)S(1)}, f32[6,64,128]{2,1,0:T(8,128)S(1)}, u32[]{:S(2)}, u32[]{:S(2)}) collective-permute-start(f32[6,64,128]{2,1,0:T(8,128)S(1)} %get-tuple-element.51), channel_id=1, source_target_pairs={{4,8},{8,4},{12,16},{16,12},{20,24},{24,20},{5,9},{9,5},{13,17},{1... | collective-permute-start | bytes 589832 | tf_op jit(solution)/shard_map/ppermute | solution.py:450
  20.3 0.0 collective-permute-done.4.grp_a.from_a
  20.3 0.4 %collective-permute-done.5.grp_b.from_b = f32[6,48,128]{2,1,0:T(8,128)S(1)} collective-permute-done((f32[6,48,128]{2,1,0:T(8,128)S(1)}, f32[6,48,128]{2,1,0:T(8,128)S(1)}, u32[]{:S(2)}, u32[]{:S(2)}) %collective-permute-start.5) | collective-permute-done | bytes 147488 | tf_op jit(solution)/shard_map/ppermute | solution.py:450
  20.8 4.4 %collective-permute-start.8 = (f32[6,16,128]{2,1,0:T(8,128)S(1)}, f32[6,16,128]{2,1,0:T(8,128)S(1)}, u32[]{:S(2)}, u32[]{:S(2)}) collective-permute-start(f32[6,16,128]{2,1,0:T(8,128)S(1)} %get-tuple-element.52), channel_id=1, source_target_pairs={{4,8},{8,4},{12,16},{16,12},{20,24},{24,20},{5,9},{9,5},{13,17},{1... | collective-permute-start | bytes 147464 | tf_op jit(solution)/shard_map/ppermute | solution.py:450
  25.2 0.6 %collective-permute-start.9 = (f32[6,16,128]{2,1,0:T(8,128)S(1)}, f32[6,16,128]{2,1,0:T(8,128)S(1)}, u32[]{:S(2)}, u32[]{:S(2)}) collective-permute-start(f32[6,16,128]{2,1,0:T(8,128)S(1)} %get-tuple-element.53), channel_id=1, source_target_pairs={{0,4},{4,0},{8,12},{12,8},{16,20},{20,16},{24,28},{28,24},{1,5},{5... | collective-permute-start | bytes 147464 | tf_op jit(solution)/shard_map/ppermute | solution.py:450
  25.8 1.5 %assemble_nodes.1 = (f32[6,512,128]{2,1,0:T(8,128)S(1)}, bf16[3,512,128]{2,1,0:T(8,128)(2,1)}) custom-call(bf16[512,256]{1,0:T(8,128)(2,1)S(1)} %get-tuple-element.28.count, bf16[768,256]{1,0:T(8,128)(2,1)S(1)} %get-tuple-element.41.stress, f32[128,1536]{1,0:T(8,128)S(1)} %get-tuple-element.38.free_t, ...), custom_call_target="tpu_custom_call" | custom-call | flops 400000000 | bytes 2000000 | tf_op jit(solution)/shard_map/assemble_nodes/pallas_call | solution.py:604
  27.2 0.6 %collective-permute-done.6.sub_a = f32[6,64,128]{2,1,0:T(8,128)S(1)} collective-permute-done((f32[6,64,128]{2,1,0:T(8,128)S(1)}, f32[6,64,128]{2,1,0:T(8,128)S(1)}, u32[]{:S(2)}, u32[]{:S(2)}) %collective-permute-start.6) | collective-permute-done | bytes 196640 | tf_op jit(solution)/shard_map/ppermute | solution.py:450
  27.8 0.0 collective-permute-done.7.sub_b
  27.8 0.0 collective-permute-done.8.edge_b
  27.8 1.5 %collective-permute-done.9.edge_a = f32[6,16,128]{2,1,0:T(8,128)S(1)} collective-permute-done((f32[6,16,128]{2,1,0:T(8,128)S(1)}, f32[6,16,128]{2,1,0:T(8,128)S(1)}, u32[]{:S(2)}, u32[]{:S(2)}) %collective-permute-start.9) | collective-permute-done | bytes 49184 | tf_op jit(solution)/shard_map/ppermute | solution.py:450
  29.3 1.2 %add_last.1 = bf16[6,512,128]{2,1,0:T(8,128)(2,1)} custom-call(bf16[512,256]{1,0:T(8,128)(2,1)S(1)} %get-tuple-element.47.placing, f32[6,512,128]{2,1,0:T(8,128)S(1)} %get-tuple-element.48.partial, f32[512,128]{1,0:T(8,128)S(1)} %get-tuple-element.49.inverse_volume, f32[6,64,128]{2,1,0:T(8,128)S(1)} %collective-permute-done.6.sub_a, ...), custom_call_target="tpu_custom_call" | custom-call | flops 400000000 | bytes 3000000 | tf_op jit(solution)/shard_map/add_last/pallas_call | solution.py:613
  (3 shorter events, 0.0 us)
Async XLA Ops:
  0.6 8.0 %copy-start = (bf16[1536,24]{0,1:T(8,128)(2,1)S(1)}, bf16[1536,24]{0,1:T(8,128)(2,1)}, u32[]{:S(2)}) copy-start(bf16[1536,24]{0,1:T(8,128)(2,1)} %param.13) | copy-start | bytes 221188
  0.6 7.1 %collective-permute-start = (f32[24,128]{1,0:T(8,128)}, f32[24,128]{1,0:T(8,128)S(1)}, u32[]{:S(2)}, u32[]{:S(2)}) collective-permute-start(f32[24,128]{1,0:T(8,128)} %refs_6_.1), channel_id=1, source_target_pairs={{4,8},{8,4},{12,16},{16,12},{20,24},{24,20},{5,9},{9,5},{13,17},{1... | collective-permute-start | bytes 36872 | tf_op jit(solution)/shard_map/ppermute | solution.py:450
  4.1 4.0 %collective-permute-start.1 = (f32[24,128]{1,0:T(8,128)}, f32[24,128]{1,0:T(8,128)S(1)}, u32[]{:S(2)}, u32[]{:S(2)}) collective-permute-start(f32[24,128]{1,0:T(8,128)} %refs_6_.1), channel_id=1, source_target_pairs={{0,4},{4,0},{8,12},{12,8},{16,20},{20,16},{24,28},{28,24},{1,5},{5... | collective-permute-start | bytes 36872 | tf_op jit(solution)/shard_map/ppermute | solution.py:450
  8.1 4.0 %collective-permute-start.2 = (f32[72,128]{1,0:T(8,128)S(1)}, f32[72,128]{1,0:T(8,128)S(1)}, u32[]{:S(2)}, u32[]{:S(2)}) collective-permute-start(f32[72,128]{1,0:T(8,128)S(1)} %join_blocks.2.refs_0_), channel_id=1, source_target_pairs={{0,2},{1,3},{2,0},{3,1},{4,6},{5,7},{6,4},{7,5},{8,10},{9,11},{10,... | collective-permute-start | bytes 110600 | tf_op jit(solution)/shard_map/ppermute | solution.py:476
  12.0 1.3 %collective-permute-start.3 = (f32[144,128]{1,0:T(8,128)S(1)}, f32[144,128]{1,0:T(8,128)S(1)}, u32[]{:S(2)}, u32[]{:S(2)}) collective-permute-start(f32[144,128]{1,0:T(8,128)S(1)} %join_blocks.3.near), channel_id=1, source_target_pairs={{0,1},{1,0},{2,3},{3,2},{4,5},{5,4},{6,7},{7,6},{8,9},{9,8},{10,11... | collective-permute-start | bytes 221192 | tf_op jit(solution)/shard_map/ppermute | solution.py:476
  14.1 6.3 %collective-permute-start.4 = (f32[6,48,128]{2,1,0:T(8,128)S(1)}, f32[6,48,128]{2,1,0:T(8,128)S(1)}, u32[]{:S(2)}, u32[]{:S(2)}) collective-permute-start(f32[6,48,128]{2,1,0:T(8,128)S(1)} %get-tuple-element.44.grp_a), channel_id=1, source_target_pairs={{0,1},{1,0},{2,3},{3,2},{4,5},{5,4},{6,7},{7,6},{8,9},{9,8},{10,11... | collective-permute-start | bytes 442376 | tf_op jit(solution)/shard_map/ppermute | solution.py:450
  14.3 6.5 %collective-permute-start.5 = (f32[6,48,128]{2,1,0:T(8,128)S(1)}, f32[6,48,128]{2,1,0:T(8,128)S(1)}, u32[]{:S(2)}, u32[]{:S(2)}) collective-permute-start(f32[6,48,128]{2,1,0:T(8,128)S(1)} %get-tuple-element.45.grp_b), channel_id=1, source_target_pairs={{1,2},{2,1},{5,6},{6,5},{9,10},{10,9},{13,14},{14,13},{17,18},{18,... | collective-permute-start | bytes 442376 | tf_op jit(solution)/shard_map/ppermute | solution.py:450
  16.7 11.2 %collective-permute-start.6 = (f32[6,64,128]{2,1,0:T(8,128)S(1)}, f32[6,64,128]{2,1,0:T(8,128)S(1)}, u32[]{:S(2)}, u32[]{:S(2)}) collective-permute-start(f32[6,64,128]{2,1,0:T(8,128)S(1)} %get-tuple-element.50), channel_id=1, source_target_pairs={{0,4},{4,0},{8,12},{12,8},{16,20},{20,16},{24,28},{28,24},{1,5},{5... | collective-permute-start | bytes 589832 | tf_op jit(solution)/shard_map/ppermute | solution.py:450
  18.4 9.5 %collective-permute-start.7 = (f32[6,64,128]{2,1,0:T(8,128)S(1)}, f32[6,64,128]{2,1,0:T(8,128)S(1)}, u32[]{:S(2)}, u32[]{:S(2)}) collective-permute-start(f32[6,64,128]{2,1,0:T(8,128)S(1)} %get-tuple-element.51), channel_id=1, source_target_pairs={{4,8},{8,4},{12,16},{16,12},{20,24},{24,20},{5,9},{9,5},{13,17},{1... | collective-permute-start | bytes 589832 | tf_op jit(solution)/shard_map/ppermute | solution.py:450
  20.8 7.1 %collective-permute-start.8 = (f32[6,16,128]{2,1,0:T(8,128)S(1)}, f32[6,16,128]{2,1,0:T(8,128)S(1)}, u32[]{:S(2)}, u32[]{:S(2)}) collective-permute-start(f32[6,16,128]{2,1,0:T(8,128)S(1)} %get-tuple-element.52), channel_id=1, source_target_pairs={{4,8},{8,4},{12,16},{16,12},{20,24},{24,20},{5,9},{9,5},{13,17},{1... | collective-permute-start | bytes 147464 | tf_op jit(solution)/shard_map/ppermute | solution.py:450
  25.2 4.2 %collective-permute-start.9 = (f32[6,16,128]{2,1,0:T(8,128)S(1)}, f32[6,16,128]{2,1,0:T(8,128)S(1)}, u32[]{:S(2)}, u32[]{:S(2)}) collective-permute-start(f32[6,16,128]{2,1,0:T(8,128)S(1)} %get-tuple-element.53), channel_id=1, source_target_pairs={{0,4},{4,0},{8,12},{12,8},{16,20},{20,16},{24,28},{28,24},{1,5},{5... | collective-permute-start | bytes 147464 | tf_op jit(solution)/shard_map/ppermute | solution.py:450

commit v18 on v17

--- a/solution.py
+++ b/solution.py
@@ -357,7 +357,7 @@
         grp_b[i] = jnp.concatenate([part[2 * NIS + NIG : EDGES], edge[1], edge[3]], axis=0)
 
 
-def edge_kernel(grp_a, grp_b, from_a, from_b, edge_b, edge_a):
+def edge_kernel(grp_a, grp_b, from_a, from_b, edge_a, edge_b):
     split = NIG + NED
     edge_a[:, :NED, :] = grp_a[:, NIG:split, :] + from_a[:, NIG:split, :]
     edge_a[:, NED:, :] = grp_b[:, NIG:split, :] + from_b[:, NIG:split, :]
@@ -391,7 +391,7 @@
 
 
 def finish_kernel(
-    placing, partial, inverse_volume, sub_a, sub_b, edge_b, edge_a, out, received, nodal, sems
+    placing, partial, inverse_volume, sub_a, sub_b, edge_a, edge_b, out, received, nodal, sems
 ):
     scale = inverse_volume[...]
     copies = []
@@ -592,15 +592,15 @@
     from_sub_a = exchange(sub_a, "sub", 0)
     from_grp_a = exchange(grp_a, "grp", 0)
     from_grp_b = exchange(grp_b, "grp", 1)
-    edge_b, edge_a = call(
+    edge_a, edge_b = call(
         edge_kernel,
         "sum_edges",
         (array((COMPS, 2 * NED, cases)), array((COMPS, 2 * NED, cases))),
         vmem(4),
     )(grp_a, grp_b, from_grp_a, from_grp_b)
     from_sub_b = exchange(sub_b, "sub", 1)
+    from_edge_a = exchange(edge_a, "sub", 0)
     from_edge_b = exchange(edge_b, "sub", 1)
-    from_edge_a = exchange(edge_a, "sub", 0)
     partial, disp = call(
         partial_kernel,
         "assemble_nodes",
@@ -623,7 +623,7 @@
         flops=400000000,
         moved=3000000,
         out_specs=hbm(1),
-    )(placing_last, partial, inverse_volume, from_sub_a, from_sub_b, from_edge_b, from_edge_a)
+    )(placing_last, partial, inverse_volume, from_sub_a, from_sub_b, from_edge_a, from_edge_b)
     return jnp.transpose(disp, (1, 0, 2)), jnp.transpose(nodal, (1, 0, 2))
 
 

time: 30.9 us -> 31.8 us (1.029)
  waiting for transfers between devices: 4.56 us -> 5.96 us
  starting transfers between devices: 16.9 us -> 16.5 us
    ppermute x8, waiting for transfers between devices: 2.84 us -> 4.24 us  [exchange(): return lax.ppermute(block, axis, pairs)]
    ppermute x8, starting transfers between devices: 16.4 us -> 16 us  [exchange(): return lax.ppermute(block, axis, pairs)]
  transfers between devices with their start and end apart: 10 -> 10, of which waited for: 6 -> 7; matrix products, arithmetic and copies ran while one was open for 0% -> 0% of each run, Pallas kernels for 21% -> 20%
where the time goes in v18:
time: 31.8 us; the launch traced here: 31.5 us
  starting transfers between devices  16.5 us (52%)
  Pallas kernels  8.33 us (26%)
  waiting for transfers between devices  5.96 us (19%)
  between operations  0.73 us (2%)
    ppermute x8, starting transfers between devices, exchange(): return lax.ppermute(block, axis, pairs)  16 us
    ppermute x8, waiting for transfers between devices, exchange(): return lax.ppermute(block, axis, pairs)  4.24 us
    pallas_call x1, Pallas kernels, shards(): call(prepare_panels, 'prepare_panels', (array((cases, dofs)), array((2 *...  2.13 us
    pallas_call x1, Pallas kernels, shards(): call(lists, 'prepare_lists', (array(coarse.shape), array(panel_nodes.shap...  1.91 us
    ppermute x2, waiting for transfers between devices, gather_near(): parts = [block, lax.ppermute(block, 'grp', pairs)]  1.72 us
    pallas_call x1, Pallas kernels, shards(): call(partial_kernel, 'assemble_nodes', (array((COMPS, nodes, cases)), arr...  1.47 us
    pallas_call x1, Pallas kernels, shards(): call(finish_kernel, 'add_last', (array((COMPS, nodes, cases), BF16),), vm...  1.22 us
    pallas_call x1, Pallas kernels, shards(): call(stress_kernel, 'stress_of_loads', (array((COMPS, cases - first, LANE...  0.81 us
  transfers between devices with their start and end apart: 10, of which 7 were waited for; matrix products, arithmetic and copies ran while one was open for 0% of the time, Pallas kernels for 20%

profile of v18, /device:TPU:10, one launch (start us, length us, event | category | flops | bytes accessed | tf_op | source)
XLA Modules:
  0.0 31.5 jit_solution(17813089590946828737)
XLA Ops:
  0.6 0.0 copy-start
  0.6 3.4 %collective-permute-start = (f32[24,128]{1,0:T(8,128)}, f32[24,128]{1,0:T(8,128)S(1)}, u32[]{:S(2)}, u32[]{:S(2)}) collective-permute-start(f32[24,128]{1,0:T(8,128)} %refs_6_.1), channel_id=1, source_target_pairs={{4,8},{8,4},{12,16},{16,12},{20,24},{24,20},{5,9},{9,5},{13,17},{1... | collective-permute-start | bytes 36872 | tf_op jit(solution)/shard_map/ppermute | solution.py:450
  4.1 1.7 %collective-permute-start.1 = (f32[24,128]{1,0:T(8,128)}, f32[24,128]{1,0:T(8,128)S(1)}, u32[]{:S(2)}, u32[]{:S(2)}) collective-permute-start(f32[24,128]{1,0:T(8,128)} %refs_6_.1), channel_id=1, source_target_pairs={{0,4},{4,0},{8,12},{12,8},{16,20},{20,16},{24,28},{28,24},{1,5},{5... | collective-permute-start | bytes 36872 | tf_op jit(solution)/shard_map/ppermute | solution.py:450
  5.8 1.9 %prepare_lists.1 = (f32[24,128]{1,0:T(8,128)S(1)}, s32[1,4]{1,0:T(1,128)S(1)}, bf16[3,512,128]{2,1,0:T(8,128)(2,1)S(1)}, bf16[4,384,384]{2,1,0:T(8,128)(2,1)S(1)...) custom-call(s32[1,24]{1,0:T(1,128)} %refs_0_.1, ...), custom_call_target="tpu_custom_call" | custom-call | flops 100000000 | bytes 4000000 | tf_op jit(solution)/shard_map/prepare_lists/pallas_call | solution.py:501
  7.7 0.0 collective-permute-done.refs_1_
  7.7 0.3 %collective-permute-done.1.refs_2_ = f32[24,128]{1,0:T(8,128)S(1)} collective-permute-done((f32[24,128]{1,0:T(8,128)}, f32[24,128]{1,0:T(8,128)S(1)}, u32[]{:S(2)}, u32[]{:S(2)}) %collective-permute-start.1) | collective-permute-done | bytes 12320 | tf_op jit(solution)/shard_map/ppermute | solution.py:450
  8.1 0.5 %collective-permute-start.2 = (f32[72,128]{1,0:T(8,128)S(1)}, f32[72,128]{1,0:T(8,128)S(1)}, u32[]{:S(2)}, u32[]{:S(2)}) collective-permute-start(f32[72,128]{1,0:T(8,128)S(1)} %join_blocks.2.refs_0_), channel_id=1, source_target_pairs={{0,2},{1,3},{2,0},{3,1},{4,6},{5,7},{6,4},{7,5},{8,10},{9,11},{10,... | collective-permute-start | bytes 110600 | tf_op jit(solution)/shard_map/ppermute | solution.py:476
  8.6 0.0 copy-done
  8.6 2.1 %prepare_panels.1 = (f32[128,1536]{1,0:T(8,128)S(1)}, bf16[256,1536]{1,0:T(8,128)(2,1)S(1)}, f32[6,64,128]{2,1,0:T(8,128)S(1)}, bf16[256,768]{1,0:T(8,128)(2,1)S(1)}) custom-call(bf16[24,1536]{1,0:T(8,128)(2,1)S(1)} %bitcast.7, s32[1,4]{1,0:T(1,128)S(1)} %get-tuple-element.31.panel_v, bf16[3,512,128]{2,1,0:T(8,128)(2,1)S(1)} %get-tuple-element.32.force_v, ...), custom_call_target="tpu_custom_call" | custom-call | flops 400000000 | bytes 4000000 | tf_op jit(solution)/shard_map/prepare_panels/pallas_call | solution.py:546
  10.7 1.3 %collective-permute-done.2.refs_1_ = f32[72,128]{1,0:T(8,128)S(1)} collective-permute-done((f32[72,128]{1,0:T(8,128)S(1)}, f32[72,128]{1,0:T(8,128)S(1)}, u32[]{:S(2)}, u32[]{:S(2)}) %collective-permute-start.2) | collective-permute-done | bytes 36896 | tf_op jit(solution)/shard_map/ppermute | solution.py:476
  12.0 0.0 collective-permute-start.3
  12.0 0.8 %stress_of_loads.1.stress_rest = f32[6,64,128]{2,1,0:T(8,128)S(1)} custom-call(f32[128,1536]{1,0:T(8,128)S(1)} %get-tuple-element.38.free_t, bf16[512,1024]{1,0:T(8,128)(2,1)S(1)} %get-tuple-element.34.onehot, f32[144,8,128]{2,1,0:T(8,128)S(1)} %get-tuple-element.35.scaled), custom_call_target="tpu_custom_call" | custom-call | flops 400000000 | bytes 4000000 | tf_op jit(solution)/shard_map/stress_of_loads/pallas_call | solution.py:565
  12.9 0.4 %collective-permute-done.3.across = f32[144,128]{1,0:T(8,128)S(1)} collective-permute-done((f32[144,128]{1,0:T(8,128)S(1)}, f32[144,128]{1,0:T(8,128)S(1)}, u32[]{:S(2)}, u32[]{:S(2)}) %collective-permute-start.3) | collective-permute-done | bytes 73760 | tf_op jit(solution)/shard_map/ppermute | solution.py:476
  13.3 0.8 %stress_and_rows.1 = (bf16[128,256]{1,0:T(8,128)(2,1)S(1)}, bf16[768,256]{1,0:T(8,128)(2,1)S(1)}, f32[6,64,128]{2,1,0:T(8,128)S(1)}, f32[6,64,128]{2,1,0:T(8,128...) custom-call(f32[144,128]{1,0:T(8,128)S(1)} %join_blocks.3.near, ...), custom_call_target="tpu_custom_call" | custom-call | flops 300000000 | bytes 3000000 | tf_op jit(solution)/shard_map/stress_and_rows/pallas_call | solution.py:576
  14.1 0.2 collective-permute-start.4
  14.3 2.4 %collective-permute-start.5 = (f32[6,48,128]{2,1,0:T(8,128)S(1)}, f32[6,48,128]{2,1,0:T(8,128)S(1)}, u32[]{:S(2)}, u32[]{:S(2)}) collective-permute-start(f32[6,48,128]{2,1,0:T(8,128)S(1)} %get-tuple-element.45.grp_b), channel_id=1, source_target_pairs={{1,2},{2,1},{5,6},{6,5},{9,10},{10,9},{13,14},{14,13},{17,18},{18,... | collective-permute-start | bytes 442376 | tf_op jit(solution)/shard_map/ppermute | solution.py:450
  16.7 1.7 %collective-permute-start.6 = (f32[6,64,128]{2,1,0:T(8,128)S(1)}, f32[6,64,128]{2,1,0:T(8,128)S(1)}, u32[]{:S(2)}, u32[]{:S(2)}) collective-permute-start(f32[6,64,128]{2,1,0:T(8,128)S(1)} %get-tuple-element.50), channel_id=1, source_target_pairs={{0,4},{4,0},{8,12},{12,8},{16,20},{20,16},{24,28},{28,24},{1,5},{5... | collective-permute-start | bytes 589832 | tf_op jit(solution)/shard_map/ppermute | solution.py:450
  18.4 1.9 %collective-permute-start.7 = (f32[6,64,128]{2,1,0:T(8,128)S(1)}, f32[6,64,128]{2,1,0:T(8,128)S(1)}, u32[]{:S(2)}, u32[]{:S(2)}) collective-permute-start(f32[6,64,128]{2,1,0:T(8,128)S(1)} %get-tuple-element.51), channel_id=1, source_target_pairs={{4,8},{8,4},{12,16},{16,12},{20,24},{24,20},{5,9},{9,5},{13,17},{1... | collective-permute-start | bytes 589832 | tf_op jit(solution)/shard_map/ppermute | solution.py:450
  20.3 0.0 collective-permute-done.4.grp_a.from_a
  20.3 0.4 %collective-permute-done.5.grp_b.from_b = f32[6,48,128]{2,1,0:T(8,128)S(1)} collective-permute-done((f32[6,48,128]{2,1,0:T(8,128)S(1)}, f32[6,48,128]{2,1,0:T(8,128)S(1)}, u32[]{:S(2)}, u32[]{:S(2)}) %collective-permute-start.5) | collective-permute-done | bytes 147488 | tf_op jit(solution)/shard_map/ppermute | solution.py:450
  20.8 2.7 %collective-permute-start.8 = (f32[6,16,128]{2,1,0:T(8,128)S(1)}, f32[6,16,128]{2,1,0:T(8,128)S(1)}, u32[]{:S(2)}, u32[]{:S(2)}) collective-permute-start(f32[6,16,128]{2,1,0:T(8,128)S(1)} %get-tuple-element.52), channel_id=1, source_target_pairs={{0,4},{4,0},{8,12},{12,8},{16,20},{20,16},{24,28},{28,24},{1,5},{5... | collective-permute-start | bytes 147464 | tf_op jit(solution)/shard_map/ppermute | solution.py:450
  23.4 1.9 %collective-permute-start.9 = (f32[6,16,128]{2,1,0:T(8,128)S(1)}, f32[6,16,128]{2,1,0:T(8,128)S(1)}, u32[]{:S(2)}, u32[]{:S(2)}) collective-permute-start(f32[6,16,128]{2,1,0:T(8,128)S(1)} %get-tuple-element.53), channel_id=1, source_target_pairs={{4,8},{8,4},{12,16},{16,12},{20,24},{24,20},{5,9},{9,5},{13,17},{1... | collective-permute-start | bytes 147464 | tf_op jit(solution)/shard_map/ppermute | solution.py:450
  25.4 1.5 %assemble_nodes.1 = (f32[6,512,128]{2,1,0:T(8,128)S(1)}, bf16[3,512,128]{2,1,0:T(8,128)(2,1)}) custom-call(bf16[512,256]{1,0:T(8,128)(2,1)S(1)} %get-tuple-element.28.count, bf16[768,256]{1,0:T(8,128)(2,1)S(1)} %get-tuple-element.41.stress, f32[128,1536]{1,0:T(8,128)S(1)} %get-tuple-element.38.free_t, ...), custom_call_target="tpu_custom_call" | custom-call | flops 400000000 | bytes 2000000 | tf_op jit(solution)/shard_map/assemble_nodes/pallas_call | solution.py:604
  26.8 0.0 collective-permute-done.6.sub_a
  26.8 0.2 collective-permute-done.7.sub_b
  27.1 1.2 %collective-permute-done.8.edge_a = f32[6,16,128]{2,1,0:T(8,128)S(1)} collective-permute-done((f32[6,16,128]{2,1,0:T(8,128)S(1)}, f32[6,16,128]{2,1,0:T(8,128)S(1)}, u32[]{:S(2)}, u32[]{:S(2)}) %collective-permute-start.8) | collective-permute-done | bytes 49184 | tf_op jit(solution)/shard_map/ppermute | solution.py:450
  28.2 2.1 %collective-permute-done.9.edge_b = f32[6,16,128]{2,1,0:T(8,128)S(1)} collective-permute-done((f32[6,16,128]{2,1,0:T(8,128)S(1)}, f32[6,16,128]{2,1,0:T(8,128)S(1)}, u32[]{:S(2)}, u32[]{:S(2)}) %collective-permute-start.9) | collective-permute-done | bytes 49184 | tf_op jit(solution)/shard_map/ppermute | solution.py:450
  30.3 1.2 %add_last.1 = bf16[6,512,128]{2,1,0:T(8,128)(2,1)} custom-call(bf16[512,256]{1,0:T(8,128)(2,1)S(1)} %get-tuple-element.47.placing, f32[6,512,128]{2,1,0:T(8,128)S(1)} %get-tuple-element.48.partial, f32[512,128]{1,0:T(8,128)S(1)} %get-tuple-element.49.inverse_volume, f32[6,64,128]{2,1,0:T(8,128)S(1)} %collective-permute-done.6.sub_a, ...), custom_call_target="tpu_custom_call" | custom-call | flops 400000000 | bytes 3000000 | tf_op jit(solution)/shard_map/add_last/pallas_call | solution.py:613
  (3 shorter events, 0.0 us)
Async XLA Ops:
  0.6 8.0 %copy-start = (bf16[1536,24]{0,1:T(8,128)(2,1)S(1)}, bf16[1536,24]{0,1:T(8,128)(2,1)}, u32[]{:S(2)}) copy-start(bf16[1536,24]{0,1:T(8,128)(2,1)} %param.13) | copy-start | bytes 221188
  0.6 7.1 %collective-permute-start = (f32[24,128]{1,0:T(8,128)}, f32[24,128]{1,0:T(8,128)S(1)}, u32[]{:S(2)}, u32[]{:S(2)}) collective-permute-start(f32[24,128]{1,0:T(8,128)} %refs_6_.1), channel_id=1, source_target_pairs={{4,8},{8,4},{12,16},{16,12},{20,24},{24,20},{5,9},{9,5},{13,17},{1... | collective-permute-start | bytes 36872 | tf_op jit(solution)/shard_map/ppermute | solution.py:450
  4.1 4.0 %collective-permute-start.1 = (f32[24,128]{1,0:T(8,128)}, f32[24,128]{1,0:T(8,128)S(1)}, u32[]{:S(2)}, u32[]{:S(2)}) collective-permute-start(f32[24,128]{1,0:T(8,128)} %refs_6_.1), channel_id=1, source_target_pairs={{0,4},{4,0},{8,12},{12,8},{16,20},{20,16},{24,28},{28,24},{1,5},{5... | collective-permute-start | bytes 36872 | tf_op jit(solution)/shard_map/ppermute | solution.py:450
  8.1 4.0 %collective-permute-start.2 = (f32[72,128]{1,0:T(8,128)S(1)}, f32[72,128]{1,0:T(8,128)S(1)}, u32[]{:S(2)}, u32[]{:S(2)}) collective-permute-start(f32[72,128]{1,0:T(8,128)S(1)} %join_blocks.2.refs_0_), channel_id=1, source_target_pairs={{0,2},{1,3},{2,0},{3,1},{4,6},{5,7},{6,4},{7,5},{8,10},{9,11},{10,... | collective-permute-start | bytes 110600 | tf_op jit(solution)/shard_map/ppermute | solution.py:476
  12.0 1.3 %collective-permute-start.3 = (f32[144,128]{1,0:T(8,128)S(1)}, f32[144,128]{1,0:T(8,128)S(1)}, u32[]{:S(2)}, u32[]{:S(2)}) collective-permute-start(f32[144,128]{1,0:T(8,128)S(1)} %join_blocks.3.near), channel_id=1, source_target_pairs={{0,1},{1,0},{2,3},{3,2},{4,5},{5,4},{6,7},{7,6},{8,9},{9,8},{10,11... | collective-permute-start | bytes 221192 | tf_op jit(solution)/shard_map/ppermute | solution.py:476
  14.1 6.3 %collective-permute-start.4 = (f32[6,48,128]{2,1,0:T(8,128)S(1)}, f32[6,48,128]{2,1,0:T(8,128)S(1)}, u32[]{:S(2)}, u32[]{:S(2)}) collective-permute-start(f32[6,48,128]{2,1,0:T(8,128)S(1)} %get-tuple-element.44.grp_a), channel_id=1, source_target_pairs={{0,1},{1,0},{2,3},{3,2},{4,5},{5,4},{6,7},{7,6},{8,9},{9,8},{10,11... | collective-permute-start | bytes 442376 | tf_op jit(solution)/shard_map/ppermute | solution.py:450
  14.3 6.5 %collective-permute-start.5 = (f32[6,48,128]{2,1,0:T(8,128)S(1)}, f32[6,48,128]{2,1,0:T(8,128)S(1)}, u32[]{:S(2)}, u32[]{:S(2)}) collective-permute-start(f32[6,48,128]{2,1,0:T(8,128)S(1)} %get-tuple-element.45.grp_b), channel_id=1, source_target_pairs={{1,2},{2,1},{5,6},{6,5},{9,10},{10,9},{13,14},{14,13},{17,18},{18,... | collective-permute-start | bytes 442376 | tf_op jit(solution)/shard_map/ppermute | solution.py:450
  16.7 10.2 %collective-permute-start.6 = (f32[6,64,128]{2,1,0:T(8,128)S(1)}, f32[6,64,128]{2,1,0:T(8,128)S(1)}, u32[]{:S(2)}, u32[]{:S(2)}) collective-permute-start(f32[6,64,128]{2,1,0:T(8,128)S(1)} %get-tuple-element.50), channel_id=1, source_target_pairs={{0,4},{4,0},{8,12},{12,8},{16,20},{20,16},{24,28},{28,24},{1,5},{5... | collective-permute-start | bytes 589832 | tf_op jit(solution)/shard_map/ppermute | solution.py:450
  18.4 8.7 %collective-permute-start.7 = (f32[6,64,128]{2,1,0:T(8,128)S(1)}, f32[6,64,128]{2,1,0:T(8,128)S(1)}, u32[]{:S(2)}, u32[]{:S(2)}) collective-permute-start(f32[6,64,128]{2,1,0:T(8,128)S(1)} %get-tuple-element.51), channel_id=1, source_target_pairs={{4,8},{8,4},{12,16},{16,12},{20,24},{24,20},{5,9},{9,5},{13,17},{1... | collective-permute-start | bytes 589832 | tf_op jit(solution)/shard_map/ppermute | solution.py:450
  20.8 7.5 %collective-permute-start.8 = (f32[6,16,128]{2,1,0:T(8,128)S(1)}, f32[6,16,128]{2,1,0:T(8,128)S(1)}, u32[]{:S(2)}, u32[]{:S(2)}) collective-permute-start(f32[6,16,128]{2,1,0:T(8,128)S(1)} %get-tuple-element.52), channel_id=1, source_target_pairs={{0,4},{4,0},{8,12},{12,8},{16,20},{20,16},{24,28},{28,24},{1,5},{5... | collective-permute-start | bytes 147464 | tf_op jit(solution)/shard_map/ppermute | solution.py:450
  23.4 6.9 %collective-permute-start.9 = (f32[6,16,128]{2,1,0:T(8,128)S(1)}, f32[6,16,128]{2,1,0:T(8,128)S(1)}, u32[]{:S(2)}, u32[]{:S(2)}) collective-permute-start(f32[6,16,128]{2,1,0:T(8,128)S(1)} %get-tuple-element.53), channel_id=1, source_target_pairs={{4,8},{8,4},{12,16},{16,12},{20,24},{24,20},{5,9},{9,5},{13,17},{1... | collective-permute-start | bytes 147464 | tf_op jit(solution)/shard_map/ppermute | solution.py:450

commit v19 on v17

--- a/solution.py
+++ b/solution.py
@@ -210,15 +210,16 @@
     aside = 1 - 2 * (s & 1)
     row = jnp.full((TERM, 3 * LANES), -1, jnp.int32)
     base = 0
-    for member in range(members):
-        distance, bits, turn = members // 2, member, 0
-        while distance:
-            turn += (bits & 1) * distance
-            distance, bits = distance // 2, bits >> 1
+    for core in range(2):
         for owner in (s, s - aside, s + aside):
-            first = (owner * members + (g ^ turn)) * block_rows
-            row = jnp.where((lane >= base) & (lane < base + block_rows), first - base + lane, row)
-            base += block_rows
+            for member in range(members // 2):
+                distance, bits, turn = members // 2, member, core
+                while distance > 1:
+                    turn += (bits & 1) * distance
+                    distance, bits = distance // 2, bits >> 1
+                first = (owner * members + (g ^ turn)) * block_rows
+                row = jnp.where((lane >= base) & (lane < base + block_rows), first - base + lane, row)
+                base += block_rows
     for b in range(3):
         cols = slice(b * LANES, (b + 1) * LANES)
         hit = (wanted == row[:, cols].astype(F32)) & (entry < q)
@@ -455,27 +456,32 @@
 
 
 def gather_near(coarse, own, ahead):
-    beyond = exchange(coarse, "sub", 1)
-    beside = exchange(coarse, "sub", 0)
-    parts = [own, beyond, beside]
-    distance = lax.axis_size("grp") // 2
-    while distance:
+    def join(parts, before):
+        def kernel(*refs):
+            join_kernel(*refs[: len(parts)], refs[-1])
+
         rows = sum(x.shape[0] for x in parts)
-        before, ahead = ahead[:1], ahead[1:]
-
-        def join(*refs, skip=len(before)):
-            join_kernel(*refs[: len(refs) - 1 - skip], refs[-1])
-
         (block,) = call(
-            join,
+            kernel,
             "join_blocks",
             (array((rows, parts[0].shape[1])),),
-            vmem(len(parts)) + anywhere(len(before)),
-        )(*parts, *before)
-        pairs = [(i, i ^ distance) for i in range(lax.axis_size("grp"))]
-        parts = [block, lax.ppermute(block, "grp", pairs)]
+            vmem(len(parts)) + anywhere(1),
+        )(*parts, before)
+        return block
+
+    def across(block, distance):
+        return lax.ppermute(block, "grp", [(i, i ^ distance) for i in range(lax.axis_size("grp"))])
+
+    distance = lax.axis_size("grp") // 2
+    sent, block = coarse, own
+    while distance > 1:
+        block = join([block, across(sent, distance)], ahead[0])
+        sent = block
         distance //= 2
-    return parts
+    beyond = exchange(sent, "sub", 1)
+    beside = exchange(sent, "sub", 0)
+    block = join([block, beyond, beside], ahead[1])
+    return [block, across(block, 1)]
 
 
 def shards(

time: 30.9 us -> 30.7 us (level)
  waiting for transfers between devices: 4.56 us -> 4.12 us
    ppermute x8, waiting for transfers between devices: 2.84 us -> 2.23 us  [exchange(): return lax.ppermute(block, axis, pairs)]
  transfers between devices with their start and end apart: 10 -> 10, of which waited for: 6 -> 5; matrix products, arithmetic and copies ran while one was open for 0% -> 0% of each run, Pallas kernels for 21% -> 21%
where the time goes in v19:
time: 30.7 us; the launch traced here: 30.3 us
  starting transfers between devices  17.2 us (56%)
  Pallas kernels  8.33 us (27%)
  waiting for transfers between devices  4.12 us (13%)
  between operations  0.74 us (2%)
    ppermute x8, starting transfers between devices, exchange(): return lax.ppermute(block, axis, pairs)  16.5 us
    ppermute x8, waiting for transfers between devices, exchange(): return lax.ppermute(block, axis, pairs)  2.23 us
    pallas_call x1, Pallas kernels, shards(): call(prepare_panels, 'prepare_panels', (array((cases, dofs)), array((2 *...  2.14 us
    pallas_call x1, Pallas kernels, shards(): call(lists, 'prepare_lists', (array(coarse.shape), array(panel_nodes.shap...  1.91 us
    ppermute x2, waiting for transfers between devices, across(): lax.ppermute(block, 'grp', [(i, i ^ distance) for i in range(lax.axis_siz...  1.88 us
    pallas_call x1, Pallas kernels, shards(): call(partial_kernel, 'assemble_nodes', (array((COMPS, nodes, cases)), arr...  1.47 us
    pallas_call x1, Pallas kernels, shards(): call(finish_kernel, 'add_last', (array((COMPS, nodes, cases), BF16),), vm...  1.22 us
    pallas_call x1, Pallas kernels, shards(): call(stress_kernel, 'stress_of_loads', (array((COMPS, cases - first, LANE...  0.81 us
  transfers between devices with their start and end apart: 10, of which 5 were waited for; matrix products, arithmetic and copies ran while one was open for 0% of the time, Pallas kernels for 21%

profile of v19, /device:TPU:10, one launch (start us, length us, event | category | flops | bytes accessed | tf_op | source)
XLA Modules:
  0.0 30.3 jit_solution(10162220984609960098)
XLA Ops:
  0.6 0.0 copy-start
  0.6 0.6 %collective-permute-start = (f32[24,128]{1,0:T(8,128)}, f32[24,128]{1,0:T(8,128)S(1)}, u32[]{:S(2)}, u32[]{:S(2)}) collective-permute-start(f32[24,128]{1,0:T(8,128)} %refs_6_.1), channel_id=1, source_target_pairs={{0,2},{1,3},{2,0},{3,1},{4,6},{5,7},{6,4},{7,5},{8,10},{9,11},{10,... | collective-permute-start | bytes 36872 | tf_op jit(solution)/shard_map/ppermute | solution.py:473
  1.2 1.9 %prepare_lists.1 = (f32[24,128]{1,0:T(8,128)S(1)}, s32[1,4]{1,0:T(1,128)S(1)}, bf16[3,512,128]{2,1,0:T(8,128)(2,1)S(1)}, bf16[4,384,384]{2,1,0:T(8,128)(2,1)S(1)...) custom-call(s32[1,24]{1,0:T(1,128)} %refs_0_.1, ...), custom_call_target="tpu_custom_call" | custom-call | flops 100000000 | bytes 4000000 | tf_op jit(solution)/shard_map/prepare_lists/pallas_call | solution.py:507
  3.2 1.4 %collective-permute-done.refs_1_ = f32[24,128]{1,0:T(8,128)S(1)} collective-permute-done((f32[24,128]{1,0:T(8,128)}, f32[24,128]{1,0:T(8,128)S(1)}, u32[]{:S(2)}, u32[]{:S(2)}) %collective-permute-start) | collective-permute-done | bytes 12320 | tf_op jit(solution)/shard_map/ppermute | solution.py:473
  4.6 3.3 %collective-permute-start.1 = (f32[48,128]{1,0:T(8,128)S(1)}, f32[48,128]{1,0:T(8,128)S(1)}, u32[]{:S(2)}, u32[]{:S(2)}) collective-permute-start(f32[48,128]{1,0:T(8,128)S(1)} %join_blocks.2.refs_0_), channel_id=1, source_target_pairs={{4,8},{8,4},{12,16},{16,12},{20,24},{24,20},{5,9},{9,5},{13,17},{1... | collective-permute-start | bytes 73736 | tf_op jit(solution)/shard_map/ppermute | solution.py:451
  7.9 1.7 %collective-permute-start.2 = (f32[48,128]{1,0:T(8,128)S(1)}, f32[48,128]{1,0:T(8,128)S(1)}, u32[]{:S(2)}, u32[]{:S(2)}) collective-permute-start(f32[48,128]{1,0:T(8,128)S(1)} %join_blocks.2.refs_0_), channel_id=1, source_target_pairs={{0,4},{4,0},{8,12},{12,8},{16,20},{20,16},{24,28},{28,24},{1,5},{5... | collective-permute-start | bytes 73736 | tf_op jit(solution)/shard_map/ppermute | solution.py:451
  9.6 0.0 copy-done
  9.6 2.1 %prepare_panels.1 = (f32[128,1536]{1,0:T(8,128)S(1)}, bf16[256,1536]{1,0:T(8,128)(2,1)S(1)}, f32[6,64,128]{2,1,0:T(8,128)S(1)}, bf16[256,768]{1,0:T(8,128)(2,1)S(1)}) custom-call(bf16[24,1536]{1,0:T(8,128)(2,1)S(1)} %bitcast.7, s32[1,4]{1,0:T(1,128)S(1)} %get-tuple-element.31.panel_v, bf16[3,512,128]{2,1,0:T(8,128)(2,1)S(1)} %get-tuple-element.32.force_v, ...), custom_call_target="tpu_custom_call" | custom-call | flops 400000000 | bytes 4000000 | tf_op jit(solution)/shard_map/prepare_panels/pallas_call | solution.py:552
  11.8 0.0 collective-permute-done.1.refs_1_
  11.8 0.0 collective-permute-done.2.refs_2_
  11.8 0.1 collective-permute-start.3
  11.9 0.8 %stress_of_loads.1.stress_rest = f32[6,64,128]{2,1,0:T(8,128)S(1)} custom-call(f32[128,1536]{1,0:T(8,128)S(1)} %get-tuple-element.38.free_t, bf16[512,1024]{1,0:T(8,128)(2,1)S(1)} %get-tuple-element.34.onehot, f32[144,8,128]{2,1,0:T(8,128)S(1)} %get-tuple-element.35.scaled), custom_call_target="tpu_custom_call" | custom-call | flops 400000000 | bytes 4000000 | tf_op jit(solution)/shard_map/stress_of_loads/pallas_call | solution.py:571
  12.7 0.4 %collective-permute-done.3.across = f32[144,128]{1,0:T(8,128)S(1)} collective-permute-done((f32[144,128]{1,0:T(8,128)S(1)}, f32[144,128]{1,0:T(8,128)S(1)}, u32[]{:S(2)}, u32[]{:S(2)}) %collective-permute-start.3) | collective-permute-done | bytes 73760 | tf_op jit(solution)/shard_map/ppermute | solution.py:473
  13.1 0.8 %stress_and_rows.1 = (bf16[128,256]{1,0:T(8,128)(2,1)S(1)}, bf16[768,256]{1,0:T(8,128)(2,1)S(1)}, f32[6,64,128]{2,1,0:T(8,128)S(1)}, f32[6,64,128]{2,1,0:T(8,128...) custom-call(f32[144,128]{1,0:T(8,128)S(1)} %join_blocks.3.near, ...), custom_call_target="tpu_custom_call" | custom-call | flops 300000000 | bytes 3000000 | tf_op jit(solution)/shard_map/stress_and_rows/pallas_call | solution.py:582
  13.9 0.2 collective-permute-start.4
  14.1 2.4 %collective-permute-start.5 = (f32[6,48,128]{2,1,0:T(8,128)S(1)}, f32[6,48,128]{2,1,0:T(8,128)S(1)}, u32[]{:S(2)}, u32[]{:S(2)}) collective-permute-start(f32[6,48,128]{2,1,0:T(8,128)S(1)} %get-tuple-element.45.grp_b), channel_id=1, source_target_pairs={{1,2},{2,1},{5,6},{6,5},{9,10},{10,9},{13,14},{14,13},{17,18},{18,... | collective-permute-start | bytes 442376 | tf_op jit(solution)/shard_map/ppermute | solution.py:451
  16.5 1.6 %collective-permute-start.6 = (f32[6,64,128]{2,1,0:T(8,128)S(1)}, f32[6,64,128]{2,1,0:T(8,128)S(1)}, u32[]{:S(2)}, u32[]{:S(2)}) collective-permute-start(f32[6,64,128]{2,1,0:T(8,128)S(1)} %get-tuple-element.50), channel_id=1, source_target_pairs={{0,4},{4,0},{8,12},{12,8},{16,20},{20,16},{24,28},{28,24},{1,5},{5... | collective-permute-start | bytes 589832 | tf_op jit(solution)/shard_map/ppermute | solution.py:451
  18.2 2.2 %collective-permute-start.7 = (f32[6,64,128]{2,1,0:T(8,128)S(1)}, f32[6,64,128]{2,1,0:T(8,128)S(1)}, u32[]{:S(2)}, u32[]{:S(2)}) collective-permute-start(f32[6,64,128]{2,1,0:T(8,128)S(1)} %get-tuple-element.51), channel_id=1, source_target_pairs={{4,8},{8,4},{12,16},{16,12},{20,24},{24,20},{5,9},{9,5},{13,17},{1... | collective-permute-start | bytes 589832 | tf_op jit(solution)/shard_map/ppermute | solution.py:451
  20.4 0.0 collective-permute-done.4.grp_a.from_a
  20.4 0.2 collective-permute-done.5.grp_b.from_b
  20.6 4.4 %collective-permute-start.8 = (f32[6,16,128]{2,1,0:T(8,128)S(1)}, f32[6,16,128]{2,1,0:T(8,128)S(1)}, u32[]{:S(2)}, u32[]{:S(2)}) collective-permute-start(f32[6,16,128]{2,1,0:T(8,128)S(1)} %get-tuple-element.52), channel_id=1, source_target_pairs={{4,8},{8,4},{12,16},{16,12},{20,24},{24,20},{5,9},{9,5},{13,17},{1... | collective-permute-start | bytes 147464 | tf_op jit(solution)/shard_map/ppermute | solution.py:451
  25.0 0.7 %collective-permute-start.9 = (f32[6,16,128]{2,1,0:T(8,128)S(1)}, f32[6,16,128]{2,1,0:T(8,128)S(1)}, u32[]{:S(2)}, u32[]{:S(2)}) collective-permute-start(f32[6,16,128]{2,1,0:T(8,128)S(1)} %get-tuple-element.53), channel_id=1, source_target_pairs={{0,4},{4,0},{8,12},{12,8},{16,20},{20,16},{24,28},{28,24},{1,5},{5... | collective-permute-start | bytes 147464 | tf_op jit(solution)/shard_map/ppermute | solution.py:451
  25.6 1.5 %assemble_nodes.1 = (f32[6,512,128]{2,1,0:T(8,128)S(1)}, bf16[3,512,128]{2,1,0:T(8,128)(2,1)}) custom-call(bf16[512,256]{1,0:T(8,128)(2,1)S(1)} %get-tuple-element.28.count, bf16[768,256]{1,0:T(8,128)(2,1)S(1)} %get-tuple-element.41.stress, f32[128,1536]{1,0:T(8,128)S(1)} %get-tuple-element.38.free_t, ...), custom_call_target="tpu_custom_call" | custom-call | flops 400000000 | bytes 2000000 | tf_op jit(solution)/shard_map/assemble_nodes/pallas_call | solution.py:610
  27.1 0.6 %collective-permute-done.6.sub_a = f32[6,64,128]{2,1,0:T(8,128)S(1)} collective-permute-done((f32[6,64,128]{2,1,0:T(8,128)S(1)}, f32[6,64,128]{2,1,0:T(8,128)S(1)}, u32[]{:S(2)}, u32[]{:S(2)}) %collective-permute-start.6) | collective-permute-done | bytes 196640 | tf_op jit(solution)/shard_map/ppermute | solution.py:451
  27.7 0.0 collective-permute-done.7.sub_b
  27.7 0.0 collective-permute-done.8.edge_b
  27.7 1.4 %collective-permute-done.9.edge_a = f32[6,16,128]{2,1,0:T(8,128)S(1)} collective-permute-done((f32[6,16,128]{2,1,0:T(8,128)S(1)}, f32[6,16,128]{2,1,0:T(8,128)S(1)}, u32[]{:S(2)}, u32[]{:S(2)}) %collective-permute-start.9) | collective-permute-done | bytes 49184 | tf_op jit(solution)/shard_map/ppermute | solution.py:451
  29.1 1.2 %add_last.1 = bf16[6,512,128]{2,1,0:T(8,128)(2,1)} custom-call(bf16[512,256]{1,0:T(8,128)(2,1)S(1)} %get-tuple-element.47.placing, f32[6,512,128]{2,1,0:T(8,128)S(1)} %get-tuple-element.48.partial, f32[512,128]{1,0:T(8,128)S(1)} %get-tuple-element.49.inverse_volume, f32[6,64,128]{2,1,0:T(8,128)S(1)} %collective-permute-done.6.sub_a, ...), custom_call_target="tpu_custom_call" | custom-call | flops 400000000 | bytes 3000000 | tf_op jit(solution)/shard_map/add_last/pallas_call | solution.py:619
  (3 shorter events, 0.0 us)
Async XLA Ops:
  0.6 9.0 %copy-start = (bf16[1536,24]{0,1:T(8,128)(2,1)S(1)}, bf16[1536,24]{0,1:T(8,128)(2,1)}, u32[]{:S(2)}) copy-start(bf16[1536,24]{0,1:T(8,128)(2,1)} %param.13) | copy-start | bytes 221188
  0.6 4.0 %collective-permute-start = (f32[24,128]{1,0:T(8,128)}, f32[24,128]{1,0:T(8,128)S(1)}, u32[]{:S(2)}, u32[]{:S(2)}) collective-permute-start(f32[24,128]{1,0:T(8,128)} %refs_6_.1), channel_id=1, source_target_pairs={{0,2},{1,3},{2,0},{3,1},{4,6},{5,7},{6,4},{7,5},{8,10},{9,11},{10,... | collective-permute-start | bytes 36872 | tf_op jit(solution)/shard_map/ppermute | solution.py:473
  4.6 7.2 %collective-permute-start.1 = (f32[48,128]{1,0:T(8,128)S(1)}, f32[48,128]{1,0:T(8,128)S(1)}, u32[]{:S(2)}, u32[]{:S(2)}) collective-permute-start(f32[48,128]{1,0:T(8,128)S(1)} %join_blocks.2.refs_0_), channel_id=1, source_target_pairs={{4,8},{8,4},{12,16},{16,12},{20,24},{24,20},{5,9},{9,5},{13,17},{1... | collective-permute-start | bytes 73736 | tf_op jit(solution)/shard_map/ppermute | solution.py:451
  7.9 3.9 %collective-permute-start.2 = (f32[48,128]{1,0:T(8,128)S(1)}, f32[48,128]{1,0:T(8,128)S(1)}, u32[]{:S(2)}, u32[]{:S(2)}) collective-permute-start(f32[48,128]{1,0:T(8,128)S(1)} %join_blocks.2.refs_0_), channel_id=1, source_target_pairs={{0,4},{4,0},{8,12},{12,8},{16,20},{20,16},{24,28},{28,24},{1,5},{5... | collective-permute-start | bytes 73736 | tf_op jit(solution)/shard_map/ppermute | solution.py:451
  11.8 1.3 %collective-permute-start.3 = (f32[144,128]{1,0:T(8,128)S(1)}, f32[144,128]{1,0:T(8,128)S(1)}, u32[]{:S(2)}, u32[]{:S(2)}) collective-permute-start(f32[144,128]{1,0:T(8,128)S(1)} %join_blocks.3.near), channel_id=1, source_target_pairs={{0,1},{1,0},{2,3},{3,2},{4,5},{5,4},{6,7},{7,6},{8,9},{9,8},{10,11... | collective-permute-start | bytes 221192 | tf_op jit(solution)/shard_map/ppermute | solution.py:473
  13.9 6.5 %collective-permute-start.4 = (f32[6,48,128]{2,1,0:T(8,128)S(1)}, f32[6,48,128]{2,1,0:T(8,128)S(1)}, u32[]{:S(2)}, u32[]{:S(2)}) collective-permute-start(f32[6,48,128]{2,1,0:T(8,128)S(1)} %get-tuple-element.44.grp_a), channel_id=1, source_target_pairs={{0,1},{1,0},{2,3},{3,2},{4,5},{5,4},{6,7},{7,6},{8,9},{9,8},{10,11... | collective-permute-start | bytes 442376 | tf_op jit(solution)/shard_map/ppermute | solution.py:451
  14.1 6.5 %collective-permute-start.5 = (f32[6,48,128]{2,1,0:T(8,128)S(1)}, f32[6,48,128]{2,1,0:T(8,128)S(1)}, u32[]{:S(2)}, u32[]{:S(2)}) collective-permute-start(f32[6,48,128]{2,1,0:T(8,128)S(1)} %get-tuple-element.45.grp_b), channel_id=1, source_target_pairs={{1,2},{2,1},{5,6},{6,5},{9,10},{10,9},{13,14},{14,13},{17,18},{18,... | collective-permute-start | bytes 442376 | tf_op jit(solution)/shard_map/ppermute | solution.py:451
  16.5 11.2 %collective-permute-start.6 = (f32[6,64,128]{2,1,0:T(8,128)S(1)}, f32[6,64,128]{2,1,0:T(8,128)S(1)}, u32[]{:S(2)}, u32[]{:S(2)}) collective-permute-start(f32[6,64,128]{2,1,0:T(8,128)S(1)} %get-tuple-element.50), channel_id=1, source_target_pairs={{0,4},{4,0},{8,12},{12,8},{16,20},{20,16},{24,28},{28,24},{1,5},{5... | collective-permute-start | bytes 589832 | tf_op jit(solution)/shard_map/ppermute | solution.py:451
  18.2 9.6 %collective-permute-start.7 = (f32[6,64,128]{2,1,0:T(8,128)S(1)}, f32[6,64,128]{2,1,0:T(8,128)S(1)}, u32[]{:S(2)}, u32[]{:S(2)}) collective-permute-start(f32[6,64,128]{2,1,0:T(8,128)S(1)} %get-tuple-element.51), channel_id=1, source_target_pairs={{4,8},{8,4},{12,16},{16,12},{20,24},{24,20},{5,9},{9,5},{13,17},{1... | collective-permute-start | bytes 589832 | tf_op jit(solution)/shard_map/ppermute | solution.py:451
  20.6 7.1 %collective-permute-start.8 = (f32[6,16,128]{2,1,0:T(8,128)S(1)}, f32[6,16,128]{2,1,0:T(8,128)S(1)}, u32[]{:S(2)}, u32[]{:S(2)}) collective-permute-start(f32[6,16,128]{2,1,0:T(8,128)S(1)} %get-tuple-element.52), channel_id=1, source_target_pairs={{4,8},{8,4},{12,16},{16,12},{20,24},{24,20},{5,9},{9,5},{13,17},{1... | collective-permute-start | bytes 147464 | tf_op jit(solution)/shard_map/ppermute | solution.py:451
  25.0 4.2 %collective-permute-start.9 = (f32[6,16,128]{2,1,0:T(8,128)S(1)}, f32[6,16,128]{2,1,0:T(8,128)S(1)}, u32[]{:S(2)}, u32[]{:S(2)}) collective-permute-start(f32[6,16,128]{2,1,0:T(8,128)S(1)} %get-tuple-element.53), channel_id=1, source_target_pairs={{0,4},{4,0},{8,12},{12,8},{16,20},{20,16},{24,28},{28,24},{1,5},{5... | collective-permute-start | bytes 147464 | tf_op jit(solution)/shard_map/ppermute | solution.py:451

commit v20 on v19

--- a/solution.py
+++ b/solution.py
@@ -16,6 +16,7 @@
 LANES = 128
 TERM = 32
 SPARE = 8
+GRP_A = 64
 TERMS = ((0, 0), (0, 1), (0, 2), (1, 0), (1, 1), (2, 0))
 
 POISSON = 0.3
@@ -180,17 +181,33 @@
     ids[0:1, 0:NIF] = interface_v[...].astype(F32)
     order_lists(ids)
     lane = lax.broadcasted_iota(jnp.int32, (8, LANES), 1)
-    edges = pltpu.roll(ids[:, LANES:], LANES - NIS, 1)
-    again = pltpu.roll(ids[:, :LANES], LANES - NIS + 4 * NED, 1)
-    last = jnp.where(lane < 4 * NED, edges, again)
-    last = jnp.where(lane < LATE, last, pltpu.roll(edges, LATE, 1))
-    for row, target in ((ids[0:1, LANES:], 0), (ids[0:1, :LANES], 1), (last[0:1], 2)):
-        hit = jnp.where(row.astype(jnp.int32) == node_of, 1.0, 0.0).astype(BF16)
-        if target == 0:
-            placing[:, :LANES] = hit
-            placing[:, LANES:] = hit
-        else:
-            placing_last[:, (target - 1) * LANES : target * LANES] = hit
+    faces, others = ids[:, :LANES], ids[:, LANES:]
+    turned = pltpu.roll(others, NIS, 1)
+    lists = (
+        (placing, 0, jnp.where(lane < NIS, faces, turned)),
+        (placing, 1, jnp.where(lane < 4 * NED, turned, pltpu.roll(others, 4 * NED, 1))),
+        (
+            placing_last,
+            0,
+            jnp.where(
+                lane < NIS,
+                pltpu.roll(faces, NIS, 1),
+                jnp.where(lane < LATE, others, pltpu.roll(faces, 4 * NED, 1)),
+            ),
+        ),
+        (
+            placing_last,
+            1,
+            jnp.where(
+                lane < 4 * NED,
+                pltpu.roll(faces, 4 * NED, 1),
+                jnp.where(lane < 8 * NED, pltpu.roll(others, LATE, 1), -1.0),
+            ),
+        ),
+    )
+    for target, half, row in lists:
+        hit = jnp.where(row[0:1].astype(jnp.int32) == node_of, 1.0, 0.0).astype(BF16)
+        target[:, half * LANES : (half + 1) * LANES] = hit
     connect_f = connect_v[...].astype(F32)
     for half in range(2):
         id_col = column(ids[0:1, half * LANES : (half + 1) * LANES])
@@ -354,7 +371,8 @@
         edge = [part[EDGES + NED * k : EDGES + NED * (k + 1)] for k in range(4)]
         sub_a[i] = part[:NIS]
         sub_b[i] = part[NIS : 2 * NIS]
-        grp_a[i] = jnp.concatenate([part[2 * NIS : 2 * NIS + NIG], edge[0], edge[2]], axis=0)
+        gap = jnp.zeros((GRP_A - NIG - 2 * NED, LANES), F32)
+        grp_a[i] = jnp.concatenate([part[2 * NIS : 2 * NIS + NIG], edge[0], edge[2], gap], axis=0)
         grp_b[i] = jnp.concatenate([part[2 * NIS + NIG : EDGES], edge[1], edge[3]], axis=0)
 
 
@@ -362,12 +380,12 @@
     split = NIG + NED
     edge_a[:, :NED, :] = grp_a[:, NIG:split, :] + from_a[:, NIG:split, :]
     edge_a[:, NED:, :] = grp_b[:, NIG:split, :] + from_b[:, NIG:split, :]
-    edge_b[:, :NED, :] = grp_a[:, split:, :] + from_a[:, split:, :]
+    edge_b[:, :NED, :] = grp_a[:, split : split + NED, :] + from_a[:, split : split + NED, :]
     edge_b[:, NED:, :] = grp_b[:, split:, :] + from_b[:, split:, :]
 
 
 def partial_kernel(
-    count, stress, free_t, corner_t, values, placing, grp_a, grp_b, partial, disp_out, received
+    count, stress, free_t, corner_t, values, placing, sub_a, grp_a, grp_b, partial, disp_out, received
 ):
     nodes = disp_out.shape[1]
     for c in range(3):
@@ -378,11 +396,12 @@
     split = NIG + NED
     for i in range(COMPS):
         low, high = grp_a[i], grp_b[i]
-        rows = [low[:NIG], high[:NIG], low[NIG:split], high[NIG:split], low[split:], high[split:]]
-        rows.append(jnp.zeros((2 * LANES - NIF, LANES), F32))
+        rows = [low[:NIG], high[:NIG], low[NIG:split], high[NIG:split], low[split : split + NED], high[split:]]
         first, second = split_two(jnp.concatenate(rows, axis=0))
-        received[:LANES, i * LANES : (i + 1) * LANES] = first
-        received[LANES:, i * LANES : (i + 1) * LANES] = second
+        cols = slice(i * LANES, (i + 1) * LANES)
+        received[:NIS, cols] = sub_a[i].astype(BF16)
+        received[NIS : NIS + LATE, cols] = first
+        received[NIS + LATE :, cols] = second
     for i in range(0, COMPS, 2):
         cols = slice(i * LANES, (i + 2) * LANES)
         own = dot_nt(count[...], stress[cols, :])
@@ -392,8 +411,9 @@
 
 
 def finish_kernel(
-    placing, partial, inverse_volume, sub_a, sub_b, edge_b, edge_a, out, received, nodal, sems
+    placing, partial, inverse_volume, sub_b, edge_b, edge_a, out, received, nodal, sems
 ):
+    received[2 * LATE :, :] = jnp.zeros((received.shape[0] - 2 * LATE, received.shape[1]), BF16)
     scale = inverse_volume[...]
     copies = []
     for i in range(0, COMPS, 2):
@@ -401,9 +421,8 @@
             cols = slice(k * LANES, (k + 1) * LANES)
             late = jnp.concatenate([sub_b[k], edge_a[k], edge_b[k]], axis=0)
             first, second = split_two(late)
-            received[:NIS, cols] = sub_a[k].astype(BF16)
-            received[NIS : NIS + LATE, cols] = first
-            received[NIS + LATE :, cols] = second
+            received[:LATE, cols] = first
+            received[LATE : 2 * LATE, cols] = second
         added = dot(placing[...], received[:, i * LANES : (i + 2) * LANES])
         nodal[i] = ((partial[i] + added[:, :LANES]) * scale).astype(BF16)
         nodal[i + 1] = ((partial[i + 1] + added[:, LANES:]) * scale).astype(BF16)
@@ -587,7 +606,7 @@
             array((COMPS * cases, 2 * LANES), BF16),
             array((COMPS, NIS, cases)),
             array((COMPS, NIS, cases)),
-            array((COMPS, NIG + 2 * NED, cases)),
+            array((COMPS, GRP_A, cases)),
             array((COMPS, NIG + 2 * NED, cases)),
         ),
         vmem(7),
@@ -611,25 +630,25 @@
         partial_kernel,
         "assemble_nodes",
         (array((COMPS, nodes, cases)), array((3, nodes, cases), BF16)),
-        vmem(8),
-        (pltpu.VMEM((2 * LANES, COMPS * cases), BF16),),
+        vmem(9),
+        (pltpu.VMEM((NIS + 2 * LATE, COMPS * cases), BF16),),
         flops=400000000,
         moved=2000000,
-    )(count, stress, free_t, corner_t, values, placing, from_grp_a, from_grp_b)
+    )(count, stress, free_t, corner_t, values, placing, from_sub_a, from_grp_a, from_grp_b)
     (nodal,) = call(
         finish_kernel,
         "add_last",
         (array((COMPS, nodes, cases), BF16),),
-        vmem(7),
-        (
-            pltpu.VMEM((NIS + 2 * LATE, COMPS * cases), BF16),
+        vmem(6),
+        (
+            pltpu.VMEM((2 * LANES, COMPS * cases), BF16),
             pltpu.VMEM((COMPS, nodes, cases), BF16),
             pltpu.SemaphoreType.DMA((COMPS // 2,)),
         ),
         flops=400000000,
         moved=3000000,
         out_specs=hbm(1),
-    )(placing_last, partial, inverse_volume, from_sub_a, from_sub_b, from_edge_b, from_edge_a)
+    )(placing_last, partial, inverse_volume, from_sub_b, from_edge_b, from_edge_a)
     return jnp.transpose(disp, (1, 0, 2)), jnp.transpose(nodal, (1, 0, 2))
 
 

time: 30.7 us -> 31.2 us (1.016)
  waiting for transfers between devices: 4.12 us -> 4.9 us
  starting transfers between devices: 17.2 us -> 16.8 us
    ppermute x8, waiting for transfers between devices: 2.23 us -> 3.05 us  [exchange(): return lax.ppermute(block, axis, pairs)]
    ppermute x8, starting transfers between devices: 16.5 us -> 16.2 us  [exchange(): return lax.ppermute(block, axis, pairs)]
where the time goes in v20:
time: 31.2 us; the launch traced here: 30.8 us
  starting transfers between devices  16.8 us (54%)
  Pallas kernels  8.37 us (27%)
  waiting for transfers between devices  4.9 us (16%)
  between operations  0.73 us (2%)
    ppermute x8, starting transfers between devices, exchange(): return lax.ppermute(block, axis, pairs)  16.2 us
    ppermute x8, waiting for transfers between devices, exchange(): return lax.ppermute(block, axis, pairs)  3.05 us
    pallas_call x1, Pallas kernels, shards(): call(prepare_panels, 'prepare_panels', (array((cases, dofs)), array((2 *...  2.14 us
    pallas_call x1, Pallas kernels, shards(): call(lists, 'prepare_lists', (array(coarse.shape), array(panel_nodes.shap...  1.95 us
    ppermute x2, waiting for transfers between devices, across(): lax.ppermute(block, 'grp', [(i, i ^ distance) for i in range(lax.axis_siz...  1.85 us
    pallas_call x1, Pallas kernels, shards(): call(partial_kernel, 'assemble_nodes', (array((COMPS, nodes, cases)), arr...  1.47 us
    pallas_call x1, Pallas kernels, shards(): call(finish_kernel, 'add_last', (array((COMPS, nodes, cases), BF16),), vm...  1.22 us
    pallas_call x1, Pallas kernels, shards(): call(stress_kernel, 'stress_of_loads', (array((COMPS, cases - first, LANE...  0.81 us
  transfers between devices with their start and end apart: 10, of which 5 were waited for; matrix products, arithmetic and copies ran while one was open for 0% of the time, Pallas kernels for 21%

profile of v20, /device:TPU:10, one launch (start us, length us, event | category | flops | bytes accessed | tf_op | source)
XLA Modules:
  0.0 30.8 jit_solution(8315614496014920863)
XLA Ops:
  0.6 0.0 copy-start
  0.6 0.6 %collective-permute-start = (f32[24,128]{1,0:T(8,128)}, f32[24,128]{1,0:T(8,128)S(1)}, u32[]{:S(2)}, u32[]{:S(2)}) collective-permute-start(f32[24,128]{1,0:T(8,128)} %refs_6_.1), channel_id=1, source_target_pairs={{0,2},{1,3},{2,0},{3,1},{4,6},{5,7},{6,4},{7,5},{8,10},{9,11},{10,... | collective-permute-start | bytes 36872 | tf_op jit(solution)/shard_map/ppermute | solution.py:492
  1.2 2.0 %prepare_lists.1 = (f32[24,128]{1,0:T(8,128)S(1)}, s32[1,4]{1,0:T(1,128)S(1)}, bf16[3,512,128]{2,1,0:T(8,128)(2,1)S(1)}, bf16[4,384,384]{2,1,0:T(8,128)(2,1)S(1)...) custom-call(s32[1,24]{1,0:T(1,128)} %refs_0_.1, ...), custom_call_target="tpu_custom_call" | custom-call | flops 100000000 | bytes 4000000 | tf_op jit(solution)/shard_map/prepare_lists/pallas_call | solution.py:526
  3.2 1.4 %collective-permute-done.refs_1_ = f32[24,128]{1,0:T(8,128)S(1)} collective-permute-done((f32[24,128]{1,0:T(8,128)}, f32[24,128]{1,0:T(8,128)S(1)}, u32[]{:S(2)}, u32[]{:S(2)}) %collective-permute-start) | collective-permute-done | bytes 12320 | tf_op jit(solution)/shard_map/ppermute | solution.py:492
  4.6 3.3 %collective-permute-start.1 = (f32[48,128]{1,0:T(8,128)S(1)}, f32[48,128]{1,0:T(8,128)S(1)}, u32[]{:S(2)}, u32[]{:S(2)}) collective-permute-start(f32[48,128]{1,0:T(8,128)S(1)} %join_blocks.2.refs_0_), channel_id=1, source_target_pairs={{4,8},{8,4},{12,16},{16,12},{20,24},{24,20},{5,9},{9,5},{13,17},{1... | collective-permute-start | bytes 73736 | tf_op jit(solution)/shard_map/ppermute | solution.py:470
  7.9 1.7 %collective-permute-start.2 = (f32[48,128]{1,0:T(8,128)S(1)}, f32[48,128]{1,0:T(8,128)S(1)}, u32[]{:S(2)}, u32[]{:S(2)}) collective-permute-start(f32[48,128]{1,0:T(8,128)S(1)} %join_blocks.2.refs_0_), channel_id=1, source_target_pairs={{0,4},{4,0},{8,12},{12,8},{16,20},{20,16},{24,28},{28,24},{1,5},{5... | collective-permute-start | bytes 73736 | tf_op jit(solution)/shard_map/ppermute | solution.py:470
  9.6 0.0 copy-done
  9.6 2.1 %prepare_panels.1 = (f32[128,1536]{1,0:T(8,128)S(1)}, bf16[256,1536]{1,0:T(8,128)(2,1)S(1)}, f32[6,64,128]{2,1,0:T(8,128)S(1)}, bf16[256,768]{1,0:T(8,128)(2,1)S(1)}) custom-call(bf16[24,1536]{1,0:T(8,128)(2,1)S(1)} %bitcast.7, s32[1,4]{1,0:T(1,128)S(1)} %get-tuple-element.31.panel_v, bf16[3,512,128]{2,1,0:T(8,128)(2,1)S(1)} %get-tuple-element.32.force_v, ...), custom_call_target="tpu_custom_call" | custom-call | flops 400000000 | bytes 4000000 | tf_op jit(solution)/shard_map/prepare_panels/pallas_call | solution.py:571
  11.8 0.0 collective-permute-done.1.refs_1_
  11.8 0.0 collective-permute-done.2.refs_2_
  11.8 0.1 collective-permute-start.3
  11.9 0.8 %stress_of_loads.1.stress_rest = f32[6,64,128]{2,1,0:T(8,128)S(1)} custom-call(f32[128,1536]{1,0:T(8,128)S(1)} %get-tuple-element.38.free_t, bf16[512,1024]{1,0:T(8,128)(2,1)S(1)} %get-tuple-element.34.onehot, f32[144,8,128]{2,1,0:T(8,128)S(1)} %get-tuple-element.35.scaled), custom_call_target="tpu_custom_call" | custom-call | flops 400000000 | bytes 4000000 | tf_op jit(solution)/shard_map/stress_of_loads/pallas_call | solution.py:590
  12.7 0.4 %collective-permute-done.3.across = f32[144,128]{1,0:T(8,128)S(1)} collective-permute-done((f32[144,128]{1,0:T(8,128)S(1)}, f32[144,128]{1,0:T(8,128)S(1)}, u32[]{:S(2)}, u32[]{:S(2)}) %collective-permute-start.3) | collective-permute-done | bytes 73760 | tf_op jit(solution)/shard_map/ppermute | solution.py:492
  13.1 0.8 %stress_and_rows.1 = (bf16[128,256]{1,0:T(8,128)(2,1)S(1)}, bf16[768,256]{1,0:T(8,128)(2,1)S(1)}, f32[6,64,128]{2,1,0:T(8,128)S(1)}, f32[6,64,128]{2,1,0:T(8,128...) custom-call(f32[144,128]{1,0:T(8,128)S(1)} %join_blocks.3.near, ...), custom_call_target="tpu_custom_call" | custom-call | flops 300000000 | bytes 3000000 | tf_op jit(solution)/shard_map/stress_and_rows/pallas_call | solution.py:601
  13.9 0.2 collective-permute-start.5
  14.1 1.6 %collective-permute-start.4 = (f32[6,64,128]{2,1,0:T(8,128)S(1)}, f32[6,64,128]{2,1,0:T(8,128)S(1)}, u32[]{:S(2)}, u32[]{:S(2)}) collective-permute-start(f32[6,64,128]{2,1,0:T(8,128)S(1)} %get-tuple-element.44), channel_id=1, source_target_pairs={{0,4},{4,0},{8,12},{12,8},{16,20},{20,16},{24,28},{28,24},{1,5},{5... | collective-permute-start | bytes 589832 | tf_op jit(solution)/shard_map/ppermute | solution.py:470
  15.7 2.1 %collective-permute-start.6 = (f32[6,48,128]{2,1,0:T(8,128)S(1)}, f32[6,48,128]{2,1,0:T(8,128)S(1)}, u32[]{:S(2)}, u32[]{:S(2)}) collective-permute-start(f32[6,48,128]{2,1,0:T(8,128)S(1)} %get-tuple-element.46.grp_b), channel_id=1, source_target_pairs={{1,2},{2,1},{5,6},{6,5},{9,10},{10,9},{13,14},{14,13},{17,18},{18,... | collective-permute-start | bytes 442376 | tf_op jit(solution)/shard_map/ppermute | solution.py:470
  17.8 2.2 %collective-permute-start.7 = (f32[6,64,128]{2,1,0:T(8,128)S(1)}, f32[6,64,128]{2,1,0:T(8,128)S(1)}, u32[]{:S(2)}, u32[]{:S(2)}) collective-permute-start(f32[6,64,128]{2,1,0:T(8,128)S(1)} %get-tuple-element.51), channel_id=1, source_target_pairs={{4,8},{8,4},{12,16},{16,12},{20,24},{24,20},{5,9},{9,5},{13,17},{1... | collective-permute-start | bytes 589832 | tf_op jit(solution)/shard_map/ppermute | solution.py:470
  20.1 2.1 %collective-permute-done.6.grp_b.from_b = f32[6,48,128]{2,1,0:T(8,128)S(1)} collective-permute-done((f32[6,48,128]{2,1,0:T(8,128)S(1)}, f32[6,48,128]{2,1,0:T(8,128)S(1)}, u32[]{:S(2)}, u32[]{:S(2)}) %collective-permute-start.6) | collective-permute-done | bytes 147488 | tf_op jit(solution)/shard_map/ppermute | solution.py:470
  22.2 0.0 collective-permute-done.5.grp_a.from_a
  22.2 2.4 %collective-permute-start.8 = (f32[6,16,128]{2,1,0:T(8,128)S(1)}, f32[6,16,128]{2,1,0:T(8,128)S(1)}, u32[]{:S(2)}, u32[]{:S(2)}) collective-permute-start(f32[6,16,128]{2,1,0:T(8,128)S(1)} %get-tuple-element.52), channel_id=1, source_target_pairs={{4,8},{8,4},{12,16},{16,12},{20,24},{24,20},{5,9},{9,5},{13,17},{1... | collective-permute-start | bytes 147464 | tf_op jit(solution)/shard_map/ppermute | solution.py:470
  24.6 2.6 %collective-permute-start.9 = (f32[6,16,128]{2,1,0:T(8,128)S(1)}, f32[6,16,128]{2,1,0:T(8,128)S(1)}, u32[]{:S(2)}, u32[]{:S(2)}) collective-permute-start(f32[6,16,128]{2,1,0:T(8,128)S(1)} %get-tuple-element.53), channel_id=1, source_target_pairs={{0,4},{4,0},{8,12},{12,8},{16,20},{20,16},{24,28},{28,24},{1,5},{5... | collective-permute-start | bytes 147464 | tf_op jit(solution)/shard_map/ppermute | solution.py:470
  27.2 0.0 collective-permute-done.4.sub_a
  27.2 1.5 %assemble_nodes.1 = (f32[6,512,128]{2,1,0:T(8,128)S(1)}, bf16[3,512,128]{2,1,0:T(8,128)(2,1)}) custom-call(bf16[512,256]{1,0:T(8,128)(2,1)S(1)} %get-tuple-element.28.count, bf16[768,256]{1,0:T(8,128)(2,1)S(1)} %get-tuple-element.41.stress, f32[128,1536]{1,0:T(8,128)S(1)} %get-tuple-element.38.free_t, ...), custom_call_target="tpu_custom_call" | custom-call | flops 400000000 | bytes 2000000 | tf_op jit(solution)/shard_map/assemble_nodes/pallas_call | solution.py:629
  28.7 0.0 collective-permute-done.7.sub_b
  28.7 0.4 %collective-permute-done.8.edge_b = f32[6,16,128]{2,1,0:T(8,128)S(1)} collective-permute-done((f32[6,16,128]{2,1,0:T(8,128)S(1)}, f32[6,16,128]{2,1,0:T(8,128)S(1)}, u32[]{:S(2)}, u32[]{:S(2)}) %collective-permute-start.8) | collective-permute-done | bytes 49184 | tf_op jit(solution)/shard_map/ppermute | solution.py:470
  29.1 0.5 %collective-permute-done.9.edge_a = f32[6,16,128]{2,1,0:T(8,128)S(1)} collective-permute-done((f32[6,16,128]{2,1,0:T(8,128)S(1)}, f32[6,16,128]{2,1,0:T(8,128)S(1)}, u32[]{:S(2)}, u32[]{:S(2)}) %collective-permute-start.9) | collective-permute-done | bytes 49184 | tf_op jit(solution)/shard_map/ppermute | solution.py:470
  29.6 1.2 %add_last.1 = bf16[6,512,128]{2,1,0:T(8,128)(2,1)} custom-call(bf16[512,256]{1,0:T(8,128)(2,1)S(1)} %get-tuple-element.48.placing, f32[6,512,128]{2,1,0:T(8,128)S(1)} %get-tuple-element.49.partial, f32[512,128]{1,0:T(8,128)S(1)} %get-tuple-element.50.inverse_volume, f32[6,64,128]{2,1,0:T(8,128)S(1)} %collective-permute-done.7.sub_b, ...), custom_call_target="tpu_custom_call" | custom-call | flops 400000000 | bytes 3000000 | tf_op jit(solution)/shard_map/add_last/pallas_call | solution.py:638
  (3 shorter events, 0.0 us)
Async XLA Ops:
  0.6 9.0 %copy-start = (bf16[1536,24]{0,1:T(8,128)(2,1)S(1)}, bf16[1536,24]{0,1:T(8,128)(2,1)}, u32[]{:S(2)}) copy-start(bf16[1536,24]{0,1:T(8,128)(2,1)} %param.13) | copy-start | bytes 221188
  0.6 4.0 %collective-permute-start = (f32[24,128]{1,0:T(8,128)}, f32[24,128]{1,0:T(8,128)S(1)}, u32[]{:S(2)}, u32[]{:S(2)}) collective-permute-start(f32[24,128]{1,0:T(8,128)} %refs_6_.1), channel_id=1, source_target_pairs={{0,2},{1,3},{2,0},{3,1},{4,6},{5,7},{6,4},{7,5},{8,10},{9,11},{10,... | collective-permute-start | bytes 36872 | tf_op jit(solution)/shard_map/ppermute | solution.py:492
  4.6 7.2 %collective-permute-start.1 = (f32[48,128]{1,0:T(8,128)S(1)}, f32[48,128]{1,0:T(8,128)S(1)}, u32[]{:S(2)}, u32[]{:S(2)}) collective-permute-start(f32[48,128]{1,0:T(8,128)S(1)} %join_blocks.2.refs_0_), channel_id=1, source_target_pairs={{4,8},{8,4},{12,16},{16,12},{20,24},{24,20},{5,9},{9,5},{13,17},{1... | collective-permute-start | bytes 73736 | tf_op jit(solution)/shard_map/ppermute | solution.py:470
  7.9 3.9 %collective-permute-start.2 = (f32[48,128]{1,0:T(8,128)S(1)}, f32[48,128]{1,0:T(8,128)S(1)}, u32[]{:S(2)}, u32[]{:S(2)}) collective-permute-start(f32[48,128]{1,0:T(8,128)S(1)} %join_blocks.2.refs_0_), channel_id=1, source_target_pairs={{0,4},{4,0},{8,12},{12,8},{16,20},{20,16},{24,28},{28,24},{1,5},{5... | collective-permute-start | bytes 73736 | tf_op jit(solution)/shard_map/ppermute | solution.py:470
  11.8 1.3 %collective-permute-start.3 = (f32[144,128]{1,0:T(8,128)S(1)}, f32[144,128]{1,0:T(8,128)S(1)}, u32[]{:S(2)}, u32[]{:S(2)}) collective-permute-start(f32[144,128]{1,0:T(8,128)S(1)} %join_blocks.3.near), channel_id=1, source_target_pairs={{0,1},{1,0},{2,3},{3,2},{4,5},{5,4},{6,7},{7,6},{8,9},{9,8},{10,11... | collective-permute-start | bytes 221192 | tf_op jit(solution)/shard_map/ppermute | solution.py:492
  13.9 8.3 %collective-permute-start.5 = (f32[6,64,128]{2,1,0:T(8,128)S(1)}, f32[6,64,128]{2,1,0:T(8,128)S(1)}, u32[]{:S(2)}, u32[]{:S(2)}) collective-permute-start(f32[6,64,128]{2,1,0:T(8,128)S(1)} %get-tuple-element.45.grp_a), channel_id=1, source_target_pairs={{0,1},{1,0},{2,3},{3,2},{4,5},{5,4},{6,7},{7,6},{8,9},{9,8},{10,11... | collective-permute-start | bytes 589832 | tf_op jit(solution)/shard_map/ppermute | solution.py:470
  14.1 13.1 %collective-permute-start.4 = (f32[6,64,128]{2,1,0:T(8,128)S(1)}, f32[6,64,128]{2,1,0:T(8,128)S(1)}, u32[]{:S(2)}, u32[]{:S(2)}) collective-permute-start(f32[6,64,128]{2,1,0:T(8,128)S(1)} %get-tuple-element.44), channel_id=1, source_target_pairs={{0,4},{4,0},{8,12},{12,8},{16,20},{20,16},{24,28},{28,24},{1,5},{5... | collective-permute-start | bytes 589832 | tf_op jit(solution)/shard_map/ppermute | solution.py:470
  15.7 6.5 %collective-permute-start.6 = (f32[6,48,128]{2,1,0:T(8,128)S(1)}, f32[6,48,128]{2,1,0:T(8,128)S(1)}, u32[]{:S(2)}, u32[]{:S(2)}) collective-permute-start(f32[6,48,128]{2,1,0:T(8,128)S(1)} %get-tuple-element.46.grp_b), channel_id=1, source_target_pairs={{1,2},{2,1},{5,6},{6,5},{9,10},{10,9},{13,14},{14,13},{17,18},{18,... | collective-permute-start | bytes 442376 | tf_op jit(solution)/shard_map/ppermute | solution.py:470
  17.8 10.8 %collective-permute-start.7 = (f32[6,64,128]{2,1,0:T(8,128)S(1)}, f32[6,64,128]{2,1,0:T(8,128)S(1)}, u32[]{:S(2)}, u32[]{:S(2)}) collective-permute-start(f32[6,64,128]{2,1,0:T(8,128)S(1)} %get-tuple-element.51), channel_id=1, source_target_pairs={{4,8},{8,4},{12,16},{16,12},{20,24},{24,20},{5,9},{9,5},{13,17},{1... | collective-permute-start | bytes 589832 | tf_op jit(solution)/shard_map/ppermute | solution.py:470
  22.2 6.9 %collective-permute-start.8 = (f32[6,16,128]{2,1,0:T(8,128)S(1)}, f32[6,16,128]{2,1,0:T(8,128)S(1)}, u32[]{:S(2)}, u32[]{:S(2)}) collective-permute-start(f32[6,16,128]{2,1,0:T(8,128)S(1)} %get-tuple-element.52), channel_id=1, source_target_pairs={{4,8},{8,4},{12,16},{16,12},{20,24},{24,20},{5,9},{9,5},{13,17},{1... | collective-permute-start | bytes 147464 | tf_op jit(solution)/shard_map/ppermute | solution.py:470
  24.6 5.0 %collective-permute-start.9 = (f32[6,16,128]{2,1,0:T(8,128)S(1)}, f32[6,16,128]{2,1,0:T(8,128)S(1)}, u32[]{:S(2)}, u32[]{:S(2)}) collective-permute-start(f32[6,16,128]{2,1,0:T(8,128)S(1)} %get-tuple-element.53), channel_id=1, source_target_pairs={{0,4},{4,0},{8,12},{12,8},{16,20},{20,16},{24,28},{28,24},{1,5},{5... | collective-permute-start | bytes 147464 | tf_op jit(solution)/shard_map/ppermute | solution.py:470

commit v21 on v19

--- a/solution.py
+++ b/solution.py
@@ -16,6 +16,7 @@
 LANES = 128
 TERM = 32
 SPARE = 8
+HALF = 256
 TERMS = ((0, 0), (0, 1), (0, 2), (1, 0), (1, 1), (2, 0))
 
 POISSON = 0.3
@@ -204,13 +205,13 @@
     copies[2].wait()
     ids[0:1, 0:q] = corner_v[...].astype(F32)
     wanted = column(ids[0:1, :LANES])[:TERM]
-    lane = lax.broadcasted_iota(jnp.int32, (TERM, 3 * LANES), 1)
+    lane = lax.broadcasted_iota(jnp.int32, (TERM, 2 * HALF), 1)
     entry = lax.broadcasted_iota(jnp.int32, (TERM, LANES), 0)
     s, g = lax.axis_index("sub"), lax.axis_index("grp")
     aside = 1 - 2 * (s & 1)
-    row = jnp.full((TERM, 3 * LANES), -1, jnp.int32)
-    base = 0
+    row = jnp.full((TERM, 2 * HALF), -1, jnp.int32)
     for core in range(2):
+        base = core * HALF
         for owner in (s, s - aside, s + aside):
             for member in range(members // 2):
                 distance, bits, turn = members // 2, member, core
@@ -220,7 +221,7 @@
                 first = (owner * members + (g ^ turn)) * block_rows
                 row = jnp.where((lane >= base) & (lane < base + block_rows), first - base + lane, row)
                 base += block_rows
-    for b in range(3):
+    for b in range(2 * HALF // LANES):
         cols = slice(b * LANES, (b + 1) * LANES)
         hit = (wanted == row[:, cols].astype(F32)) & (entry < q)
         select[:, cols] = jnp.where(hit, 1.0, 0.0).astype(BF16)
@@ -299,7 +300,17 @@
     free_stress(free_t, 0, stress_first.shape[1], onehot, scaled, sofar, stress_first)
 
 
-def stress_kernel(free_t, onehot, scaled, out, sofar):
+def pick_rows(select, block, terms):
+    rows = block.shape[0]
+    terms[:, rows:, :] = jnp.zeros((3, terms.shape[1] - rows, terms.shape[2]), BF16)
+    for t, value in enumerate(split_three(block[...])):
+        terms[t, :rows, :] = value
+    return [dot(select, terms[t]) for t in range(3)]
+
+
+def stress_kernel(free_t, onehot, scaled, near, select, out, picked, sofar, terms):
+    for t, value in enumerate(pick_rows(select[:, :HALF], near, terms)):
+        picked[t] = value
     rows = out.shape[1]
     free_stress(free_t, free_t.shape[0] - rows, rows, onehot, scaled, sofar, out)
 
@@ -313,8 +324,8 @@
 
 
 def solve_kernel(
-    near,
     across,
+    picked_near,
     select,
     stress_first,
     stress_rest,
@@ -328,12 +339,8 @@
     grp_b,
     terms,
 ):
-    rows = near.shape[0]
-    terms[:, 2 * rows :, :] = jnp.zeros((3, terms.shape[1] - 2 * rows, terms.shape[2]), BF16)
-    for b, block in enumerate((near, across)):
-        for t, value in enumerate(split_three(block[...])):
-            terms[t, b * rows : (b + 1) * rows, :] = value
-    picked = [dot(select[...], terms[t]) for t in range(3)]
+    picked = pick_rows(select[:, HALF:], across, terms)
+    picked = [picked[t] + picked_near[t] for t in range(3)]
     ordered = [picked[term] for _, term in TERMS]
     ordered += [jnp.zeros_like(picked[0])] * (stress_corner.shape[0] // TERM - len(ordered))
     per = LANES // TERM
@@ -407,9 +414,10 @@
         added = dot(placing[...], received[:, i * LANES : (i + 2) * LANES])
         nodal[i] = ((partial[i] + added[:, :LANES]) * scale).astype(BF16)
         nodal[i + 1] = ((partial[i + 1] + added[:, LANES:]) * scale).astype(BF16)
-        copy = pltpu.make_async_copy(nodal.at[pl.ds(i, 2)], out.at[pl.ds(i, 2)], sems.at[i // 2])
-        copy.start()
-        copies.append(copy)
+        for k in (i, i + 1):
+            copy = pltpu.make_async_copy(nodal.at[k], out.at[k], sems.at[k])
+            copy.start()
+            copies.append(copy)
     for copy in copies:
         copy.wait()
 
@@ -512,7 +520,7 @@
             array(panel_nodes.shape, jnp.int32),
             array((3, nodes, cases), BF16),
             array(panel_inv.shape, BF16),
-            array((TERM, 3 * LANES), BF16),
+            array((TERM, 2 * HALF), BF16),
             array((nodes, CORNERS * LANES), BF16),
             array((NIF, 2 * LANES), BF16),
             array((COMPS * 24, 8, LANES)),
@@ -568,17 +576,19 @@
         flops=400000000,
         moved=4000000,
     )(coupling.T, *panels, onehot, scaled)
-    (stress_rest,) = call(
+    near, across = gather_near(coarse, own, [select, corner_t])
+    stress_rest, picked_near = call(
         stress_kernel,
         "stress_of_loads",
-        (array((COMPS, cases - first, LANES)),),
-        vmem(3),
-        (pltpu.VMEM((COMPS, cases - first, LANES), F32),),
+        (array((COMPS, cases - first, LANES)), array((3, TERM, cases))),
+        vmem(5),
+        (
+            pltpu.VMEM((COMPS, cases - first, LANES), F32),
+            pltpu.VMEM((3, HALF, cases), BF16),
+        ),
         flops=400000000,
         moved=4000000,
-    )(free_t, onehot, scaled)
-
-    near = gather_near(coarse, own, [select, corner_t])
+    )(free_t, onehot, scaled, near, select)
     values, stress, sub_a, sub_b, grp_a, grp_b = call(
         solve_kernel,
         "stress_and_rows",
@@ -591,10 +601,10 @@
             array((COMPS, NIG + 2 * NED, cases)),
         ),
         vmem(7),
-        (pltpu.VMEM((3, 3 * LANES, cases), BF16),),
+        (pltpu.VMEM((3, HALF, cases), BF16),),
         flops=300000000,
         moved=3000000,
-    )(*near, select, stress_first, stress_rest, stress_corner, face)
+    )(across, picked_near, select, stress_first, stress_rest, stress_corner, face)
     from_sub_a = exchange(sub_a, "sub", 0)
     from_grp_a = exchange(grp_a, "grp", 0)
     from_grp_b = exchange(grp_b, "grp", 1)
@@ -624,7 +634,7 @@
         (
             pltpu.VMEM((NIS + 2 * LATE, COMPS * cases), BF16),
             pltpu.VMEM((COMPS, nodes, cases), BF16),
-            pltpu.SemaphoreType.DMA((COMPS // 2,)),
+            pltpu.SemaphoreType.DMA((COMPS,)),
         ),
         flops=400000000,
         moved=3000000,

time: 30.7 us -> 30.7 us (level)
  no operation moved by 1% of the time
where the time goes in v21:
time: 30.7 us; the launch traced here: 30.3 us
  starting transfers between devices  17.1 us (56%)
  Pallas kernels  8.31 us (27%)
  waiting for transfers between devices  4.11 us (13%)
  between operations  0.74 us (2%)
    ppermute x8, starting transfers between devices, exchange(): return lax.ppermute(block, axis, pairs)  16.5 us
    ppermute x8, waiting for transfers between devices, exchange(): return lax.ppermute(block, axis, pairs)  2.25 us
    pallas_call x1, Pallas kernels, shards(): call(prepare_panels, 'prepare_panels', (array((cases, dofs)), array((2 *...  2.14 us
    pallas_call x1, Pallas kernels, shards(): call(lists, 'prepare_lists', (array(coarse.shape), array(panel_nodes.shap...  1.91 us
    ppermute x2, waiting for transfers between devices, across(): lax.ppermute(block, 'grp', [(i, i ^ distance) for i in range(lax.axis_siz...  1.86 us
    pallas_call x1, Pallas kernels, shards(): call(partial_kernel, 'assemble_nodes', (array((COMPS, nodes, cases)), arr...  1.46 us
    pallas_call x1, Pallas kernels, shards(): call(finish_kernel, 'add_last', (array((COMPS, nodes, cases), BF16),), vm...  1.23 us
    pallas_call x1, Pallas kernels, shards(): call(stress_kernel, 'stress_of_loads', (array((COMPS, cases - first, LANE...  0.83 us
  transfers between devices with their start and end apart: 10, of which 5 were waited for; matrix products, arithmetic and copies ran while one was open for 0% of the time, Pallas kernels for 21%

profile of v21, /device:TPU:10, one launch (start us, length us, event | category | flops | bytes accessed | tf_op | source)
XLA Modules:
  0.0 30.3 jit_solution(8850959004710880219)
XLA Ops:
  0.6 0.0 copy-start
  0.6 0.6 %collective-permute-start = (f32[24,128]{1,0:T(8,128)}, f32[24,128]{1,0:T(8,128)S(1)}, u32[]{:S(2)}, u32[]{:S(2)}) collective-permute-start(f32[24,128]{1,0:T(8,128)} %refs_6_.1), channel_id=1, source_target_pairs={{0,2},{1,3},{2,0},{3,1},{4,6},{5,7},{6,4},{7,5},{8,10},{9,11},{10,... | collective-permute-start | bytes 36872 | tf_op jit(solution)/shard_map/ppermute | solution.py:481
  1.2 1.9 %prepare_lists.1 = (f32[24,128]{1,0:T(8,128)S(1)}, s32[1,4]{1,0:T(1,128)S(1)}, bf16[3,512,128]{2,1,0:T(8,128)(2,1)S(1)}, bf16[4,384,384]{2,1,0:T(8,128)(2,1)S(1)...) custom-call(s32[1,24]{1,0:T(1,128)} %refs_0_.1, ...), custom_call_target="tpu_custom_call" | custom-call | flops 100000000 | bytes 4000000 | tf_op jit(solution)/shard_map/prepare_lists/pallas_call | solution.py:515
  3.2 1.4 %collective-permute-done.refs_1_ = f32[24,128]{1,0:T(8,128)S(1)} collective-permute-done((f32[24,128]{1,0:T(8,128)}, f32[24,128]{1,0:T(8,128)S(1)}, u32[]{:S(2)}, u32[]{:S(2)}) %collective-permute-start) | collective-permute-done | bytes 12320 | tf_op jit(solution)/shard_map/ppermute | solution.py:481
  4.6 3.3 %collective-permute-start.1 = (f32[48,128]{1,0:T(8,128)S(1)}, f32[48,128]{1,0:T(8,128)S(1)}, u32[]{:S(2)}, u32[]{:S(2)}) collective-permute-start(f32[48,128]{1,0:T(8,128)S(1)} %join_blocks.2.refs_0_), channel_id=1, source_target_pairs={{4,8},{8,4},{12,16},{16,12},{20,24},{24,20},{5,9},{9,5},{13,17},{1... | collective-permute-start | bytes 73736 | tf_op jit(solution)/shard_map/ppermute | solution.py:459
  7.9 1.7 %collective-permute-start.2 = (f32[48,128]{1,0:T(8,128)S(1)}, f32[48,128]{1,0:T(8,128)S(1)}, u32[]{:S(2)}, u32[]{:S(2)}) collective-permute-start(f32[48,128]{1,0:T(8,128)S(1)} %join_blocks.2.refs_0_), channel_id=1, source_target_pairs={{0,4},{4,0},{8,12},{12,8},{16,20},{20,16},{24,28},{28,24},{1,5},{5... | collective-permute-start | bytes 73736 | tf_op jit(solution)/shard_map/ppermute | solution.py:459
  9.6 0.0 copy-done
  9.6 2.1 %prepare_panels.1 = (f32[128,1536]{1,0:T(8,128)S(1)}, bf16[256,1536]{1,0:T(8,128)(2,1)S(1)}, f32[6,64,128]{2,1,0:T(8,128)S(1)}, bf16[256,768]{1,0:T(8,128)(2,1)S(1)}) custom-call(bf16[24,1536]{1,0:T(8,128)(2,1)S(1)} %bitcast.7, s32[1,4]{1,0:T(1,128)S(1)} %get-tuple-element.33.panel_v, bf16[3,512,128]{2,1,0:T(8,128)(2,1)S(1)} %get-tuple-element.34.force_v, ...), custom_call_target="tpu_custom_call" | custom-call | flops 400000000 | bytes 4000000 | tf_op jit(solution)/shard_map/prepare_panels/pallas_call | solution.py:560
  11.8 0.0 collective-permute-done.1.refs_1_
  11.8 0.0 collective-permute-done.2.refs_2_
  11.8 0.1 collective-permute-start.3
  11.9 0.8 %stress_of_loads.1 = (f32[6,64,128]{2,1,0:T(8,128)S(1)}, f32[3,32,128]{2,1,0:T(8,128)S(1)}) custom-call(f32[128,1536]{1,0:T(8,128)S(1)} %get-tuple-element.39.free_t, bf16[512,1024]{1,0:T(8,128)(2,1)S(1)} %get-tuple-element.36.onehot, f32[144,8,128]{2,1,0:T(8,128)S(1)} %get-tuple-element.37.scaled, f32[144,128]{1,0:T(8,128)S(1)} %join_blocks.3.near, ...), custom_call_target="tpu_custom_call" | custom-call | flops 400000000 | bytes 4000000 | tf_op jit(solution)/shard_map/stress_of_loads/pallas_call | solution.py:580
  12.7 0.4 %collective-permute-done.3.across = f32[144,128]{1,0:T(8,128)S(1)} collective-permute-done((f32[144,128]{1,0:T(8,128)S(1)}, f32[144,128]{1,0:T(8,128)S(1)}, u32[]{:S(2)}, u32[]{:S(2)}) %collective-permute-start.3) | collective-permute-done | bytes 73760 | tf_op jit(solution)/shard_map/ppermute | solution.py:481
  13.2 0.7 %stress_and_rows.1 = (bf16[128,256]{1,0:T(8,128)(2,1)S(1)}, bf16[768,256]{1,0:T(8,128)(2,1)S(1)}, f32[6,64,128]{2,1,0:T(8,128)S(1)}, f32[6,64,128]{2,1,0:T(8,128...) custom-call(f32[144,128]{1,0:T(8,128)S(1)} %collective-permute-done.3.across, ...), custom_call_target="tpu_custom_call" | custom-call | flops 300000000 | bytes 3000000 | tf_op jit(solution)/shard_map/stress_and_rows/pallas_call | solution.py:592
  13.9 0.2 collective-permute-start.4
  14.1 2.4 %collective-permute-start.5 = (f32[6,48,128]{2,1,0:T(8,128)S(1)}, f32[6,48,128]{2,1,0:T(8,128)S(1)}, u32[]{:S(2)}, u32[]{:S(2)}) collective-permute-start(f32[6,48,128]{2,1,0:T(8,128)S(1)} %get-tuple-element.49.grp_b), channel_id=1, source_target_pairs={{1,2},{2,1},{5,6},{6,5},{9,10},{10,9},{13,14},{14,13},{17,18},{18,... | collective-permute-start | bytes 442376 | tf_op jit(solution)/shard_map/ppermute | solution.py:459
  16.5 1.6 %collective-permute-start.6 = (f32[6,64,128]{2,1,0:T(8,128)S(1)}, f32[6,64,128]{2,1,0:T(8,128)S(1)}, u32[]{:S(2)}, u32[]{:S(2)}) collective-permute-start(f32[6,64,128]{2,1,0:T(8,128)S(1)} %get-tuple-element.54), channel_id=1, source_target_pairs={{0,4},{4,0},{8,12},{12,8},{16,20},{20,16},{24,28},{28,24},{1,5},{5... | collective-permute-start | bytes 589832 | tf_op jit(solution)/shard_map/ppermute | solution.py:459
  18.1 2.2 %collective-permute-start.7 = (f32[6,64,128]{2,1,0:T(8,128)S(1)}, f32[6,64,128]{2,1,0:T(8,128)S(1)}, u32[]{:S(2)}, u32[]{:S(2)}) collective-permute-start(f32[6,64,128]{2,1,0:T(8,128)S(1)} %get-tuple-element.55), channel_id=1, source_target_pairs={{4,8},{8,4},{12,16},{16,12},{20,24},{24,20},{5,9},{9,5},{13,17},{1... | collective-permute-start | bytes 589832 | tf_op jit(solution)/shard_map/ppermute | solution.py:459
  20.4 0.0 collective-permute-done.4.grp_a.from_a
  20.4 0.2 collective-permute-done.5.grp_b.from_b
  20.6 4.4 %collective-permute-start.8 = (f32[6,16,128]{2,1,0:T(8,128)S(1)}, f32[6,16,128]{2,1,0:T(8,128)S(1)}, u32[]{:S(2)}, u32[]{:S(2)}) collective-permute-start(f32[6,16,128]{2,1,0:T(8,128)S(1)} %get-tuple-element.56), channel_id=1, source_target_pairs={{4,8},{8,4},{12,16},{16,12},{20,24},{24,20},{5,9},{9,5},{13,17},{1... | collective-permute-start | bytes 147464 | tf_op jit(solution)/shard_map/ppermute | solution.py:459
  24.9 0.7 %collective-permute-start.9 = (f32[6,16,128]{2,1,0:T(8,128)S(1)}, f32[6,16,128]{2,1,0:T(8,128)S(1)}, u32[]{:S(2)}, u32[]{:S(2)}) collective-permute-start(f32[6,16,128]{2,1,0:T(8,128)S(1)} %get-tuple-element.57), channel_id=1, source_target_pairs={{0,4},{4,0},{8,12},{12,8},{16,20},{20,16},{24,28},{28,24},{1,5},{5... | collective-permute-start | bytes 147464 | tf_op jit(solution)/shard_map/ppermute | solution.py:459
  25.6 1.5 %assemble_nodes.1 = (f32[6,512,128]{2,1,0:T(8,128)S(1)}, bf16[3,512,128]{2,1,0:T(8,128)(2,1)}) custom-call(bf16[512,256]{1,0:T(8,128)(2,1)S(1)} %get-tuple-element.30.count, bf16[768,256]{1,0:T(8,128)(2,1)S(1)} %get-tuple-element.45.stress, f32[128,1536]{1,0:T(8,128)S(1)} %get-tuple-element.39.free_t, ...), custom_call_target="tpu_custom_call" | custom-call | flops 400000000 | bytes 2000000 | tf_op jit(solution)/shard_map/assemble_nodes/pallas_call | solution.py:620
  27.0 0.7 %collective-permute-done.6.sub_a = f32[6,64,128]{2,1,0:T(8,128)S(1)} collective-permute-done((f32[6,64,128]{2,1,0:T(8,128)S(1)}, f32[6,64,128]{2,1,0:T(8,128)S(1)}, u32[]{:S(2)}, u32[]{:S(2)}) %collective-permute-start.6) | collective-permute-done | bytes 196640 | tf_op jit(solution)/shard_map/ppermute | solution.py:459
  27.7 0.0 collective-permute-done.7.sub_b
  27.7 0.0 collective-permute-done.8.edge_b
  27.7 1.4 %collective-permute-done.9.edge_a = f32[6,16,128]{2,1,0:T(8,128)S(1)} collective-permute-done((f32[6,16,128]{2,1,0:T(8,128)S(1)}, f32[6,16,128]{2,1,0:T(8,128)S(1)}, u32[]{:S(2)}, u32[]{:S(2)}) %collective-permute-start.9) | collective-permute-done | bytes 49184 | tf_op jit(solution)/shard_map/ppermute | solution.py:459
  29.1 1.2 %add_last.1 = bf16[6,512,128]{2,1,0:T(8,128)(2,1)} custom-call(bf16[512,256]{1,0:T(8,128)(2,1)S(1)} %get-tuple-element.51.placing, f32[6,512,128]{2,1,0:T(8,128)S(1)} %get-tuple-element.52.partial, f32[512,128]{1,0:T(8,128)S(1)} %get-tuple-element.53.inverse_volume, f32[6,64,128]{2,1,0:T(8,128)S(1)} %collective-permute-done.6.sub_a, ...), custom_call_target="tpu_custom_call" | custom-call | flops 400000000 | bytes 3000000 | tf_op jit(solution)/shard_map/add_last/pallas_call | solution.py:629
  (3 shorter events, 0.0 us)
Async XLA Ops:
  0.6 9.0 %copy-start = (bf16[1536,24]{0,1:T(8,128)(2,1)S(1)}, bf16[1536,24]{0,1:T(8,128)(2,1)}, u32[]{:S(2)}) copy-start(bf16[1536,24]{0,1:T(8,128)(2,1)} %param.13) | copy-start | bytes 221188
  0.6 4.0 %collective-permute-start = (f32[24,128]{1,0:T(8,128)}, f32[24,128]{1,0:T(8,128)S(1)}, u32[]{:S(2)}, u32[]{:S(2)}) collective-permute-start(f32[24,128]{1,0:T(8,128)} %refs_6_.1), channel_id=1, source_target_pairs={{0,2},{1,3},{2,0},{3,1},{4,6},{5,7},{6,4},{7,5},{8,10},{9,11},{10,... | collective-permute-start | bytes 36872 | tf_op jit(solution)/shard_map/ppermute | solution.py:481
  4.6 7.2 %collective-permute-start.1 = (f32[48,128]{1,0:T(8,128)S(1)}, f32[48,128]{1,0:T(8,128)S(1)}, u32[]{:S(2)}, u32[]{:S(2)}) collective-permute-start(f32[48,128]{1,0:T(8,128)S(1)} %join_blocks.2.refs_0_), channel_id=1, source_target_pairs={{4,8},{8,4},{12,16},{16,12},{20,24},{24,20},{5,9},{9,5},{13,17},{1... | collective-permute-start | bytes 73736 | tf_op jit(solution)/shard_map/ppermute | solution.py:459
  7.9 3.9 %collective-permute-start.2 = (f32[48,128]{1,0:T(8,128)S(1)}, f32[48,128]{1,0:T(8,128)S(1)}, u32[]{:S(2)}, u32[]{:S(2)}) collective-permute-start(f32[48,128]{1,0:T(8,128)S(1)} %join_blocks.2.refs_0_), channel_id=1, source_target_pairs={{0,4},{4,0},{8,12},{12,8},{16,20},{20,16},{24,28},{28,24},{1,5},{5... | collective-permute-start | bytes 73736 | tf_op jit(solution)/shard_map/ppermute | solution.py:459
  11.8 1.3 %collective-permute-start.3 = (f32[144,128]{1,0:T(8,128)S(1)}, f32[144,128]{1,0:T(8,128)S(1)}, u32[]{:S(2)}, u32[]{:S(2)}) collective-permute-start(f32[144,128]{1,0:T(8,128)S(1)} %join_blocks.3.near), channel_id=1, source_target_pairs={{0,1},{1,0},{2,3},{3,2},{4,5},{5,4},{6,7},{7,6},{8,9},{9,8},{10,11... | collective-permute-start | bytes 221192 | tf_op jit(solution)/shard_map/ppermute | solution.py:481
  13.9 6.5 %collective-permute-start.4 = (f32[6,48,128]{2,1,0:T(8,128)S(1)}, f32[6,48,128]{2,1,0:T(8,128)S(1)}, u32[]{:S(2)}, u32[]{:S(2)}) collective-permute-start(f32[6,48,128]{2,1,0:T(8,128)S(1)} %get-tuple-element.48.grp_a), channel_id=1, source_target_pairs={{0,1},{1,0},{2,3},{3,2},{4,5},{5,4},{6,7},{7,6},{8,9},{9,8},{10,11... | collective-permute-start | bytes 442376 | tf_op jit(solution)/shard_map/ppermute | solution.py:459
  14.1 6.5 %collective-permute-start.5 = (f32[6,48,128]{2,1,0:T(8,128)S(1)}, f32[6,48,128]{2,1,0:T(8,128)S(1)}, u32[]{:S(2)}, u32[]{:S(2)}) collective-permute-start(f32[6,48,128]{2,1,0:T(8,128)S(1)} %get-tuple-element.49.grp_b), channel_id=1, source_target_pairs={{1,2},{2,1},{5,6},{6,5},{9,10},{10,9},{13,14},{14,13},{17,18},{18,... | collective-permute-start | bytes 442376 | tf_op jit(solution)/shard_map/ppermute | solution.py:459
  16.5 11.2 %collective-permute-start.6 = (f32[6,64,128]{2,1,0:T(8,128)S(1)}, f32[6,64,128]{2,1,0:T(8,128)S(1)}, u32[]{:S(2)}, u32[]{:S(2)}) collective-permute-start(f32[6,64,128]{2,1,0:T(8,128)S(1)} %get-tuple-element.54), channel_id=1, source_target_pairs={{0,4},{4,0},{8,12},{12,8},{16,20},{20,16},{24,28},{28,24},{1,5},{5... | collective-permute-start | bytes 589832 | tf_op jit(solution)/shard_map/ppermute | solution.py:459
  18.1 9.6 %collective-permute-start.7 = (f32[6,64,128]{2,1,0:T(8,128)S(1)}, f32[6,64,128]{2,1,0:T(8,128)S(1)}, u32[]{:S(2)}, u32[]{:S(2)}) collective-permute-start(f32[6,64,128]{2,1,0:T(8,128)S(1)} %get-tuple-element.55), channel_id=1, source_target_pairs={{4,8},{8,4},{12,16},{16,12},{20,24},{24,20},{5,9},{9,5},{13,17},{1... | collective-permute-start | bytes 589832 | tf_op jit(solution)/shard_map/ppermute | solution.py:459
  20.6 7.1 %collective-permute-start.8 = (f32[6,16,128]{2,1,0:T(8,128)S(1)}, f32[6,16,128]{2,1,0:T(8,128)S(1)}, u32[]{:S(2)}, u32[]{:S(2)}) collective-permute-start(f32[6,16,128]{2,1,0:T(8,128)S(1)} %get-tuple-element.56), channel_id=1, source_target_pairs={{4,8},{8,4},{12,16},{16,12},{20,24},{24,20},{5,9},{9,5},{13,17},{1... | collective-permute-start | bytes 147464 | tf_op jit(solution)/shard_map/ppermute | solution.py:459
  24.9 4.2 %collective-permute-start.9 = (f32[6,16,128]{2,1,0:T(8,128)S(1)}, f32[6,16,128]{2,1,0:T(8,128)S(1)}, u32[]{:S(2)}, u32[]{:S(2)}) collective-permute-start(f32[6,16,128]{2,1,0:T(8,128)S(1)} %get-tuple-element.57), channel_id=1, source_target_pairs={{0,4},{4,0},{8,12},{12,8},{16,20},{20,16},{24,28},{28,24},{1,5},{5... | collective-permute-start | bytes 147464 | tf_op jit(solution)/shard_map/ppermute | solution.py:459

commit v22 on v21

--- a/solution.py
+++ b/solution.py
@@ -403,21 +403,21 @@
 ):
     scale = inverse_volume[...]
     copies = []
-    for i in range(0, COMPS, 2):
-        for k in (i, i + 1):
+    for i in range(0, COMPS, 3):
+        for k in range(i, i + 3):
             cols = slice(k * LANES, (k + 1) * LANES)
             late = jnp.concatenate([sub_b[k], edge_a[k], edge_b[k]], axis=0)
             first, second = split_two(late)
             received[:NIS, cols] = sub_a[k].astype(BF16)
             received[NIS : NIS + LATE, cols] = first
             received[NIS + LATE :, cols] = second
-        added = dot(placing[...], received[:, i * LANES : (i + 2) * LANES])
-        nodal[i] = ((partial[i] + added[:, :LANES]) * scale).astype(BF16)
-        nodal[i + 1] = ((partial[i + 1] + added[:, LANES:]) * scale).astype(BF16)
-        for k in (i, i + 1):
-            copy = pltpu.make_async_copy(nodal.at[k], out.at[k], sems.at[k])
-            copy.start()
-            copies.append(copy)
+        added = dot(placing[...], received[:, i * LANES : (i + 3) * LANES])
+        for k in range(3):
+            total = partial[i + k] + added[:, k * LANES : (k + 1) * LANES]
+            nodal[i + k] = (total * scale).astype(BF16)
+        copy = pltpu.make_async_copy(nodal.at[pl.ds(i, 3)], out.at[pl.ds(i, 3)], sems.at[i // 3])
+        copy.start()
+        copies.append(copy)
     for copy in copies:
         copy.wait()
 
@@ -634,7 +634,7 @@
         (
             pltpu.VMEM((NIS + 2 * LATE, COMPS * cases), BF16),
             pltpu.VMEM((COMPS, nodes, cases), BF16),
-            pltpu.SemaphoreType.DMA((COMPS,)),
+            pltpu.SemaphoreType.DMA((COMPS // 3,)),
         ),
         flops=400000000,
         moved=3000000,

time: 30.7 us -> 30.7 us (level)
  no operation moved by 1% of the time
where the time goes in v22:
time: 30.7 us; the launch traced here: 30.3 us
  starting transfers between devices  17.1 us (56%)
  Pallas kernels  8.31 us (27%)
  waiting for transfers between devices  4.11 us (13%)
  between operations  0.74 us (2%)
    ppermute x8, starting transfers between devices, exchange(): return lax.ppermute(block, axis, pairs)  16.5 us
    ppermute x8, waiting for transfers between devices, exchange(): return lax.ppermute(block, axis, pairs)  2.25 us
    pallas_call x1, Pallas kernels, shards(): call(prepare_panels, 'prepare_panels', (array((cases, dofs)), array((2 *...  2.14 us
    pallas_call x1, Pallas kernels, shards(): call(lists, 'prepare_lists', (array(coarse.shape), array(panel_nodes.shap...  1.91 us
    ppermute x2, waiting for transfers between devices, across(): lax.ppermute(block, 'grp', [(i, i ^ distance) for i in range(lax.axis_siz...  1.86 us
    pallas_call x1, Pallas kernels, shards(): call(partial_kernel, 'assemble_nodes', (array((COMPS, nodes, cases)), arr...  1.46 us
    pallas_call x1, Pallas kernels, shards(): call(finish_kernel, 'add_last', (array((COMPS, nodes, cases), BF16),), vm...  1.23 us
    pallas_call x1, Pallas kernels, shards(): call(stress_kernel, 'stress_of_loads', (array((COMPS, cases - first, LANE...  0.83 us
  transfers between devices with their start and end apart: 10, of which 5 were waited for; matrix products, arithmetic and copies ran while one was open for 0% of the time, Pallas kernels for 21%

profile of v22, /device:TPU:10, one launch (start us, length us, event | category | flops | bytes accessed | tf_op | source)
XLA Modules:
  0.0 30.3 jit_solution(5605268976088841173)
XLA Ops:
  0.6 0.0 copy-start
  0.6 0.6 %collective-permute-start = (f32[24,128]{1,0:T(8,128)}, f32[24,128]{1,0:T(8,128)S(1)}, u32[]{:S(2)}, u32[]{:S(2)}) collective-permute-start(f32[24,128]{1,0:T(8,128)} %refs_6_.1), channel_id=1, source_target_pairs={{0,2},{1,3},{2,0},{3,1},{4,6},{5,7},{6,4},{7,5},{8,10},{9,11},{10,... | collective-permute-start | bytes 36872 | tf_op jit(solution)/shard_map/ppermute | solution.py:481
  1.2 1.9 %prepare_lists.1 = (f32[24,128]{1,0:T(8,128)S(1)}, s32[1,4]{1,0:T(1,128)S(1)}, bf16[3,512,128]{2,1,0:T(8,128)(2,1)S(1)}, bf16[4,384,384]{2,1,0:T(8,128)(2,1)S(1)...) custom-call(s32[1,24]{1,0:T(1,128)} %refs_0_.1, ...), custom_call_target="tpu_custom_call" | custom-call | flops 100000000 | bytes 4000000 | tf_op jit(solution)/shard_map/prepare_lists/pallas_call | solution.py:515
  3.2 1.4 %collective-permute-done.refs_1_ = f32[24,128]{1,0:T(8,128)S(1)} collective-permute-done((f32[24,128]{1,0:T(8,128)}, f32[24,128]{1,0:T(8,128)S(1)}, u32[]{:S(2)}, u32[]{:S(2)}) %collective-permute-start) | collective-permute-done | bytes 12320 | tf_op jit(solution)/shard_map/ppermute | solution.py:481
  4.6 3.3 %collective-permute-start.1 = (f32[48,128]{1,0:T(8,128)S(1)}, f32[48,128]{1,0:T(8,128)S(1)}, u32[]{:S(2)}, u32[]{:S(2)}) collective-permute-start(f32[48,128]{1,0:T(8,128)S(1)} %join_blocks.2.refs_0_), channel_id=1, source_target_pairs={{4,8},{8,4},{12,16},{16,12},{20,24},{24,20},{5,9},{9,5},{13,17},{1... | collective-permute-start | bytes 73736 | tf_op jit(solution)/shard_map/ppermute | solution.py:459
  7.9 1.7 %collective-permute-start.2 = (f32[48,128]{1,0:T(8,128)S(1)}, f32[48,128]{1,0:T(8,128)S(1)}, u32[]{:S(2)}, u32[]{:S(2)}) collective-permute-start(f32[48,128]{1,0:T(8,128)S(1)} %join_blocks.2.refs_0_), channel_id=1, source_target_pairs={{0,4},{4,0},{8,12},{12,8},{16,20},{20,16},{24,28},{28,24},{1,5},{5... | collective-permute-start | bytes 73736 | tf_op jit(solution)/shard_map/ppermute | solution.py:459
  9.6 0.0 copy-done
  9.6 2.1 %prepare_panels.1 = (f32[128,1536]{1,0:T(8,128)S(1)}, bf16[256,1536]{1,0:T(8,128)(2,1)S(1)}, f32[6,64,128]{2,1,0:T(8,128)S(1)}, bf16[256,768]{1,0:T(8,128)(2,1)S(1)}) custom-call(bf16[24,1536]{1,0:T(8,128)(2,1)S(1)} %bitcast.7, s32[1,4]{1,0:T(1,128)S(1)} %get-tuple-element.33.panel_v, bf16[3,512,128]{2,1,0:T(8,128)(2,1)S(1)} %get-tuple-element.34.force_v, ...), custom_call_target="tpu_custom_call" | custom-call | flops 400000000 | bytes 4000000 | tf_op jit(solution)/shard_map/prepare_panels/pallas_call | solution.py:560
  11.8 0.0 collective-permute-done.1.refs_1_
  11.8 0.0 collective-permute-done.2.refs_2_
  11.8 0.1 collective-permute-start.3
  11.9 0.8 %stress_of_loads.1 = (f32[6,64,128]{2,1,0:T(8,128)S(1)}, f32[3,32,128]{2,1,0:T(8,128)S(1)}) custom-call(f32[128,1536]{1,0:T(8,128)S(1)} %get-tuple-element.39.free_t, bf16[512,1024]{1,0:T(8,128)(2,1)S(1)} %get-tuple-element.36.onehot, f32[144,8,128]{2,1,0:T(8,128)S(1)} %get-tuple-element.37.scaled, f32[144,128]{1,0:T(8,128)S(1)} %join_blocks.3.near, ...), custom_call_target="tpu_custom_call" | custom-call | flops 400000000 | bytes 4000000 | tf_op jit(solution)/shard_map/stress_of_loads/pallas_call | solution.py:580
  12.7 0.4 %collective-permute-done.3.across = f32[144,128]{1,0:T(8,128)S(1)} collective-permute-done((f32[144,128]{1,0:T(8,128)S(1)}, f32[144,128]{1,0:T(8,128)S(1)}, u32[]{:S(2)}, u32[]{:S(2)}) %collective-permute-start.3) | collective-permute-done | bytes 73760 | tf_op jit(solution)/shard_map/ppermute | solution.py:481
  13.2 0.7 %stress_and_rows.1 = (bf16[128,256]{1,0:T(8,128)(2,1)S(1)}, bf16[768,256]{1,0:T(8,128)(2,1)S(1)}, f32[6,64,128]{2,1,0:T(8,128)S(1)}, f32[6,64,128]{2,1,0:T(8,128...) custom-call(f32[144,128]{1,0:T(8,128)S(1)} %collective-permute-done.3.across, ...), custom_call_target="tpu_custom_call" | custom-call | flops 300000000 | bytes 3000000 | tf_op jit(solution)/shard_map/stress_and_rows/pallas_call | solution.py:592
  13.9 0.2 collective-permute-start.4
  14.1 2.4 %collective-permute-start.5 = (f32[6,48,128]{2,1,0:T(8,128)S(1)}, f32[6,48,128]{2,1,0:T(8,128)S(1)}, u32[]{:S(2)}, u32[]{:S(2)}) collective-permute-start(f32[6,48,128]{2,1,0:T(8,128)S(1)} %get-tuple-element.49.grp_b), channel_id=1, source_target_pairs={{1,2},{2,1},{5,6},{6,5},{9,10},{10,9},{13,14},{14,13},{17,18},{18,... | collective-permute-start | bytes 442376 | tf_op jit(solution)/shard_map/ppermute | solution.py:459
  16.5 1.6 %collective-permute-start.6 = (f32[6,64,128]{2,1,0:T(8,128)S(1)}, f32[6,64,128]{2,1,0:T(8,128)S(1)}, u32[]{:S(2)}, u32[]{:S(2)}) collective-permute-start(f32[6,64,128]{2,1,0:T(8,128)S(1)} %get-tuple-element.54), channel_id=1, source_target_pairs={{0,4},{4,0},{8,12},{12,8},{16,20},{20,16},{24,28},{28,24},{1,5},{5... | collective-permute-start | bytes 589832 | tf_op jit(solution)/shard_map/ppermute | solution.py:459
  18.1 2.2 %collective-permute-start.7 = (f32[6,64,128]{2,1,0:T(8,128)S(1)}, f32[6,64,128]{2,1,0:T(8,128)S(1)}, u32[]{:S(2)}, u32[]{:S(2)}) collective-permute-start(f32[6,64,128]{2,1,0:T(8,128)S(1)} %get-tuple-element.55), channel_id=1, source_target_pairs={{4,8},{8,4},{12,16},{16,12},{20,24},{24,20},{5,9},{9,5},{13,17},{1... | collective-permute-start | bytes 589832 | tf_op jit(solution)/shard_map/ppermute | solution.py:459
  20.4 0.0 collective-permute-done.4.grp_a.from_a
  20.4 0.2 collective-permute-done.5.grp_b.from_b
  20.6 4.4 %collective-permute-start.8 = (f32[6,16,128]{2,1,0:T(8,128)S(1)}, f32[6,16,128]{2,1,0:T(8,128)S(1)}, u32[]{:S(2)}, u32[]{:S(2)}) collective-permute-start(f32[6,16,128]{2,1,0:T(8,128)S(1)} %get-tuple-element.56), channel_id=1, source_target_pairs={{4,8},{8,4},{12,16},{16,12},{20,24},{24,20},{5,9},{9,5},{13,17},{1... | collective-permute-start | bytes 147464 | tf_op jit(solution)/shard_map/ppermute | solution.py:459
  24.9 0.7 %collective-permute-start.9 = (f32[6,16,128]{2,1,0:T(8,128)S(1)}, f32[6,16,128]{2,1,0:T(8,128)S(1)}, u32[]{:S(2)}, u32[]{:S(2)}) collective-permute-start(f32[6,16,128]{2,1,0:T(8,128)S(1)} %get-tuple-element.57), channel_id=1, source_target_pairs={{0,4},{4,0},{8,12},{12,8},{16,20},{20,16},{24,28},{28,24},{1,5},{5... | collective-permute-start | bytes 147464 | tf_op jit(solution)/shard_map/ppermute | solution.py:459
  25.6 1.5 %assemble_nodes.1 = (f32[6,512,128]{2,1,0:T(8,128)S(1)}, bf16[3,512,128]{2,1,0:T(8,128)(2,1)}) custom-call(bf16[512,256]{1,0:T(8,128)(2,1)S(1)} %get-tuple-element.30.count, bf16[768,256]{1,0:T(8,128)(2,1)S(1)} %get-tuple-element.45.stress, f32[128,1536]{1,0:T(8,128)S(1)} %get-tuple-element.39.free_t, ...), custom_call_target="tpu_custom_call" | custom-call | flops 400000000 | bytes 2000000 | tf_op jit(solution)/shard_map/assemble_nodes/pallas_call | solution.py:620
  27.0 0.7 %collective-permute-done.6.sub_a = f32[6,64,128]{2,1,0:T(8,128)S(1)} collective-permute-done((f32[6,64,128]{2,1,0:T(8,128)S(1)}, f32[6,64,128]{2,1,0:T(8,128)S(1)}, u32[]{:S(2)}, u32[]{:S(2)}) %collective-permute-start.6) | collective-permute-done | bytes 196640 | tf_op jit(solution)/shard_map/ppermute | solution.py:459
  27.7 0.0 collective-permute-done.7.sub_b
  27.7 0.0 collective-permute-done.8.edge_b
  27.7 1.4 %collective-permute-done.9.edge_a = f32[6,16,128]{2,1,0:T(8,128)S(1)} collective-permute-done((f32[6,16,128]{2,1,0:T(8,128)S(1)}, f32[6,16,128]{2,1,0:T(8,128)S(1)}, u32[]{:S(2)}, u32[]{:S(2)}) %collective-permute-start.9) | collective-permute-done | bytes 49184 | tf_op jit(solution)/shard_map/ppermute | solution.py:459
  29.1 1.2 %add_last.1 = bf16[6,512,128]{2,1,0:T(8,128)(2,1)} custom-call(bf16[512,256]{1,0:T(8,128)(2,1)S(1)} %get-tuple-element.51.placing, f32[6,512,128]{2,1,0:T(8,128)S(1)} %get-tuple-element.52.partial, f32[512,128]{1,0:T(8,128)S(1)} %get-tuple-element.53.inverse_volume, f32[6,64,128]{2,1,0:T(8,128)S(1)} %collective-permute-done.6.sub_a, ...), custom_call_target="tpu_custom_call" | custom-call | flops 400000000 | bytes 3000000 | tf_op jit(solution)/shard_map/add_last/pallas_call | solution.py:629
  (3 shorter events, 0.0 us)
Async XLA Ops:
  0.6 9.0 %copy-start = (bf16[1536,24]{0,1:T(8,128)(2,1)S(1)}, bf16[1536,24]{0,1:T(8,128)(2,1)}, u32[]{:S(2)}) copy-start(bf16[1536,24]{0,1:T(8,128)(2,1)} %param.13) | copy-start | bytes 221188
  0.6 4.0 %collective-permute-start = (f32[24,128]{1,0:T(8,128)}, f32[24,128]{1,0:T(8,128)S(1)}, u32[]{:S(2)}, u32[]{:S(2)}) collective-permute-start(f32[24,128]{1,0:T(8,128)} %refs_6_.1), channel_id=1, source_target_pairs={{0,2},{1,3},{2,0},{3,1},{4,6},{5,7},{6,4},{7,5},{8,10},{9,11},{10,... | collective-permute-start | bytes 36872 | tf_op jit(solution)/shard_map/ppermute | solution.py:481
  4.6 7.2 %collective-permute-start.1 = (f32[48,128]{1,0:T(8,128)S(1)}, f32[48,128]{1,0:T(8,128)S(1)}, u32[]{:S(2)}, u32[]{:S(2)}) collective-permute-start(f32[48,128]{1,0:T(8,128)S(1)} %join_blocks.2.refs_0_), channel_id=1, source_target_pairs={{4,8},{8,4},{12,16},{16,12},{20,24},{24,20},{5,9},{9,5},{13,17},{1... | collective-permute-start | bytes 73736 | tf_op jit(solution)/shard_map/ppermute | solution.py:459
  7.9 3.9 %collective-permute-start.2 = (f32[48,128]{1,0:T(8,128)S(1)}, f32[48,128]{1,0:T(8,128)S(1)}, u32[]{:S(2)}, u32[]{:S(2)}) collective-permute-start(f32[48,128]{1,0:T(8,128)S(1)} %join_blocks.2.refs_0_), channel_id=1, source_target_pairs={{0,4},{4,0},{8,12},{12,8},{16,20},{20,16},{24,28},{28,24},{1,5},{5... | collective-permute-start | bytes 73736 | tf_op jit(solution)/shard_map/ppermute | solution.py:459
  11.8 1.3 %collective-permute-start.3 = (f32[144,128]{1,0:T(8,128)S(1)}, f32[144,128]{1,0:T(8,128)S(1)}, u32[]{:S(2)}, u32[]{:S(2)}) collective-permute-start(f32[144,128]{1,0:T(8,128)S(1)} %join_blocks.3.near), channel_id=1, source_target_pairs={{0,1},{1,0},{2,3},{3,2},{4,5},{5,4},{6,7},{7,6},{8,9},{9,8},{10,11... | collective-permute-start | bytes 221192 | tf_op jit(solution)/shard_map/ppermute | solution.py:481
  13.9 6.5 %collective-permute-start.4 = (f32[6,48,128]{2,1,0:T(8,128)S(1)}, f32[6,48,128]{2,1,0:T(8,128)S(1)}, u32[]{:S(2)}, u32[]{:S(2)}) collective-permute-start(f32[6,48,128]{2,1,0:T(8,128)S(1)} %get-tuple-element.48.grp_a), channel_id=1, source_target_pairs={{0,1},{1,0},{2,3},{3,2},{4,5},{5,4},{6,7},{7,6},{8,9},{9,8},{10,11... | collective-permute-start | bytes 442376 | tf_op jit(solution)/shard_map/ppermute | solution.py:459
  14.1 6.5 %collective-permute-start.5 = (f32[6,48,128]{2,1,0:T(8,128)S(1)}, f32[6,48,128]{2,1,0:T(8,128)S(1)}, u32[]{:S(2)}, u32[]{:S(2)}) collective-permute-start(f32[6,48,128]{2,1,0:T(8,128)S(1)} %get-tuple-element.49.grp_b), channel_id=1, source_target_pairs={{1,2},{2,1},{5,6},{6,5},{9,10},{10,9},{13,14},{14,13},{17,18},{18,... | collective-permute-start | bytes 442376 | tf_op jit(solution)/shard_map/ppermute | solution.py:459
  16.5 11.2 %collective-permute-start.6 = (f32[6,64,128]{2,1,0:T(8,128)S(1)}, f32[6,64,128]{2,1,0:T(8,128)S(1)}, u32[]{:S(2)}, u32[]{:S(2)}) collective-permute-start(f32[6,64,128]{2,1,0:T(8,128)S(1)} %get-tuple-element.54), channel_id=1, source_target_pairs={{0,4},{4,0},{8,12},{12,8},{16,20},{20,16},{24,28},{28,24},{1,5},{5... | collective-permute-start | bytes 589832 | tf_op jit(solution)/shard_map/ppermute | solution.py:459
  18.1 9.6 %collective-permute-start.7 = (f32[6,64,128]{2,1,0:T(8,128)S(1)}, f32[6,64,128]{2,1,0:T(8,128)S(1)}, u32[]{:S(2)}, u32[]{:S(2)}) collective-permute-start(f32[6,64,128]{2,1,0:T(8,128)S(1)} %get-tuple-element.55), channel_id=1, source_target_pairs={{4,8},{8,4},{12,16},{16,12},{20,24},{24,20},{5,9},{9,5},{13,17},{1... | collective-permute-start | bytes 589832 | tf_op jit(solution)/shard_map/ppermute | solution.py:459
  20.6 7.1 %collective-permute-start.8 = (f32[6,16,128]{2,1,0:T(8,128)S(1)}, f32[6,16,128]{2,1,0:T(8,128)S(1)}, u32[]{:S(2)}, u32[]{:S(2)}) collective-permute-start(f32[6,16,128]{2,1,0:T(8,128)S(1)} %get-tuple-element.56), channel_id=1, source_target_pairs={{4,8},{8,4},{12,16},{16,12},{20,24},{24,20},{5,9},{9,5},{13,17},{1... | collective-permute-start | bytes 147464 | tf_op jit(solution)/shard_map/ppermute | solution.py:459
  24.9 4.2 %collective-permute-start.9 = (f32[6,16,128]{2,1,0:T(8,128)S(1)}, f32[6,16,128]{2,1,0:T(8,128)S(1)}, u32[]{:S(2)}, u32[]{:S(2)}) collective-permute-start(f32[6,16,128]{2,1,0:T(8,128)S(1)} %get-tuple-element.57), channel_id=1, source_target_pairs={{0,4},{4,0},{8,12},{12,8},{16,20},{20,16},{24,28},{28,24},{1,5},{5... | collective-permute-start | bytes 147464 | tf_op jit(solution)/shard_map/ppermute | solution.py:459

commit v23 on v21

--- a/solution.py
+++ b/solution.py
@@ -414,10 +414,9 @@
         added = dot(placing[...], received[:, i * LANES : (i + 2) * LANES])
         nodal[i] = ((partial[i] + added[:, :LANES]) * scale).astype(BF16)
         nodal[i + 1] = ((partial[i + 1] + added[:, LANES:]) * scale).astype(BF16)
-        for k in (i, i + 1):
-            copy = pltpu.make_async_copy(nodal.at[k], out.at[k], sems.at[k])
-            copy.start()
-            copies.append(copy)
+        copy = pltpu.make_async_copy(nodal.at[pl.ds(i, 2)], out.at[pl.ds(i, 2)], sems.at[i // 2])
+        copy.start()
+        copies.append(copy)
     for copy in copies:
         copy.wait()
 
@@ -634,7 +633,7 @@
         (
             pltpu.VMEM((NIS + 2 * LATE, COMPS * cases), BF16),
             pltpu.VMEM((COMPS, nodes, cases), BF16),
-            pltpu.SemaphoreType.DMA((COMPS,)),
+            pltpu.SemaphoreType.DMA((COMPS // 2,)),
         ),
         flops=400000000,
         moved=3000000,

time: 30.7 us -> 30.7 us (level)
  no operation moved by 1% of the time
where the time goes in v23:
time: 30.7 us; the launch traced here: 30.3 us
  starting transfers between devices  17.1 us (56%)
  Pallas kernels  8.29 us (27%)
  waiting for transfers between devices  4.11 us (13%)
  between operations  0.74 us (2%)
    ppermute x8, starting transfers between devices, exchange(): return lax.ppermute(block, axis, pairs)  16.5 us
    ppermute x8, waiting for transfers between devices, exchange(): return lax.ppermute(block, axis, pairs)  2.25 us
    pallas_call x1, Pallas kernels, shards(): call(prepare_panels, 'prepare_panels', (array((cases, dofs)), array((2 *...  2.14 us
    pallas_call x1, Pallas kernels, shards(): call(lists, 'prepare_lists', (array(coarse.shape), array(panel_nodes.shap...  1.91 us
    ppermute x2, waiting for transfers between devices, across(): lax.ppermute(block, 'grp', [(i, i ^ distance) for i in range(lax.axis_siz...  1.86 us
    pallas_call x1, Pallas kernels, shards(): call(partial_kernel, 'assemble_nodes', (array((COMPS, nodes, cases)), arr...  1.46 us
    pallas_call x1, Pallas kernels, shards(): call(finish_kernel, 'add_last', (array((COMPS, nodes, cases), BF16),), vm...  1.21 us
    pallas_call x1, Pallas kernels, shards(): call(stress_kernel, 'stress_of_loads', (array((COMPS, cases - first, LANE...  0.83 us
  transfers between devices with their start and end apart: 10, of which 5 were waited for; matrix products, arithmetic and copies ran while one was open for 0% of the time, Pallas kernels for 21%

profile of v23, /device:TPU:10, one launch (start us, length us, event | category | flops | bytes accessed | tf_op | source)
XLA Modules:
  0.0 30.3 jit_solution(7662277194318446018)
XLA Ops:
  0.6 0.0 copy-start
  0.6 0.6 %collective-permute-start = (f32[24,128]{1,0:T(8,128)}, f32[24,128]{1,0:T(8,128)S(1)}, u32[]{:S(2)}, u32[]{:S(2)}) collective-permute-start(f32[24,128]{1,0:T(8,128)} %refs_6_.1), channel_id=1, source_target_pairs={{0,2},{1,3},{2,0},{3,1},{4,6},{5,7},{6,4},{7,5},{8,10},{9,11},{10,... | collective-permute-start | bytes 36872 | tf_op jit(solution)/shard_map/ppermute | solution.py:480
  1.2 1.9 %prepare_lists.1 = (f32[24,128]{1,0:T(8,128)S(1)}, s32[1,4]{1,0:T(1,128)S(1)}, bf16[3,512,128]{2,1,0:T(8,128)(2,1)S(1)}, bf16[4,384,384]{2,1,0:T(8,128)(2,1)S(1)...) custom-call(s32[1,24]{1,0:T(1,128)} %refs_0_.1, ...), custom_call_target="tpu_custom_call" | custom-call | flops 100000000 | bytes 4000000 | tf_op jit(solution)/shard_map/prepare_lists/pallas_call | solution.py:514
  3.2 1.4 %collective-permute-done.refs_1_ = f32[24,128]{1,0:T(8,128)S(1)} collective-permute-done((f32[24,128]{1,0:T(8,128)}, f32[24,128]{1,0:T(8,128)S(1)}, u32[]{:S(2)}, u32[]{:S(2)}) %collective-permute-start) | collective-permute-done | bytes 12320 | tf_op jit(solution)/shard_map/ppermute | solution.py:480
  4.6 3.3 %collective-permute-start.1 = (f32[48,128]{1,0:T(8,128)S(1)}, f32[48,128]{1,0:T(8,128)S(1)}, u32[]{:S(2)}, u32[]{:S(2)}) collective-permute-start(f32[48,128]{1,0:T(8,128)S(1)} %join_blocks.2.refs_0_), channel_id=1, source_target_pairs={{4,8},{8,4},{12,16},{16,12},{20,24},{24,20},{5,9},{9,5},{13,17},{1... | collective-permute-start | bytes 73736 | tf_op jit(solution)/shard_map/ppermute | solution.py:458
  7.9 1.7 %collective-permute-start.2 = (f32[48,128]{1,0:T(8,128)S(1)}, f32[48,128]{1,0:T(8,128)S(1)}, u32[]{:S(2)}, u32[]{:S(2)}) collective-permute-start(f32[48,128]{1,0:T(8,128)S(1)} %join_blocks.2.refs_0_), channel_id=1, source_target_pairs={{0,4},{4,0},{8,12},{12,8},{16,20},{20,16},{24,28},{28,24},{1,5},{5... | collective-permute-start | bytes 73736 | tf_op jit(solution)/shard_map/ppermute | solution.py:458
  9.6 0.0 copy-done
  9.6 2.1 %prepare_panels.1 = (f32[128,1536]{1,0:T(8,128)S(1)}, bf16[256,1536]{1,0:T(8,128)(2,1)S(1)}, f32[6,64,128]{2,1,0:T(8,128)S(1)}, bf16[256,768]{1,0:T(8,128)(2,1)S(1)}) custom-call(bf16[24,1536]{1,0:T(8,128)(2,1)S(1)} %bitcast.7, s32[1,4]{1,0:T(1,128)S(1)} %get-tuple-element.33.panel_v, bf16[3,512,128]{2,1,0:T(8,128)(2,1)S(1)} %get-tuple-element.34.force_v, ...), custom_call_target="tpu_custom_call" | custom-call | flops 400000000 | bytes 4000000 | tf_op jit(solution)/shard_map/prepare_panels/pallas_call | solution.py:559
  11.8 0.0 collective-permute-done.1.refs_1_
  11.8 0.0 collective-permute-done.2.refs_2_
  11.8 0.1 collective-permute-start.3
  11.9 0.8 %stress_of_loads.1 = (f32[6,64,128]{2,1,0:T(8,128)S(1)}, f32[3,32,128]{2,1,0:T(8,128)S(1)}) custom-call(f32[128,1536]{1,0:T(8,128)S(1)} %get-tuple-element.39.free_t, bf16[512,1024]{1,0:T(8,128)(2,1)S(1)} %get-tuple-element.36.onehot, f32[144,8,128]{2,1,0:T(8,128)S(1)} %get-tuple-element.37.scaled, f32[144,128]{1,0:T(8,128)S(1)} %join_blocks.3.near, ...), custom_call_target="tpu_custom_call" | custom-call | flops 400000000 | bytes 4000000 | tf_op jit(solution)/shard_map/stress_of_loads/pallas_call | solution.py:579
  12.7 0.4 %collective-permute-done.3.across = f32[144,128]{1,0:T(8,128)S(1)} collective-permute-done((f32[144,128]{1,0:T(8,128)S(1)}, f32[144,128]{1,0:T(8,128)S(1)}, u32[]{:S(2)}, u32[]{:S(2)}) %collective-permute-start.3) | collective-permute-done | bytes 73760 | tf_op jit(solution)/shard_map/ppermute | solution.py:480
  13.2 0.7 %stress_and_rows.1 = (bf16[128,256]{1,0:T(8,128)(2,1)S(1)}, bf16[768,256]{1,0:T(8,128)(2,1)S(1)}, f32[6,64,128]{2,1,0:T(8,128)S(1)}, f32[6,64,128]{2,1,0:T(8,128...) custom-call(f32[144,128]{1,0:T(8,128)S(1)} %collective-permute-done.3.across, ...), custom_call_target="tpu_custom_call" | custom-call | flops 300000000 | bytes 3000000 | tf_op jit(solution)/shard_map/stress_and_rows/pallas_call | solution.py:591
  13.9 0.2 collective-permute-start.4
  14.1 2.4 %collective-permute-start.5 = (f32[6,48,128]{2,1,0:T(8,128)S(1)}, f32[6,48,128]{2,1,0:T(8,128)S(1)}, u32[]{:S(2)}, u32[]{:S(2)}) collective-permute-start(f32[6,48,128]{2,1,0:T(8,128)S(1)} %get-tuple-element.49.grp_b), channel_id=1, source_target_pairs={{1,2},{2,1},{5,6},{6,5},{9,10},{10,9},{13,14},{14,13},{17,18},{18,... | collective-permute-start | bytes 442376 | tf_op jit(solution)/shard_map/ppermute | solution.py:458
  16.5 1.6 %collective-permute-start.6 = (f32[6,64,128]{2,1,0:T(8,128)S(1)}, f32[6,64,128]{2,1,0:T(8,128)S(1)}, u32[]{:S(2)}, u32[]{:S(2)}) collective-permute-start(f32[6,64,128]{2,1,0:T(8,128)S(1)} %get-tuple-element.54), channel_id=1, source_target_pairs={{0,4},{4,0},{8,12},{12,8},{16,20},{20,16},{24,28},{28,24},{1,5},{5... | collective-permute-start | bytes 589832 | tf_op jit(solution)/shard_map/ppermute | solution.py:458
  18.1 2.2 %collective-permute-start.7 = (f32[6,64,128]{2,1,0:T(8,128)S(1)}, f32[6,64,128]{2,1,0:T(8,128)S(1)}, u32[]{:S(2)}, u32[]{:S(2)}) collective-permute-start(f32[6,64,128]{2,1,0:T(8,128)S(1)} %get-tuple-element.55), channel_id=1, source_target_pairs={{4,8},{8,4},{12,16},{16,12},{20,24},{24,20},{5,9},{9,5},{13,17},{1... | collective-permute-start | bytes 589832 | tf_op jit(solution)/shard_map/ppermute | solution.py:458
  20.4 0.0 collective-permute-done.4.grp_a.from_a
  20.4 0.2 collective-permute-done.5.grp_b.from_b
  20.6 4.4 %collective-permute-start.8 = (f32[6,16,128]{2,1,0:T(8,128)S(1)}, f32[6,16,128]{2,1,0:T(8,128)S(1)}, u32[]{:S(2)}, u32[]{:S(2)}) collective-permute-start(f32[6,16,128]{2,1,0:T(8,128)S(1)} %get-tuple-element.56), channel_id=1, source_target_pairs={{4,8},{8,4},{12,16},{16,12},{20,24},{24,20},{5,9},{9,5},{13,17},{1... | collective-permute-start | bytes 147464 | tf_op jit(solution)/shard_map/ppermute | solution.py:458
  24.9 0.7 %collective-permute-start.9 = (f32[6,16,128]{2,1,0:T(8,128)S(1)}, f32[6,16,128]{2,1,0:T(8,128)S(1)}, u32[]{:S(2)}, u32[]{:S(2)}) collective-permute-start(f32[6,16,128]{2,1,0:T(8,128)S(1)} %get-tuple-element.57), channel_id=1, source_target_pairs={{0,4},{4,0},{8,12},{12,8},{16,20},{20,16},{24,28},{28,24},{1,5},{5... | collective-permute-start | bytes 147464 | tf_op jit(solution)/shard_map/ppermute | solution.py:458
  25.6 1.5 %assemble_nodes.1 = (f32[6,512,128]{2,1,0:T(8,128)S(1)}, bf16[3,512,128]{2,1,0:T(8,128)(2,1)}) custom-call(bf16[512,256]{1,0:T(8,128)(2,1)S(1)} %get-tuple-element.30.count, bf16[768,256]{1,0:T(8,128)(2,1)S(1)} %get-tuple-element.45.stress, f32[128,1536]{1,0:T(8,128)S(1)} %get-tuple-element.39.free_t, ...), custom_call_target="tpu_custom_call" | custom-call | flops 400000000 | bytes 2000000 | tf_op jit(solution)/shard_map/assemble_nodes/pallas_call | solution.py:619
  27.0 0.7 %collective-permute-done.6.sub_a = f32[6,64,128]{2,1,0:T(8,128)S(1)} collective-permute-done((f32[6,64,128]{2,1,0:T(8,128)S(1)}, f32[6,64,128]{2,1,0:T(8,128)S(1)}, u32[]{:S(2)}, u32[]{:S(2)}) %collective-permute-start.6) | collective-permute-done | bytes 196640 | tf_op jit(solution)/shard_map/ppermute | solution.py:458
  27.7 0.0 collective-permute-done.7.sub_b
  27.7 0.0 collective-permute-done.8.edge_b
  27.7 1.4 %collective-permute-done.9.edge_a = f32[6,16,128]{2,1,0:T(8,128)S(1)} collective-permute-done((f32[6,16,128]{2,1,0:T(8,128)S(1)}, f32[6,16,128]{2,1,0:T(8,128)S(1)}, u32[]{:S(2)}, u32[]{:S(2)}) %collective-permute-start.9) | collective-permute-done | bytes 49184 | tf_op jit(solution)/shard_map/ppermute | solution.py:458
  29.1 1.2 %add_last.1 = bf16[6,512,128]{2,1,0:T(8,128)(2,1)} custom-call(bf16[512,256]{1,0:T(8,128)(2,1)S(1)} %get-tuple-element.51.placing, f32[6,512,128]{2,1,0:T(8,128)S(1)} %get-tuple-element.52.partial, f32[512,128]{1,0:T(8,128)S(1)} %get-tuple-element.53.inverse_volume, f32[6,64,128]{2,1,0:T(8,128)S(1)} %collective-permute-done.6.sub_a, ...), custom_call_target="tpu_custom_call" | custom-call | flops 400000000 | bytes 3000000 | tf_op jit(solution)/shard_map/add_last/pallas_call | solution.py:628
  (3 shorter events, 0.0 us)
Async XLA Ops:
  0.6 9.0 %copy-start = (bf16[1536,24]{0,1:T(8,128)(2,1)S(1)}, bf16[1536,24]{0,1:T(8,128)(2,1)}, u32[]{:S(2)}) copy-start(bf16[1536,24]{0,1:T(8,128)(2,1)} %param.13) | copy-start | bytes 221188
  0.6 4.0 %collective-permute-start = (f32[24,128]{1,0:T(8,128)}, f32[24,128]{1,0:T(8,128)S(1)}, u32[]{:S(2)}, u32[]{:S(2)}) collective-permute-start(f32[24,128]{1,0:T(8,128)} %refs_6_.1), channel_id=1, source_target_pairs={{0,2},{1,3},{2,0},{3,1},{4,6},{5,7},{6,4},{7,5},{8,10},{9,11},{10,... | collective-permute-start | bytes 36872 | tf_op jit(solution)/shard_map/ppermute | solution.py:480
  4.6 7.2 %collective-permute-start.1 = (f32[48,128]{1,0:T(8,128)S(1)}, f32[48,128]{1,0:T(8,128)S(1)}, u32[]{:S(2)}, u32[]{:S(2)}) collective-permute-start(f32[48,128]{1,0:T(8,128)S(1)} %join_blocks.2.refs_0_), channel_id=1, source_target_pairs={{4,8},{8,4},{12,16},{16,12},{20,24},{24,20},{5,9},{9,5},{13,17},{1... | collective-permute-start | bytes 73736 | tf_op jit(solution)/shard_map/ppermute | solution.py:458
  7.9 3.9 %collective-permute-start.2 = (f32[48,128]{1,0:T(8,128)S(1)}, f32[48,128]{1,0:T(8,128)S(1)}, u32[]{:S(2)}, u32[]{:S(2)}) collective-permute-start(f32[48,128]{1,0:T(8,128)S(1)} %join_blocks.2.refs_0_), channel_id=1, source_target_pairs={{0,4},{4,0},{8,12},{12,8},{16,20},{20,16},{24,28},{28,24},{1,5},{5... | collective-permute-start | bytes 73736 | tf_op jit(solution)/shard_map/ppermute | solution.py:458
  11.8 1.3 %collective-permute-start.3 = (f32[144,128]{1,0:T(8,128)S(1)}, f32[144,128]{1,0:T(8,128)S(1)}, u32[]{:S(2)}, u32[]{:S(2)}) collective-permute-start(f32[144,128]{1,0:T(8,128)S(1)} %join_blocks.3.near), channel_id=1, source_target_pairs={{0,1},{1,0},{2,3},{3,2},{4,5},{5,4},{6,7},{7,6},{8,9},{9,8},{10,11... | collective-permute-start | bytes 221192 | tf_op jit(solution)/shard_map/ppermute | solution.py:480
  13.9 6.5 %collective-permute-start.4 = (f32[6,48,128]{2,1,0:T(8,128)S(1)}, f32[6,48,128]{2,1,0:T(8,128)S(1)}, u32[]{:S(2)}, u32[]{:S(2)}) collective-permute-start(f32[6,48,128]{2,1,0:T(8,128)S(1)} %get-tuple-element.48.grp_a), channel_id=1, source_target_pairs={{0,1},{1,0},{2,3},{3,2},{4,5},{5,4},{6,7},{7,6},{8,9},{9,8},{10,11... | collective-permute-start | bytes 442376 | tf_op jit(solution)/shard_map/ppermute | solution.py:458
  14.1 6.5 %collective-permute-start.5 = (f32[6,48,128]{2,1,0:T(8,128)S(1)}, f32[6,48,128]{2,1,0:T(8,128)S(1)}, u32[]{:S(2)}, u32[]{:S(2)}) collective-permute-start(f32[6,48,128]{2,1,0:T(8,128)S(1)} %get-tuple-element.49.grp_b), channel_id=1, source_target_pairs={{1,2},{2,1},{5,6},{6,5},{9,10},{10,9},{13,14},{14,13},{17,18},{18,... | collective-permute-start | bytes 442376 | tf_op jit(solution)/shard_map/ppermute | solution.py:458
  16.5 11.2 %collective-permute-start.6 = (f32[6,64,128]{2,1,0:T(8,128)S(1)}, f32[6,64,128]{2,1,0:T(8,128)S(1)}, u32[]{:S(2)}, u32[]{:S(2)}) collective-permute-start(f32[6,64,128]{2,1,0:T(8,128)S(1)} %get-tuple-element.54), channel_id=1, source_target_pairs={{0,4},{4,0},{8,12},{12,8},{16,20},{20,16},{24,28},{28,24},{1,5},{5... | collective-permute-start | bytes 589832 | tf_op jit(solution)/shard_map/ppermute | solution.py:458
  18.1 9.6 %collective-permute-start.7 = (f32[6,64,128]{2,1,0:T(8,128)S(1)}, f32[6,64,128]{2,1,0:T(8,128)S(1)}, u32[]{:S(2)}, u32[]{:S(2)}) collective-permute-start(f32[6,64,128]{2,1,0:T(8,128)S(1)} %get-tuple-element.55), channel_id=1, source_target_pairs={{4,8},{8,4},{12,16},{16,12},{20,24},{24,20},{5,9},{9,5},{13,17},{1... | collective-permute-start | bytes 589832 | tf_op jit(solution)/shard_map/ppermute | solution.py:458
  20.6 7.1 %collective-permute-start.8 = (f32[6,16,128]{2,1,0:T(8,128)S(1)}, f32[6,16,128]{2,1,0:T(8,128)S(1)}, u32[]{:S(2)}, u32[]{:S(2)}) collective-permute-start(f32[6,16,128]{2,1,0:T(8,128)S(1)} %get-tuple-element.56), channel_id=1, source_target_pairs={{4,8},{8,4},{12,16},{16,12},{20,24},{24,20},{5,9},{9,5},{13,17},{1... | collective-permute-start | bytes 147464 | tf_op jit(solution)/shard_map/ppermute | solution.py:458
  24.9 4.2 %collective-permute-start.9 = (f32[6,16,128]{2,1,0:T(8,128)S(1)}, f32[6,16,128]{2,1,0:T(8,128)S(1)}, u32[]{:S(2)}, u32[]{:S(2)}) collective-permute-start(f32[6,16,128]{2,1,0:T(8,128)S(1)} %get-tuple-element.57), channel_id=1, source_target_pairs={{0,4},{4,0},{8,12},{12,8},{16,20},{20,16},{24,28},{28,24},{1,5},{5... | collective-permute-start | bytes 147464 | tf_op jit(solution)/shard_map/ppermute | solution.py:458

commit v24 on v23

--- a/solution.py
+++ b/solution.py
@@ -348,21 +348,21 @@
         block = jnp.concatenate(ordered[k : k + per], axis=0).T.astype(BF16)
         values[:, k * TERM : (k + per) * TERM] = block
     moved = dot(values[...], stress_corner[...])
-    for i in range(COMPS):
-        cols = slice(i * LANES, (i + 1) * LANES)
-        free = jnp.concatenate([stress_first[i], stress_rest[i]], axis=0)
-        high, low = split_two(free - moved[:, cols])
-        stress[cols, 0:LANES] = high
-        stress[cols, LANES : 2 * LANES] = low
-
-    rows = dot_nt(face[...], stress[...])
-    for i in range(COMPS):
-        part = rows[:, i * LANES : (i + 1) * LANES]
-        edge = [part[EDGES + NED * k : EDGES + NED * (k + 1)] for k in range(4)]
-        sub_a[i] = part[:NIS]
-        sub_b[i] = part[NIS : 2 * NIS]
-        grp_a[i] = jnp.concatenate([part[2 * NIS : 2 * NIS + NIG], edge[0], edge[2]], axis=0)
-        grp_b[i] = jnp.concatenate([part[2 * NIS + NIG : EDGES], edge[1], edge[3]], axis=0)
+    for pair in range(0, COMPS, 2):
+        for i in (pair, pair + 1):
+            cols = slice(i * LANES, (i + 1) * LANES)
+            free = jnp.concatenate([stress_first[i], stress_rest[i]], axis=0)
+            high, low = split_two(free - moved[:, cols])
+            stress[cols, 0:LANES] = high
+            stress[cols, LANES : 2 * LANES] = low
+        rows = dot_nt(face[...], stress[pair * LANES : (pair + 2) * LANES, :])
+        for i in (pair, pair + 1):
+            part = rows[:, (i - pair) * LANES : (i - pair + 1) * LANES]
+            edge = [part[EDGES + NED * k : EDGES + NED * (k + 1)] for k in range(4)]
+            sub_a[i] = part[:NIS]
+            sub_b[i] = part[NIS : 2 * NIS]
+            grp_a[i] = jnp.concatenate([part[2 * NIS : 2 * NIS + NIG], edge[0], edge[2]], axis=0)
+            grp_b[i] = jnp.concatenate([part[2 * NIS + NIG : EDGES], edge[1], edge[3]], axis=0)
 
 
 def edge_kernel(grp_a, grp_b, from_a, from_b, edge_b, edge_a):

time: 30.7 us -> 30.7 us (level)
  no operation moved by 1% of the time
where the time goes in v24:
time: 30.7 us; the launch traced here: 30.3 us
  starting transfers between devices  17.1 us (56%)
  Pallas kernels  8.29 us (27%)
  waiting for transfers between devices  4.11 us (13%)
  between operations  0.74 us (2%)
    ppermute x8, starting transfers between devices, exchange(): return lax.ppermute(block, axis, pairs)  16.5 us
    ppermute x8, waiting for transfers between devices, exchange(): return lax.ppermute(block, axis, pairs)  2.25 us
    pallas_call x1, Pallas kernels, shards(): call(prepare_panels, 'prepare_panels', (array((cases, dofs)), array((2 *...  2.14 us
    pallas_call x1, Pallas kernels, shards(): call(lists, 'prepare_lists', (array(coarse.shape), array(panel_nodes.shap...  1.91 us
    ppermute x2, waiting for transfers between devices, across(): lax.ppermute(block, 'grp', [(i, i ^ distance) for i in range(lax.axis_siz...  1.86 us
    pallas_call x1, Pallas kernels, shards(): call(partial_kernel, 'assemble_nodes', (array((COMPS, nodes, cases)), arr...  1.46 us
    pallas_call x1, Pallas kernels, shards(): call(finish_kernel, 'add_last', (array((COMPS, nodes, cases), BF16),), vm...  1.21 us
    pallas_call x1, Pallas kernels, shards(): call(stress_kernel, 'stress_of_loads', (array((COMPS, cases - first, LANE...  0.83 us
  transfers between devices with their start and end apart: 10, of which 5 were waited for; matrix products, arithmetic and copies ran while one was open for 0% of the time, Pallas kernels for 21%

profile of v24, /device:TPU:10, one launch (start us, length us, event | category | flops | bytes accessed | tf_op | source)
XLA Modules:
  0.0 30.3 jit_solution(7662277194318446018)
XLA Ops:
  0.6 0.0 copy-start
  0.6 0.6 %collective-permute-start = (f32[24,128]{1,0:T(8,128)}, f32[24,128]{1,0:T(8,128)S(1)}, u32[]{:S(2)}, u32[]{:S(2)}) collective-permute-start(f32[24,128]{1,0:T(8,128)} %refs_6_.1), channel_id=1, source_target_pairs={{0,2},{1,3},{2,0},{3,1},{4,6},{5,7},{6,4},{7,5},{8,10},{9,11},{10,... | collective-permute-start | bytes 36872 | tf_op jit(solution)/shard_map/ppermute | solution.py:480
  1.2 1.9 %prepare_lists.1 = (f32[24,128]{1,0:T(8,128)S(1)}, s32[1,4]{1,0:T(1,128)S(1)}, bf16[3,512,128]{2,1,0:T(8,128)(2,1)S(1)}, bf16[4,384,384]{2,1,0:T(8,128)(2,1)S(1)...) custom-call(s32[1,24]{1,0:T(1,128)} %refs_0_.1, ...), custom_call_target="tpu_custom_call" | custom-call | flops 100000000 | bytes 4000000 | tf_op jit(solution)/shard_map/prepare_lists/pallas_call | solution.py:514
  3.2 1.4 %collective-permute-done.refs_1_ = f32[24,128]{1,0:T(8,128)S(1)} collective-permute-done((f32[24,128]{1,0:T(8,128)}, f32[24,128]{1,0:T(8,128)S(1)}, u32[]{:S(2)}, u32[]{:S(2)}) %collective-permute-start) | collective-permute-done | bytes 12320 | tf_op jit(solution)/shard_map/ppermute | solution.py:480
  4.6 3.3 %collective-permute-start.1 = (f32[48,128]{1,0:T(8,128)S(1)}, f32[48,128]{1,0:T(8,128)S(1)}, u32[]{:S(2)}, u32[]{:S(2)}) collective-permute-start(f32[48,128]{1,0:T(8,128)S(1)} %join_blocks.2.refs_0_), channel_id=1, source_target_pairs={{4,8},{8,4},{12,16},{16,12},{20,24},{24,20},{5,9},{9,5},{13,17},{1... | collective-permute-start | bytes 73736 | tf_op jit(solution)/shard_map/ppermute | solution.py:458
  7.9 1.7 %collective-permute-start.2 = (f32[48,128]{1,0:T(8,128)S(1)}, f32[48,128]{1,0:T(8,128)S(1)}, u32[]{:S(2)}, u32[]{:S(2)}) collective-permute-start(f32[48,128]{1,0:T(8,128)S(1)} %join_blocks.2.refs_0_), channel_id=1, source_target_pairs={{0,4},{4,0},{8,12},{12,8},{16,20},{20,16},{24,28},{28,24},{1,5},{5... | collective-permute-start | bytes 73736 | tf_op jit(solution)/shard_map/ppermute | solution.py:458
  9.6 0.0 copy-done
  9.6 2.1 %prepare_panels.1 = (f32[128,1536]{1,0:T(8,128)S(1)}, bf16[256,1536]{1,0:T(8,128)(2,1)S(1)}, f32[6,64,128]{2,1,0:T(8,128)S(1)}, bf16[256,768]{1,0:T(8,128)(2,1)S(1)}) custom-call(bf16[24,1536]{1,0:T(8,128)(2,1)S(1)} %bitcast.7, s32[1,4]{1,0:T(1,128)S(1)} %get-tuple-element.33.panel_v, bf16[3,512,128]{2,1,0:T(8,128)(2,1)S(1)} %get-tuple-element.34.force_v, ...), custom_call_target="tpu_custom_call" | custom-call | flops 400000000 | bytes 4000000 | tf_op jit(solution)/shard_map/prepare_panels/pallas_call | solution.py:559
  11.8 0.0 collective-permute-done.1.refs_1_
  11.8 0.0 collective-permute-done.2.refs_2_
  11.8 0.1 collective-permute-start.3
  11.9 0.8 %stress_of_loads.1 = (f32[6,64,128]{2,1,0:T(8,128)S(1)}, f32[3,32,128]{2,1,0:T(8,128)S(1)}) custom-call(f32[128,1536]{1,0:T(8,128)S(1)} %get-tuple-element.39.free_t, bf16[512,1024]{1,0:T(8,128)(2,1)S(1)} %get-tuple-element.36.onehot, f32[144,8,128]{2,1,0:T(8,128)S(1)} %get-tuple-element.37.scaled, f32[144,128]{1,0:T(8,128)S(1)} %join_blocks.3.near, ...), custom_call_target="tpu_custom_call" | custom-call | flops 400000000 | bytes 4000000 | tf_op jit(solution)/shard_map/stress_of_loads/pallas_call | solution.py:579
  12.7 0.4 %collective-permute-done.3.across = f32[144,128]{1,0:T(8,128)S(1)} collective-permute-done((f32[144,128]{1,0:T(8,128)S(1)}, f32[144,128]{1,0:T(8,128)S(1)}, u32[]{:S(2)}, u32[]{:S(2)}) %collective-permute-start.3) | collective-permute-done | bytes 73760 | tf_op jit(solution)/shard_map/ppermute | solution.py:480
  13.2 0.7 %stress_and_rows.1 = (bf16[128,256]{1,0:T(8,128)(2,1)S(1)}, bf16[768,256]{1,0:T(8,128)(2,1)S(1)}, f32[6,64,128]{2,1,0:T(8,128)S(1)}, f32[6,64,128]{2,1,0:T(8,128...) custom-call(f32[144,128]{1,0:T(8,128)S(1)} %collective-permute-done.3.across, ...), custom_call_target="tpu_custom_call" | custom-call | flops 300000000 | bytes 3000000 | tf_op jit(solution)/shard_map/stress_and_rows/pallas_call | solution.py:591
  13.9 0.2 collective-permute-start.4
  14.1 2.4 %collective-permute-start.5 = (f32[6,48,128]{2,1,0:T(8,128)S(1)}, f32[6,48,128]{2,1,0:T(8,128)S(1)}, u32[]{:S(2)}, u32[]{:S(2)}) collective-permute-start(f32[6,48,128]{2,1,0:T(8,128)S(1)} %get-tuple-element.49.grp_b), channel_id=1, source_target_pairs={{1,2},{2,1},{5,6},{6,5},{9,10},{10,9},{13,14},{14,13},{17,18},{18,... | collective-permute-start | bytes 442376 | tf_op jit(solution)/shard_map/ppermute | solution.py:458
  16.5 1.6 %collective-permute-start.6 = (f32[6,64,128]{2,1,0:T(8,128)S(1)}, f32[6,64,128]{2,1,0:T(8,128)S(1)}, u32[]{:S(2)}, u32[]{:S(2)}) collective-permute-start(f32[6,64,128]{2,1,0:T(8,128)S(1)} %get-tuple-element.54), channel_id=1, source_target_pairs={{0,4},{4,0},{8,12},{12,8},{16,20},{20,16},{24,28},{28,24},{1,5},{5... | collective-permute-start | bytes 589832 | tf_op jit(solution)/shard_map/ppermute | solution.py:458
  18.1 2.2 %collective-permute-start.7 = (f32[6,64,128]{2,1,0:T(8,128)S(1)}, f32[6,64,128]{2,1,0:T(8,128)S(1)}, u32[]{:S(2)}, u32[]{:S(2)}) collective-permute-start(f32[6,64,128]{2,1,0:T(8,128)S(1)} %get-tuple-element.55), channel_id=1, source_target_pairs={{4,8},{8,4},{12,16},{16,12},{20,24},{24,20},{5,9},{9,5},{13,17},{1... | collective-permute-start | bytes 589832 | tf_op jit(solution)/shard_map/ppermute | solution.py:458
  20.4 0.0 collective-permute-done.4.grp_a.from_a
  20.4 0.2 collective-permute-done.5.grp_b.from_b
  20.6 4.4 %collective-permute-start.8 = (f32[6,16,128]{2,1,0:T(8,128)S(1)}, f32[6,16,128]{2,1,0:T(8,128)S(1)}, u32[]{:S(2)}, u32[]{:S(2)}) collective-permute-start(f32[6,16,128]{2,1,0:T(8,128)S(1)} %get-tuple-element.56), channel_id=1, source_target_pairs={{4,8},{8,4},{12,16},{16,12},{20,24},{24,20},{5,9},{9,5},{13,17},{1... | collective-permute-start | bytes 147464 | tf_op jit(solution)/shard_map/ppermute | solution.py:458
  24.9 0.7 %collective-permute-start.9 = (f32[6,16,128]{2,1,0:T(8,128)S(1)}, f32[6,16,128]{2,1,0:T(8,128)S(1)}, u32[]{:S(2)}, u32[]{:S(2)}) collective-permute-start(f32[6,16,128]{2,1,0:T(8,128)S(1)} %get-tuple-element.57), channel_id=1, source_target_pairs={{0,4},{4,0},{8,12},{12,8},{16,20},{20,16},{24,28},{28,24},{1,5},{5... | collective-permute-start | bytes 147464 | tf_op jit(solution)/shard_map/ppermute | solution.py:458
  25.6 1.5 %assemble_nodes.1 = (f32[6,512,128]{2,1,0:T(8,128)S(1)}, bf16[3,512,128]{2,1,0:T(8,128)(2,1)}) custom-call(bf16[512,256]{1,0:T(8,128)(2,1)S(1)} %get-tuple-element.30.count, bf16[768,256]{1,0:T(8,128)(2,1)S(1)} %get-tuple-element.45.stress, f32[128,1536]{1,0:T(8,128)S(1)} %get-tuple-element.39.free_t, ...), custom_call_target="tpu_custom_call" | custom-call | flops 400000000 | bytes 2000000 | tf_op jit(solution)/shard_map/assemble_nodes/pallas_call | solution.py:619
  27.0 0.7 %collective-permute-done.6.sub_a = f32[6,64,128]{2,1,0:T(8,128)S(1)} collective-permute-done((f32[6,64,128]{2,1,0:T(8,128)S(1)}, f32[6,64,128]{2,1,0:T(8,128)S(1)}, u32[]{:S(2)}, u32[]{:S(2)}) %collective-permute-start.6) | collective-permute-done | bytes 196640 | tf_op jit(solution)/shard_map/ppermute | solution.py:458
  27.7 0.0 collective-permute-done.7.sub_b
  27.7 0.0 collective-permute-done.8.edge_b
  27.7 1.4 %collective-permute-done.9.edge_a = f32[6,16,128]{2,1,0:T(8,128)S(1)} collective-permute-done((f32[6,16,128]{2,1,0:T(8,128)S(1)}, f32[6,16,128]{2,1,0:T(8,128)S(1)}, u32[]{:S(2)}, u32[]{:S(2)}) %collective-permute-start.9) | collective-permute-done | bytes 49184 | tf_op jit(solution)/shard_map/ppermute | solution.py:458
  29.1 1.2 %add_last.1 = bf16[6,512,128]{2,1,0:T(8,128)(2,1)} custom-call(bf16[512,256]{1,0:T(8,128)(2,1)S(1)} %get-tuple-element.51.placing, f32[6,512,128]{2,1,0:T(8,128)S(1)} %get-tuple-element.52.partial, f32[512,128]{1,0:T(8,128)S(1)} %get-tuple-element.53.inverse_volume, f32[6,64,128]{2,1,0:T(8,128)S(1)} %collective-permute-done.6.sub_a, ...), custom_call_target="tpu_custom_call" | custom-call | flops 400000000 | bytes 3000000 | tf_op jit(solution)/shard_map/add_last/pallas_call | solution.py:628
  (3 shorter events, 0.0 us)
Async XLA Ops:
  0.6 9.0 %copy-start = (bf16[1536,24]{0,1:T(8,128)(2,1)S(1)}, bf16[1536,24]{0,1:T(8,128)(2,1)}, u32[]{:S(2)}) copy-start(bf16[1536,24]{0,1:T(8,128)(2,1)} %param.13) | copy-start | bytes 221188
  0.6 4.0 %collective-permute-start = (f32[24,128]{1,0:T(8,128)}, f32[24,128]{1,0:T(8,128)S(1)}, u32[]{:S(2)}, u32[]{:S(2)}) collective-permute-start(f32[24,128]{1,0:T(8,128)} %refs_6_.1), channel_id=1, source_target_pairs={{0,2},{1,3},{2,0},{3,1},{4,6},{5,7},{6,4},{7,5},{8,10},{9,11},{10,... | collective-permute-start | bytes 36872 | tf_op jit(solution)/shard_map/ppermute | solution.py:480
  4.6 7.2 %collective-permute-start.1 = (f32[48,128]{1,0:T(8,128)S(1)}, f32[48,128]{1,0:T(8,128)S(1)}, u32[]{:S(2)}, u32[]{:S(2)}) collective-permute-start(f32[48,128]{1,0:T(8,128)S(1)} %join_blocks.2.refs_0_), channel_id=1, source_target_pairs={{4,8},{8,4},{12,16},{16,12},{20,24},{24,20},{5,9},{9,5},{13,17},{1... | collective-permute-start | bytes 73736 | tf_op jit(solution)/shard_map/ppermute | solution.py:458
  7.9 3.9 %collective-permute-start.2 = (f32[48,128]{1,0:T(8,128)S(1)}, f32[48,128]{1,0:T(8,128)S(1)}, u32[]{:S(2)}, u32[]{:S(2)}) collective-permute-start(f32[48,128]{1,0:T(8,128)S(1)} %join_blocks.2.refs_0_), channel_id=1, source_target_pairs={{0,4},{4,0},{8,12},{12,8},{16,20},{20,16},{24,28},{28,24},{1,5},{5... | collective-permute-start | bytes 73736 | tf_op jit(solution)/shard_map/ppermute | solution.py:458
  11.8 1.3 %collective-permute-start.3 = (f32[144,128]{1,0:T(8,128)S(1)}, f32[144,128]{1,0:T(8,128)S(1)}, u32[]{:S(2)}, u32[]{:S(2)}) collective-permute-start(f32[144,128]{1,0:T(8,128)S(1)} %join_blocks.3.near), channel_id=1, source_target_pairs={{0,1},{1,0},{2,3},{3,2},{4,5},{5,4},{6,7},{7,6},{8,9},{9,8},{10,11... | collective-permute-start | bytes 221192 | tf_op jit(solution)/shard_map/ppermute | solution.py:480
  13.9 6.5 %collective-permute-start.4 = (f32[6,48,128]{2,1,0:T(8,128)S(1)}, f32[6,48,128]{2,1,0:T(8,128)S(1)}, u32[]{:S(2)}, u32[]{:S(2)}) collective-permute-start(f32[6,48,128]{2,1,0:T(8,128)S(1)} %get-tuple-element.48.grp_a), channel_id=1, source_target_pairs={{0,1},{1,0},{2,3},{3,2},{4,5},{5,4},{6,7},{7,6},{8,9},{9,8},{10,11... | collective-permute-start | bytes 442376 | tf_op jit(solution)/shard_map/ppermute | solution.py:458
  14.1 6.5 %collective-permute-start.5 = (f32[6,48,128]{2,1,0:T(8,128)S(1)}, f32[6,48,128]{2,1,0:T(8,128)S(1)}, u32[]{:S(2)}, u32[]{:S(2)}) collective-permute-start(f32[6,48,128]{2,1,0:T(8,128)S(1)} %get-tuple-element.49.grp_b), channel_id=1, source_target_pairs={{1,2},{2,1},{5,6},{6,5},{9,10},{10,9},{13,14},{14,13},{17,18},{18,... | collective-permute-start | bytes 442376 | tf_op jit(solution)/shard_map/ppermute | solution.py:458
  16.5 11.2 %collective-permute-start.6 = (f32[6,64,128]{2,1,0:T(8,128)S(1)}, f32[6,64,128]{2,1,0:T(8,128)S(1)}, u32[]{:S(2)}, u32[]{:S(2)}) collective-permute-start(f32[6,64,128]{2,1,0:T(8,128)S(1)} %get-tuple-element.54), channel_id=1, source_target_pairs={{0,4},{4,0},{8,12},{12,8},{16,20},{20,16},{24,28},{28,24},{1,5},{5... | collective-permute-start | bytes 589832 | tf_op jit(solution)/shard_map/ppermute | solution.py:458
  18.1 9.6 %collective-permute-start.7 = (f32[6,64,128]{2,1,0:T(8,128)S(1)}, f32[6,64,128]{2,1,0:T(8,128)S(1)}, u32[]{:S(2)}, u32[]{:S(2)}) collective-permute-start(f32[6,64,128]{2,1,0:T(8,128)S(1)} %get-tuple-element.55), channel_id=1, source_target_pairs={{4,8},{8,4},{12,16},{16,12},{20,24},{24,20},{5,9},{9,5},{13,17},{1... | collective-permute-start | bytes 589832 | tf_op jit(solution)/shard_map/ppermute | solution.py:458
  20.6 7.1 %collective-permute-start.8 = (f32[6,16,128]{2,1,0:T(8,128)S(1)}, f32[6,16,128]{2,1,0:T(8,128)S(1)}, u32[]{:S(2)}, u32[]{:S(2)}) collective-permute-start(f32[6,16,128]{2,1,0:T(8,128)S(1)} %get-tuple-element.56), channel_id=1, source_target_pairs={{4,8},{8,4},{12,16},{16,12},{20,24},{24,20},{5,9},{9,5},{13,17},{1... | collective-permute-start | bytes 147464 | tf_op jit(solution)/shard_map/ppermute | solution.py:458
  24.9 4.2 %collective-permute-start.9 = (f32[6,16,128]{2,1,0:T(8,128)S(1)}, f32[6,16,128]{2,1,0:T(8,128)S(1)}, u32[]{:S(2)}, u32[]{:S(2)}) collective-permute-start(f32[6,16,128]{2,1,0:T(8,128)S(1)} %get-tuple-element.57), channel_id=1, source_target_pairs={{0,4},{4,0},{8,12},{12,8},{16,20},{20,16},{24,28},{28,24},{1,5},{5... | collective-permute-start | bytes 147464 | tf_op jit(solution)/shard_map/ppermute | solution.py:458
